TPU v7x, 32 devices: a whole 2x2x4 slice. The times are simulated.
32 devices in a mesh: dp: 2 (over y), row: 4 (over x, core), col: 4 (over z).
Axes of the slice: x: 2, y: 2, z: 4, core: 2. Of those that a mesh axis runs over, the one named last changes fastest.
Arguments:
- tokens_in: bfloat16 [16384, 768], P(('dp', 'row', 'col')), may hold values from -6 to 6
- segment_ids: int32 [32, 512], P('dp'), may hold values from 0 to 3, never falling along the last dimension, each value on 1 to 256 neighbouring positions
- attn_gain: float32 [768], replicated, may hold values from 0.5 to 1.5
- attn_shift: float32 [768], replicated, may hold values from -1.25 to 1.25
- mlp_gain: float32 [768], replicated, may hold values from 0.5 to 1.5
- mlp_shift: float32 [768], replicated, may hold values from -1.25 to 1.25
- qkv_weight: bfloat16 [768, 2304], P('row', 'col'), may hold values from -0.21875 to 0.21875
- qkv_bias: float32 [2304], replicated, may hold values from -1.75 to 1.75
- out_weight: bfloat16 [768, 768], P('col', 'row'), may hold values from -0.875 to 0.875
- out_bias: float32 [768], replicated, may hold values from -1.75 to 1.75
- up_weight: bfloat16 [768, 3072], P('row', 'col'), may hold values from -0.21875 to 0.21875
- up_bias: float32 [3072], replicated, may hold values from -1.75 to 1.75
- down_weight: bfloat16 [3072, 768], P('col', 'row'), may hold values from -0.109375 to 0.109375
- down_bias: float32 [768], replicated, may hold values from -1.75 to 1.75
- out_cotangent: bfloat16 [16384, 768], P(('dp', 'row', 'col')), may hold values from -6 to 6
Outputs:
- block_out: bfloat16 [16384, 768], P(('dp', 'row', 'col'))
- in_grad: bfloat16 [16384, 768], P(('dp', 'row', 'col'))
- grad_attn_gain: float32 [768], replicated
- grad_attn_shift: float32 [768], replicated
- grad_mlp_gain: float32 [768], replicated
- grad_mlp_shift: float32 [768], replicated
- grad_qkv_weight: float32 [768, 2304], P('row', 'col')
- grad_qkv_bias: float32 [2304], replicated
- grad_out_weight: float32 [768, 768], P('col', 'row')
- grad_out_bias: float32 [768], replicated
- grad_up_weight: float32 [768, 3072], P('row', 'col')
- grad_up_bias: float32 [3072], replicated
- grad_down_weight: float32 [3072, 768], P('col', 'row')
- grad_down_bias: float32 [768], replicated
Inputs may be any that keep to these rules, and one draw needn't show every extreme that they name: `segment_ids`: along each sequence the numbers never fall; each document has 1 to 256 tokens, and some document of each sequence has exactly 256.
All inputs are finite; a program needn't handle non-finite values.
Results may differ from a plain program's by a relative error of at most 0.011.
Values may be sent and summed in bfloat16 or wider, within the bound.
No kernel may reach another device: no remote copies, remote signals or barrier semaphores. Data moves between devices by JAX's collectives and lax.ppermute only.
A program may use at most 384 MiB of HBM per device.

v0:
```python
import functools
import math

import jax
import jax.numpy as jnp
from jax import lax
from jax.experimental import pallas as pl
from jax.experimental.pallas import tpu as pltpu
from jax.sharding import PartitionSpec as P

HD = 64
ROT = 16
QKV = 3 * HD
HEAD = 4 * HD
EPSILON = 1e-05
ROPE_BASE = 10000.0
NEAR = 128
LONGEST = 256
F32 = jnp.float32
BF16 = jnp.bfloat16


def dot_nn(a, b):
    return lax.dot_general(a, b, (((1,), (0,)), ((), ())), preferred_element_type=F32)


def dot_nt(a, b):
    return lax.dot_general(a, b, (((1,), (1,)), ((), ())), preferred_element_type=F32)


def gathered_order(order, core_bit):
    held = [0]
    for bit in order[:-1]:
        held = held + [j | bit for j in held]
    came = [j | order[-1] for j in held]
    return held, came, [j | core_bit for j in held], [j | core_bit for j in came]


def reduced_order(order):
    kept = [0]
    for bit in order[::-1]:
        kept = kept + [j | bit for j in kept]
    return kept


def assemble(me_ref, w_refs, held, w_scr, at_col):
    for ref, pieces in zip(w_refs, held):
        _, _, rows, cols = ref.shape
        for t, j in enumerate(pieces):
            at = pl.multiple_of((me_ref[0] ^ j) * rows, 16)
            w_scr[pl.ds(at, rows), at_col : at_col + cols] = ref[t, 0]


def hand_out(me_ref, g_scr, at_col, keep_ref, send_ref, first, order, core_bit):
    _, slots, rows, cols = keep_ref.shape
    for t, j in enumerate(reduced_order(order)):
        for ref, piece in ((keep_ref, j), (send_ref, j | core_bit)):
            at = pl.multiple_of((me_ref[0] ^ piece) * rows, 16)
            for slot in range(slots):
                left = at_col + slot * cols
                ref[first + t, slot] = g_scr[pl.ds(at, rows), left : left + cols]


def normalize(x):
    center = x - jnp.mean(x, axis=1, keepdims=True)
    inv_std = lax.rsqrt(jnp.mean(center * center, axis=1, keepdims=True) + EPSILON)
    return center * inv_std, inv_std


def prep_kernel(
    x_ref, cot_ref, ga_ref, sa_ref, gm_ref, sm_ref, segc_ref, segr_ref, freq_ref,
    na_ref, naT_ref, nm_ref, nmT_ref, cotT_ref, keep_ref, ahead_ref, behind_ref, mask_ref,
):
    length = x_ref.shape[0]
    tile = 128

    @pl.loop(0, length // tile)
    def _(t):
        rows = pl.ds(pl.multiple_of(t * tile, tile), tile)
        normed, _ = normalize(x_ref[rows, :].astype(F32))
        na_ref[rows, :] = (normed * ga_ref[...] + sa_ref[...]).astype(BF16)
        nm_ref[rows, :] = (normed * gm_ref[...] + sm_ref[...]).astype(BF16)
        same = segc_ref[rows, :] == segr_ref[...]
        cols = lax.broadcasted_iota(jnp.int32, (tile, length), 1)
        ids = lax.broadcasted_iota(jnp.int32, (tile, length), 0) + t * tile
        mask_ref[rows, :] = jnp.where(same & (cols <= ids), 0.0, -jnp.inf)
        starts = jnp.min(jnp.where(same, cols, length).astype(F32), axis=1, keepdims=True)
        places = ids[:, :1].astype(F32) - starts
        angles = places * freq_ref[...]
        lane = lax.broadcasted_iota(jnp.int32, (tile, 2 * HD), 1) % HD
        cosine, sine = jnp.cos(angles), jnp.sin(angles)
        keep_ref[rows, :] = jnp.where(lane < ROT, cosine, 1.0)
        ahead_ref[rows, :] = jnp.where(lane < ROT // 2, -sine, 0.0)
        behind_ref[rows, :] = jnp.where((lane < ROT) & (lane >= ROT // 2), sine, 0.0)

    naT_ref[...] = na_ref[...].T
    nmT_ref[...] = nm_ref[...].T
    cotT_ref[...] = cot_ref[...].T


def full(*shape):
    return pl.BlockSpec(shape, lambda *_: (0,) * len(shape), pipeline_mode=pl.Buffered(1))


ANY = pl.BlockSpec(memory_space=pl.ANY)
SCALAR = pl.BlockSpec(memory_space=pltpu.SMEM)


def cost(us):
    return pl.CostEstimate(flops=int(us * 1.15e9), bytes_accessed=2**20, transcendentals=0)


def shaped(shape, dtype):
    return jax.ShapeDtypeStruct(shape, dtype)


def prep_part(tokens, cot, gains, seg_row):
    length, width = tokens.shape
    halves = ROT // 2
    step = (lax.iota(jnp.int32, 2 * HD) % HD % halves).astype(F32)
    freq = (ROPE_BASE ** (-(step * (2.0 / ROT))))[None, :]
    table = shaped((length, 2 * HD), F32)
    return pl.pallas_call(
        prep_kernel,
        grid=(1,),
        in_specs=[full(length, width)] * 2 + [full(1, width)] * 4
        + [full(length, 1), full(1, length), full(1, 2 * HD)],
        out_specs=[full(length, width), full(width, length)] * 2 + [full(width, length)]
        + [full(length, 2 * HD)] * 3 + [full(length, length)],
        out_shape=[shaped((length, width), BF16), shaped((width, length), BF16)] * 2
        + [shaped((width, length), BF16)] + [table] * 3 + [shaped((length, length), F32)],
        compiler_params=pltpu.CompilerParams(vmem_limit_bytes=60 * 2**20),
        cost_estimate=cost(6),
    )(tokens, cot, *gains, seg_row[:, None], seg_row[None, :], freq)


def attention_kernel(orders, core_bit, waits, me_ref, na_ref, naT_ref, cot_ref, cotT_ref, *rest):
    left, right, rest = rest[:4], rest[4:8], rest[8:]
    bias_ref, keep_ref, ahead_ref, behind_ref, mask_ref = rest[:5]
    dqkv_ref, mix_ref, dbias_ref, gk_ref, gs_ref, w_scr, wv_scr, qkv_scr, dattn_scr, g_scr = rest[5 + waits :]
    length, width = na_ref.shape
    block_cols = w_scr.shape[1]
    heads = block_cols // HEAD
    kept = gk_ref.shape[0] // 2
    tile = 256
    assemble(me_ref, left, gathered_order(orders[0], core_bit), w_scr, 0)
    assemble(me_ref, right, gathered_order(orders[1], core_bit), w_scr, block_cols // 2)
    for i in range(heads):
        wv_scr[:, i * 2 * HD : (i + 1) * 2 * HD] = w_scr[:, i * HEAD + 2 * HD : (i + 1) * HEAD]

    @pl.loop(0, length // tile)
    def _(t):
        rows = pl.ds(pl.multiple_of(t * tile, tile), tile)
        qkv_scr[rows, :] = dot_nn(na_ref[rows, :], w_scr[...]) + bias_ref[0]
        dattn_scr[rows, :] = dot_nn(cot_ref[rows, :], wv_scr[...]).astype(BF16)

    low = lax.broadcasted_iota(jnp.int32, (length, 2 * HD), 1) < HD
    keep, ahead, behind = keep_ref[...], ahead_ref[...], behind_ref[...]
    none = jnp.zeros((length, 2 * HD), BF16)
    spans = [(b * NEAR, (b + 1) * NEAR, max(0, b * NEAR - LONGEST)) for b in range(length // NEAR)]
    q0, k0, v1, go1, qT, goT = [], [], [], [], [], []
    for i in range(heads):
        qk = qkv_scr[:, i * HEAD : i * HEAD + 2 * HD]
        qk = qk * keep + pltpu.roll(qk, 2 * HD - ROT // 2, 1) * ahead + pltpu.roll(qk, ROT // 2, 1) * behind
        q0.append(jnp.where(low, qk * (1.0 / math.sqrt(HD)), 0.0).astype(BF16))
        k0.append(jnp.where(low, pltpu.roll(qk, HD, 1), 0.0).astype(BF16))
        value = pltpu.roll(qkv_scr[:, i * HEAD + 2 * HD : (i + 1) * HEAD], HD, 1)
        v1.append(jnp.where(low, 0.0, value).astype(BF16))
        go = dattn_scr[:, i * 2 * HD : (i + 1) * 2 * HD]
        go1.append(jnp.where(low, none, go))
        qT.append(q0[i].T[:HD])
        goT.append(go.T[HD:])
    parts = [(i, r0, r1, lo) for i in range(heads) for r0, r1, lo in spans]
    s = [dot_nt(q0[i][r0:r1], k0[i][lo:r1]) + mask_ref[r0:r1, lo:r1] for i, r0, r1, lo in parts]
    dp = [dot_nt(go1[i][r0:r1], v1[i][lo:r1]) for i, r0, r1, lo in parts]
    peak = [jnp.max(one, axis=1, keepdims=True) for one in s]
    e = [jnp.exp(one - top) for one, top in zip(s, peak)]
    norm = [1.0 / jnp.sum(one, axis=1, keepdims=True) for one in e]
    p = [one * scale for one, scale in zip(e, norm)]
    p_low = [one.astype(BF16) for one in p]
    mix = [dot_nn(one, v1[i][lo:r1]) for one, (i, r0, r1, lo) in zip(p_low, parts)]
    delta = [
        jnp.sum(one * go1[i][r0:r1].astype(F32), axis=1, keepdims=True) for one, (i, r0, r1, lo) in zip(mix, parts)
    ]
    ds = [(one * (grad - centre)).astype(BF16) for one, grad, centre in zip(p, dp, delta)]
    dq = [dot_nn(one, k0[i][lo:r1]) for one, (i, r0, r1, lo) in zip(ds, parts)]
    dkT = [dot_nn(qT[i][:, r0:r1], one) for one, (i, r0, r1, lo) in zip(ds, parts)]
    dvT = [dot_nn(goT[i][:, r0:r1], one) for one, (i, r0, r1, lo) in zip(p_low, parts)]
    for i in range(heads):
        mine = slice(i * len(spans), (i + 1) * len(spans))
        sums = []
        for group in (dvT[mine], dkT[mine]):
            total = [None] * len(spans)
            for part, (r0, r1, lo) in zip(group, spans):
                for n in range(lo // NEAR, r1 // NEAR):
                    one = part[:, n * NEAR - lo : (n + 1) * NEAR - lo]
                    total[n] = one if total[n] is None else total[n] + one
            sums.append(jnp.concatenate(total, axis=1))
        dvk = jnp.concatenate(sums, axis=0).T
        dqk = jnp.where(low, jnp.concatenate(dq[mine], axis=0) * (1.0 / math.sqrt(HD)), dvk)
        dqk = dqk * keep - pltpu.roll(dqk, 2 * HD - ROT // 2, 1) * ahead - pltpu.roll(dqk, ROT // 2, 1) * behind
        dqkv_ref[0, :, i * HEAD : i * HEAD + 2 * HD] = dqk.astype(BF16)
        dqkv_ref[0, :, i * HEAD + 2 * HD : (i + 1) * HEAD] = jnp.where(low, dvk, 0.0).astype(BF16)
        mix_ref[0, :, i * 2 * HD : (i + 1) * 2 * HD] = jnp.concatenate(mix[mine], axis=0).astype(BF16)

    dbias_ref[0] = jnp.sum(dqkv_ref[0].astype(F32), axis=0, keepdims=True)

    @pl.loop(0, width // tile)
    def _(t):
        rows = pl.ds(pl.multiple_of(t * tile, tile), tile)
        g_in = dot_nn(naT_ref[rows, :], dqkv_ref[0])
        g_out = dot_nn(cotT_ref[rows, :], mix_ref[0])
        for i in range(heads):
            at = i * HEAD
            g_scr[rows, at : at + 2 * HD] = g_in[:, at : at + 2 * HD].astype(BF16)
            g_scr[rows, at + 2 * HD : at + HEAD] = (
                g_in[:, at + 2 * HD : at + HEAD] + g_out[:, i * 2 * HD : (i + 1) * 2 * HD]
            ).astype(BF16)

    hand_out(me_ref, g_scr, 0, gk_ref, gs_ref, 0, orders[0], core_bit)
    hand_out(me_ref, g_scr, block_cols // 2, gk_ref, gs_ref, kept, orders[1], core_bit)


def mlp_kernel(orders, core_bit, waits, me_ref, nm_ref, nmT_ref, cot_ref, cotT_ref, *rest):
    left, right, bias_ref, rest = rest[:4], rest[4:8], rest[8], rest[9 + waits :]
    act_ref, dh_ref, dbias_ref, gk_ref, gs_ref, wu_scr, wd_scr, g_scr = rest
    length, width = nm_ref.shape
    up_cols = wu_scr.shape[1]
    kept = gk_ref.shape[0] // 2
    tile = 256
    assemble(me_ref, left, gathered_order(orders[0], core_bit), wu_scr, 0)
    assemble(me_ref, right, gathered_order(orders[1], core_bit), wd_scr, 0)
    dbias_ref[0] = jnp.zeros_like(dbias_ref[0])

    @pl.loop(0, length // tile)
    def _(t):
        rows = pl.ds(pl.multiple_of(t * tile, tile), tile)
        for n in range(0, up_cols, tile):
            hidden = dot_nn(nm_ref[rows, :], wu_scr[:, n : n + tile]) + bias_ref[0, :, n : n + tile]
            d_act = dot_nn(cot_ref[rows, :], wd_scr[:, n : n + tile])
            gate = 0.5 * (1.0 + lax.erf(hidden * (1.0 / math.sqrt(2.0))))
            act_ref[0, rows, n : n + tile] = (hidden * gate).astype(BF16)
            slope = gate + hidden * jnp.exp(-0.5 * hidden * hidden) * (1.0 / math.sqrt(2.0 * math.pi))
            dh = (d_act * slope).astype(BF16)
            dh_ref[0, rows, n : n + tile] = dh
            dbias_ref[0, :, n : n + tile] += jnp.sum(dh.astype(F32), axis=0, keepdims=True)

    for side, lhs, rhs in ((0, nmT_ref, dh_ref), (1, cotT_ref, act_ref)):

        @pl.loop(0, width // tile)
        def _(t):
            rows = pl.ds(pl.multiple_of(t * tile, tile), tile)
            g_scr[rows, :] = dot_nn(lhs[rows, :], rhs[0]).astype(BF16)

        hand_out(me_ref, g_scr, 0, gk_ref, gs_ref, side * kept, orders[side], core_bit)


def weight_spec(array, block_of):
    count, _, rows, cols = array.shape
    return pl.BlockSpec((count, 1, rows, cols), lambda s: (0, block_of(s), 0, 0))


def block_part(kernel, w0, k0, count, slots, slot0, into, orders, core_bit, after, me, norm, norm_t, cot, cot_t,
               left, right, vectors, mid_cols, g_cols, scratch, us):
    length, width = norm.shape
    rows = left[0].shape[2]
    pieces = width // rows
    cols = vectors[0].shape[-1]
    per_step, total_slots = slots
    g_spec = pl.BlockSpec((pieces, per_step, rows, g_cols), lambda s: (0, slot0 + s, 0, 0))
    after = list(after) + list(into)
    fixed = 5 + len(left + right) + len(vectors) + len(after)
    return pl.pallas_call(
        functools.partial(kernel, orders, core_bit, len(after)),
        grid=(count,),
        in_specs=[SCALAR, full(length, width), full(width, length), full(length, width), full(width, length)]
        + [weight_spec(w, lambda s: w0 + s) for w in left + right]
        + [pl.BlockSpec((1, 1, cols), lambda s: (k0 + s, 0, 0))]
        + [full(*v.shape) for v in vectors[1:]]
        + [ANY] * len(after),
        out_specs=[pl.BlockSpec((1, length, m), lambda s: (s, 0, 0)) for m in mid_cols]
        + [pl.BlockSpec((1, 1, cols), lambda s: (s, 0, 0))] + [g_spec] * 2,
        out_shape=[shaped((count, length, m), BF16) for m in mid_cols]
        + [shaped((count, 1, cols), F32)] + [shaped((pieces, total_slots, rows, g_cols), BF16)] * 2,
        input_output_aliases={fixed - 2: len(mid_cols) + 1, fixed - 1: len(mid_cols) + 2} if into else {},
        scratch_shapes=scratch,
        compiler_params=pltpu.CompilerParams(vmem_limit_bytes=60 * 2**20),
        cost_estimate=cost(us * count),
    )(me, norm, norm_t, cot, cot_t, *left, *right, *vectors, *after)


def pick(refs, begins, scr):
    step = pl.program_id(0)
    for ref, begin, end in zip(refs, begins, begins[1:]):

        @pl.when((step >= begin) & (step < end))
        def _():
            scr[...] = ref[0]


def attention_tail_kernel(orders, core_bit, begins, waits, me_ref, *rest):
    left, right, rest = rest[:4], rest[4:8], rest[8:]
    calls = len(begins) - 1
    dqkv_refs, mix_refs, rest = rest[:calls], rest[calls : 2 * calls], rest[2 * calls :]
    sums_in, rest = rest[: len(rest) - waits - 6], rest[len(rest) - 6 :]
    branch_ref, dna_ref, w_scr, wv_scr, dqkv_scr, mix_scr = rest
    block_cols = w_scr.shape[1]

    @pl.when(pl.program_id(0) == 0)
    def _():
        branch_ref[...] = sums_in[0][...] if sums_in else jnp.zeros_like(branch_ref)
        dna_ref[...] = sums_in[1][...] if len(sums_in) > 1 else jnp.zeros_like(dna_ref)

    pick(dqkv_refs, begins, dqkv_scr)
    pick(mix_refs, begins, mix_scr)
    assemble(me_ref, left, gathered_order(orders[0], core_bit), w_scr, 0)
    assemble(me_ref, right, gathered_order(orders[1], core_bit), w_scr, block_cols // 2)
    for i in range(block_cols // HEAD):
        wv_scr[:, i * 2 * HD : (i + 1) * 2 * HD] = w_scr[:, i * HEAD + 2 * HD : (i + 1) * HEAD]
    tile = 256

    @pl.loop(0, branch_ref.shape[0] // tile)
    def _(t):
        rows = pl.ds(pl.multiple_of(t * tile, tile), tile)
        branch_ref[rows, :] += dot_nt(mix_scr[rows, :], wv_scr[...])
        dna_ref[rows, :] += dot_nt(dqkv_scr[rows, :], w_scr[...])


def mlp_tail_kernel(orders, core_bit, sums, small_ks, waits, me_ref, *rest):
    left, right, dh_ref, act_ref, rest = rest[:4], rest[4:8], rest[8], rest[9], rest[10:]
    sums_in, rest = rest[:sums], rest[sums:]
    last = small_ks is not None
    if last:
        dna_ref, x_ref, cot_ref, ga_ref, gm_ref, bo_ref, bd_ref = rest[:7]
        small_refs = rest[7 : 7 + len(small_ks)]
        block_ref, grad_ref, stats_ref, branch_ref, dnm_ref, wu_scr, wd_scr = rest[7 + len(small_ks) + waits :]
    else:
        branch_ref, dnm_ref, wu_scr, wd_scr = rest[waits:]
    length = branch_ref.shape[0]
    step = pl.program_id(0)

    @pl.when(step == 0)
    def _():
        branch_ref[...] = sums_in[0][...] if sums else jnp.zeros_like(branch_ref)
        dnm_ref[...] = sums_in[1][...] if sums > 1 else jnp.zeros_like(dnm_ref)

    assemble(me_ref, left, gathered_order(orders[0], core_bit), wu_scr, 0)
    assemble(me_ref, right, gathered_order(orders[1], core_bit), wd_scr, 0)
    tile = 256

    @pl.loop(0, length // tile)
    def _(t):
        rows = pl.ds(pl.multiple_of(t * tile, tile), tile)
        branch_ref[rows, :] += dot_nt(act_ref[0, rows, :], wd_scr[...])
        dnm_ref[rows, :] += dot_nt(dh_ref[0, rows, :], wu_scr[...])

    if not last:
        return

    @pl.when(step == pl.num_programs(0) - 1)
    def _():
        stats_ref[...] = jnp.zeros_like(stats_ref)
        small = 128

        @pl.loop(0, length // small)
        def _(t):
            rows = pl.ds(pl.multiple_of(t * small, small), small)
            x = x_ref[rows, :].astype(F32)
            cot = cot_ref[rows, :].astype(F32)
            normed, inv_std = normalize(x)
            block_ref[rows, :] = (x + branch_ref[rows, :] + bo_ref[...] + bd_ref[...]).astype(BF16)
            dna, dnm = dna_ref[rows, :], dnm_ref[rows, :]
            d_normed = dna * ga_ref[...] + dnm * gm_ref[...]
            pulled = (
                d_normed
                - jnp.mean(d_normed, axis=1, keepdims=True)
                - normed * jnp.mean(d_normed * normed, axis=1, keepdims=True)
            )
            grad_ref[rows, :] = (cot + inv_std * pulled).astype(BF16)
            for at, term in enumerate((cot, dna * normed, dna, dnm * normed, dnm)):
                stats_ref[at : at + 1, :] += jnp.sum(term, axis=0, keepdims=True)

        for ref, (first, k0, blocks) in zip(small_refs, small_ks):
            for i in range(ref.shape[0]):
                block = lax.rem(me_ref[1] + (blocks - k0 - i), blocks)
                stats_ref[pl.ds(first + block, 1), :] = ref[i]


def attention_tail_part(begins, starts, orders, core_bit, after, me, left, right, mids, sums, us):
    steps = left[0].shape[1]
    pieces = 2 * sum(w.shape[0] for w in left) // 2
    width = pieces * left[0].shape[2]
    length = mids[0][0].shape[1]

    def mid_spec(array, n):
        begin, end = begins[n], begins[n + 1]
        return pl.BlockSpec(
            (1,) + array.shape[1:], lambda s: (jnp.clip(s - begin, 0, end - begin - 1), 0, 0)
        )

    def block_of(step):
        block = step
        for begin, start in zip(begins, starts):
            block = jnp.where(step >= begin, start + step - begin, block)
        return block

    block_cols, half_cols = mids[0][0].shape[2], mids[1][0].shape[2]
    outs = [shaped((length, width), F32)] * 2
    return pl.pallas_call(
        functools.partial(attention_tail_kernel, orders, core_bit, begins, len(after)),
        grid=(steps,),
        in_specs=[SCALAR] + [weight_spec(w, lambda s: block_of(s)) for w in left + right]
        + [mid_spec(array, n) for group in mids for n, array in enumerate(group)]
        + [full(*e.shape) for e in sums] + [ANY] * len(after),
        out_specs=[full(*o.shape) for o in outs],
        out_shape=outs,
        scratch_shapes=[pltpu.VMEM((width, block_cols), BF16), pltpu.VMEM((width, half_cols), BF16)]
        + [pltpu.VMEM(group[0].shape[1:], BF16) for group in mids],
        compiler_params=pltpu.CompilerParams(vmem_limit_bytes=60 * 2**20),
        cost_estimate=cost(us),
    )(me, *left, *right, *[array for group in mids for array in group], *sums, *after)


def mlp_tail_part(w0, orders, core_bit, after, me, left, right, act, dh, sums, finals, smalls, us):
    count, length, cols = dh.shape
    width = sum(w.shape[0] for w in left) * left[0].shape[2]
    mid_spec = pl.BlockSpec((1, length, cols), lambda s: (s, 0, 0))
    total = shaped((length, width), F32)
    scratch = [pltpu.VMEM((width, cols), BF16)] * 2
    outs, small_ks = [total] * 2, None
    if finals:
        small_ks, arrays = smalls
        blocks = small_ks[0][2]
        outs = [shaped((length, width), BF16)] * 2 + [shaped((-(-(5 + 2 * blocks) // 8) * 8, width), F32)]
        scratch = [pltpu.VMEM((length, width), F32)] * 2 + scratch
        finals = list(finals) + list(arrays)
    extra = list(sums) + list(finals)
    return pl.pallas_call(
        functools.partial(mlp_tail_kernel, orders, core_bit, len(sums), small_ks, len(after)),
        grid=(count,),
        in_specs=[SCALAR] + [weight_spec(w, lambda s: w0 + s) for w in left + right] + [mid_spec] * 2
        + [full(*e.shape) for e in extra] + [ANY] * len(after),
        out_specs=[full(*o.shape) for o in outs],
        out_shape=outs,
        scratch_shapes=scratch,
        compiler_params=pltpu.CompilerParams(vmem_limit_bytes=60 * 2**20),
        cost_estimate=cost(us),
    )(me, *left, *right, dh, act, *extra, *after)


def fence_kernel(*_):
    pass


def fence(values, after=()):
    count = len(values)
    return pl.pallas_call(
        fence_kernel,
        in_specs=[ANY] * (count + len(after)),
        out_specs=[ANY] * count,
        out_shape=[shaped(value.shape, value.dtype) for value in values],
        input_output_aliases={n: n for n in range(count)},
        cost_estimate=cost(1),
    )(*values, *after)


def swap(value, bit):
    axis, flip = ("dp", 1) if bit == 1 else ("row", bit // 2)
    return flipped(value, axis, flip)


def flipped(value, axis, flip):
    return lax.ppermute(value, axis, [(i, i ^ flip) for i in range(lax.axis_size(axis))])


def shifted(value, by):
    size = lax.axis_size("col")
    return lax.ppermute(value, "col", [(i, (i + by) % size) for i in range(size)])


class Gather:
    def __init__(self, blocks, orders, core_bit):
        cut = blocks.shape[2] // 2
        self.orders, self.core_bit, self.done = orders, core_bit, 0
        self.block = blocks[0]
        self.held = [blocks[None, :, :, :cut], blocks[None, :, :, cut:]]

    def advance(self):
        if self.done > 0:
            self.held = [jnp.concatenate(pair, axis=0) for pair in zip(self.held, self.moving)]
        self.moving = [swap(one, order[self.done]) for one, order in zip(self.held, self.orders)]
        self.done += 1

    def cross(self):
        self.over = [swap(one, self.core_bit) for one in self.held + self.moving]

    def sides(self):
        return ([self.held[i], self.moving[i], self.over[i], self.over[i + 2]] for i in range(2))


class Reduction:
    def __init__(self, keep, send, orders, core_bit):
        self.keep, self.orders, self.came = keep, orders, swap(send, core_bit)
        self.later = [[] for _ in orders]
        self.done = 0

    def half(self):
        return self.keep.shape[0] // len(self.orders) >> (self.done + 1)


def merge_kernel(layout, ins, first_out, *refs):
    outs = refs[first_out : first_out + len(layout)]
    at = 0
    for group, out in zip(layout, outs):
        column = 0
        for terms in group:
            total = refs[at][...].astype(F32)
            for ref in refs[at + 1 : at + terms]:
                total = total + ref[...].astype(F32)
            at += terms
            cols = total.shape[-1]
            out[..., column : column + cols] = total.astype(BF16)
            column += cols
    assert at == ins


def merge(reductions, after, values=()):
    specs, arrays, layout, shapes, plans = [], [], [], [], []

    def block(array, count, index):
        shape = (count,) + array.shape[1:]
        return pl.BlockSpec(shape, lambda s: (index,) + (0,) * (len(shape) - 1), pipeline_mode=pl.Buffered(1))

    for r in reductions:
        half = r.half()
        count = max(half, 1)
        size = r.keep.shape[0] // len(r.orders)
        groups = []
        for side in range(len(r.orders)):
            terms = [(one, (side * size + half) // count) for one in (r.keep, r.came)]
            terms += [(one, half // count) for one in r.later[side]]
            for one, index in terms:
                specs.append(block(one, count, index))
                arrays.append(one)
            groups.append(len(terms))
        _, slots, rows, cols = r.keep.shape
        if half:
            layout += [(terms,) for terms in groups]
            shapes += [(half, slots, rows, cols)] * len(groups)
        else:
            layout.append(tuple(groups))
            shapes.append((1, slots, rows, cols * len(groups)))
        plans.append((r, half))
    out = list(pl.pallas_call(
        functools.partial(merge_kernel, layout, len(arrays), len(arrays) + len(values) + len(after)),
        grid=(1,),
        in_specs=specs + [ANY] * (len(values) + len(after)),
        out_specs=[full(*shape) for shape in shapes] + [ANY] * len(values),
        out_shape=[shaped(shape, BF16) for shape in shapes] + [shaped(v.shape, v.dtype) for v in values],
        input_output_aliases={len(arrays) + n: len(shapes) + n for n in range(len(values))},
        compiler_params=pltpu.CompilerParams(vmem_limit_bytes=60 * 2**20),
        cost_estimate=cost(3),
    )(*arrays, *values, *after))
    token, finished = out[0], []
    passed = out[len(shapes) :]
    for r, half in plans:
        if half:
            for side, order in enumerate(r.orders):
                r.later[side].append(swap(out.pop(0), order[r.done]))
            r.done += 1
        else:
            finished.append(out.pop(0)[0])
    return finished, [token], passed


def phase(users, values=(), after=()):
    values = list(values)
    out = list(fence(values + [one for user in users for one in user.moving], after))
    at = len(values)
    for user in users:
        user.moving = out[at : at + len(user.moving)]
        at += len(user.moving)
    return out


def sum_over(value, axes):
    for axis in axes:
        flip = 1
        while flip < lax.axis_size(axis):
            value = value + flipped(value, axis, flip)
            flip *= 2
    return value


def on_device(
    tokens_in,
    segment_ids,
    attn_gain,
    attn_shift,
    mlp_gain,
    mlp_shift,
    qkv_weight,
    qkv_bias,
    out_weight,
    out_bias,
    up_weight,
    up_bias,
    down_weight,
    down_bias,
    out_cotangent,
):
    row_size = lax.axis_size("row")
    col_size = lax.axis_size("col")
    length, width = tokens_in.shape
    rows = qkv_weight.shape[0]
    half_rows = rows // 2
    local_heads = qkv_weight.shape[1] // QKV
    block_cols = local_heads * HEAD
    up_cols = up_weight.shape[1]
    row_id = lax.axis_index("row")
    col_id = lax.axis_index("col")
    half = lax.axis_index("dp") % 2
    me = jnp.stack([row_id * 2 + half, col_id]).astype(jnp.int32)
    row_bits = [2 << i for i in range(row_size.bit_length() - 1)]
    core_bit, far_bits = row_bits[0], row_bits[1:][::-1]
    orders = (far_bits + [1], [1] + far_bits)

    head_weight = jnp.concatenate(
        [qkv_weight.reshape(rows, local_heads, QKV), out_weight.T.reshape(rows, local_heads, HD)], axis=2
    ).reshape(rows, block_cols)
    attn_own = lax.dynamic_slice_in_dim(head_weight, half * half_rows, half_rows, axis=0)
    mlp_own = jnp.concatenate(
        [
            lax.dynamic_slice_in_dim(up_weight, half * half_rows, half_rows, axis=0),
            lax.dynamic_slice_in_dim(down_weight, half * half_rows, half_rows, axis=1).T,
        ],
        axis=1,
    )
    cut = block_cols // 2

    seg_row = lax.dynamic_index_in_dim(segment_ids, row_id * col_size + col_id, axis=0, keepdims=False)
    na, na_t, nm, nm_t, cot_t, keep, ahead, behind, mask = prep_part(
        tokens_in, out_cotangent, [v[None, :] for v in (attn_gain, attn_shift, mlp_gain, mlp_shift)], seg_row,
    )
    blocks_here = (col_id - jnp.arange(col_size)) % col_size
    head_bias = jnp.pad(
        qkv_bias.reshape(col_size, local_heads, QKV), ((0, 0), (0, 0), (0, HEAD - QKV))
    ).reshape(col_size, 1, block_cols)
    head_bias = jnp.take(head_bias, blocks_here, axis=0)
    hidden_bias = jnp.take(up_bias.reshape(col_size, 1, up_cols), blocks_here, axis=0)

    far = len(orders[0])

    def gather_col(own):
        return [own] + [shifted(own, k) for k in range(1, col_size)]

    attn = Gather(jnp.stack(gather_col(attn_own)), orders, core_bit)
    mlp_blocks = gather_col(fence([mlp_own], [attn.held[0]])[0])
    for _ in range(far):
        attn.advance()
        phase([attn], [], [na] if attn.done == 1 else [])
    mlp_blocks = fence(mlp_blocks, attn.moving)
    attn.cross()
    mlp = Gather(jnp.stack(mlp_blocks), orders, core_bit)
    mlp.advance()

    def attention_call(weights, w0, k0, count, slots, slot0, into, after):
        return block_part(
            attention_kernel, w0, k0, count, slots, slot0, into, orders, core_bit, after, me, na, na_t, out_cotangent,
            cot_t, *weights.sides(), [head_bias, keep, ahead, behind, mask], [block_cols, cut], cut,
            [
                pltpu.VMEM((width, block_cols), BF16), pltpu.VMEM((width, cut), BF16),
                pltpu.VMEM((length, block_cols), F32), pltpu.VMEM((length, cut), BF16),
                pltpu.VMEM((width, block_cols), BF16),
            ],
            10,
        )

    def mlp_call(weights, w0, k0, count, slots, slot0, into, after):
        return block_part(
            mlp_kernel, w0, k0, count, slots, slot0, into, orders, core_bit, after, me, nm, nm_t, out_cotangent, cot_t,
            *weights.sides(), [hidden_bias], [up_cols, up_cols], cut, [pltpu.VMEM((width, up_cols), BF16)] * 3, 6,
        )

    per_mlp = up_cols // cut
    per_call = 2
    starts = list(range(0, col_size, per_call))[::-1]
    attn_calls, into, token = [], [], []
    for k0 in starts:
        outs = attention_call(attn, k0, k0, per_call, (1, col_size), k0 // 1, into, token)
        attn_calls.append(outs)
        into = list(outs[3:])
        sent = into[1:] if k0 == starts[-1] else []
        token = phase([mlp], sent, [outs[2]])
        sent, token = token[: len(sent)], token[-1:]
        if mlp.done < far:
            mlp.advance()
            while mlp.done < far and k0 == starts[-1]:
                phase([mlp])
                mlp.advance()
    while mlp.done < far:
        mlp.advance()
        token = phase([mlp])[:1]
    mlp.cross()
    attn_sum = Reduction(into[0], sent[0], orders, core_bit)

    mlp_calls, mlp_sums = [], []
    for k0 in starts:
        outs = mlp_call(mlp, k0, k0, per_call, (per_mlp, per_mlp * per_call), 0, [], token)
        mlp_calls.append(outs)
        _, token, sent = merge([attn_sum] + mlp_sums, [outs[2]], [outs[4]])
        mlp_sums.append(Reduction(outs[3], sent[0], orders, core_bit))
    begins = list(range(0, col_size + 1, per_call))
    branch, d_norm_attn = attention_tail_part(
        begins, starts, orders, core_bit, token, me, *attn.sides(), [[c[0] for c in attn_calls], [c[1] for c in attn_calls]],
        [], 11,
    )
    totals = {}

    def go_on(after):
        open_ones = [r for r in [attn_sum] + mlp_sums if id(r) not in totals]
        ending = [r for r in open_ones if not r.half()]
        finished, token, _ = merge(open_ones, after)
        for r, total in zip(ending, finished):
            totals[id(r)] = total
        return token

    moves = {}

    def send_home(k, parts):
        part = jnp.concatenate(parts, axis=1)
        moves[k] = part if k == 0 else shifted(part, -k)

    small_ks = tuple((5, k0, col_size) for k0 in starts) + tuple((5 + col_size, k0, col_size) for k0 in starts)
    small_parts = [c[2] for c in mlp_calls] + [c[2] for c in attn_calls]
    token = go_on([branch])
    d_norm_mlp = None
    for n, k0 in enumerate(starts):
        last = n == len(starts) - 1
        sums = [branch] if n == 0 else [branch, d_norm_mlp]
        finals = [
            d_norm_attn, tokens_in, out_cotangent, attn_gain[None, :], mlp_gain[None, :], out_bias[None, :],
            down_bias[None, :],
        ]
        result = mlp_tail_part(
            k0, orders, core_bit, token, me, *mlp.sides(), mlp_calls[n][0], mlp_calls[n][1], sums,
            finals if last else [], (small_ks, small_parts) if last else None, 9,
        )
        token = go_on(result[2:] if last else result[:1])
        if last:
            block_out, in_grad, smalls = result
        else:
            branch, d_norm_mlp = result
        for at, k1 in enumerate(starts):
            if id(mlp_sums[at]) in totals and id(attn_sum) in totals and k1 not in moves:
                attn_total, mlp_total = totals[id(attn_sum)], totals[id(mlp_sums[at])]
                for i in range(per_call):
                    send_home(k1 + i, [attn_total[k1 + i]] + [mlp_total[i * per_mlp + j] for j in range(per_mlp)])
    while len(moves) < col_size:
        token = go_on(token)
        for at, k1 in enumerate(starts):
            if id(mlp_sums[at]) in totals and k1 not in moves:
                attn_total, mlp_total = totals[id(attn_sum)], totals[id(mlp_sums[at])]
                for i in range(per_call):
                    send_home(k1 + i, [attn_total[k1 + i]] + [mlp_total[i * per_mlp + j] for j in range(per_mlp)])
    head_row, up_row = 5 + col_size, 5
    smalls = sum_over(smalls, ("row", "dp"))
    smalls, *came = fence([smalls] + [moves[k] for k in range(1, col_size)])

    total = sum((move.astype(F32) for move in came), moves[0].astype(F32))
    flip = 2
    while flip < lax.axis_size("dp"):
        total = total + flipped(total, "dp", flip)
        flip *= 2
    mine = total.astype(BF16)
    other = swap(mine, 1)
    first = half == 0
    grads = jnp.concatenate([jnp.where(first, mine, other), jnp.where(first, other, mine)], axis=0).astype(F32)
    g_heads = grads[:, :block_cols].reshape(rows, local_heads, HEAD)
    sides = grads[:, block_cols:].reshape(rows, per_mlp, 2, cut)
    g_up = sides[:, :, 0].reshape(rows, up_cols)
    g_down = sides[:, :, 1].reshape(rows, up_cols)
    smalls = sum_over(smalls, ("col",))
    return (
        block_out,
        in_grad,
        smalls[1],
        smalls[2],
        smalls[3],
        smalls[4],
        g_heads[:, :, :QKV].reshape(rows, local_heads * QKV),
        smalls[head_row : head_row + col_size].reshape(col_size * local_heads, HEAD)[:, :QKV].reshape(-1),
        g_heads[:, :, QKV:].reshape(rows, local_heads * HD).T,
        smalls[0],
        g_up,
        smalls[up_row : up_row + col_size].reshape(-1),
        g_down.T,
        smalls[0],
    )


def solution(mesh):
    return jax.shard_map(
        on_device,
        mesh=mesh,
        in_specs=(
            P(("dp", "row", "col"), None),
            P("dp", None),
            P(),
            P(),
            P(),
            P(),
            P("row", "col"),
            P(),
            P("col", "row"),
            P(),
            P("row", "col"),
            P(),
            P("col", "row"),
            P(),
            P(("dp", "row", "col"), None),
        ),
        out_specs=(
            P(("dp", "row", "col"), None),
            P(("dp", "row", "col"), None),
            P(),
            P(),
            P(),
            P(),
            P("row", "col"),
            P(),
            P("col", "row"),
            P(),
            P("row", "col"),
            P(),
            P("col", "row"),
            P(),
        ),
        check_vma=False,
    )
```

profile of v0, /device:TPU:0, one launch (start us, length us, event | category | flops | bytes accessed | tf_op | source)
XLA Modules:
  0.0 288.2 jit_solution(831267899630379587)
XLA Ops:
  3.1 5.1 %collective-permute-start.2 = (bf16[96,768]{1,0:T(8,128)(2,1)S(1)}, bf16[96,768]{1,0:T(8,128)(2,1)S(1)}, u32[]{:S(2)}, u32[]{:S(2)}) collective-permute-start(bf16[96,768]{1,0:T(8,128)(2,1)S(1)} %copy.66), channel_id=1, source_target_pairs={{0,3},{1,0},{2,1},{3,2},{4,7},{5,4},{6,5},{7,6},{8,11},{9,8},{10,9... | collective-permute-start | bytes 442376 | tf_op jit(solution)/shard_map/ppermute | solution.py:478
  15.0 6.0 %shard_map.255 = (bf16[512,768]{1,0:T(8,128)(2,1)}, bf16[768,512]{1,0:T(8,128)(2,1)}, bf16[512,768]{1,0:T(8,128)(2,1)}, bf16[768,512]{1,0:T(8,128)(2,1)}, bf16[7...) custom-call(bf16[512,768]{1,0:T(8,128)(2,1)} %rest_13_.1, ...), custom_call_target="tpu_custom_call" | custom-call | flops 6899999744 | bytes 1048576 | tf_op jit(solution)/shard_map/pallas_call | solution.py:123
  21.3 1.6 collective-permute-start.6
  22.9 1.5 collective-permute-start.7
  24.5 4.8 %collective-permute-done.6.__0_ = bf16[1,4,96,384]{3,2,1,0:T(8,128)(2,1)S(1)} collective-permute-done((bf16[1,4,96,384]{3,2,1,0:T(8,128)(2,1)S(1)}, bf16[1,4,96,384]{3,2,1,0:T(8,128)(2,1)S(1)}, u32[]{:S(2)}, u32[]{:S(2)}) %collective-permute-start.6) | collective-permute-done | bytes 294944 | tf_op jit(solution)/shard_map/ppermute | solution.py:473
  32.3 1.6 collective-permute-start.8
  37.1 2.5 collective-permute-start.3
  40.7 1.8 collective-permute-start.5
  43.3 2.3 collective-permute-done.8.__0_
  46.9 2.2 collective-permute-done.3.__1_
  49.1 9.0 %collective-permute-done.4.__2_ = bf16[96,1536]{1,0:T(8,128)(2,1)S(1)} collective-permute-done((bf16[96,1536]{1,0:T(8,128)(2,1)}, bf16[96,1536]{1,0:T(8,128)(2,1)S(1)}, u32[]{:S(2)}, u32[]{:S(2)}) %collective-permute-start.4) | collective-permute-done | bytes 294944 | tf_op jit(solution)/shard_map/ppermute | solution.py:478
  61.0 1.5 collective-permute-start.10
  63.0 17.2 %shard_map.259 = (bf16[2,512,768]{2,1,0:T(8,128)(2,1)}, bf16[2,512,384]{2,1,0:T(8,128)(2,1)}, f32[2,1,768]{2,1,0:T(1,128)}, bf16[8,4,96,384]{3,2,1,0:T(8,128)(2,1)}, bf16[8,4,96,384]{3,2,1,0:T(8,128)(2,1)}) custom-call(s32[2]{0:T(128)} %pad_add_fusion.me_ref, bf16[512,768]{1,0:T(8,128)(2,1)} %get-tuple-element.84.__2_.na_ref, ...), custom_call_target="tpu_custom_call" | custom-call | flops 23000000512 | bytes 1048576 | tf_op jit(solution)/shard_map/pallas_call | solution.py:273
  81.2 2.3 pad_maximum_fusion.1.rest_0_
  83.5 1.5 collective-permute-start.16
  87.1 17.0 %shard_map.261 = (bf16[2,512,768]{2,1,0:T(8,128)(2,1)}, bf16[2,512,384]{2,1,0:T(8,128)(2,1)}, f32[2,1,768]{2,1,0:T(1,128)}, bf16[8,4,96,384]{3,2,1,0:T(8,128)(2,1)}, bf16[8,4,96,384]{3,2,1,0:T(8,128)(2,1)}) custom-call(s32[2]{0:T(128)} %pad_add_fusion.me_ref, ...), custom_call_target="tpu_custom_call", output_to_operand_aliasing={{3}: (19, {}), {4}: (20, {})} | custom-call | flops 23000000512 | bytes 1048576 | tf_op jit(solution)/shard_map/pallas_call | solution.py:273
  104.1 6.9 %collective-permute-done.16.__1_ = bf16[2,4,96,768]{3,2,1,0:T(8,128)(2,1)S(1)} collective-permute-done((bf16[2,4,96,768]{3,2,1,0:T(8,128)(2,1)}, bf16[2,4,96,768]{3,2,1,0:T(8,128)(2,1)S(1)}, u32[]{:S(2)}, u32[]{:S(2)}) %collective-permute-start.16) | collective-permute-done | bytes 1179680 | tf_op jit(solution)/shard_map/ppermute | solution.py:473
  110.9 3.9 %collective-permute-done.17.__2_ = bf16[2,4,96,768]{3,2,1,0:T(8,128)(2,1)S(1)} collective-permute-done((bf16[2,4,96,768]{3,2,1,0:T(8,128)(2,1)}, bf16[2,4,96,768]{3,2,1,0:T(8,128)(2,1)S(1)}, u32[]{:S(2)}, u32[]{:S(2)}) %collective-permute-start.17) | collective-permute-done | bytes 1179680 | tf_op jit(solution)/shard_map/ppermute | solution.py:473
  116.4 4.2 %collective-permute-done.19.rest_3_ = bf16[2,4,96,768]{3,2,1,0:T(8,128)(2,1)S(1)} collective-permute-done((bf16[2,4,96,768]{3,2,1,0:T(8,128)(2,1)}, bf16[2,4,96,768]{3,2,1,0:T(8,128)(2,1)S(1)}, u32[]{:S(2)}, u32[]{:S(2)}) %collective-permute-start.19) | collective-permute-done | bytes 1179680 | tf_op jit(solution)/shard_map/ppermute | solution.py:473
  120.6 1.5 collective-permute-done.21.rest_7_
  122.1 13.5 %shard_map.263 = (bf16[2,512,768]{2,1,0:T(8,128)(2,1)}, bf16[2,512,768]{2,1,0:T(8,128)(2,1)}, f32[2,1,768]{2,1,0:T(1,128)}, bf16[8,4,96,384]{3,2,1,0:T(8,128)(2,1)}, bf16[8,4,96,384]{3,2,1,0:T(8,128)(2,1)}) custom-call(s32[2]{0:T(128)} %pad_add_fusion.me_ref, bf16[512,768]{1,0:T(8,128)(2,1)} %get-tuple-element.108.nm_ref, ...), custom_call_target="tpu_custom_call" | custom-call | flops 13799999488 | bytes 1048576 | tf_op jit(solution)/shard_map/pallas_call | solution.py:273
  135.5 1.5 copy-done.3
  137.0 2.7 shard_map.264
  141.3 13.4 %shard_map.265 = (bf16[2,512,768]{2,1,0:T(8,128)(2,1)}, bf16[2,512,768]{2,1,0:T(8,128)(2,1)}, f32[2,1,768]{2,1,0:T(1,128)}, bf16[8,4,96,384]{3,2,1,0:T(8,128)(2,1)}, bf16[8,4,96,384]{3,2,1,0:T(8,128)(2,1)}) custom-call(s32[2]{0:T(128)} %pad_add_fusion.me_ref, bf16[512,768]{1,0:T(8,128)(2,1)} %get-tuple-element.108.nm_ref, ...), custom_call_target="tpu_custom_call" | custom-call | flops 13799999488 | bytes 1048576 | tf_op jit(solution)/shard_map/pallas_call | solution.py:273
  157.8 3.5 %shard_map.266 = (bf16[1,4,96,384]{3,2,1,0:T(8,128)(2,1)}, bf16[1,4,96,384]{3,2,1,0:T(8,128)(2,1)}, bf16[2,4,96,384]{3,2,1,0:T(8,128)(2,1)}, bf16[2,4,96,384]{3,2,1,0:T(8,128)(2,1)}, bf16[8,4,96,384]{3,2,1,0:T(8,128)(2,1)}) custom-call(bf16[8,4,96,384]{3,2,1,0:T(8,128)(2,1)} %get-tuple-element.110.refs_0_.refs_2_.refs_3_.refs_4_, ...), custom_call_target="tpu_custom_call", output_to_operand_aliasing={{4}: (10, {})} | custom-call | flops 3449999872 | bytes 1048576 | tf_op jit(solution)/shard_map/pallas_call | solution.py:554
  165.0 1.5 collective-permute-start.29
  166.5 11.3 %shard_map.267 = (f32[512,768]{1,0:T(8,128)}, f32[512,768]{1,0:T(8,128)}) custom-call(s32[2]{0:T(128)} %pad_add_fusion.me_ref, bf16[2,4,96,384]{3,2,1,0:T(8,128)(2,1)} %copy-done.14, bf16[2,4,96,384]{3,2,1,0:T(8,128)(2,1)} %get-tuple-element.87.__4_.rest_1_, bf16[2,4,96,384]{3,2,1,0:T(8,128)(2,1)} %collective-permute-done.12.rest_2_, ...), custom_call_target="tpu_custom_call" | custom-call | flops 12650000384 | bytes 1048576 | tf_op jit(solution)/shard_map/pallas_call | solution.py:409
  177.8 7.1 %collective-permute-done.28.refs_10_.refs_2_ = bf16[2,4,96,384]{3,2,1,0:T(8,128)(2,1)S(1)} collective-permute-done((bf16[2,4,96,384]{3,2,1,0:T(8,128)(2,1)}, bf16[2,4,96,384]{3,2,1,0:T(8,128)(2,1)S(1)}, u32[]{:S(2)}, u32[]{:S(2)}) %collective-permute-start.28) | collective-permute-done | bytes 589856 | tf_op jit(solution)/shard_map/ppermute | solution.py:473
  186.8 4.5 %shard_map.268 = (bf16[1,4,96,768]{3,2,1,0:T(8,128)(2,1)}, bf16[1,4,96,384]{3,2,1,0:T(8,128)(2,1)}, bf16[1,4,96,384]{3,2,1,0:T(8,128)(2,1)}, bf16[2,4,96,384]{3,2,1,0:T(8,128)(2,1)}, bf16[2,4,96,384]{3,2,1,0:T(8,128)(2,1)}) custom-call(bf16[8,4,96,384]{3,2,1,0:T(8,128)(2,1)} %get-tuple-element.110.refs_0_.refs_2_.refs_3_.refs_4_, ...), custom_call_target="tpu_custom_call" | custom-call | flops 3449999872 | bytes 1048576 | tf_op jit(solution)/shard_map/pallas_call | solution.py:554
  191.3 1.5 collective-permute-start.31
  195.4 8.3 %shard_map.269 = (f32[512,768]{1,0:T(8,128)}, f32[512,768]{1,0:T(8,128)}) custom-call(s32[2]{0:T(128)} %pad_add_fusion.me_ref, bf16[2,4,96,768]{3,2,1,0:T(8,128)(2,1)} %pad_maximum_fusion.1.rest_0_, bf16[2,4,96,768]{3,2,1,0:T(8,128)(2,1)} %get-tuple-element.106.rest_1_, bf16[2,4,96,768]{3,2,1,0:T(8,128)(2,1)} %collective-permute-done.18.rest_2_, ...), custom_call_target="tpu_custom_call" | custom-call | flops 10350000128 | bytes 1048576 | tf_op jit(solution)/shard_map/pallas_call | solution.py:438
  203.7 10.0 %collective-permute-done.33.refs_10_.refs_2_ = bf16[2,4,96,384]{3,2,1,0:T(8,128)(2,1)S(1)} collective-permute-done((bf16[2,4,96,384]{3,2,1,0:T(8,128)(2,1)}, bf16[2,4,96,384]{3,2,1,0:T(8,128)(2,1)S(1)}, u32[]{:S(2)}, u32[]{:S(2)}) %collective-permute-start.33) | collective-permute-done | bytes 589856 | tf_op jit(solution)/shard_map/ppermute | solution.py:473
  214.7 3.4 %shard_map.270 = (bf16[1,4,96,768]{3,2,1,0:T(8,128)(2,1)}, bf16[1,4,96,384]{3,2,1,0:T(8,128)(2,1)}, bf16[1,4,96,384]{3,2,1,0:T(8,128)(2,1)}) custom-call(bf16[8,4,96,384]{3,2,1,0:T(8,128)(2,1)} %get-tuple-element.124.refs_6_.refs_8_.refs_11_.refs_0_.refs_4_, bf16[8,4,96,384]{3,2,1,0:T(8,128)(2,1)} %copy-done.2, bf16[2,4,96,384]{3,2,1,0:T(8,128)(2,1)} %copy-done.5, ...), custom_call_target="tpu_custom_call" | custom-call | flops 3449999872 | bytes 1048576 | tf_op jit(solution)/shard_map/pallas_call | solution.py:554
  221.3 5.2 %collective-permute-start.41 = (bf16[96,2304]{1,0:T(8,128)(2,1)S(1)}, bf16[96,2304]{1,0:T(8,128)(2,1)S(1)}, u32[]{:S(2)}, u32[]{:S(2)}) collective-permute-start(bf16[96,2304]{1,0:T(8,128)(2,1)S(1)} %pad_maximum_fusion.8), channel_id=1, source_target_pairs={{0,2},{1,3},{2,0},{3,1},{4,6},{5,7},{6,4},{7,5},{8,10},{9,11},{10,... | collective-permute-start | bytes 1327112 | tf_op jit(solution)/shard_map/ppermute | solution.py:478
  226.6 3.5 %collective-permute-start.42 = (bf16[96,2304]{1,0:T(8,128)(2,1)S(1)}, bf16[96,2304]{1,0:T(8,128)(2,1)S(1)}, u32[]{:S(2)}, u32[]{:S(2)}) collective-permute-start(bf16[96,2304]{1,0:T(8,128)(2,1)S(1)} %pad_maximum_fusion.9), channel_id=1, source_target_pairs={{0,1},{1,2},{2,3},{3,0},{4,5},{5,6},{6,7},{7,4},{8,9},{9,10},{10,1... | collective-permute-start | bytes 1327112 | tf_op jit(solution)/shard_map/ppermute | solution.py:478
  230.1 10.8 %shard_map.271 = (bf16[512,768]{1,0:T(8,128)(2,1)}, bf16[512,768]{1,0:T(8,128)(2,1)}, f32[16,768]{1,0:T(8,128)}) custom-call(s32[2]{0:T(128)} %pad_add_fusion.me_ref, bf16[2,4,96,768]{3,2,1,0:T(8,128)(2,1)} %pad_maximum_fusion.1.rest_0_, bf16[2,4,96,768]{3,2,1,0:T(8,128)(2,1)} %get-tuple-element.106.rest_1_, ...), custom_call_target="tpu_custom_call" | custom-call | flops 10350000128 | bytes 1048576 | tf_op jit(solution)/shard_map/pallas_call | solution.py:438
  241.7 2.7 shard_map.272
  248.2 3.5 %collective-permute-done.36 = f32[16,768]{1,0:T(8,128)S(1)} collective-permute-done((f32[16,768]{1,0:T(8,128)S(1)}, f32[16,768]{1,0:T(8,128)S(1)}, u32[]{:S(2)}, u32[]{:S(2)}) %collective-permute-start.36) | collective-permute-done | bytes 49184 | tf_op jit(solution)/shard_map/ppermute | solution.py:473
  251.7 1.6 collective-permute-start.37
  253.3 2.6 collective-permute-done.37
  256.6 6.3 %collective-permute-done.40.__1_ = bf16[96,2304]{1,0:T(8,128)(2,1)S(1)} collective-permute-done((bf16[96,2304]{1,0:T(8,128)(2,1)S(1)}, bf16[96,2304]{1,0:T(8,128)(2,1)S(1)}, u32[]{:S(2)}, u32[]{:S(2)}) %collective-permute-start.40) | collective-permute-done | bytes 442400 | tf_op jit(solution)/shard_map/ppermute | solution.py:478
  263.7 1.5 add_convert_fusion
  265.2 1.6 collective-permute-start.45
  266.8 1.5 collective-permute-start.43
  268.3 2.6 collective-permute-done.43
  270.9 3.5 %collective-permute-start.44 = (f32[16,768]{1,0:T(8,128)S(1)}, f32[16,768]{1,0:T(8,128)S(1)}, u32[]{:S(2)}, u32[]{:S(2)}) collective-permute-start(f32[16,768]{1,0:T(8,128)S(1)} %add.89), channel_id=1, source_target_pairs={{0,2},{1,3},{2,0},{3,1},{4,6},{5,7},{6,4},{7,5},{8,10},{9,11},{10,... | collective-permute-start | bytes 147464 | tf_op jit(solution)/shard_map/ppermute | solution.py:473
  274.4 2.1 collective-permute-done.44
  282.2 3.7 %slice_reduce_fusion = (f32[192,2,384]{2,1,0:T(2,128)S(1)}, f32[192,2,384]{2,1,0:T(2,128)S(1)}) fusion(f32[192,2,2,384]{3,2,1,0:T(2,128)S(1)} %reshape.200), kind=kLoop, calls=%fused_computation.6 | loop fusion | bytes 2359296 | tf_op jit(solution)/shard_map/slice | solution.py:782
  (226 shorter events, 57.7 us)
Async XLA Ops:
  0.6 23.8 %copy-start = (bf16[768,192]{0,1:T(8,128)(2,1)S(1)}, bf16[768,192]{0,1:T(8,128)(2,1)}, u32[]{:S(2)}) copy-start(bf16[768,192]{0,1:T(8,128)(2,1)} %param.29) | copy-start | bytes 884740
  3.1 18.0 %collective-permute-start.2 = (bf16[96,768]{1,0:T(8,128)(2,1)S(1)}, bf16[96,768]{1,0:T(8,128)(2,1)S(1)}, u32[]{:S(2)}, u32[]{:S(2)}) collective-permute-start(bf16[96,768]{1,0:T(8,128)(2,1)S(1)} %copy.66), channel_id=1, source_target_pairs={{0,3},{1,0},{2,1},{3,2},{4,7},{5,4},{6,5},{7,6},{8,11},{9,8},{10,9... | collective-permute-start | bytes 442376 | tf_op jit(solution)/shard_map/ppermute | solution.py:478
  8.2 12.9 %collective-permute-start.1 = (bf16[96,768]{1,0:T(8,128)(2,1)S(1)}, bf16[96,768]{1,0:T(8,128)(2,1)S(1)}, u32[]{:S(2)}, u32[]{:S(2)}) collective-permute-start(bf16[96,768]{1,0:T(8,128)(2,1)S(1)} %copy.66), channel_id=1, source_target_pairs={{0,2},{1,3},{2,0},{3,1},{4,6},{5,7},{6,4},{7,5},{8,10},{9,11},{10,... | collective-permute-start | bytes 442376 | tf_op jit(solution)/shard_map/ppermute | solution.py:478
  8.2 12.9 %collective-permute-start = (bf16[96,768]{1,0:T(8,128)(2,1)S(1)}, bf16[96,768]{1,0:T(8,128)(2,1)S(1)}, u32[]{:S(2)}, u32[]{:S(2)}) collective-permute-start(bf16[96,768]{1,0:T(8,128)(2,1)S(1)} %copy.66), channel_id=1, source_target_pairs={{0,1},{1,2},{2,3},{3,0},{4,5},{5,6},{6,7},{7,4},{8,9},{9,10},{10,1... | collective-permute-start | bytes 442376 | tf_op jit(solution)/shard_map/ppermute | solution.py:478
  21.3 8.0 %collective-permute-start.6 = (bf16[1,4,96,384]{3,2,1,0:T(8,128)(2,1)S(1)}, bf16[1,4,96,384]{3,2,1,0:T(8,128)(2,1)S(1)}, u32[]{:S(2)}, u32[]{:S(2)}) collective-permute-start(bf16[1,4,96,384]{3,2,1,0:T(8,128)(2,1)S(1)} %get-tuple-element.205.__1_), channel_id=1, source_target_pairs={{0,8},{4,12},{8,0},{12,4},{1,9},{5,13},{9,1},{13,5},{2,10},{6,14},... | collective-permute-start | bytes 884744 | tf_op jit(solution)/shard_map/ppermute | solution.py:473
  22.9 7.6 %collective-permute-start.7 = (bf16[1,4,96,384]{3,2,1,0:T(8,128)(2,1)S(1)}, bf16[1,4,96,384]{3,2,1,0:T(8,128)(2,1)S(1)}, u32[]{:S(2)}, u32[]{:S(2)}) collective-permute-start(bf16[1,4,96,384]{3,2,1,0:T(8,128)(2,1)S(1)} %get-tuple-element.204), channel_id=1, source_target_pairs={{0,16},{16,0},{1,17},{17,1},{2,18},{18,2},{3,19},{19,3},{4,20},{20... | collective-permute-start | bytes 884744 | tf_op jit(solution)/shard_map/ppermute | solution.py:473
  32.3 13.2 %copy-start.14 = (bf16[2,4,96,384]{3,2,1,0:T(8,128)(2,1)}, bf16[2,4,96,384]{3,2,1,0:T(8,128)(2,1)S(1)}, u32[]{:S(2)}) copy-start(bf16[2,4,96,384]{3,2,1,0:T(8,128)(2,1)S(1)} %pad_maximum_fusion.5.rest_0_) | copy-start | bytes 1769476
  32.3 13.2 %collective-permute-start.8 = (bf16[2,4,96,384]{3,2,1,0:T(8,128)(2,1)S(1)}, bf16[2,4,96,384]{3,2,1,0:T(8,128)(2,1)}, u32[]{:S(2)}, u32[]{:S(2)}) collective-permute-start(bf16[2,4,96,384]{3,2,1,0:T(8,128)(2,1)S(1)} %pad_maximum_fusion.5.rest_0_), channel_id=1, source_target_pairs={{0,16},{16,0},{1,17},{17,1},{2,18},{18,2},{3,19},{19,3},{4,20},{20... | collective-permute-start | bytes 1769480 | tf_op jit(solution)/shard_map/ppermute | solution.py:473
  34.0 12.9 %collective-permute-start.9 = (bf16[2,4,96,384]{3,2,1,0:T(8,128)(2,1)S(1)}, bf16[2,4,96,384]{3,2,1,0:T(8,128)(2,1)}, u32[]{:S(2)}, u32[]{:S(2)}) collective-permute-start(bf16[2,4,96,384]{3,2,1,0:T(8,128)(2,1)S(1)} %pad_maximum_fusion.6.rest_4_), channel_id=1, source_target_pairs={{0,8},{4,12},{8,0},{12,4},{1,9},{5,13},{9,1},{13,5},{2,10},{6,14},... | collective-permute-start | bytes 1769480 | tf_op jit(solution)/shard_map/ppermute | solution.py:473
  37.1 12.0 %collective-permute-start.3 = (bf16[96,1536]{1,0:T(8,128)(2,1)}, bf16[96,1536]{1,0:T(8,128)(2,1)S(1)}, u32[]{:S(2)}, u32[]{:S(2)}) collective-permute-start(bf16[96,1536]{1,0:T(8,128)(2,1)} %shard_map.254.__0_), channel_id=1, source_target_pairs={{0,1},{1,2},{2,3},{3,0},{4,5},{5,6},{6,7},{7,4},{8,9},{9,10},{10,1... | collective-permute-start | bytes 884744 | tf_op jit(solution)/shard_map/ppermute | solution.py:478
  39.5 18.6 %collective-permute-start.4 = (bf16[96,1536]{1,0:T(8,128)(2,1)}, bf16[96,1536]{1,0:T(8,128)(2,1)S(1)}, u32[]{:S(2)}, u32[]{:S(2)}) collective-permute-start(bf16[96,1536]{1,0:T(8,128)(2,1)} %shard_map.254.__0_), channel_id=1, source_target_pairs={{0,2},{1,3},{2,0},{3,1},{4,6},{5,7},{6,4},{7,5},{8,10},{9,11},{10,... | collective-permute-start | bytes 884744 | tf_op jit(solution)/shard_map/ppermute | solution.py:478
  40.7 17.4 %collective-permute-start.5 = (bf16[96,1536]{1,0:T(8,128)(2,1)}, bf16[96,1536]{1,0:T(8,128)(2,1)S(1)}, u32[]{:S(2)}, u32[]{:S(2)}) collective-permute-start(bf16[96,1536]{1,0:T(8,128)(2,1)} %shard_map.254.__0_), channel_id=1, source_target_pairs={{0,3},{1,0},{2,1},{3,2},{4,7},{5,4},{6,5},{7,6},{8,11},{9,8},{10,9... | collective-permute-start | bytes 884744 | tf_op jit(solution)/shard_map/ppermute | solution.py:478
  45.5 17.0 %collective-permute-start.12 = (bf16[2,4,96,384]{3,2,1,0:T(8,128)(2,1)S(1)}, bf16[2,4,96,384]{3,2,1,0:T(8,128)(2,1)}, u32[]{:S(2)}, u32[]{:S(2)}) collective-permute-start(bf16[2,4,96,384]{3,2,1,0:T(8,128)(2,1)S(1)} %pad_maximum_fusion.5.rest_0_), channel_id=1, source_target_pairs={{0,4},{4,0},{8,12},{12,8},{1,5},{5,1},{9,13},{13,9},{2,6},{6,2},{1... | collective-permute-start | bytes 1769480 | tf_op jit(solution)/shard_map/ppermute | solution.py:473
  46.9 16.1 %collective-permute-start.14 = (bf16[2,4,96,384]{3,2,1,0:T(8,128)(2,1)S(1)}, bf16[2,4,96,384]{3,2,1,0:T(8,128)(2,1)}, u32[]{:S(2)}, u32[]{:S(2)}) collective-permute-start(bf16[2,4,96,384]{3,2,1,0:T(8,128)(2,1)S(1)} %pad_maximum_fusion.6.rest_4_), channel_id=1, source_target_pairs={{0,4},{4,0},{8,12},{12,8},{1,5},{5,1},{9,13},{13,9},{2,6},{6,2},{1... | collective-permute-start | bytes 1769480 | tf_op jit(solution)/shard_map/ppermute | solution.py:473
  49.1 13.9 %collective-permute-start.13 = (bf16[2,4,96,384]{3,2,1,0:T(8,128)(2,1)}, bf16[2,4,96,384]{3,2,1,0:T(8,128)(2,1)}, u32[]{:S(2)}, u32[]{:S(2)}) collective-permute-start(bf16[2,4,96,384]{3,2,1,0:T(8,128)(2,1)} %get-tuple-element.87.__4_.rest_1_), channel_id=1, source_target_pairs={{0,4},{4,0},{8,12},{12,8},{1,5},{5,1},{9,13},{13,9},{2,6},{6,2},{1... | collective-permute-start | bytes 1769480 | tf_op jit(solution)/shard_map/ppermute | solution.py:473
  58.1 4.9 %collective-permute-start.15 = (bf16[2,4,96,384]{3,2,1,0:T(8,128)(2,1)}, bf16[2,4,96,384]{3,2,1,0:T(8,128)(2,1)}, u32[]{:S(2)}, u32[]{:S(2)}) collective-permute-start(bf16[2,4,96,384]{3,2,1,0:T(8,128)(2,1)} %get-tuple-element.88.__5_.rest_5_), channel_id=1, source_target_pairs={{0,4},{4,0},{8,12},{12,8},{1,5},{5,1},{9,13},{13,9},{2,6},{6,2},{1... | collective-permute-start | bytes 1769480 | tf_op jit(solution)/shard_map/ppermute | solution.py:473
  61.0 19.2 %collective-permute-start.10 = (bf16[1,4,96,768]{3,2,1,0:T(8,128)(2,1)S(1)}, bf16[1,4,96,768]{3,2,1,0:T(8,128)(2,1)S(1)}, u32[]{:S(2)}, u32[]{:S(2)}) collective-permute-start(bf16[1,4,96,768]{3,2,1,0:T(8,128)(2,1)S(1)} %get-tuple-element.189), channel_id=1, source_target_pairs={{0,8},{4,12},{8,0},{12,4},{1,9},{5,13},{9,1},{13,5},{2,10},{6,14},... | collective-permute-start | bytes 1769480 | tf_op jit(solution)/shard_map/ppermute | solution.py:473
  62.5 17.7 %collective-permute-start.11 = (bf16[1,4,96,768]{3,2,1,0:T(8,128)(2,1)S(1)}, bf16[1,4,96,768]{3,2,1,0:T(8,128)(2,1)S(1)}, u32[]{:S(2)}, u32[]{:S(2)}) collective-permute-start(bf16[1,4,96,768]{3,2,1,0:T(8,128)(2,1)S(1)} %get-tuple-element.188), channel_id=1, source_target_pairs={{0,16},{16,0},{1,17},{17,1},{2,18},{18,2},{3,19},{19,3},{4,20},{20... | collective-permute-start | bytes 1769480 | tf_op jit(solution)/shard_map/ppermute | solution.py:473
  83.5 27.4 %collective-permute-start.16 = (bf16[2,4,96,768]{3,2,1,0:T(8,128)(2,1)}, bf16[2,4,96,768]{3,2,1,0:T(8,128)(2,1)S(1)}, u32[]{:S(2)}, u32[]{:S(2)}) collective-permute-start(bf16[2,4,96,768]{3,2,1,0:T(8,128)(2,1)} %pad_maximum_fusion.1.rest_0_), channel_id=1, source_target_pairs={{0,16},{16,0},{1,17},{17,1},{2,18},{18,2},{3,19},{19,3},{4,20},{20... | collective-permute-start | bytes 3538952 | tf_op jit(solution)/shard_map/ppermute | solution.py:473
  85.0 31.4 %collective-permute-start.18 = (bf16[2,4,96,768]{3,2,1,0:T(8,128)(2,1)}, bf16[2,4,96,768]{3,2,1,0:T(8,128)(2,1)}, u32[]{:S(2)}, u32[]{:S(2)}) collective-permute-start(bf16[2,4,96,768]{3,2,1,0:T(8,128)(2,1)} %pad_maximum_fusion.1.rest_0_), channel_id=1, source_target_pairs={{0,4},{4,0},{8,12},{12,8},{1,5},{5,1},{9,13},{13,9},{2,6},{6,2},{1... | collective-permute-start | bytes 3538952 | tf_op jit(solution)/shard_map/ppermute | solution.py:473
  86.2 28.6 %collective-permute-start.17 = (bf16[2,4,96,768]{3,2,1,0:T(8,128)(2,1)}, bf16[2,4,96,768]{3,2,1,0:T(8,128)(2,1)S(1)}, u32[]{:S(2)}, u32[]{:S(2)}) collective-permute-start(bf16[2,4,96,768]{3,2,1,0:T(8,128)(2,1)} %pad_maximum_fusion.2.rest_4_), channel_id=1, source_target_pairs={{0,8},{4,12},{8,0},{12,4},{1,9},{5,13},{9,1},{13,5},{2,10},{6,14},... | collective-permute-start | bytes 3538952 | tf_op jit(solution)/shard_map/ppermute | solution.py:473
  86.8 29.6 %collective-permute-start.20 = (bf16[2,4,96,768]{3,2,1,0:T(8,128)(2,1)}, bf16[2,4,96,768]{3,2,1,0:T(8,128)(2,1)}, u32[]{:S(2)}, u32[]{:S(2)}) collective-permute-start(bf16[2,4,96,768]{3,2,1,0:T(8,128)(2,1)} %pad_maximum_fusion.2.rest_4_), channel_id=1, source_target_pairs={{0,4},{4,0},{8,12},{12,8},{1,5},{5,1},{9,13},{13,9},{2,6},{6,2},{1... | collective-permute-start | bytes 3538952 | tf_op jit(solution)/shard_map/ppermute | solution.py:473
  115.9 4.7 %collective-permute-start.19 = (bf16[2,4,96,768]{3,2,1,0:T(8,128)(2,1)}, bf16[2,4,96,768]{3,2,1,0:T(8,128)(2,1)S(1)}, u32[]{:S(2)}, u32[]{:S(2)}) collective-permute-start(bf16[2,4,96,768]{3,2,1,0:T(8,128)(2,1)} %get-tuple-element.106.rest_1_), channel_id=1, source_target_pairs={{0,4},{4,0},{8,12},{12,8},{1,5},{5,1},{9,13},{13,9},{2,6},{6,2},{1... | collective-permute-start | bytes 3538952 | tf_op jit(solution)/shard_map/ppermute | solution.py:473
  115.9 6.2 %collective-permute-start.21 = (bf16[2,4,96,768]{3,2,1,0:T(8,128)(2,1)}, bf16[2,4,96,768]{3,2,1,0:T(8,128)(2,1)}, u32[]{:S(2)}, u32[]{:S(2)}) collective-permute-start(bf16[2,4,96,768]{3,2,1,0:T(8,128)(2,1)} %get-tuple-element.107.rest_5_.rest_9_), channel_id=1, source_target_pairs={{0,4},{4,0},{8,12},{12,8},{1,5},{5,1},{9,13},{13,9},{2,6},{6,2},{1... | collective-permute-start | bytes 3538952 | tf_op jit(solution)/shard_map/ppermute | solution.py:473
  116.4 19.2 %collective-permute-start.22 = (bf16[8,4,96,384]{3,2,1,0:T(8,128)(2,1)}, bf16[8,4,96,384]{3,2,1,0:T(8,128)(2,1)S(1)}, u32[]{:S(2)}, u32[]{:S(2)}) collective-permute-start(bf16[8,4,96,384]{3,2,1,0:T(8,128)(2,1)} %get-tuple-element.111), channel_id=1, source_target_pairs={{0,4},{4,0},{8,12},{12,8},{1,5},{5,1},{9,13},{13,9},{2,6},{6,2},{1... | collective-permute-start | bytes 7077896 | tf_op jit(solution)/shard_map/ppermute | solution.py:473
  139.8 16.3 %collective-permute-start.25 = (bf16[8,4,96,384]{3,2,1,0:T(8,128)(2,1)}, bf16[8,4,96,384]{3,2,1,0:T(8,128)(2,1)S(1)}, u32[]{:S(2)}, u32[]{:S(2)}) collective-permute-start(bf16[8,4,96,384]{3,2,1,0:T(8,128)(2,1)} %get-tuple-element.125), channel_id=1, source_target_pairs={{0,4},{4,0},{8,12},{12,8},{1,5},{5,1},{9,13},{13,9},{2,6},{6,2},{1... | collective-permute-start | bytes 7077896 | tf_op jit(solution)/shard_map/ppermute | solution.py:473
  140.2 15.6 %collective-permute-start.23 = (bf16[2,4,96,384]{3,2,1,0:T(8,128)(2,1)}, bf16[2,4,96,384]{3,2,1,0:T(8,128)(2,1)S(1)}, u32[]{:S(2)}, u32[]{:S(2)}) collective-permute-start(bf16[2,4,96,384]{3,2,1,0:T(8,128)(2,1)} %get-tuple-element.114.rest_9_), channel_id=1, source_target_pairs={{0,8},{4,12},{8,0},{12,4},{1,9},{5,13},{9,1},{13,5},{2,10},{6,14},... | collective-permute-start | bytes 1769480 | tf_op jit(solution)/shard_map/ppermute | solution.py:473
  140.8 15.3 %collective-permute-start.24 = (bf16[2,4,96,384]{3,2,1,0:T(8,128)(2,1)}, bf16[2,4,96,384]{3,2,1,0:T(8,128)(2,1)S(1)}, u32[]{:S(2)}, u32[]{:S(2)}) collective-permute-start(bf16[2,4,96,384]{3,2,1,0:T(8,128)(2,1)} %get-tuple-element.123), channel_id=1, source_target_pairs={{0,16},{16,0},{1,17},{17,1},{2,18},{18,2},{3,19},{19,3},{4,20},{20... | collective-permute-start | bytes 1769480 | tf_op jit(solution)/shard_map/ppermute | solution.py:473
  161.3 23.7 %collective-permute-start.30 = (bf16[8,4,96,384]{3,2,1,0:T(8,128)(2,1)}, bf16[8,4,96,384]{3,2,1,0:T(8,128)(2,1)S(1)}, u32[]{:S(2)}, u32[]{:S(2)}) collective-permute-start(bf16[8,4,96,384]{3,2,1,0:T(8,128)(2,1)} %get-tuple-element.134), channel_id=1, source_target_pairs={{0,4},{4,0},{8,12},{12,8},{1,5},{5,1},{9,13},{13,9},{2,6},{6,2},{1... | collective-permute-start | bytes 7077896 | tf_op jit(solution)/shard_map/ppermute | solution.py:473
  162.5 15.3 %collective-permute-start.26 = (bf16[1,4,96,384]{3,2,1,0:T(8,128)(2,1)}, bf16[1,4,96,384]{3,2,1,0:T(8,128)(2,1)S(1)}, u32[]{:S(2)}, u32[]{:S(2)}) collective-permute-start(bf16[1,4,96,384]{3,2,1,0:T(8,128)(2,1)} %get-tuple-element.128.rest_12_), channel_id=1, source_target_pairs={{0,16},{16,0},{1,17},{17,1},{2,18},{18,2},{3,19},{19,3},{4,20},{20... | collective-permute-start | bytes 884744 | tf_op jit(solution)/shard_map/ppermute | solution.py:473
  163.0 14.8 %collective-permute-start.27 = (bf16[1,4,96,384]{3,2,1,0:T(8,128)(2,1)}, bf16[1,4,96,384]{3,2,1,0:T(8,128)(2,1)S(1)}, u32[]{:S(2)}, u32[]{:S(2)}) collective-permute-start(bf16[1,4,96,384]{3,2,1,0:T(8,128)(2,1)} %get-tuple-element.130), channel_id=1, source_target_pairs={{0,8},{4,12},{8,0},{12,4},{1,9},{5,13},{9,1},{13,5},{2,10},{6,14},... | collective-permute-start | bytes 884744 | tf_op jit(solution)/shard_map/ppermute | solution.py:473
  164.4 20.6 %collective-permute-start.28 = (bf16[2,4,96,384]{3,2,1,0:T(8,128)(2,1)}, bf16[2,4,96,384]{3,2,1,0:T(8,128)(2,1)S(1)}, u32[]{:S(2)}, u32[]{:S(2)}) collective-permute-start(bf16[2,4,96,384]{3,2,1,0:T(8,128)(2,1)} %get-tuple-element.131), channel_id=1, source_target_pairs={{0,8},{4,12},{8,0},{12,4},{1,9},{5,13},{9,1},{13,5},{2,10},{6,14},... | collective-permute-start | bytes 1769480 | tf_op jit(solution)/shard_map/ppermute | solution.py:473
  165.0 20.0 %collective-permute-start.29 = (bf16[2,4,96,384]{3,2,1,0:T(8,128)(2,1)}, bf16[2,4,96,384]{3,2,1,0:T(8,128)(2,1)S(1)}, u32[]{:S(2)}, u32[]{:S(2)}) collective-permute-start(bf16[2,4,96,384]{3,2,1,0:T(8,128)(2,1)} %get-tuple-element.132), channel_id=1, source_target_pairs={{0,16},{16,0},{1,17},{17,1},{2,18},{18,2},{3,19},{19,3},{4,20},{20... | collective-permute-start | bytes 1769480 | tf_op jit(solution)/shard_map/ppermute | solution.py:473
  191.3 12.4 %collective-permute-start.31 = (bf16[1,4,96,384]{3,2,1,0:T(8,128)(2,1)}, bf16[1,4,96,384]{3,2,1,0:T(8,128)(2,1)S(1)}, u32[]{:S(2)}, u32[]{:S(2)}) collective-permute-start(bf16[1,4,96,384]{3,2,1,0:T(8,128)(2,1)} %get-tuple-element.139), channel_id=1, source_target_pairs={{0,16},{16,0},{1,17},{17,1},{2,18},{18,2},{3,19},{19,3},{4,20},{20... | collective-permute-start | bytes 884744 | tf_op jit(solution)/shard_map/ppermute | solution.py:473
  192.8 10.9 %collective-permute-start.32 = (bf16[1,4,96,384]{3,2,1,0:T(8,128)(2,1)}, bf16[1,4,96,384]{3,2,1,0:T(8,128)(2,1)S(1)}, u32[]{:S(2)}, u32[]{:S(2)}) collective-permute-start(bf16[1,4,96,384]{3,2,1,0:T(8,128)(2,1)} %get-tuple-element.140), channel_id=1, source_target_pairs={{0,8},{4,12},{8,0},{12,4},{1,9},{5,13},{9,1},{13,5},{2,10},{6,14},... | collective-permute-start | bytes 884744 | tf_op jit(solution)/shard_map/ppermute | solution.py:473
  194.2 19.5 %collective-permute-start.33 = (bf16[2,4,96,384]{3,2,1,0:T(8,128)(2,1)}, bf16[2,4,96,384]{3,2,1,0:T(8,128)(2,1)S(1)}, u32[]{:S(2)}, u32[]{:S(2)}) collective-permute-start(bf16[2,4,96,384]{3,2,1,0:T(8,128)(2,1)} %get-tuple-element.141), channel_id=1, source_target_pairs={{0,8},{4,12},{8,0},{12,4},{1,9},{5,13},{9,1},{13,5},{2,10},{6,14},... | collective-permute-start | bytes 1769480 | tf_op jit(solution)/shard_map/ppermute | solution.py:473
  194.8 18.9 %collective-permute-start.34 = (bf16[2,4,96,384]{3,2,1,0:T(8,128)(2,1)}, bf16[2,4,96,384]{3,2,1,0:T(8,128)(2,1)S(1)}, u32[]{:S(2)}, u32[]{:S(2)}) collective-permute-start(bf16[2,4,96,384]{3,2,1,0:T(8,128)(2,1)} %get-tuple-element.142), channel_id=1, source_target_pairs={{0,16},{16,0},{1,17},{17,1},{2,18},{18,2},{3,19},{19,3},{4,20},{20... | collective-permute-start | bytes 1769480 | tf_op jit(solution)/shard_map/ppermute | solution.py:473
  218.2 22.7 %collective-permute-start.38 = (bf16[1,4,96,384]{3,2,1,0:T(8,128)(2,1)}, bf16[1,4,96,384]{3,2,1,0:T(8,128)(2,1)S(1)}, u32[]{:S(2)}, u32[]{:S(2)}) collective-permute-start(bf16[1,4,96,384]{3,2,1,0:T(8,128)(2,1)} %get-tuple-element.147), channel_id=1, source_target_pairs={{0,16},{16,0},{1,17},{17,1},{2,18},{18,2},{3,19},{19,3},{4,20},{20... | collective-permute-start | bytes 884744 | tf_op jit(solution)/shard_map/ppermute | solution.py:473
  218.7 22.3 %collective-permute-start.39 = (bf16[1,4,96,384]{3,2,1,0:T(8,128)(2,1)}, bf16[1,4,96,384]{3,2,1,0:T(8,128)(2,1)S(1)}, u32[]{:S(2)}, u32[]{:S(2)}) collective-permute-start(bf16[1,4,96,384]{3,2,1,0:T(8,128)(2,1)} %get-tuple-element.148), channel_id=1, source_target_pairs={{0,8},{4,12},{8,0},{12,4},{1,9},{5,13},{9,1},{13,5},{2,10},{6,14},... | collective-permute-start | bytes 884744 | tf_op jit(solution)/shard_map/ppermute | solution.py:473
  221.3 35.3 %collective-permute-start.41 = (bf16[96,2304]{1,0:T(8,128)(2,1)S(1)}, bf16[96,2304]{1,0:T(8,128)(2,1)S(1)}, u32[]{:S(2)}, u32[]{:S(2)}) collective-permute-start(bf16[96,2304]{1,0:T(8,128)(2,1)S(1)} %pad_maximum_fusion.8), channel_id=1, source_target_pairs={{0,2},{1,3},{2,0},{3,1},{4,6},{5,7},{6,4},{7,5},{8,10},{9,11},{10,... | collective-permute-start | bytes 1327112 | tf_op jit(solution)/shard_map/ppermute | solution.py:478
  226.6 30.0 %collective-permute-start.42 = (bf16[96,2304]{1,0:T(8,128)(2,1)S(1)}, bf16[96,2304]{1,0:T(8,128)(2,1)S(1)}, u32[]{:S(2)}, u32[]{:S(2)}) collective-permute-start(bf16[96,2304]{1,0:T(8,128)(2,1)S(1)} %pad_maximum_fusion.9), channel_id=1, source_target_pairs={{0,1},{1,2},{2,3},{3,0},{4,5},{5,6},{6,7},{7,4},{8,9},{9,10},{10,1... | collective-permute-start | bytes 1327112 | tf_op jit(solution)/shard_map/ppermute | solution.py:478
  245.6 17.3 %collective-permute-start.40 = (bf16[96,2304]{1,0:T(8,128)(2,1)S(1)}, bf16[96,2304]{1,0:T(8,128)(2,1)S(1)}, u32[]{:S(2)}, u32[]{:S(2)}) collective-permute-start(bf16[96,2304]{1,0:T(8,128)(2,1)S(1)} %pad_maximum_fusion.7), channel_id=1, source_target_pairs={{0,3},{1,0},{2,1},{3,2},{4,7},{5,4},{6,5},{7,6},{8,11},{9,8},{10,9... | collective-permute-start | bytes 1327112 | tf_op jit(solution)/shard_map/ppermute | solution.py:478
  246.3 1.2 collective-permute-start.35
  247.5 4.2 %collective-permute-start.36 = (f32[16,768]{1,0:T(8,128)S(1)}, f32[16,768]{1,0:T(8,128)S(1)}, u32[]{:S(2)}, u32[]{:S(2)}) collective-permute-start(f32[16,768]{1,0:T(8,128)S(1)} %add.86), channel_id=1, source_target_pairs={{0,8},{4,12},{8,0},{12,4},{1,9},{5,13},{9,1},{13,5},{2,10},{6,14},... | collective-permute-start | bytes 147464 | tf_op jit(solution)/shard_map/ppermute | solution.py:473
  251.7 4.2 %collective-permute-start.37 = (f32[16,768]{1,0:T(8,128)S(1)}, f32[16,768]{1,0:T(8,128)S(1)}, u32[]{:S(2)}, u32[]{:S(2)}) collective-permute-start(f32[16,768]{1,0:T(8,128)S(1)} %add.87), channel_id=1, source_target_pairs={{0,16},{16,0},{1,17},{17,1},{2,18},{18,2},{3,19},{19,3},{4,20},{20... | collective-permute-start | bytes 147464 | tf_op jit(solution)/shard_map/ppermute | solution.py:473
  265.2 13.2 %collective-permute-start.45 = (bf16[96,2304]{1,0:T(8,128)(2,1)S(1)}, bf16[96,2304]{1,0:T(8,128)(2,1)S(1)}, u32[]{:S(2)}, u32[]{:S(2)}) collective-permute-start(bf16[96,2304]{1,0:T(8,128)(2,1)S(1)} %add_convert_fusion), channel_id=1, source_target_pairs={{0,16},{16,0},{1,17},{17,1},{2,18},{18,2},{3,19},{19,3},{4,20},{20... | collective-permute-start | bytes 1327112 | tf_op jit(solution)/shard_map/ppermute | solution.py:473
  266.8 4.1 %collective-permute-start.43 = (f32[16,768]{1,0:T(8,128)S(1)}, f32[16,768]{1,0:T(8,128)S(1)}, u32[]{:S(2)}, u32[]{:S(2)}) collective-permute-start(f32[16,768]{1,0:T(8,128)S(1)} %copy-done.33), channel_id=1, source_target_pairs={{0,1},{1,0},{2,3},{3,2},{4,5},{5,4},{6,7},{7,6},{8,9},{9,8},{10,11... | collective-permute-start | bytes 147464 | tf_op jit(solution)/shard_map/ppermute | solution.py:473
  270.9 5.6 %collective-permute-start.44 = (f32[16,768]{1,0:T(8,128)S(1)}, f32[16,768]{1,0:T(8,128)S(1)}, u32[]{:S(2)}, u32[]{:S(2)}) collective-permute-start(f32[16,768]{1,0:T(8,128)S(1)} %add.89), channel_id=1, source_target_pairs={{0,2},{1,3},{2,0},{3,1},{4,6},{5,7},{6,4},{7,5},{8,10},{9,11},{10,... | collective-permute-start | bytes 147464 | tf_op jit(solution)/shard_map/ppermute | solution.py:473
  (46 other events, 203.2 us)
where the time goes:
time: 289 us; the launch traced here: 288 us
  Pallas kernels  114 us (39%)
  waiting for transfers between devices  74.2 us (26%)
  starting transfers between devices  51.6 us (18%)
  local copies, waits for them, and re-layouts  34.8 us (12%)
  other arithmetic  12.1 us (4%)
    pallas_call x4, Pallas kernels, block_part(): pl.pallas_call(functools.partial(kernel, orders, core_bit, len(after)), g...  61 us
    ppermute x37, waiting for transfers between devices, flipped(): lax.ppermute(value, axis, [(i, i ^ flip) for i in range(lax.axis_size(axi...  56.6 us
    ppermute x37, starting transfers between devices, flipped(): lax.ppermute(value, axis, [(i, i ^ flip) for i in range(lax.axis_size(axi...  30.5 us
    ppermute x9, starting transfers between devices, shifted(): lax.ppermute(value, 'col', [(i, (i + by) % size) for i in range(size)])  21 us
    pallas_call x2, Pallas kernels, mlp_tail_part(): pl.pallas_call(functools.partial(mlp_tail_kernel, orders, core_bit, len(s...  19.1 us
    ppermute x9, waiting for transfers between devices, shifted(): lax.ppermute(value, 'col', [(i, (i + by) % size) for i in range(size)])  17.7 us
    pallas_call x5, Pallas kernels, merge(): pl.pallas_call(functools.partial(merge_kernel, layout, len(arrays), len(a...  16.9 us
    unnamed x104, local copies, waits for them, and re-layouts  16.4 us
  transfers between devices with their start and end apart: 46, of which 21 were waited for; matrix products, arithmetic and copies ran while one was open for 6% of the time, Pallas kernels for 35%

commit v1 on v0

--- a/solution.py
+++ b/solution.py
@@ -148,9 +148,8 @@
     for i in range(heads):
         wv_scr[:, i * 2 * HD : (i + 1) * 2 * HD] = w_scr[:, i * HEAD + 2 * HD : (i + 1) * HEAD]
 
-    @pl.loop(0, length // tile)
-    def _(t):
-        rows = pl.ds(pl.multiple_of(t * tile, tile), tile)
+    for t in range(length // tile):
+        rows = slice(t * tile, (t + 1) * tile)
         qkv_scr[rows, :] = dot_nn(na_ref[rows, :], w_scr[...]) + bias_ref[0]
         dattn_scr[rows, :] = dot_nn(cot_ref[rows, :], wv_scr[...]).astype(BF16)
 
@@ -205,9 +204,8 @@
 
     dbias_ref[0] = jnp.sum(dqkv_ref[0].astype(F32), axis=0, keepdims=True)
 
-    @pl.loop(0, width // tile)
-    def _(t):
-        rows = pl.ds(pl.multiple_of(t * tile, tile), tile)
+    for t in range(width // tile):
+        rows = slice(t * tile, (t + 1) * tile)
         g_in = dot_nn(naT_ref[rows, :], dqkv_ref[0])
         g_out = dot_nn(cotT_ref[rows, :], mix_ref[0])
         for i in range(heads):
@@ -232,9 +230,8 @@
     assemble(me_ref, right, gathered_order(orders[1], core_bit), wd_scr, 0)
     dbias_ref[0] = jnp.zeros_like(dbias_ref[0])
 
-    @pl.loop(0, length // tile)
-    def _(t):
-        rows = pl.ds(pl.multiple_of(t * tile, tile), tile)
+    for t in range(length // tile):
+        rows = slice(t * tile, (t + 1) * tile)
         for n in range(0, up_cols, tile):
             hidden = dot_nn(nm_ref[rows, :], wu_scr[:, n : n + tile]) + bias_ref[0, :, n : n + tile]
             d_act = dot_nn(cot_ref[rows, :], wd_scr[:, n : n + tile])
@@ -247,9 +244,8 @@
 
     for side, lhs, rhs in ((0, nmT_ref, dh_ref), (1, cotT_ref, act_ref)):
 
-        @pl.loop(0, width // tile)
-        def _(t):
-            rows = pl.ds(pl.multiple_of(t * tile, tile), tile)
+        for t in range(width // tile):
+            rows = slice(t * tile, (t + 1) * tile)
             g_scr[rows, :] = dot_nn(lhs[rows, :], rhs[0]).astype(BF16)
 
         hand_out(me_ref, g_scr, 0, gk_ref, gs_ref, side * kept, orders[side], core_bit)
@@ -319,9 +315,8 @@
         wv_scr[:, i * 2 * HD : (i + 1) * 2 * HD] = w_scr[:, i * HEAD + 2 * HD : (i + 1) * HEAD]
     tile = 256
 
-    @pl.loop(0, branch_ref.shape[0] // tile)
-    def _(t):
-        rows = pl.ds(pl.multiple_of(t * tile, tile), tile)
+    for t in range(branch_ref.shape[0] // tile):
+        rows = slice(t * tile, (t + 1) * tile)
         branch_ref[rows, :] += dot_nt(mix_scr[rows, :], wv_scr[...])
         dna_ref[rows, :] += dot_nt(dqkv_scr[rows, :], w_scr[...])
 
@@ -348,9 +343,8 @@
     assemble(me_ref, right, gathered_order(orders[1], core_bit), wd_scr, 0)
     tile = 256
 
-    @pl.loop(0, length // tile)
-    def _(t):
-        rows = pl.ds(pl.multiple_of(t * tile, tile), tile)
+    for t in range(length // tile):
+        rows = slice(t * tile, (t + 1) * tile)
         branch_ref[rows, :] += dot_nt(act_ref[0, rows, :], wd_scr[...])
         dnm_ref[rows, :] += dot_nt(dh_ref[0, rows, :], wu_scr[...])
 
@@ -658,7 +652,7 @@
     mlp_blocks = gather_col(fence([mlp_own], [attn.held[0]])[0])
     for _ in range(far):
         attn.advance()
-        phase([attn], [], [na] if attn.done == 1 else [])
+        phase([attn], [], [na, mlp_blocks[1]] if attn.done == 1 else mlp_blocks[2:])
     mlp_blocks = fence(mlp_blocks, attn.moving)
     attn.cross()
     mlp = Gather(jnp.stack(mlp_blocks), orders, core_bit)
@@ -704,36 +698,53 @@
     mlp.cross()
     attn_sum = Reduction(into[0], sent[0], orders, core_bit)
 
+    totals = {}
+
+    def go_on(reductions, after, values=()):
+        reductions = [r for r in reductions if id(r) not in totals]
+        ending = [r for r in reductions if not r.half()]
+        finished, token, passed = merge(reductions, after, values)
+        totals.update(zip((id(r) for r in ending), finished))
+        return token, passed
+
+    token, _ = go_on([attn_sum], mlp.over[2:])
     mlp_calls, mlp_sums = [], []
-    for k0 in starts:
+    for n, k0 in enumerate(starts):
         outs = mlp_call(mlp, k0, k0, per_call, (per_mlp, per_mlp * per_call), 0, [], token)
         mlp_calls.append(outs)
-        _, token, sent = merge([attn_sum] + mlp_sums, [outs[2]], [outs[4]])
+        token, sent = go_on([attn_sum] + mlp_sums, [outs[2]], [outs[4]])
         mlp_sums.append(Reduction(outs[3], sent[0], orders, core_bit))
+    while id(attn_sum) not in totals:
+        token, _ = go_on([attn_sum], token)
+    attn_total = totals[id(attn_sum)]
+    attn_moves = {0: attn_total[0]}
+    for k in range(2, col_size):
+        attn_moves[k] = shifted(attn_total[k], -k)
     begins = list(range(0, col_size + 1, per_call))
     branch, d_norm_attn = attention_tail_part(
         begins, starts, orders, core_bit, token, me, *attn.sides(), [[c[0] for c in attn_calls], [c[1] for c in attn_calls]],
         [], 11,
     )
-    totals = {}
-
-    def go_on(after):
-        open_ones = [r for r in [attn_sum] + mlp_sums if id(r) not in totals]
-        ending = [r for r in open_ones if not r.half()]
-        finished, token, _ = merge(open_ones, after)
-        for r, total in zip(ending, finished):
-            totals[id(r)] = total
-        return token
-
-    moves = {}
-
-    def send_home(k, parts):
-        part = jnp.concatenate(parts, axis=1)
-        moves[k] = part if k == 0 else shifted(part, -k)
+    token, passed = go_on(mlp_sums, [branch], [attn_moves[k] for k in range(2, col_size)])
+    attn_moves.update(zip(range(2, col_size), passed))
+    attn_moves[1] = shifted(attn_total[1], -1)
+
+    def settle(parts):
+        total = sum((part.astype(F32) for part in parts[1:]), parts[0].astype(F32))
+        flip = 2
+        while flip < lax.axis_size("dp"):
+            total = total + flipped(total, "dp", flip)
+            flip *= 2
+        mine = total.astype(BF16)
+        return mine, swap(mine, 1)
+
+    def whole_block(mine, other):
+        first = half == 0
+        return jnp.concatenate([jnp.where(first, mine, other), jnp.where(first, other, mine)], axis=0).astype(F32)
 
     small_ks = tuple((5, k0, col_size) for k0 in starts) + tuple((5 + col_size, k0, col_size) for k0 in starts)
     small_parts = [c[2] for c in mlp_calls] + [c[2] for c in attn_calls]
-    token = go_on([branch])
+    mlp_moves = {}
     d_norm_mlp = None
     for n, k0 in enumerate(starts):
         last = n == len(starts) - 1
@@ -746,40 +757,32 @@
             k0, orders, core_bit, token, me, *mlp.sides(), mlp_calls[n][0], mlp_calls[n][1], sums,
             finals if last else [], (small_ks, small_parts) if last else None, 9,
         )
-        token = go_on(result[2:] if last else result[:1])
+        if n == 0:
+            token, passed = go_on(mlp_sums, result[:1], [attn_moves[1]])
+            attn_moves[1] = passed[0]
+            attn_mine, attn_other = settle([attn_moves[k] for k in range(col_size)])
+        else:
+            token, passed = go_on(mlp_sums, result[:1], result[2:])
         if last:
-            block_out, in_grad, smalls = result
+            block_out, in_grad, _ = result
+            smalls = passed[0]
         else:
             branch, d_norm_mlp = result
-        for at, k1 in enumerate(starts):
-            if id(mlp_sums[at]) in totals and id(attn_sum) in totals and k1 not in moves:
-                attn_total, mlp_total = totals[id(attn_sum)], totals[id(mlp_sums[at])]
+        while last and any(id(r) not in totals for r in mlp_sums):
+            token, _ = go_on(mlp_sums, token)
+        for k1, r in zip(starts, mlp_sums):
+            if id(r) in totals and k1 not in mlp_moves:
                 for i in range(per_call):
-                    send_home(k1 + i, [attn_total[k1 + i]] + [mlp_total[i * per_mlp + j] for j in range(per_mlp)])
-    while len(moves) < col_size:
-        token = go_on(token)
-        for at, k1 in enumerate(starts):
-            if id(mlp_sums[at]) in totals and k1 not in moves:
-                attn_total, mlp_total = totals[id(attn_sum)], totals[id(mlp_sums[at])]
-                for i in range(per_call):
-                    send_home(k1 + i, [attn_total[k1 + i]] + [mlp_total[i * per_mlp + j] for j in range(per_mlp)])
+                    slots = [totals[id(r)][i * per_mlp + j] for j in range(per_mlp)]
+                    part = jnp.concatenate([s[:, :cut] for s in slots] + [s[:, cut:] for s in slots], axis=1)
+                    mlp_moves[k1 + i] = part if k1 + i == 0 else shifted(part, -(k1 + i))
     head_row, up_row = 5 + col_size, 5
     smalls = sum_over(smalls, ("row", "dp"))
-    smalls, *came = fence([smalls] + [moves[k] for k in range(1, col_size)])
-
-    total = sum((move.astype(F32) for move in came), moves[0].astype(F32))
-    flip = 2
-    while flip < lax.axis_size("dp"):
-        total = total + flipped(total, "dp", flip)
-        flip *= 2
-    mine = total.astype(BF16)
-    other = swap(mine, 1)
-    first = half == 0
-    grads = jnp.concatenate([jnp.where(first, mine, other), jnp.where(first, other, mine)], axis=0).astype(F32)
-    g_heads = grads[:, :block_cols].reshape(rows, local_heads, HEAD)
-    sides = grads[:, block_cols:].reshape(rows, per_mlp, 2, cut)
-    g_up = sides[:, :, 0].reshape(rows, up_cols)
-    g_down = sides[:, :, 1].reshape(rows, up_cols)
+    smalls, *came = fence([smalls] + [mlp_moves[k] for k in range(1, col_size)])
+    mlp_mine, mlp_other = settle([mlp_moves[0]] + came)
+    g_heads = whole_block(attn_mine, attn_other).reshape(rows, local_heads, HEAD)
+    g_mlp = whole_block(mlp_mine, mlp_other)
+    g_up, g_down = g_mlp[:, :up_cols], g_mlp[:, up_cols:]
     smalls = sum_over(smalls, ("col",))
     return (
         block_out,

time: 289 us -> 269 us (0.931)
  waiting for transfers between devices: 74.2 us -> 63.6 us
  Pallas kernels: 114 us -> 105 us
    pallas_call x4, Pallas kernels: 61 us -> 52 us  [block_part(): pl.pallas_call(functools.partial(kernel, orders, core_bit, len(after)), g...]
    ppermute x37 -> x38, waiting for transfers between devices: 56.6 us -> 47.6 us  [flipped(): lax.ppermute(value, axis, [(i, i ^ flip) for i in range(lax.axis_size(axi...]
    slice x1 -> x4, local copies, waits for them, and re-layouts: 3.7 us -> 0.14 us  [on_device(): s[:, :cut]]
    ppermute x9 -> x12, starting transfers between devices: 21 us -> 24.5 us  [shifted(): lax.ppermute(value, 'col', [(i, (i + by) % size) for i in range(size)])]
    ppermute x37 -> x38, starting transfers between devices: 30.5 us -> 27.3 us  [flipped(): lax.ppermute(value, axis, [(i, i ^ flip) for i in range(lax.axis_size(axi...]
    pallas_call x5 -> x6, Pallas kernels: 16.9 us -> 18.5 us  [merge(): pl.pallas_call(functools.partial(merge_kernel, layout, len(arrays), len(a...]
    ppermute x9 -> x12, waiting for transfers between devices: 17.7 us -> 16 us  [shifted(): lax.ppermute(value, 'col', [(i, (i + by) % size) for i in range(size)])]
    unnamed x104 -> x112, local copies, waits for them, and re-layouts: 16.4 us -> 16.9 us
  transfers between devices with their start and end apart: 46 -> 50, of which waited for: 21 -> 15; matrix products, arithmetic and copies ran while one was open for 6% -> 9% of each run, Pallas kernels for 35% -> 35%
where the time goes in v1:
time: 269 us; the launch traced here: 268 us
  Pallas kernels  105 us (39%)
  waiting for transfers between devices  63.6 us (24%)
  starting transfers between devices  51.8 us (19%)
  local copies, waits for them, and re-layouts  32.9 us (12%)
  other arithmetic  13.8 us (5%)
    pallas_call x4, Pallas kernels, block_part(): pl.pallas_call(functools.partial(kernel, orders, core_bit, len(after)), g...  52 us
    ppermute x38, waiting for transfers between devices, flipped(): lax.ppermute(value, axis, [(i, i ^ flip) for i in range(lax.axis_size(axi...  47.6 us
    ppermute x38, starting transfers between devices, flipped(): lax.ppermute(value, axis, [(i, i ^ flip) for i in range(lax.axis_size(axi...  27.3 us
    ppermute x12, starting transfers between devices, shifted(): lax.ppermute(value, 'col', [(i, (i + by) % size) for i in range(size)])  24.5 us
    pallas_call x6, Pallas kernels, merge(): pl.pallas_call(functools.partial(merge_kernel, layout, len(arrays), len(a...  18.5 us
    pallas_call x2, Pallas kernels, mlp_tail_part(): pl.pallas_call(functools.partial(mlp_tail_kernel, orders, core_bit, len(s...  18 us
    unnamed x112, local copies, waits for them, and re-layouts  16.9 us
    ppermute x12, waiting for transfers between devices, shifted(): lax.ppermute(value, 'col', [(i, (i + by) % size) for i in range(size)])  16 us
  transfers between devices with their start and end apart: 50, of which 15 were waited for; matrix products, arithmetic and copies ran while one was open for 9% of the time, Pallas kernels for 35%

profile of v1, /device:TPU:0, one launch (start us, length us, event | category | flops | bytes accessed | tf_op | source)
XLA Modules:
  0.0 268.1 jit_solution(1064471501106521833)
XLA Ops:
  0.7 1.2 copy.63
  3.2 5.1 %collective-permute-start.2 = (bf16[96,768]{1,0:T(8,128)(2,1)S(1)}, bf16[96,768]{1,0:T(8,128)(2,1)S(1)}, u32[]{:S(2)}, u32[]{:S(2)}) collective-permute-start(bf16[96,768]{1,0:T(8,128)(2,1)S(1)} %copy.70), channel_id=1, source_target_pairs={{0,3},{1,0},{2,1},{3,2},{4,7},{5,4},{6,5},{7,6},{8,11},{9,8},{10,9... | collective-permute-start | bytes 442376 | tf_op jit(solution)/shard_map/ppermute | solution.py:472
  14.5 1.3 constant_dynamic-slice_fusion.segr_ref
  15.8 4.9 %collective-permute-done.1 = bf16[96,768]{1,0:T(8,128)(2,1)S(1)} collective-permute-done((bf16[96,768]{1,0:T(8,128)(2,1)S(1)}, bf16[96,768]{1,0:T(8,128)(2,1)S(1)}, u32[]{:S(2)}, u32[]{:S(2)}) %collective-permute-start.1) | collective-permute-done | bytes 147488 | tf_op jit(solution)/shard_map/ppermute | solution.py:472
  20.9 1.6 collective-permute-start.6
  23.3 1.5 collective-permute-start.7
  24.9 6.0 %shard_map.255 = (bf16[512,768]{1,0:T(8,128)(2,1)}, bf16[768,512]{1,0:T(8,128)(2,1)}, bf16[512,768]{1,0:T(8,128)(2,1)}, bf16[768,512]{1,0:T(8,128)(2,1)}, bf16[7...) custom-call(bf16[512,768]{1,0:T(8,128)(2,1)} %rest_13_.1, ...), custom_call_target="tpu_custom_call" | custom-call | flops 6899999744 | bytes 1048576 | tf_op jit(solution)/shard_map/pallas_call | solution.py:123
  31.0 1.5 collective-permute-done.3.__3_.__1_
  35.5 1.6 collective-permute-start.8
  40.2 2.2 collective-permute-start.5
  43.8 9.6 %collective-permute-done.4.__2_ = bf16[96,1536]{1,0:T(8,128)(2,1)S(1)} collective-permute-done((bf16[96,1536]{1,0:T(8,128)(2,1)S(1)}, bf16[96,1536]{1,0:T(8,128)(2,1)S(1)}, u32[]{:S(2)}, u32[]{:S(2)}) %collective-permute-start.4) | collective-permute-done | bytes 294944 | tf_op jit(solution)/shard_map/ppermute | solution.py:472
  54.9 1.4 pad_maximum_fusion
  56.3 1.2 collective-permute-start.10
  58.6 15.0 %shard_map.259 = (bf16[2,512,768]{2,1,0:T(8,128)(2,1)}, bf16[2,512,384]{2,1,0:T(8,128)(2,1)}, f32[2,1,768]{2,1,0:T(1,128)}, bf16[8,4,96,384]{3,2,1,0:T(8,128)(2,1)}, bf16[8,4,96,384]{3,2,1,0:T(8,128)(2,1)}) custom-call(s32[2]{0:T(128)} %pad_add_fusion.me_ref, bf16[512,768]{1,0:T(8,128)(2,1)} %get-tuple-element.89.__2_.na_ref, ...), custom_call_target="tpu_custom_call" | custom-call | flops 23000000512 | bytes 1048576 | tf_op jit(solution)/shard_map/pallas_call | solution.py:269
  74.7 2.3 pad_maximum_fusion.1.rest_0_
  77.9 1.1 pad_maximum_fusion.2.rest_4_
  79.9 14.8 %shard_map.261 = (bf16[2,512,768]{2,1,0:T(8,128)(2,1)}, bf16[2,512,384]{2,1,0:T(8,128)(2,1)}, f32[2,1,768]{2,1,0:T(1,128)}, bf16[8,4,96,384]{3,2,1,0:T(8,128)(2,1)}, bf16[8,4,96,384]{3,2,1,0:T(8,128)(2,1)}) custom-call(s32[2]{0:T(128)} %pad_add_fusion.me_ref, ...), custom_call_target="tpu_custom_call", output_to_operand_aliasing={{3}: (19, {}), {4}: (20, {})} | custom-call | flops 23000000512 | bytes 1048576 | tf_op jit(solution)/shard_map/pallas_call | solution.py:269
  94.8 10.1 %collective-permute-done.16.__1_ = bf16[2,4,96,768]{3,2,1,0:T(8,128)(2,1)S(1)} collective-permute-done((bf16[2,4,96,768]{3,2,1,0:T(8,128)(2,1)}, bf16[2,4,96,768]{3,2,1,0:T(8,128)(2,1)S(1)}, u32[]{:S(2)}, u32[]{:S(2)}) %collective-permute-start.16) | collective-permute-done | bytes 1179680 | tf_op jit(solution)/shard_map/ppermute | solution.py:467
  104.9 1.8 collective-permute-done.17.__2_
  108.8 7.1 %collective-permute-done.19.refs_4_.rest_3_ = bf16[2,4,96,768]{3,2,1,0:T(8,128)(2,1)S(1)} collective-permute-done((bf16[2,4,96,768]{3,2,1,0:T(8,128)(2,1)}, bf16[2,4,96,768]{3,2,1,0:T(8,128)(2,1)S(1)}, u32[]{:S(2)}, u32[]{:S(2)}) %collective-permute-start.19) | collective-permute-done | bytes 1179680 | tf_op jit(solution)/shard_map/ppermute | solution.py:467
  115.9 3.4 %collective-permute-done.21.refs_5_.rest_7_ = bf16[2,4,96,768]{3,2,1,0:T(8,128)(2,1)S(1)} collective-permute-done((bf16[2,4,96,768]{3,2,1,0:T(8,128)(2,1)}, bf16[2,4,96,768]{3,2,1,0:T(8,128)(2,1)S(1)}, u32[]{:S(2)}, u32[]{:S(2)}) %collective-permute-start.21) | collective-permute-done | bytes 1179680 | tf_op jit(solution)/shard_map/ppermute | solution.py:467
  120.3 1.5 copy-done.3
  121.8 2.7 %shard_map.263 = (bf16[2,4,96,384]{3,2,1,0:T(8,128)(2,1)}, bf16[2,4,96,384]{3,2,1,0:T(8,128)(2,1)}) custom-call(bf16[8,4,96,384]{3,2,1,0:T(8,128)(2,1)} %get-tuple-element.115.refs_0_.refs_2_.refs_3_.refs_4_, bf16[8,4,96,384]{3,2,1,0:T(8,128)(2,1)} %copy-done.3, bf16[8,4,96,384]{3,2,1,0:T(8,128)(2,1)} %get-tuple-element.115.refs_0_.refs_2_.refs_3_.refs_4_, ...), custom_call_target="tpu_custom_call" | custom-call | flops 3449999872 | bytes 1048576 | tf_op jit(solution)/shard_map/pallas_call | solution.py:548
  126.5 11.2 %shard_map.264 = (bf16[2,512,768]{2,1,0:T(8,128)(2,1)}, bf16[2,512,768]{2,1,0:T(8,128)(2,1)}, f32[2,1,768]{2,1,0:T(1,128)}, bf16[8,4,96,384]{3,2,1,0:T(8,128)(2,1)}, bf16[8,4,96,384]{3,2,1,0:T(8,128)(2,1)}) custom-call(s32[2]{0:T(128)} %pad_add_fusion.me_ref, bf16[512,768]{1,0:T(8,128)(2,1)} %get-tuple-element.113.nm_ref, ...), custom_call_target="tpu_custom_call" | custom-call | flops 13799999488 | bytes 1048576 | tf_op jit(solution)/shard_map/pallas_call | solution.py:269
  137.8 2.4 collective-permute-done.23.refs_2_
  141.5 2.3 shard_map.265
  146.1 10.9 %shard_map.266 = (bf16[2,512,768]{2,1,0:T(8,128)(2,1)}, bf16[2,512,768]{2,1,0:T(8,128)(2,1)}, f32[2,1,768]{2,1,0:T(1,128)}, bf16[8,4,96,384]{3,2,1,0:T(8,128)(2,1)}, bf16[8,4,96,384]{3,2,1,0:T(8,128)(2,1)}) custom-call(s32[2]{0:T(128)} %pad_add_fusion.me_ref, bf16[512,768]{1,0:T(8,128)(2,1)} %get-tuple-element.113.nm_ref, ...), custom_call_target="tpu_custom_call" | custom-call | flops 13799999488 | bytes 1048576 | tf_op jit(solution)/shard_map/pallas_call | solution.py:269
  158.7 3.8 %shard_map.267 = (bf16[1,4,96,768]{3,2,1,0:T(8,128)(2,1)}, bf16[2,4,96,384]{3,2,1,0:T(8,128)(2,1)}, bf16[2,4,96,384]{3,2,1,0:T(8,128)(2,1)}, bf16[8,4,96,384]{3,2,1,0:T(8,128)(2,1)}) custom-call(bf16[8,4,96,384]{3,2,1,0:T(8,128)(2,1)} %get-tuple-element.115.refs_0_.refs_2_.refs_3_.refs_4_, ...), custom_call_target="tpu_custom_call", output_to_operand_aliasing={{3}: (12, {})} | custom-call | flops 3449999872 | bytes 1048576 | tf_op jit(solution)/shard_map/pallas_call | solution.py:548
  166.6 5.3 %collective-permute-start.31 = (bf16[96,768]{1,0:T(8,128)(2,1)S(1)}, bf16[96,768]{1,0:T(8,128)(2,1)S(1)}, u32[]{:S(2)}, u32[]{:S(2)}) collective-permute-start(bf16[96,768]{1,0:T(8,128)(2,1)S(1)} %get-tuple-element.212), channel_id=1, source_target_pairs={{0,2},{1,3},{2,0},{3,1},{4,6},{5,7},{6,4},{7,5},{8,10},{9,11},{10,... | collective-permute-start | bytes 442376 | tf_op jit(solution)/shard_map/ppermute | solution.py:472
  171.9 2.8 %collective-permute-start.32 = (bf16[96,768]{1,0:T(8,128)(2,1)S(1)}, bf16[96,768]{1,0:T(8,128)(2,1)S(1)}, u32[]{:S(2)}, u32[]{:S(2)}) collective-permute-start(bf16[96,768]{1,0:T(8,128)(2,1)S(1)} %get-tuple-element.211), channel_id=1, source_target_pairs={{0,1},{1,2},{2,3},{3,0},{4,5},{5,6},{6,7},{7,4},{8,9},{9,10},{10,1... | collective-permute-start | bytes 442376 | tf_op jit(solution)/shard_map/ppermute | solution.py:472
  174.7 10.0 %shard_map.268 = (f32[512,768]{1,0:T(8,128)}, f32[512,768]{1,0:T(8,128)}) custom-call(s32[2]{0:T(128)} %pad_add_fusion.me_ref, bf16[2,4,96,384]{3,2,1,0:T(8,128)(2,1)} %copy-done.17, bf16[2,4,96,384]{3,2,1,0:T(8,128)(2,1)} %get-tuple-element.92.__4_.rest_1_, bf16[2,4,96,384]{3,2,1,0:T(8,128)(2,1)} %collective-permute-done.12.rest_2_, ...), custom_call_target="tpu_custom_call" | custom-call | flops 12650000384 | bytes 1048576 | tf_op jit(solution)/shard_map/pallas_call | solution.py:403
  187.5 3.5 %shard_map.269 = (bf16[1,4,96,384]{3,2,1,0:T(8,128)(2,1)}, bf16[1,4,96,384]{3,2,1,0:T(8,128)(2,1)}, bf16[2,4,96,384]{3,2,1,0:T(8,128)(2,1)}, bf16[2,4,96,384]{3,...) custom-call(bf16[8,4,96,384]{3,2,1,0:T(8,128)(2,1)} %get-tuple-eleme, ...), custom_call_target="tpu_custom_call", output_to_operand_aliasing={{4}: (10, {}), {5}: (11, {})} | custom-call | flops 3449999872 | bytes 1048576 | tf_op jit(solution)/shard_map/pallas_call | solution.py:548
  193.8 1.2 collective-permute-start.36
  195.1 7.7 %shard_map.270 = (f32[512,768]{1,0:T(8,128)}, f32[512,768]{1,0:T(8,128)}) custom-call(s32[2]{0:T(128)} %pad_add_fusion.me_ref, bf16[2,4,96,768]{3,2,1,0:T(8,128)(2,1)} %pad_maximum_fusion.1.rest_0_, bf16[2,4,96,768]{3,2,1,0:T(8,128)(2,1)} %get-tuple-element.111.rest_1_, bf16[2,4,96,768]{3,2,1,0:T(8,128)(2,1)} %collective-permute-done.18.rest_2_, ...), custom_call_target="tpu_custom_call" | custom-call | flops 10350000128 | bytes 1048576 | tf_op jit(solution)/shard_map/pallas_call | solution.py:432
  202.8 9.6 %collective-permute-done.35.refs_10_.refs_2_ = bf16[2,4,96,384]{3,2,1,0:T(8,128)(2,1)S(1)} collective-permute-done((bf16[2,4,96,384]{3,2,1,0:T(8,128)(2,1)}, bf16[2,4,96,384]{3,2,1,0:T(8,128)(2,1)S(1)}, u32[]{:S(2)}, u32[]{:S(2)}) %collective-permute-start.35) | collective-permute-done | bytes 589856 | tf_op jit(solution)/shard_map/ppermute | solution.py:467
  213.4 3.5 %shard_map.271 = (bf16[1,4,96,768]{3,2,1,0:T(8,128)(2,1)}, bf16[1,4,96,384]{3,2,1,0:T(8,128)(2,1)}, bf16[1,4,96,384]{3,2,1,0:T(8,128)(2,1)}, bf16[96,768]{1,0:T(8,128)(2,1)}) custom-call(bf16[8,4,96,384]{3,2,1,0:T(8,128)(2,1)} %get-tuple-element.131.refs_8_.refs_10_.refs_0_.refs_3_.refs_4_, ...), custom_call_target="tpu_custom_call", output_to_operand_aliasing={{3}: (14, {})} | custom-call | flops 3449999872 | bytes 1048576 | tf_op jit(solution)/shard_map/pallas_call | solution.py:548
  216.9 1.2 collective-permute-start.38
  218.9 1.2 slice_bitcast_fusion.8
  221.1 2.1 collective-permute-start.45
  225.1 10.3 %shard_map.272 = (bf16[512,768]{1,0:T(8,128)(2,1)}, bf16[512,768]{1,0:T(8,128)(2,1)}, f32[16,768]{1,0:T(8,128)}) custom-call(s32[2]{0:T(128)} %pad_add_fusion.me_ref, bf16[2,4,96,768]{3,2,1,0:T(8,128)(2,1)} %pad_maximum_fusion.1.rest_0_, bf16[2,4,96,768]{3,2,1,0:T(8,128)(2,1)} %get-tuple-element.111.rest_1_, ...), custom_call_target="tpu_custom_call" | custom-call | flops 10350000128 | bytes 1048576 | tf_op jit(solution)/shard_map/pallas_call | solution.py:432
  236.2 2.7 %shard_map.273 = (bf16[1,4,96,768]{3,2,1,0:T(8,128)(2,1)}, f32[16,768]{1,0:T(8,128)}) custom-call(bf16[8,4,96,384]{3,2,1,0:T(8,128)(2,1)} %get-tuple-element.139.refs_6_.refs_8_.refs_11_.refs_0_.refs_4_, bf16[8,4,96,384]{3,2,1,0:T(8,128)(2,1)} %copy-done.4, bf16[2,4,96,384]{3,2,1,0:T(8,128)(2,1)} %copy-done.15, ...), custom_call_target="tpu_custom_call", output_to_operand_aliasing={{1}: (8, {})} | custom-call | flops 3449999872 | bytes 1048576 | tf_op jit(solution)/shard_map/pallas_call | solution.py:548
  238.9 1.2 slice_bitcast_fusion.6
  240.1 2.3 collective-permute-start.43
  243.6 3.0 %collective-permute-done.41 = f32[16,768]{1,0:T(8,128)S(1)} collective-permute-done((f32[16,768]{1,0:T(8,128)S(1)}, f32[16,768]{1,0:T(8,128)S(1)}, u32[]{:S(2)}, u32[]{:S(2)}) %collective-permute-start.41) | collective-permute-done | bytes 49184 | tf_op jit(solution)/shard_map/ppermute | solution.py:467
  252.1 4.3 %collective-permute-done.46 = f32[16,768]{1,0:T(8,128)S(1)} collective-permute-done((f32[16,768]{1,0:T(8,128)}, f32[16,768]{1,0:T(8,128)S(1)}, u32[]{:S(2)}, u32[]{:S(2)}) %collective-permute-start.46) | collective-permute-done | bytes 49184 | tf_op jit(solution)/shard_map/ppermute | solution.py:467
  257.4 1.3 add_convert_fusion
  259.7 2.5 collective-permute-done.47
  264.1 2.1 collective-permute-done.49
  (249 shorter events, 59.3 us)
Async XLA Ops:
  3.2 12.7 %collective-permute-start.2 = (bf16[96,768]{1,0:T(8,128)(2,1)S(1)}, bf16[96,768]{1,0:T(8,128)(2,1)S(1)}, u32[]{:S(2)}, u32[]{:S(2)}) collective-permute-start(bf16[96,768]{1,0:T(8,128)(2,1)S(1)} %copy.70), channel_id=1, source_target_pairs={{0,3},{1,0},{2,1},{3,2},{4,7},{5,4},{6,5},{7,6},{8,11},{9,8},{10,9... | collective-permute-start | bytes 442376 | tf_op jit(solution)/shard_map/ppermute | solution.py:472
  8.3 12.5 %collective-permute-start.1 = (bf16[96,768]{1,0:T(8,128)(2,1)S(1)}, bf16[96,768]{1,0:T(8,128)(2,1)S(1)}, u32[]{:S(2)}, u32[]{:S(2)}) collective-permute-start(bf16[96,768]{1,0:T(8,128)(2,1)S(1)} %copy.70), channel_id=1, source_target_pairs={{0,2},{1,3},{2,0},{3,1},{4,6},{5,7},{6,4},{7,5},{8,10},{9,11},{10,... | collective-permute-start | bytes 442376 | tf_op jit(solution)/shard_map/ppermute | solution.py:472
  8.3 12.5 %collective-permute-start = (bf16[96,768]{1,0:T(8,128)(2,1)S(1)}, bf16[96,768]{1,0:T(8,128)(2,1)S(1)}, u32[]{:S(2)}, u32[]{:S(2)}) collective-permute-start(bf16[96,768]{1,0:T(8,128)(2,1)S(1)} %copy.70), channel_id=1, source_target_pairs={{0,1},{1,2},{2,3},{3,0},{4,5},{5,6},{6,7},{7,4},{8,9},{9,10},{10,1... | collective-permute-start | bytes 442376 | tf_op jit(solution)/shard_map/ppermute | solution.py:472
  20.9 11.6 %collective-permute-start.6 = (bf16[1,4,96,384]{3,2,1,0:T(8,128)(2,1)S(1)}, bf16[1,4,96,384]{3,2,1,0:T(8,128)(2,1)S(1)}, u32[]{:S(2)}, u32[]{:S(2)}) collective-permute-start(bf16[1,4,96,384]{3,2,1,0:T(8,128)(2,1)S(1)} %get-tuple-element.214.__1_), channel_id=1, source_target_pairs={{0,8},{4,12},{8,0},{12,4},{1,9},{5,13},{9,1},{13,5},{2,10},{6,14},... | collective-permute-start | bytes 884744 | tf_op jit(solution)/shard_map/ppermute | solution.py:467
  22.5 10.0 %collective-permute-start.3 = (bf16[96,1536]{1,0:T(8,128)(2,1)}, bf16[96,1536]{1,0:T(8,128)(2,1)S(1)}, u32[]{:S(2)}, u32[]{:S(2)}) collective-permute-start(bf16[96,1536]{1,0:T(8,128)(2,1)} %shard_map.254.__0_), channel_id=1, source_target_pairs={{0,1},{1,2},{2,3},{3,0},{4,5},{5,6},{6,7},{7,4},{8,9},{9,10},{10,1... | collective-permute-start | bytes 884744 | tf_op jit(solution)/shard_map/ppermute | solution.py:472
  23.3 9.2 %collective-permute-start.7 = (bf16[1,4,96,384]{3,2,1,0:T(8,128)(2,1)S(1)}, bf16[1,4,96,384]{3,2,1,0:T(8,128)(2,1)S(1)}, u32[]{:S(2)}, u32[]{:S(2)}) collective-permute-start(bf16[1,4,96,384]{3,2,1,0:T(8,128)(2,1)S(1)} %get-tuple-element.213), channel_id=1, source_target_pairs={{0,16},{16,0},{1,17},{17,1},{2,18},{18,2},{3,19},{19,3},{4,20},{20... | collective-permute-start | bytes 884744 | tf_op jit(solution)/shard_map/ppermute | solution.py:467
  35.5 17.9 %collective-permute-start.8 = (bf16[2,4,96,384]{3,2,1,0:T(8,128)(2,1)S(1)}, bf16[2,4,96,384]{3,2,1,0:T(8,128)(2,1)S(1)}, u32[]{:S(2)}, u32[]{:S(2)}) collective-permute-start(bf16[2,4,96,384]{3,2,1,0:T(8,128)(2,1)S(1)} %pad_maximum_fusion.4.rest_0_), channel_id=1, source_target_pairs={{0,16},{16,0},{1,17},{17,1},{2,18},{18,2},{3,19},{19,3},{4,20},{20... | collective-permute-start | bytes 1769480 | tf_op jit(solution)/shard_map/ppermute | solution.py:467
  37.1 16.3 %collective-permute-start.9 = (bf16[2,4,96,384]{3,2,1,0:T(8,128)(2,1)S(1)}, bf16[2,4,96,384]{3,2,1,0:T(8,128)(2,1)}, u32[]{:S(2)}, u32[]{:S(2)}) collective-permute-start(bf16[2,4,96,384]{3,2,1,0:T(8,128)(2,1)S(1)} %pad_maximum_fusion.5.rest_4_), channel_id=1, source_target_pairs={{0,8},{4,12},{8,0},{12,4},{1,9},{5,13},{9,1},{13,5},{2,10},{6,14},... | collective-permute-start | bytes 1769480 | tf_op jit(solution)/shard_map/ppermute | solution.py:467
  39.3 14.0 %collective-permute-start.4 = (bf16[96,1536]{1,0:T(8,128)(2,1)S(1)}, bf16[96,1536]{1,0:T(8,128)(2,1)S(1)}, u32[]{:S(2)}, u32[]{:S(2)}) collective-permute-start(bf16[96,1536]{1,0:T(8,128)(2,1)S(1)} %copy-done.8), channel_id=1, source_target_pairs={{0,2},{1,3},{2,0},{3,1},{4,6},{5,7},{6,4},{7,5},{8,10},{9,11},{10,... | collective-permute-start | bytes 884744 | tf_op jit(solution)/shard_map/ppermute | solution.py:472
  40.2 13.1 %collective-permute-start.5 = (bf16[96,1536]{1,0:T(8,128)(2,1)S(1)}, bf16[96,1536]{1,0:T(8,128)(2,1)S(1)}, u32[]{:S(2)}, u32[]{:S(2)}) collective-permute-start(bf16[96,1536]{1,0:T(8,128)(2,1)S(1)} %copy-done.8), channel_id=1, source_target_pairs={{0,3},{1,0},{2,1},{3,2},{4,7},{5,4},{6,5},{7,6},{8,11},{9,8},{10,9... | collective-permute-start | bytes 884744 | tf_op jit(solution)/shard_map/ppermute | solution.py:472
  43.8 13.8 %collective-permute-start.12 = (bf16[2,4,96,384]{3,2,1,0:T(8,128)(2,1)S(1)}, bf16[2,4,96,384]{3,2,1,0:T(8,128)(2,1)}, u32[]{:S(2)}, u32[]{:S(2)}) collective-permute-start(bf16[2,4,96,384]{3,2,1,0:T(8,128)(2,1)S(1)} %pad_maximum_fusion.4.rest_0_), channel_id=1, source_target_pairs={{0,4},{4,0},{8,12},{12,8},{1,5},{5,1},{9,13},{13,9},{2,6},{6,2},{1... | collective-permute-start | bytes 1769480 | tf_op jit(solution)/shard_map/ppermute | solution.py:467
  53.3 5.3 %collective-permute-start.14 = (bf16[2,4,96,384]{3,2,1,0:T(8,128)(2,1)S(1)}, bf16[2,4,96,384]{3,2,1,0:T(8,128)(2,1)}, u32[]{:S(2)}, u32[]{:S(2)}) collective-permute-start(bf16[2,4,96,384]{3,2,1,0:T(8,128)(2,1)S(1)} %pad_maximum_fusion.5.rest_4_), channel_id=1, source_target_pairs={{0,4},{4,0},{8,12},{12,8},{1,5},{5,1},{9,13},{13,9},{2,6},{6,2},{1... | collective-permute-start | bytes 1769480 | tf_op jit(solution)/shard_map/ppermute | solution.py:467
  54.4 4.3 %collective-permute-start.13 = (bf16[2,4,96,384]{3,2,1,0:T(8,128)(2,1)}, bf16[2,4,96,384]{3,2,1,0:T(8,128)(2,1)}, u32[]{:S(2)}, u32[]{:S(2)}) collective-permute-start(bf16[2,4,96,384]{3,2,1,0:T(8,128)(2,1)} %get-tuple-element.92.__4_.rest_1_), channel_id=1, source_target_pairs={{0,4},{4,0},{8,12},{12,8},{1,5},{5,1},{9,13},{13,9},{2,6},{6,2},{1... | collective-permute-start | bytes 1769480 | tf_op jit(solution)/shard_map/ppermute | solution.py:467
  56.3 17.3 %collective-permute-start.10 = (bf16[1,4,96,768]{3,2,1,0:T(8,128)(2,1)S(1)}, bf16[1,4,96,768]{3,2,1,0:T(8,128)(2,1)S(1)}, u32[]{:S(2)}, u32[]{:S(2)}) collective-permute-start(bf16[1,4,96,768]{3,2,1,0:T(8,128)(2,1)S(1)} %get-tuple-element.199), channel_id=1, source_target_pairs={{0,8},{4,12},{8,0},{12,4},{1,9},{5,13},{9,1},{13,5},{2,10},{6,14},... | collective-permute-start | bytes 1769480 | tf_op jit(solution)/shard_map/ppermute | solution.py:467
  57.6 16.1 %collective-permute-start.11 = (bf16[1,4,96,768]{3,2,1,0:T(8,128)(2,1)S(1)}, bf16[1,4,96,768]{3,2,1,0:T(8,128)(2,1)S(1)}, u32[]{:S(2)}, u32[]{:S(2)}) collective-permute-start(bf16[1,4,96,768]{3,2,1,0:T(8,128)(2,1)S(1)} %get-tuple-element.198), channel_id=1, source_target_pairs={{0,16},{16,0},{1,17},{17,1},{2,18},{18,2},{3,19},{19,3},{4,20},{20... | collective-permute-start | bytes 1769480 | tf_op jit(solution)/shard_map/ppermute | solution.py:467
  77.0 28.0 %collective-permute-start.16 = (bf16[2,4,96,768]{3,2,1,0:T(8,128)(2,1)}, bf16[2,4,96,768]{3,2,1,0:T(8,128)(2,1)S(1)}, u32[]{:S(2)}, u32[]{:S(2)}) collective-permute-start(bf16[2,4,96,768]{3,2,1,0:T(8,128)(2,1)} %pad_maximum_fusion.1.rest_0_), channel_id=1, source_target_pairs={{0,16},{16,0},{1,17},{17,1},{2,18},{18,2},{3,19},{19,3},{4,20},{20... | collective-permute-start | bytes 3538952 | tf_op jit(solution)/shard_map/ppermute | solution.py:467
  79.1 27.7 %collective-permute-start.17 = (bf16[2,4,96,768]{3,2,1,0:T(8,128)(2,1)}, bf16[2,4,96,768]{3,2,1,0:T(8,128)(2,1)S(1)}, u32[]{:S(2)}, u32[]{:S(2)}) collective-permute-start(bf16[2,4,96,768]{3,2,1,0:T(8,128)(2,1)} %pad_maximum_fusion.2.rest_4_), channel_id=1, source_target_pairs={{0,8},{4,12},{8,0},{12,4},{1,9},{5,13},{9,1},{13,5},{2,10},{6,14},... | collective-permute-start | bytes 3538952 | tf_op jit(solution)/shard_map/ppermute | solution.py:467
  107.8 11.5 %collective-permute-start.22 = (bf16[8,4,96,384]{3,2,1,0:T(8,128)(2,1)}, bf16[8,4,96,384]{3,2,1,0:T(8,128)(2,1)S(1)}, u32[]{:S(2)}, u32[]{:S(2)}) collective-permute-start(bf16[8,4,96,384]{3,2,1,0:T(8,128)(2,1)} %get-tuple-element.116), channel_id=1, source_target_pairs={{0,4},{4,0},{8,12},{12,8},{1,5},{5,1},{9,13},{13,9},{2,6},{6,2},{1... | collective-permute-start | bytes 7077896 | tf_op jit(solution)/shard_map/ppermute | solution.py:467
  107.8 8.1 %collective-permute-start.19 = (bf16[2,4,96,768]{3,2,1,0:T(8,128)(2,1)}, bf16[2,4,96,768]{3,2,1,0:T(8,128)(2,1)S(1)}, u32[]{:S(2)}, u32[]{:S(2)}) collective-permute-start(bf16[2,4,96,768]{3,2,1,0:T(8,128)(2,1)} %get-tuple-element.111.rest_1_), channel_id=1, source_target_pairs={{0,4},{4,0},{8,12},{12,8},{1,5},{5,1},{9,13},{13,9},{2,6},{6,2},{1... | collective-permute-start | bytes 3538952 | tf_op jit(solution)/shard_map/ppermute | solution.py:467
  108.3 11.0 %collective-permute-start.21 = (bf16[2,4,96,768]{3,2,1,0:T(8,128)(2,1)}, bf16[2,4,96,768]{3,2,1,0:T(8,128)(2,1)S(1)}, u32[]{:S(2)}, u32[]{:S(2)}) collective-permute-start(bf16[2,4,96,768]{3,2,1,0:T(8,128)(2,1)} %get-tuple-element.112.rest_5_), channel_id=1, source_target_pairs={{0,4},{4,0},{8,12},{12,8},{1,5},{5,1},{9,13},{13,9},{2,6},{6,2},{1... | collective-permute-start | bytes 3538952 | tf_op jit(solution)/shard_map/ppermute | solution.py:467
  108.3 18.2 %collective-permute-start.18 = (bf16[2,4,96,768]{3,2,1,0:T(8,128)(2,1)}, bf16[2,4,96,768]{3,2,1,0:T(8,128)(2,1)}, u32[]{:S(2)}, u32[]{:S(2)}) collective-permute-start(bf16[2,4,96,768]{3,2,1,0:T(8,128)(2,1)} %pad_maximum_fusion.1.rest_0_), channel_id=1, source_target_pairs={{0,4},{4,0},{8,12},{12,8},{1,5},{5,1},{9,13},{13,9},{2,6},{6,2},{1... | collective-permute-start | bytes 3538952 | tf_op jit(solution)/shard_map/ppermute | solution.py:467
  108.8 17.7 %collective-permute-start.20 = (bf16[2,4,96,768]{3,2,1,0:T(8,128)(2,1)}, bf16[2,4,96,768]{3,2,1,0:T(8,128)(2,1)}, u32[]{:S(2)}, u32[]{:S(2)}) collective-permute-start(bf16[2,4,96,768]{3,2,1,0:T(8,128)(2,1)} %pad_maximum_fusion.2.rest_4_), channel_id=1, source_target_pairs={{0,4},{4,0},{8,12},{12,8},{1,5},{5,1},{9,13},{13,9},{2,6},{6,2},{1... | collective-permute-start | bytes 3538952 | tf_op jit(solution)/shard_map/ppermute | solution.py:467
  124.5 15.6 %collective-permute-start.23 = (bf16[2,4,96,384]{3,2,1,0:T(8,128)(2,1)}, bf16[2,4,96,384]{3,2,1,0:T(8,128)(2,1)S(1)}, u32[]{:S(2)}, u32[]{:S(2)}) collective-permute-start(bf16[2,4,96,384]{3,2,1,0:T(8,128)(2,1)} %get-tuple-element.117.rest_9_), channel_id=1, source_target_pairs={{0,8},{4,12},{8,0},{12,4},{1,9},{5,13},{9,1},{13,5},{2,10},{6,14},... | collective-permute-start | bytes 1769480 | tf_op jit(solution)/shard_map/ppermute | solution.py:467
  125.4 15.3 %collective-permute-start.24 = (bf16[2,4,96,384]{3,2,1,0:T(8,128)(2,1)}, bf16[2,4,96,384]{3,2,1,0:T(8,128)(2,1)S(1)}, u32[]{:S(2)}, u32[]{:S(2)}) collective-permute-start(bf16[2,4,96,384]{3,2,1,0:T(8,128)(2,1)} %get-tuple-element.118), channel_id=1, source_target_pairs={{0,16},{16,0},{1,17},{17,1},{2,18},{18,2},{3,19},{19,3},{4,20},{20... | collective-permute-start | bytes 1769480 | tf_op jit(solution)/shard_map/ppermute | solution.py:467
  143.9 13.2 %collective-permute-start.27 = (bf16[8,4,96,384]{3,2,1,0:T(8,128)(2,1)}, bf16[8,4,96,384]{3,2,1,0:T(8,128)(2,1)S(1)}, u32[]{:S(2)}, u32[]{:S(2)}) collective-permute-start(bf16[8,4,96,384]{3,2,1,0:T(8,128)(2,1)} %get-tuple-element.132), channel_id=1, source_target_pairs={{0,4},{4,0},{8,12},{12,8},{1,5},{5,1},{9,13},{13,9},{2,6},{6,2},{1... | collective-permute-start | bytes 7077896 | tf_op jit(solution)/shard_map/ppermute | solution.py:467
  143.9 13.2 %collective-permute-start.25 = (bf16[1,4,96,384]{3,2,1,0:T(8,128)(2,1)}, bf16[1,4,96,384]{3,2,1,0:T(8,128)(2,1)S(1)}, u32[]{:S(2)}, u32[]{:S(2)}) collective-permute-start(bf16[1,4,96,384]{3,2,1,0:T(8,128)(2,1)} %get-tuple-element.121.rest_9_), channel_id=1, source_target_pairs={{0,16},{16,0},{1,17},{17,1},{2,18},{18,2},{3,19},{19,3},{4,20},{20... | collective-permute-start | bytes 884744 | tf_op jit(solution)/shard_map/ppermute | solution.py:467
  145.0 12.1 %collective-permute-start.26 = (bf16[1,4,96,384]{3,2,1,0:T(8,128)(2,1)}, bf16[1,4,96,384]{3,2,1,0:T(8,128)(2,1)S(1)}, u32[]{:S(2)}, u32[]{:S(2)}) collective-permute-start(bf16[1,4,96,384]{3,2,1,0:T(8,128)(2,1)} %get-tuple-element.130), channel_id=1, source_target_pairs={{0,8},{4,12},{8,0},{12,4},{1,9},{5,13},{9,1},{13,5},{2,10},{6,14},... | collective-permute-start | bytes 884744 | tf_op jit(solution)/shard_map/ppermute | solution.py:467
  162.5 23.3 %collective-permute-start.30 = (bf16[8,4,96,384]{3,2,1,0:T(8,128)(2,1)}, bf16[8,4,96,384]{3,2,1,0:T(8,128)(2,1)S(1)}, u32[]{:S(2)}, u32[]{:S(2)}) collective-permute-start(bf16[8,4,96,384]{3,2,1,0:T(8,128)(2,1)} %get-tuple-element.140), channel_id=1, source_target_pairs={{0,4},{4,0},{8,12},{12,8},{1,5},{5,1},{9,13},{13,9},{2,6},{6,2},{1... | collective-permute-start | bytes 7077896 | tf_op jit(solution)/shard_map/ppermute | solution.py:467
  163.7 22.1 %collective-permute-start.28 = (bf16[2,4,96,384]{3,2,1,0:T(8,128)(2,1)}, bf16[2,4,96,384]{3,2,1,0:T(8,128)(2,1)S(1)}, u32[]{:S(2)}, u32[]{:S(2)}) collective-permute-start(bf16[2,4,96,384]{3,2,1,0:T(8,128)(2,1)} %get-tuple-element.137), channel_id=1, source_target_pairs={{0,8},{4,12},{8,0},{12,4},{1,9},{5,13},{9,1},{13,5},{2,10},{6,14},... | collective-permute-start | bytes 1769480 | tf_op jit(solution)/shard_map/ppermute | solution.py:467
  164.6 21.2 %collective-permute-start.29 = (bf16[2,4,96,384]{3,2,1,0:T(8,128)(2,1)}, bf16[2,4,96,384]{3,2,1,0:T(8,128)(2,1)}, u32[]{:S(2)}, u32[]{:S(2)}) collective-permute-start(bf16[2,4,96,384]{3,2,1,0:T(8,128)(2,1)} %get-tuple-element.138), channel_id=1, source_target_pairs={{0,16},{16,0},{1,17},{17,1},{2,18},{18,2},{3,19},{19,3},{4,20},{20... | collective-permute-start | bytes 1769480 | tf_op jit(solution)/shard_map/ppermute | solution.py:467
  166.6 18.1 %collective-permute-start.31 = (bf16[96,768]{1,0:T(8,128)(2,1)S(1)}, bf16[96,768]{1,0:T(8,128)(2,1)S(1)}, u32[]{:S(2)}, u32[]{:S(2)}) collective-permute-start(bf16[96,768]{1,0:T(8,128)(2,1)S(1)} %get-tuple-element.212), channel_id=1, source_target_pairs={{0,2},{1,3},{2,0},{3,1},{4,6},{5,7},{6,4},{7,5},{8,10},{9,11},{10,... | collective-permute-start | bytes 442376 | tf_op jit(solution)/shard_map/ppermute | solution.py:472
  171.9 13.9 %collective-permute-start.32 = (bf16[96,768]{1,0:T(8,128)(2,1)S(1)}, bf16[96,768]{1,0:T(8,128)(2,1)S(1)}, u32[]{:S(2)}, u32[]{:S(2)}) collective-permute-start(bf16[96,768]{1,0:T(8,128)(2,1)S(1)} %get-tuple-element.211), channel_id=1, source_target_pairs={{0,1},{1,2},{2,3},{3,0},{4,5},{5,6},{6,7},{7,4},{8,9},{9,10},{10,1... | collective-permute-start | bytes 442376 | tf_op jit(solution)/shard_map/ppermute | solution.py:472
  184.7 18.0 %collective-permute-start.37 = (bf16[96,768]{1,0:T(8,128)(2,1)S(1)}, bf16[96,768]{1,0:T(8,128)(2,1)S(1)}, u32[]{:S(2)}, u32[]{:S(2)}) collective-permute-start(bf16[96,768]{1,0:T(8,128)(2,1)S(1)} %get-tuple-element.210), channel_id=1, source_target_pairs={{0,3},{1,0},{2,1},{3,2},{4,7},{5,4},{6,5},{7,6},{8,11},{9,8},{10,9... | collective-permute-start | bytes 442376 | tf_op jit(solution)/shard_map/ppermute | solution.py:472
  191.0 11.7 %collective-permute-start.33 = (bf16[1,4,96,384]{3,2,1,0:T(8,128)(2,1)}, bf16[1,4,96,384]{3,2,1,0:T(8,128)(2,1)S(1)}, u32[]{:S(2)}, u32[]{:S(2)}) collective-permute-start(bf16[1,4,96,384]{3,2,1,0:T(8,128)(2,1)} %get-tuple-element.141.rest_11_), channel_id=1, source_target_pairs={{0,16},{16,0},{1,17},{17,1},{2,18},{18,2},{3,19},{19,3},{4,20},{20... | collective-permute-start | bytes 884744 | tf_op jit(solution)/shard_map/ppermute | solution.py:467
  191.8 11.0 %collective-permute-start.34 = (bf16[1,4,96,384]{3,2,1,0:T(8,128)(2,1)}, bf16[1,4,96,384]{3,2,1,0:T(8,128)(2,1)S(1)}, u32[]{:S(2)}, u32[]{:S(2)}) collective-permute-start(bf16[1,4,96,384]{3,2,1,0:T(8,128)(2,1)} %get-tuple-element.145), channel_id=1, source_target_pairs={{0,8},{4,12},{8,0},{12,4},{1,9},{5,13},{9,1},{13,5},{2,10},{6,14},... | collective-permute-start | bytes 884744 | tf_op jit(solution)/shard_map/ppermute | solution.py:467
  192.7 19.7 %collective-permute-start.35 = (bf16[2,4,96,384]{3,2,1,0:T(8,128)(2,1)}, bf16[2,4,96,384]{3,2,1,0:T(8,128)(2,1)S(1)}, u32[]{:S(2)}, u32[]{:S(2)}) collective-permute-start(bf16[2,4,96,384]{3,2,1,0:T(8,128)(2,1)} %get-tuple-element.146), channel_id=1, source_target_pairs={{0,8},{4,12},{8,0},{12,4},{1,9},{5,13},{9,1},{13,5},{2,10},{6,14},... | collective-permute-start | bytes 1769480 | tf_op jit(solution)/shard_map/ppermute | solution.py:467
  193.8 18.6 %collective-permute-start.36 = (bf16[2,4,96,384]{3,2,1,0:T(8,128)(2,1)}, bf16[2,4,96,384]{3,2,1,0:T(8,128)(2,1)S(1)}, u32[]{:S(2)}, u32[]{:S(2)}) collective-permute-start(bf16[2,4,96,384]{3,2,1,0:T(8,128)(2,1)} %get-tuple-element.147), channel_id=1, source_target_pairs={{0,16},{16,0},{1,17},{17,1},{2,18},{18,2},{3,19},{19,3},{4,20},{20... | collective-permute-start | bytes 1769480 | tf_op jit(solution)/shard_map/ppermute | solution.py:467
  216.9 18.5 %collective-permute-start.38 = (bf16[1,4,96,384]{3,2,1,0:T(8,128)(2,1)}, bf16[1,4,96,384]{3,2,1,0:T(8,128)(2,1)S(1)}, u32[]{:S(2)}, u32[]{:S(2)}) collective-permute-start(bf16[1,4,96,384]{3,2,1,0:T(8,128)(2,1)} %get-tuple-element.151), channel_id=1, source_target_pairs={{0,16},{16,0},{1,17},{17,1},{2,18},{18,2},{3,19},{19,3},{4,20},{20... | collective-permute-start | bytes 884744 | tf_op jit(solution)/shard_map/ppermute | solution.py:467
  218.1 17.3 %collective-permute-start.39 = (bf16[1,4,96,384]{3,2,1,0:T(8,128)(2,1)}, bf16[1,4,96,384]{3,2,1,0:T(8,128)(2,1)S(1)}, u32[]{:S(2)}, u32[]{:S(2)}) collective-permute-start(bf16[1,4,96,384]{3,2,1,0:T(8,128)(2,1)} %get-tuple-element.152), channel_id=1, source_target_pairs={{0,8},{4,12},{8,0},{12,4},{1,9},{5,13},{9,1},{13,5},{2,10},{6,14},... | collective-permute-start | bytes 884744 | tf_op jit(solution)/shard_map/ppermute | solution.py:467
  220.2 31.2 %collective-permute-start.44 = (bf16[96,1536]{1,0:T(8,128)(2,1)S(1)}, bf16[96,1536]{1,0:T(8,128)(2,1)S(1)}, u32[]{:S(2)}, u32[]{:S(2)}) collective-permute-start(bf16[96,1536]{1,0:T(8,128)(2,1)S(1)} %pad_maximum_fusion.9), channel_id=1, source_target_pairs={{0,2},{1,3},{2,0},{3,1},{4,6},{5,7},{6,4},{7,5},{8,10},{9,11},{10,... | collective-permute-start | bytes 884744 | tf_op jit(solution)/shard_map/ppermute | solution.py:472
  221.1 30.3 %collective-permute-start.45 = (bf16[96,1536]{1,0:T(8,128)(2,1)S(1)}, bf16[96,1536]{1,0:T(8,128)(2,1)}, u32[]{:S(2)}, u32[]{:S(2)}) collective-permute-start(bf16[96,1536]{1,0:T(8,128)(2,1)S(1)} %pad_maximum_fusion.10), channel_id=1, source_target_pairs={{0,1},{1,2},{2,3},{3,0},{4,5},{5,6},{6,7},{7,4},{8,9},{9,10},{10,1... | collective-permute-start | bytes 884744 | tf_op jit(solution)/shard_map/ppermute | solution.py:472
  224.2 19.2 %collective-permute-start.48 = (bf16[96,768]{1,0:T(8,128)(2,1)S(1)}, bf16[96,768]{1,0:T(8,128)(2,1)S(1)}, u32[]{:S(2)}, u32[]{:S(2)}) collective-permute-start(bf16[96,768]{1,0:T(8,128)(2,1)S(1)} %fusion.2), channel_id=1, source_target_pairs={{0,16},{16,0},{1,17},{17,1},{2,18},{18,2},{3,19},{19,3},{4,20},{20... | collective-permute-start | bytes 442376 | tf_op jit(solution)/shard_map/ppermute | solution.py:467
  240.1 11.2 %collective-permute-start.43 = (bf16[96,1536]{1,0:T(8,128)(2,1)S(1)}, bf16[96,1536]{1,0:T(8,128)(2,1)}, u32[]{:S(2)}, u32[]{:S(2)}) collective-permute-start(bf16[96,1536]{1,0:T(8,128)(2,1)S(1)} %pad_maximum_fusion.8), channel_id=1, source_target_pairs={{0,3},{1,0},{2,1},{3,2},{4,7},{5,4},{6,5},{7,6},{8,11},{9,8},{10,9... | collective-permute-start | bytes 884744 | tf_op jit(solution)/shard_map/ppermute | solution.py:472
  242.4 4.2 %collective-permute-start.41 = (f32[16,768]{1,0:T(8,128)S(1)}, f32[16,768]{1,0:T(8,128)S(1)}, u32[]{:S(2)}, u32[]{:S(2)}) collective-permute-start(f32[16,768]{1,0:T(8,128)S(1)} %add.95), channel_id=1, source_target_pairs={{0,8},{4,12},{8,0},{12,4},{1,9},{5,13},{9,1},{13,5},{2,10},{6,14},... | collective-permute-start | bytes 147464 | tf_op jit(solution)/shard_map/ppermute | solution.py:467
  246.6 4.2 %collective-permute-start.42 = (f32[16,768]{1,0:T(8,128)S(1)}, f32[16,768]{1,0:T(8,128)S(1)}, u32[]{:S(2)}, u32[]{:S(2)}) collective-permute-start(f32[16,768]{1,0:T(8,128)S(1)} %add.96), channel_id=1, source_target_pairs={{0,16},{16,0},{1,17},{17,1},{2,18},{18,2},{3,19},{19,3},{4,20},{20... | collective-permute-start | bytes 147464 | tf_op jit(solution)/shard_map/ppermute | solution.py:467
  252.1 4.3 %collective-permute-start.46 = (f32[16,768]{1,0:T(8,128)}, f32[16,768]{1,0:T(8,128)S(1)}, u32[]{:S(2)}, u32[]{:S(2)}) collective-permute-start(f32[16,768]{1,0:T(8,128)} %get-tuple-element.156), channel_id=1, source_target_pairs={{0,1},{1,0},{2,3},{3,2},{4,5},{5,4},{6,7},{7,6},{8,9},{9,8},{10,11... | collective-permute-start | bytes 147464 | tf_op jit(solution)/shard_map/ppermute | solution.py:467
  257.2 5.0 %collective-permute-start.47 = (f32[16,768]{1,0:T(8,128)S(1)}, f32[16,768]{1,0:T(8,128)S(1)}, u32[]{:S(2)}, u32[]{:S(2)}) collective-permute-start(f32[16,768]{1,0:T(8,128)S(1)} %add.98), channel_id=1, source_target_pairs={{0,2},{1,3},{2,0},{3,1},{4,6},{5,7},{6,4},{7,5},{8,10},{9,11},{10,... | collective-permute-start | bytes 147464 | tf_op jit(solution)/shard_map/ppermute | solution.py:467
  258.7 7.6 %collective-permute-start.49 = (bf16[96,1536]{1,0:T(8,128)(2,1)S(1)}, bf16[96,1536]{1,0:T(8,128)(2,1)S(1)}, u32[]{:S(2)}, u32[]{:S(2)}) collective-permute-start(bf16[96,1536]{1,0:T(8,128)(2,1)S(1)} %add_convert_fusion), channel_id=1, source_target_pairs={{0,16},{16,0},{1,17},{17,1},{2,18},{18,2},{3,19},{19,3},{4,20},{20... | collective-permute-start | bytes 884744 | tf_op jit(solution)/shard_map/ppermute | solution.py:467
  (55 other events, 211.7 us)

commit v2 on v1

--- a/solution.py
+++ b/solution.py
@@ -485,8 +485,11 @@
         self.moving = [swap(one, order[self.done]) for one, order in zip(self.held, self.orders)]
         self.done += 1
 
-    def cross(self):
-        self.over = [swap(one, self.core_bit) for one in self.held + self.moving]
+    def cross_held(self):
+        self.over = [swap(one, self.core_bit) for one in self.held]
+
+    def cross_moving(self):
+        self.over += [swap(one, self.core_bit) for one in self.moving]
 
     def sides(self):
         return ([self.held[i], self.moving[i], self.over[i], self.over[i + 2]] for i in range(2))
@@ -652,11 +655,15 @@
     mlp_blocks = gather_col(fence([mlp_own], [attn.held[0]])[0])
     for _ in range(far):
         attn.advance()
-        phase([attn], [], [na, mlp_blocks[1]] if attn.done == 1 else mlp_blocks[2:])
+        phase([attn], [], [na, mlp_blocks[1], mlp_blocks[-1]] if attn.done == 1 else mlp_blocks[2:-1])
     mlp_blocks = fence(mlp_blocks, attn.moving)
-    attn.cross()
-    mlp = Gather(jnp.stack(mlp_blocks), orders, core_bit)
-    mlp.advance()
+    attn.cross_held()
+    attn.cross_moving()
+    per_call = 2
+    starts = list(range(0, col_size, per_call))[::-1]
+    mlp = [Gather(jnp.stack(mlp_blocks[k0 : k0 + per_call]), orders, core_bit) for k0 in starts]
+    for one in mlp:
+        one.advance()
 
     def attention_call(weights, w0, k0, count, slots, slot0, into, after):
         return block_part(
@@ -677,27 +684,30 @@
         )
 
     per_mlp = up_cols // cut
-    per_call = 2
-    starts = list(range(0, col_size, per_call))[::-1]
     attn_calls, into, token = [], [], []
-    for k0 in starts:
-        outs = attention_call(attn, k0, k0, per_call, (1, col_size), k0 // 1, into, token)
+    for n, k0 in enumerate(starts):
+        if n == 1:
+            while mlp[0].done < far:
+                phase([one for one in mlp if one.done < far], [], token)
+                mlp[0].advance()
+                if mlp[1].done < far - 1:
+                    mlp[1].advance()
+            mlp[0].cross_held()
+            token = mlp[0].held[:1]
+        outs = attention_call(attn, k0, k0, per_call, (1, col_size), k0, into, token)
         attn_calls.append(outs)
         into = list(outs[3:])
-        sent = into[1:] if k0 == starts[-1] else []
-        token = phase([mlp], sent, [outs[2]])
-        sent, token = token[: len(sent)], token[-1:]
-        if mlp.done < far:
-            mlp.advance()
-            while mlp.done < far and k0 == starts[-1]:
-                phase([mlp])
-                mlp.advance()
-    while mlp.done < far:
-        mlp.advance()
-        token = phase([mlp])[:1]
-    mlp.cross()
+        token = [outs[2]]
+    sent = phase([mlp[0]], into[1:], token + mlp[0].over)
+    mlp[1].advance()
+    mlp[0].cross_moving()
+    token = sent[-1:]
     attn_sum = Reduction(into[0], sent[0], orders, core_bit)
-
+    begins = list(range(0, col_size + 1, per_call))
+    branch, d_norm_attn = attention_tail_part(
+        begins, starts, orders, core_bit, token, me, *attn.sides(), [[c[0] for c in attn_calls], [c[1] for c in attn_calls]],
+        [], 11,
+    )
     totals = {}
 
     def go_on(reductions, after, values=()):
@@ -707,12 +717,15 @@
         totals.update(zip((id(r) for r in ending), finished))
         return token, passed
 
-    token, _ = go_on([attn_sum], mlp.over[2:])
+    phase(mlp[1:], [], [branch] + mlp[0].over)
+    token, _ = go_on([attn_sum], [branch, mlp[1].moving[0]])
+    mlp[1].cross_held()
+    mlp[1].cross_moving()
     mlp_calls, mlp_sums = [], []
     for n, k0 in enumerate(starts):
-        outs = mlp_call(mlp, k0, k0, per_call, (per_mlp, per_mlp * per_call), 0, [], token)
+        outs = mlp_call(mlp[n], 0, k0, per_call, (per_mlp, per_mlp * per_call), 0, [], token)
         mlp_calls.append(outs)
-        token, sent = go_on([attn_sum] + mlp_sums, [outs[2]], [outs[4]])
+        token, sent = go_on([attn_sum] + mlp_sums, [outs[2]] + (mlp[1].over if n == 0 else []), [outs[4]])
         mlp_sums.append(Reduction(outs[3], sent[0], orders, core_bit))
     while id(attn_sum) not in totals:
         token, _ = go_on([attn_sum], token)
@@ -720,15 +733,6 @@
     attn_moves = {0: attn_total[0]}
     for k in range(2, col_size):
         attn_moves[k] = shifted(attn_total[k], -k)
-    begins = list(range(0, col_size + 1, per_call))
-    branch, d_norm_attn = attention_tail_part(
-        begins, starts, orders, core_bit, token, me, *attn.sides(), [[c[0] for c in attn_calls], [c[1] for c in attn_calls]],
-        [], 11,
-    )
-    token, passed = go_on(mlp_sums, [branch], [attn_moves[k] for k in range(2, col_size)])
-    attn_moves.update(zip(range(2, col_size), passed))
-    attn_moves[1] = shifted(attn_total[1], -1)
-
     def settle(parts):
         total = sum((part.astype(F32) for part in parts[1:]), parts[0].astype(F32))
         flip = 2
@@ -754,28 +758,31 @@
             down_bias[None, :],
         ]
         result = mlp_tail_part(
-            k0, orders, core_bit, token, me, *mlp.sides(), mlp_calls[n][0], mlp_calls[n][1], sums,
+            0, orders, core_bit, token, me, *mlp[n].sides(), mlp_calls[n][0], mlp_calls[n][1], sums,
             finals if last else [], (small_ks, small_parts) if last else None, 9,
         )
         if n == 0:
-            token, passed = go_on(mlp_sums, result[:1], [attn_moves[1]])
-            attn_moves[1] = passed[0]
+            token, passed = go_on(mlp_sums, result[:1], [attn_moves[k] for k in range(2, col_size)])
+            attn_moves.update(zip(range(2, col_size), passed))
+            attn_moves[1] = shifted(attn_total[1], -1)
+        else:
+            token, passed = go_on(mlp_sums, result[:1], list(result[2:]) + [attn_moves[1]])
+            attn_moves[1] = passed[-1]
             attn_mine, attn_other = settle([attn_moves[k] for k in range(col_size)])
-        else:
-            token, passed = go_on(mlp_sums, result[:1], result[2:])
         if last:
             block_out, in_grad, _ = result
             smalls = passed[0]
         else:
             branch, d_norm_mlp = result
-        while last and any(id(r) not in totals for r in mlp_sums):
-            token, _ = go_on(mlp_sums, token)
-        for k1, r in zip(starts, mlp_sums):
-            if id(r) in totals and k1 not in mlp_moves:
-                for i in range(per_call):
-                    slots = [totals[id(r)][i * per_mlp + j] for j in range(per_mlp)]
-                    part = jnp.concatenate([s[:, :cut] for s in slots] + [s[:, cut:] for s in slots], axis=1)
-                    mlp_moves[k1 + i] = part if k1 + i == 0 else shifted(part, -(k1 + i))
+        while last and len(mlp_moves) < col_size:
+            for k1, r in zip(starts, mlp_sums):
+                if id(r) in totals and k1 not in mlp_moves:
+                    for i in range(per_call):
+                        slots = [totals[id(r)][i * per_mlp + j] for j in range(per_mlp)]
+                        part = jnp.concatenate([s[:, :cut] for s in slots] + [s[:, cut:] for s in slots], axis=1)
+                        mlp_moves[k1 + i] = part if k1 + i == 0 else shifted(part, -(k1 + i))
+            if len(mlp_moves) < col_size:
+                token, _ = go_on(mlp_sums, token)
     head_row, up_row = 5 + col_size, 5
     smalls = sum_over(smalls, ("row", "dp"))
     smalls, *came = fence([smalls] + [mlp_moves[k] for k in range(1, col_size)])

time: 269 us -> 275 us (1.022)
  other arithmetic: 13.8 us -> 17.5 us
    ppermute x12, waiting for transfers between devices: 16 us -> 30.6 us  [shifted(): lax.ppermute(value, 'col', [(i, (i + by) % size) for i in range(size)])]
    ppermute x38 -> x46, waiting for transfers between devices: 47.6 us -> 35.3 us  [flipped(): lax.ppermute(value, axis, [(i, i ^ flip) for i in range(lax.axis_size(axi...]
    ppermute x38 -> x46, starting transfers between devices: 27.3 us -> 36.1 us  [flipped(): lax.ppermute(value, axis, [(i, i ^ flip) for i in range(lax.axis_size(axi...]
    ppermute x12, starting transfers between devices: 24.5 us -> 17.4 us  [shifted(): lax.ppermute(value, 'col', [(i, (i + by) % size) for i in range(size)])]
    unnamed x112 -> x118, local copies, waits for them, and re-layouts: 16.9 us -> 14.3 us
    concatenate x4 -> x6, other arithmetic: 4.54 us -> 5.92 us  [advance(): jnp.concatenate(pair, axis=0)]
  transfers between devices with their start and end apart: 50 -> 58, of which waited for: 15 -> 16; matrix products, arithmetic and copies ran while one was open for 9% -> 11% of each run, Pallas kernels for 35% -> 34%
where the time goes in v2:
time: 275 us; the launch traced here: 274 us
  Pallas kernels  104 us (38%)
  waiting for transfers between devices  65.9 us (24%)
  starting transfers between devices  53.5 us (19%)
  local copies, waits for them, and re-layouts  31.7 us (12%)
  other arithmetic  17.5 us (6%)
    pallas_call x4, Pallas kernels, block_part(): pl.pallas_call(functools.partial(kernel, orders, core_bit, len(after)), g...  52 us
    ppermute x46, starting transfers between devices, flipped(): lax.ppermute(value, axis, [(i, i ^ flip) for i in range(lax.axis_size(axi...  36.1 us
    ppermute x46, waiting for transfers between devices, flipped(): lax.ppermute(value, axis, [(i, i ^ flip) for i in range(lax.axis_size(axi...  35.3 us
    ppermute x12, waiting for transfers between devices, shifted(): lax.ppermute(value, 'col', [(i, (i + by) % size) for i in range(size)])  30.6 us
    pallas_call x6, Pallas kernels, merge(): pl.pallas_call(functools.partial(merge_kernel, layout, len(arrays), len(a...  18.5 us
    pallas_call x2, Pallas kernels, mlp_tail_part(): pl.pallas_call(functools.partial(mlp_tail_kernel, orders, core_bit, len(s...  17.7 us
    ppermute x12, starting transfers between devices, shifted(): lax.ppermute(value, 'col', [(i, (i + by) % size) for i in range(size)])  17.4 us
    unnamed x118, local copies, waits for them, and re-layouts  14.3 us
  transfers between devices with their start and end apart: 58, of which 16 were waited for; matrix products, arithmetic and copies ran while one was open for 11% of the time, Pallas kernels for 34%

profile of v2, /device:TPU:0, one launch (start us, length us, event | category | flops | bytes accessed | tf_op | source)
XLA Modules:
  0.0 274.2 jit_solution(13371009896082022404)
XLA Ops:
  3.1 5.1 %collective-permute-start.2 = (bf16[96,768]{1,0:T(8,128)(2,1)S(1)}, bf16[96,768]{1,0:T(8,128)(2,1)S(1)}, u32[]{:S(2)}, u32[]{:S(2)}) collective-permute-start(bf16[96,768]{1,0:T(8,128)(2,1)S(1)} %copy.74), channel_id=1, source_target_pairs={{0,3},{1,0},{2,1},{3,2},{4,7},{5,4},{6,5},{7,6},{8,11},{9,8},{10,9... | collective-permute-start | bytes 442376 | tf_op jit(solution)/shard_map/ppermute | solution.py:472
  15.8 4.9 %collective-permute-done.1 = bf16[96,768]{1,0:T(8,128)(2,1)S(1)} collective-permute-done((bf16[96,768]{1,0:T(8,128)(2,1)S(1)}, bf16[96,768]{1,0:T(8,128)(2,1)S(1)}, u32[]{:S(2)}, u32[]{:S(2)}) %collective-permute-start.1) | collective-permute-done | bytes 147488 | tf_op jit(solution)/shard_map/ppermute | solution.py:472
  22.5 2.9 %collective-permute-start.5 = (bf16[96,1536]{1,0:T(8,128)(2,1)}, bf16[96,1536]{1,0:T(8,128)(2,1)S(1)}, u32[]{:S(2)}, u32[]{:S(2)}) collective-permute-start(bf16[96,1536]{1,0:T(8,128)(2,1)} %shard_map.254.__0_), channel_id=1, source_target_pairs={{0,3},{1,0},{2,1},{3,2},{4,7},{5,4},{6,5},{7,6},{8,11},{9,8},{10,9... | collective-permute-start | bytes 884744 | tf_op jit(solution)/shard_map/ppermute | solution.py:472
  25.4 1.5 collective-permute-start.6
  26.9 1.5 collective-permute-start.7
  28.4 6.0 %shard_map.255 = (bf16[512,768]{1,0:T(8,128)(2,1)}, bf16[768,512]{1,0:T(8,128)(2,1)}, bf16[512,768]{1,0:T(8,128)(2,1)}, bf16[768,512]{1,0:T(8,128)(2,1)}, bf16[7...) custom-call(bf16[512,768]{1,0:T(8,128)(2,1)} %rest_13_.1, ...), custom_call_target="tpu_custom_call" | custom-call | flops 6899999744 | bytes 1048576 | tf_op jit(solution)/shard_map/pallas_call | solution.py:123
  34.4 3.2 %collective-permute-done.5.__4_.__3_ = bf16[96,1536]{1,0:T(8,128)(2,1)S(1)} collective-permute-done((bf16[96,1536]{1,0:T(8,128)(2,1)}, bf16[96,1536]{1,0:T(8,128)(2,1)S(1)}, u32[]{:S(2)}, u32[]{:S(2)}) %collective-permute-start.5) | collective-permute-done | bytes 294944 | tf_op jit(solution)/shard_map/ppermute | solution.py:472
  39.6 1.6 collective-permute-start.8
  42.3 1.6 collective-permute-start.9
  43.9 1.6 collective-permute-start.4
  46.1 12.8 %collective-permute-done.4.__2_ = bf16[96,1536]{1,0:T(8,128)(2,1)S(1)} collective-permute-done((bf16[96,1536]{1,0:T(8,128)(2,1)S(1)}, bf16[96,1536]{1,0:T(8,128)(2,1)S(1)}, u32[]{:S(2)}, u32[]{:S(2)}) %collective-permute-start.4) | collective-permute-done | bytes 294944 | tf_op jit(solution)/shard_map/ppermute | solution.py:472
  66.3 1.5 collective-permute-start.12
  67.8 1.5 collective-permute-start.13
  69.3 14.8 %shard_map.259 = (bf16[2,512,768]{2,1,0:T(8,128)(2,1)}, bf16[2,512,384]{2,1,0:T(8,128)(2,1)}, f32[2,1,768]{2,1,0:T(1,128)}, bf16[8,4,96,384]{3,2,1,0:T(8,128)(2,1)}, bf16[8,4,96,384]{3,2,1,0:T(8,128)(2,1)}) custom-call(s32[2]{0:T(128)} %pad_add_fusion.me_ref, bf16[512,768]{1,0:T(8,128)(2,1)} %get-tuple-element.92.__2_.na_ref, ...), custom_call_target="tpu_custom_call" | custom-call | flops 23000000512 | bytes 1048576 | tf_op jit(solution)/shard_map/pallas_call | solution.py:269
  88.6 15.0 %shard_map.261 = (bf16[2,512,768]{2,1,0:T(8,128)(2,1)}, bf16[2,512,384]{2,1,0:T(8,128)(2,1)}, f32[2,1,768]{2,1,0:T(1,128)}, bf16[8,4,96,384]{3,2,1,0:T(8,128)(2,1)}, bf16[8,4,96,384]{3,2,1,0:T(8,128)(2,1)}) custom-call(s32[2]{0:T(128)} %pad_add_fusion.me_ref, ...), custom_call_target="tpu_custom_call", output_to_operand_aliasing={{3}: (19, {}), {4}: (20, {})} | custom-call | flops 23000000512 | bytes 1048576 | tf_op jit(solution)/shard_map/pallas_call | solution.py:269
  106.6 1.5 collective-permute-start.18
  109.0 1.5 collective-permute-start.19
  110.7 11.7 %collective-permute-done.18.__0_ = bf16[2,2,96,768]{3,2,1,0:T(8,128)(2,1)} collective-permute-done((bf16[2,2,96,768]{3,2,1,0:T(8,128)(2,1)}, bf16[2,2,96,768]{3,2,1,0:T(8,128)(2,1)}, u32[]{:S(2)}, u32[]{:S(2)}) %collective-permute-start.18) | collective-permute-done | bytes 589856 | tf_op jit(solution)/shard_map/ppermute | solution.py:467
  122.4 10.0 %shard_map.263 = (f32[512,768]{1,0:T(8,128)}, f32[512,768]{1,0:T(8,128)}) custom-call(s32[2]{0:T(128)} %pad_add_fusion.me_ref, bf16[2,4,96,384]{3,2,1,0:T(8,128)(2,1)} %copy-done.17, bf16[2,4,96,384]{3,2,1,0:T(8,128)(2,1)} %get-tuple-element.95.__4_.rest_1_, bf16[2,4,96,384]{3,2,1,0:T(8,128)(2,1)} %copy-done.52, ...), custom_call_target="tpu_custom_call" | custom-call | flops 12650000384 | bytes 1048576 | tf_op jit(solution)/shard_map/pallas_call | solution.py:403
  134.9 2.8 %shard_map.265 = (bf16[2,4,96,384]{3,2,1,0:T(8,128)(2,1)}, bf16[2,4,96,384]{3,2,1,0:T(8,128)(2,1)}) custom-call(bf16[8,4,96,384]{3,2,1,0:T(8,128)(2,1)} %get-tuple-element.127.refs_0_.refs_2_.refs_3_.refs_4_, bf16[8,4,96,384]{3,2,1,0:T(8,128)(2,1)} %copy-done.3, bf16[8,4,96,384]{3,2,1,0:T(8,128)(2,1)} %get-tuple-element.127.refs_0_.refs_2_.refs_3_.refs_4_, ...), custom_call_target="tpu_custom_call" | custom-call | flops 3449999872 | bytes 1048576 | tf_op jit(solution)/shard_map/pallas_call | solution.py:551
  137.7 1.5 collective-permute-start.31
  139.2 1.5 collective-permute-start.32
  140.7 11.0 %shard_map.266 = (bf16[2,512,768]{2,1,0:T(8,128)(2,1)}, bf16[2,512,768]{2,1,0:T(8,128)(2,1)}, f32[2,1,768]{2,1,0:T(1,128)}, bf16[8,4,96,384]{3,2,1,0:T(8,128)(2,1)}, bf16[8,4,96,384]{3,2,1,0:T(8,128)(2,1)}) custom-call(s32[2]{0:T(128)} %pad_add_fusion.me_ref, bf16[512,768]{1,0:T(8,128)(2,1)} %get-tuple-element.125.nm_ref, ...), custom_call_target="tpu_custom_call" | custom-call | flops 13799999488 | bytes 1048576 | tf_op jit(solution)/shard_map/pallas_call | solution.py:269
  151.7 1.5 collective-permute-done.31.refs_2_
  155.2 2.3 shard_map.267
  157.6 1.5 collective-permute-start.33
  159.6 11.1 %shard_map.268 = (bf16[2,512,768]{2,1,0:T(8,128)(2,1)}, bf16[2,512,768]{2,1,0:T(8,128)(2,1)}, f32[2,1,768]{2,1,0:T(1,128)}, bf16[8,4,96,384]{3,2,1,0:T(8,128)(2,1)}, bf16[8,4,96,384]{3,2,1,0:T(8,128)(2,1)}) custom-call(s32[2]{0:T(128)} %pad_add_fusion.me_ref, bf16[512,768]{1,0:T(8,128)(2,1)} %get-tuple-element.125.nm_ref, ...), custom_call_target="tpu_custom_call" | custom-call | flops 13799999488 | bytes 1048576 | tf_op jit(solution)/shard_map/pallas_call | solution.py:269
  172.4 3.8 %shard_map.269 = (bf16[1,4,96,768]{3,2,1,0:T(8,128)(2,1)}, bf16[2,4,96,384]{3,2,1,0:T(8,128)(2,1)}, bf16[2,4,96,384]{3,2,1,0:T(8,128)(2,1)}, bf16[8,4,96,384]{3,2,1,0:T(8,128)(2,1)}) custom-call(bf16[8,4,96,384]{3,2,1,0:T(8,128)(2,1)} %get-tuple-element.127.refs_0_.refs_2_.refs_3_.refs_4_, ...), custom_call_target="tpu_custom_call", output_to_operand_aliasing={{3}: (12, {})} | custom-call | flops 3449999872 | bytes 1048576 | tf_op jit(solution)/shard_map/pallas_call | solution.py:551
  177.4 1.5 collective-permute-start.36
  179.4 1.7 slice_bitcast_fusion.11
  181.1 2.1 collective-permute-start.40
  183.2 7.4 %shard_map.270 = (f32[512,768]{1,0:T(8,128)}, f32[512,768]{1,0:T(8,128)}) custom-call(s32[2]{0:T(128)} %pad_add_fusion.me_ref, bf16[2,2,96,768]{3,2,1,0:T(8,128)(2,1)} %copy-done.15, bf16[2,2,96,768]{3,2,1,0:T(8,128)(2,1)} %get-tuple-element.122.rest_1_, bf16[2,2,96,768]{3,2,1,0:T(8,128)(2,1)} %copy-done.5, ...), custom_call_target="tpu_custom_call" | custom-call | flops 10350000128 | bytes 1048576 | tf_op jit(solution)/shard_map/pallas_call | solution.py:432
  190.6 2.3 collective-permute-done.39.refs_10_
  196.1 3.5 %shard_map.271 = (bf16[1,4,96,384]{3,2,1,0:T(8,128)(2,1)}, bf16[1,4,96,384]{3,2,1,0:T(8,128)(2,1)}, bf16[2,4,96,384]{3,2,1,0:T(8,128)(2,1)}, bf16[2,4,96,384]{3,...) custom-call(bf16[8,4,96,384]{3,2,1,0:T(8,128)(2,1)} %get-tuple-eleme, ...), custom_call_target="tpu_custom_call", output_to_operand_aliasing={{4}: (10, {}), {5}: (11, {})} | custom-call | flops 3449999872 | bytes 1048576 | tf_op jit(solution)/shard_map/pallas_call | solution.py:551
  200.6 1.5 collective-permute-start.43
  202.1 1.5 collective-permute-start.44
  203.7 10.3 %shard_map.272 = (bf16[512,768]{1,0:T(8,128)(2,1)}, bf16[512,768]{1,0:T(8,128)(2,1)}, f32[16,768]{1,0:T(8,128)}) custom-call(s32[2]{0:T(128)} %pad_add_fusion.me_ref, bf16[2,2,96,768]{3,2,1,0:T(8,128)(2,1)} %pad_maximum_fusion.3.rest_0_, bf16[2,2,96,768]{3,2,1,0:T(8,128)(2,1)} %get-tuple-element.123.refs_5_.rest_1_, bf16[2,2,96,768]{3,2,1,0:T(8,128)(2,1)} %copy-done.12, ...), custom_call_target="tpu_custom_call" | custom-call | flops 10350000128 | bytes 1048576 | tf_op jit(solution)/shard_map/pallas_call | solution.py:432
  214.0 7.2 %collective-permute-done.43.refs_10_.refs_2_ = bf16[2,4,96,384]{3,2,1,0:T(8,128)(2,1)S(1)} collective-permute-done((bf16[2,4,96,384]{3,2,1,0:T(8,128)(2,1)}, bf16[2,4,96,384]{3,2,1,0:T(8,128)(2,1)S(1)}, u32[]{:S(2)}, u32[]{:S(2)}) %collective-permute-start.43) | collective-permute-done | bytes 589856 | tf_op jit(solution)/shard_map/ppermute | solution.py:467
  222.2 3.5 %shard_map.273 = (bf16[1,4,96,768]{3,2,1,0:T(8,128)(2,1)}, bf16[1,4,96,384]{3,2,1,0:T(8,128)(2,1)}, bf16[1,4,96,384]{3,2,1,0:T(8,128)(2,1)}, f32[16,768]{1,0:T(8,128)}, bf16[96,768]{1,0:T(8,128)(2,1)}) custom-call(bf16[8,4,96,384]{3,2,1,0:T(8,128)(2,1)} %get-tuple-element.139.refs_8_.refs_10_.refs_0_.refs_3_.refs_4_, ...), custom_call_target="tpu_custom_call", output_to_operand_aliasing={{3}: (14, {}), {4}: (15, {})} | custom-call | flops 3449999872 | bytes 1048576 | tf_op jit(solution)/shard_map/pallas_call | solution.py:551
  229.6 1.8 collective-permute-start.53
  233.8 3.6 %collective-permute-done.47 = f32[16,768]{1,0:T(8,128)S(1)} collective-permute-done((f32[16,768]{1,0:T(8,128)S(1)}, f32[16,768]{1,0:T(8,128)S(1)}, u32[]{:S(2)}, u32[]{:S(2)}) %collective-permute-start.47) | collective-permute-done | bytes 49184 | tf_op jit(solution)/shard_map/ppermute | solution.py:467
  240.8 2.7 shard_map.274
  244.7 1.6 collective-permute-start.51
  250.6 1.5 collective-permute-done.52.__2_
  252.1 5.9 %collective-permute-done.51.__1_ = bf16[96,1536]{1,0:T(8,128)(2,1)} collective-permute-done((bf16[96,1536]{1,0:T(8,128)(2,1)S(1)}, bf16[96,1536]{1,0:T(8,128)(2,1)}, u32[]{:S(2)}, u32[]{:S(2)}) %collective-permute-start.51) | collective-permute-done | bytes 294944 | tf_op jit(solution)/shard_map/ppermute | solution.py:472
  258.6 3.7 %collective-permute-done.54 = f32[16,768]{1,0:T(8,128)S(1)} collective-permute-done((f32[16,768]{1,0:T(8,128)}, f32[16,768]{1,0:T(8,128)S(1)}, u32[]{:S(2)}, u32[]{:S(2)}) %collective-permute-start.54) | collective-permute-done | bytes 49184 | tf_op jit(solution)/shard_map/ppermute | solution.py:467
  265.8 2.8 %collective-permute-done.55 = f32[16,768]{1,0:T(8,128)S(1)} collective-permute-done((f32[16,768]{1,0:T(8,128)S(1)}, f32[16,768]{1,0:T(8,128)S(1)}, u32[]{:S(2)}, u32[]{:S(2)}) %collective-permute-start.55) | collective-permute-done | bytes 49184 | tf_op jit(solution)/shard_map/ppermute | solution.py:467
  270.6 1.8 collective-permute-done.57
  (274 shorter events, 67.6 us)
Async XLA Ops:
  3.1 12.7 %collective-permute-start.2 = (bf16[96,768]{1,0:T(8,128)(2,1)S(1)}, bf16[96,768]{1,0:T(8,128)(2,1)S(1)}, u32[]{:S(2)}, u32[]{:S(2)}) collective-permute-start(bf16[96,768]{1,0:T(8,128)(2,1)S(1)} %copy.74), channel_id=1, source_target_pairs={{0,3},{1,0},{2,1},{3,2},{4,7},{5,4},{6,5},{7,6},{8,11},{9,8},{10,9... | collective-permute-start | bytes 442376 | tf_op jit(solution)/shard_map/ppermute | solution.py:472
  8.2 12.5 %collective-permute-start.1 = (bf16[96,768]{1,0:T(8,128)(2,1)S(1)}, bf16[96,768]{1,0:T(8,128)(2,1)S(1)}, u32[]{:S(2)}, u32[]{:S(2)}) collective-permute-start(bf16[96,768]{1,0:T(8,128)(2,1)S(1)} %copy.74), channel_id=1, source_target_pairs={{0,2},{1,3},{2,0},{3,1},{4,6},{5,7},{6,4},{7,5},{8,10},{9,11},{10,... | collective-permute-start | bytes 442376 | tf_op jit(solution)/shard_map/ppermute | solution.py:472
  8.2 12.5 %collective-permute-start = (bf16[96,768]{1,0:T(8,128)(2,1)S(1)}, bf16[96,768]{1,0:T(8,128)(2,1)S(1)}, u32[]{:S(2)}, u32[]{:S(2)}) collective-permute-start(bf16[96,768]{1,0:T(8,128)(2,1)S(1)} %copy.74), channel_id=1, source_target_pairs={{0,1},{1,2},{2,3},{3,0},{4,5},{5,6},{6,7},{7,4},{8,9},{9,10},{10,1... | collective-permute-start | bytes 442376 | tf_op jit(solution)/shard_map/ppermute | solution.py:472
  21.6 12.8 %collective-permute-start.3 = (bf16[96,1536]{1,0:T(8,128)(2,1)}, bf16[96,1536]{1,0:T(8,128)(2,1)S(1)}, u32[]{:S(2)}, u32[]{:S(2)}) collective-permute-start(bf16[96,1536]{1,0:T(8,128)(2,1)} %shard_map.254.__0_), channel_id=1, source_target_pairs={{0,1},{1,2},{2,3},{3,0},{4,5},{5,6},{6,7},{7,4},{8,9},{9,10},{10,1... | collective-permute-start | bytes 884744 | tf_op jit(solution)/shard_map/ppermute | solution.py:472
  22.5 15.2 %collective-permute-start.5 = (bf16[96,1536]{1,0:T(8,128)(2,1)}, bf16[96,1536]{1,0:T(8,128)(2,1)S(1)}, u32[]{:S(2)}, u32[]{:S(2)}) collective-permute-start(bf16[96,1536]{1,0:T(8,128)(2,1)} %shard_map.254.__0_), channel_id=1, source_target_pairs={{0,3},{1,0},{2,1},{3,2},{4,7},{5,4},{6,5},{7,6},{8,11},{9,8},{10,9... | collective-permute-start | bytes 884744 | tf_op jit(solution)/shard_map/ppermute | solution.py:472
  25.4 12.2 %collective-permute-start.6 = (bf16[1,4,96,384]{3,2,1,0:T(8,128)(2,1)S(1)}, bf16[1,4,96,384]{3,2,1,0:T(8,128)(2,1)S(1)}, u32[]{:S(2)}, u32[]{:S(2)}) collective-permute-start(bf16[1,4,96,384]{3,2,1,0:T(8,128)(2,1)S(1)} %copy-done.11), channel_id=1, source_target_pairs={{0,8},{4,12},{8,0},{12,4},{1,9},{5,13},{9,1},{13,5},{2,10},{6,14},... | collective-permute-start | bytes 884744 | tf_op jit(solution)/shard_map/ppermute | solution.py:467
  26.9 10.7 %collective-permute-start.7 = (bf16[1,4,96,384]{3,2,1,0:T(8,128)(2,1)S(1)}, bf16[1,4,96,384]{3,2,1,0:T(8,128)(2,1)S(1)}, u32[]{:S(2)}, u32[]{:S(2)}) collective-permute-start(bf16[1,4,96,384]{3,2,1,0:T(8,128)(2,1)S(1)} %get-tuple-element.221), channel_id=1, source_target_pairs={{0,16},{16,0},{1,17},{17,1},{2,18},{18,2},{3,19},{19,3},{4,20},{20... | collective-permute-start | bytes 884744 | tf_op jit(solution)/shard_map/ppermute | solution.py:467
  39.6 19.3 %collective-permute-start.8 = (bf16[2,4,96,384]{3,2,1,0:T(8,128)(2,1)S(1)}, bf16[2,4,96,384]{3,2,1,0:T(8,128)(2,1)S(1)}, u32[]{:S(2)}, u32[]{:S(2)}) collective-permute-start(bf16[2,4,96,384]{3,2,1,0:T(8,128)(2,1)S(1)} %pad_maximum_fusion.1.rest_0_), channel_id=1, source_target_pairs={{0,16},{16,0},{1,17},{17,1},{2,18},{18,2},{3,19},{19,3},{4,20},{20... | collective-permute-start | bytes 1769480 | tf_op jit(solution)/shard_map/ppermute | solution.py:467
  42.3 16.7 %collective-permute-start.9 = (bf16[2,4,96,384]{3,2,1,0:T(8,128)(2,1)S(1)}, bf16[2,4,96,384]{3,2,1,0:T(8,128)(2,1)}, u32[]{:S(2)}, u32[]{:S(2)}) collective-permute-start(bf16[2,4,96,384]{3,2,1,0:T(8,128)(2,1)S(1)} %pad_maximum_fusion.2.rest_4_), channel_id=1, source_target_pairs={{0,8},{4,12},{8,0},{12,4},{1,9},{5,13},{9,1},{13,5},{2,10},{6,14},... | collective-permute-start | bytes 1769480 | tf_op jit(solution)/shard_map/ppermute | solution.py:467
  43.9 15.0 %collective-permute-start.4 = (bf16[96,1536]{1,0:T(8,128)(2,1)S(1)}, bf16[96,1536]{1,0:T(8,128)(2,1)S(1)}, u32[]{:S(2)}, u32[]{:S(2)}) collective-permute-start(bf16[96,1536]{1,0:T(8,128)(2,1)S(1)} %copy-done.10), channel_id=1, source_target_pairs={{0,2},{1,3},{2,0},{3,1},{4,6},{5,7},{6,4},{7,5},{8,10},{9,11},{10,... | collective-permute-start | bytes 884744 | tf_op jit(solution)/shard_map/ppermute | solution.py:472
  45.6 20.1 %collective-permute-start.14 = (bf16[2,4,96,384]{3,2,1,0:T(8,128)(2,1)S(1)}, bf16[2,4,96,384]{3,2,1,0:T(8,128)(2,1)S(1)}, u32[]{:S(2)}, u32[]{:S(2)}) collective-permute-start(bf16[2,4,96,384]{3,2,1,0:T(8,128)(2,1)S(1)} %pad_maximum_fusion.1.rest_0_), channel_id=1, source_target_pairs={{0,4},{4,0},{8,12},{12,8},{1,5},{5,1},{9,13},{13,9},{2,6},{6,2},{1... | collective-permute-start | bytes 1769480 | tf_op jit(solution)/shard_map/ppermute | solution.py:467
  45.6 20.7 %collective-permute-start.16 = (bf16[2,4,96,384]{3,2,1,0:T(8,128)(2,1)S(1)}, bf16[2,4,96,384]{3,2,1,0:T(8,128)(2,1)}, u32[]{:S(2)}, u32[]{:S(2)}) collective-permute-start(bf16[2,4,96,384]{3,2,1,0:T(8,128)(2,1)S(1)} %pad_maximum_fusion.2.rest_4_), channel_id=1, source_target_pairs={{0,4},{4,0},{8,12},{12,8},{1,5},{5,1},{9,13},{13,9},{2,6},{6,2},{1... | collective-permute-start | bytes 1769480 | tf_op jit(solution)/shard_map/ppermute | solution.py:467
  63.9 20.2 %collective-permute-start.10 = (bf16[1,2,96,768]{3,2,1,0:T(8,128)(2,1)S(1)}, bf16[1,2,96,768]{3,2,1,0:T(8,128)(2,1)S(1)}, u32[]{:S(2)}, u32[]{:S(2)}) collective-permute-start(bf16[1,2,96,768]{3,2,1,0:T(8,128)(2,1)S(1)} %get-tuple-element.220), channel_id=1, source_target_pairs={{0,8},{4,12},{8,0},{12,4},{1,9},{5,13},{9,1},{13,5},{2,10},{6,14},... | collective-permute-start | bytes 884744 | tf_op jit(solution)/shard_map/ppermute | solution.py:467
  65.7 18.4 %collective-permute-start.11 = (bf16[1,2,96,768]{3,2,1,0:T(8,128)(2,1)S(1)}, bf16[1,2,96,768]{3,2,1,0:T(8,128)(2,1)S(1)}, u32[]{:S(2)}, u32[]{:S(2)}) collective-permute-start(bf16[1,2,96,768]{3,2,1,0:T(8,128)(2,1)S(1)} %get-tuple-element.219), channel_id=1, source_target_pairs={{0,16},{16,0},{1,17},{17,1},{2,18},{18,2},{3,19},{19,3},{4,20},{20... | collective-permute-start | bytes 884744 | tf_op jit(solution)/shard_map/ppermute | solution.py:467
  66.3 17.9 %collective-permute-start.12 = (bf16[1,2,96,768]{3,2,1,0:T(8,128)(2,1)S(1)}, bf16[1,2,96,768]{3,2,1,0:T(8,128)(2,1)S(1)}, u32[]{:S(2)}, u32[]{:S(2)}) collective-permute-start(bf16[1,2,96,768]{3,2,1,0:T(8,128)(2,1)S(1)} %get-tuple-element.218), channel_id=1, source_target_pairs={{0,8},{4,12},{8,0},{12,4},{1,9},{5,13},{9,1},{13,5},{2,10},{6,14},... | collective-permute-start | bytes 884744 | tf_op jit(solution)/shard_map/ppermute | solution.py:467
  67.8 16.4 %collective-permute-start.13 = (bf16[1,2,96,768]{3,2,1,0:T(8,128)(2,1)S(1)}, bf16[1,2,96,768]{3,2,1,0:T(8,128)(2,1)S(1)}, u32[]{:S(2)}, u32[]{:S(2)}) collective-permute-start(bf16[1,2,96,768]{3,2,1,0:T(8,128)(2,1)S(1)} %get-tuple-element.217), channel_id=1, source_target_pairs={{0,16},{16,0},{1,17},{17,1},{2,18},{18,2},{3,19},{19,3},{4,20},{20... | collective-permute-start | bytes 884744 | tf_op jit(solution)/shard_map/ppermute | solution.py:467
  86.2 17.5 %collective-permute-start.20 = (bf16[2,2,96,768]{3,2,1,0:T(8,128)(2,1)S(1)}, bf16[2,2,96,768]{3,2,1,0:T(8,128)(2,1)}, u32[]{:S(2)}, u32[]{:S(2)}) collective-permute-start(bf16[2,2,96,768]{3,2,1,0:T(8,128)(2,1)S(1)} %pad_maximum_fusion.5.rest_13_.rest_0_), channel_id=1, source_target_pairs={{0,16},{16,0},{1,17},{17,1},{2,18},{18,2},{3,19},{19,3},{4,20},{20... | collective-permute-start | bytes 1769480 | tf_op jit(solution)/shard_map/ppermute | solution.py:467
  86.7 16.9 %collective-permute-start.22 = (bf16[2,2,96,768]{3,2,1,0:T(8,128)(2,1)S(1)}, bf16[2,2,96,768]{3,2,1,0:T(8,128)(2,1)S(1)}, u32[]{:S(2)}, u32[]{:S(2)}) collective-permute-start(bf16[2,2,96,768]{3,2,1,0:T(8,128)(2,1)S(1)} %pad_maximum_fusion.5.rest_13_.rest_0_), channel_id=1, source_target_pairs={{0,4},{4,0},{8,12},{12,8},{1,5},{5,1},{9,13},{13,9},{2,6},{6,2},{1... | collective-permute-start | bytes 1769480 | tf_op jit(solution)/shard_map/ppermute | solution.py:467
  87.8 15.9 %collective-permute-start.21 = (bf16[2,2,96,768]{3,2,1,0:T(8,128)(2,1)S(1)}, bf16[2,2,96,768]{3,2,1,0:T(8,128)(2,1)}, u32[]{:S(2)}, u32[]{:S(2)}) collective-permute-start(bf16[2,2,96,768]{3,2,1,0:T(8,128)(2,1)S(1)} %pad_maximum_fusion.6.rest_4_), channel_id=1, source_target_pairs={{0,8},{4,12},{8,0},{12,4},{1,9},{5,13},{9,1},{13,5},{2,10},{6,14},... | collective-permute-start | bytes 1769480 | tf_op jit(solution)/shard_map/ppermute | solution.py:467
  88.4 15.3 %collective-permute-start.23 = (bf16[2,2,96,768]{3,2,1,0:T(8,128)(2,1)S(1)}, bf16[2,2,96,768]{3,2,1,0:T(8,128)(2,1)S(1)}, u32[]{:S(2)}, u32[]{:S(2)}) collective-permute-start(bf16[2,2,96,768]{3,2,1,0:T(8,128)(2,1)S(1)} %pad_maximum_fusion.6.rest_4_), channel_id=1, source_target_pairs={{0,4},{4,0},{8,12},{12,8},{1,5},{5,1},{9,13},{13,9},{2,6},{6,2},{1... | collective-permute-start | bytes 1769480 | tf_op jit(solution)/shard_map/ppermute | solution.py:467
  104.7 28.8 %collective-permute-start.30 = (bf16[8,4,96,384]{3,2,1,0:T(8,128)(2,1)}, bf16[8,4,96,384]{3,2,1,0:T(8,128)(2,1)S(1)}, u32[]{:S(2)}, u32[]{:S(2)}) collective-permute-start(bf16[8,4,96,384]{3,2,1,0:T(8,128)(2,1)} %get-tuple-element.128), channel_id=1, source_target_pairs={{0,4},{4,0},{8,12},{12,8},{1,5},{5,1},{9,13},{13,9},{2,6},{6,2},{1... | collective-permute-start | bytes 7077896 | tf_op jit(solution)/shard_map/ppermute | solution.py:467
  106.6 15.8 %collective-permute-start.18 = (bf16[2,2,96,768]{3,2,1,0:T(8,128)(2,1)}, bf16[2,2,96,768]{3,2,1,0:T(8,128)(2,1)}, u32[]{:S(2)}, u32[]{:S(2)}) collective-permute-start(bf16[2,2,96,768]{3,2,1,0:T(8,128)(2,1)} %pad_maximum_fusion.3.rest_0_), channel_id=1, source_target_pairs={{0,16},{16,0},{1,17},{17,1},{2,18},{18,2},{3,19},{19,3},{4,20},{20... | collective-permute-start | bytes 1769480 | tf_op jit(solution)/shard_map/ppermute | solution.py:467
  108.1 31.1 %collective-permute-start.26 = (bf16[2,2,96,768]{3,2,1,0:T(8,128)(2,1)}, bf16[2,2,96,768]{3,2,1,0:T(8,128)(2,1)S(1)}, u32[]{:S(2)}, u32[]{:S(2)}) collective-permute-start(bf16[2,2,96,768]{3,2,1,0:T(8,128)(2,1)} %pad_maximum_fusion.3.rest_0_), channel_id=1, source_target_pairs={{0,4},{4,0},{8,12},{12,8},{1,5},{5,1},{9,13},{13,9},{2,6},{6,2},{1... | collective-permute-start | bytes 1769480 | tf_op jit(solution)/shard_map/ppermute | solution.py:467
  109.0 23.4 %collective-permute-start.19 = (bf16[2,2,96,768]{3,2,1,0:T(8,128)(2,1)}, bf16[2,2,96,768]{3,2,1,0:T(8,128)(2,1)}, u32[]{:S(2)}, u32[]{:S(2)}) collective-permute-start(bf16[2,2,96,768]{3,2,1,0:T(8,128)(2,1)} %pad_maximum_fusion.4.rest_4_), channel_id=1, source_target_pairs={{0,8},{4,12},{8,0},{12,4},{1,9},{5,13},{9,1},{13,5},{2,10},{6,14},... | collective-permute-start | bytes 1769480 | tf_op jit(solution)/shard_map/ppermute | solution.py:467
  110.5 22.5 %collective-permute-start.24 = (bf16[2,2,96,768]{3,2,1,0:T(8,128)(2,1)}, bf16[2,2,96,768]{3,2,1,0:T(8,128)(2,1)}, u32[]{:S(2)}, u32[]{:S(2)}) collective-permute-start(bf16[2,2,96,768]{3,2,1,0:T(8,128)(2,1)} %get-tuple-element.122.rest_1_), channel_id=1, source_target_pairs={{0,4},{4,0},{8,12},{12,8},{1,5},{5,1},{9,13},{13,9},{2,6},{6,2},{1... | collective-permute-start | bytes 1769480 | tf_op jit(solution)/shard_map/ppermute | solution.py:467
  132.4 19.3 %collective-permute-start.28 = (bf16[2,2,96,768]{3,2,1,0:T(8,128)(2,1)}, bf16[2,2,96,768]{3,2,1,0:T(8,128)(2,1)}, u32[]{:S(2)}, u32[]{:S(2)}) collective-permute-start(bf16[2,2,96,768]{3,2,1,0:T(8,128)(2,1)} %pad_maximum_fusion.4.rest_4_), channel_id=1, source_target_pairs={{0,4},{4,0},{8,12},{12,8},{1,5},{5,1},{9,13},{13,9},{2,6},{6,2},{1... | collective-permute-start | bytes 1769480 | tf_op jit(solution)/shard_map/ppermute | solution.py:467
  133.0 18.7 %collective-permute-start.27 = (bf16[2,2,96,768]{3,2,1,0:T(8,128)(2,1)}, bf16[2,2,96,768]{3,2,1,0:T(8,128)(2,1)}, u32[]{:S(2)}, u32[]{:S(2)}) collective-permute-start(bf16[2,2,96,768]{3,2,1,0:T(8,128)(2,1)} %get-tuple-element.123.refs_5_.rest_1_), channel_id=1, source_target_pairs={{0,4},{4,0},{8,12},{12,8},{1,5},{5,1},{9,13},{13,9},{2,6},{6,2},{1... | collective-permute-start | bytes 1769480 | tf_op jit(solution)/shard_map/ppermute | solution.py:467
  133.1 18.6 %collective-permute-start.29 = (bf16[2,2,96,768]{3,2,1,0:T(8,128)(2,1)}, bf16[2,2,96,768]{3,2,1,0:T(8,128)(2,1)}, u32[]{:S(2)}, u32[]{:S(2)}) collective-permute-start(bf16[2,2,96,768]{3,2,1,0:T(8,128)(2,1)} %get-tuple-element.124.rest_5_), channel_id=1, source_target_pairs={{0,4},{4,0},{8,12},{12,8},{1,5},{5,1},{9,13},{13,9},{2,6},{6,2},{1... | collective-permute-start | bytes 1769480 | tf_op jit(solution)/shard_map/ppermute | solution.py:467
  137.7 15.5 %collective-permute-start.31 = (bf16[2,4,96,384]{3,2,1,0:T(8,128)(2,1)}, bf16[2,4,96,384]{3,2,1,0:T(8,128)(2,1)S(1)}, u32[]{:S(2)}, u32[]{:S(2)}) collective-permute-start(bf16[2,4,96,384]{3,2,1,0:T(8,128)(2,1)} %get-tuple-element.129.rest_9_), channel_id=1, source_target_pairs={{0,8},{4,12},{8,0},{12,4},{1,9},{5,13},{9,1},{13,5},{2,10},{6,14},... | collective-permute-start | bytes 1769480 | tf_op jit(solution)/shard_map/ppermute | solution.py:467
  139.2 15.3 %collective-permute-start.32 = (bf16[2,4,96,384]{3,2,1,0:T(8,128)(2,1)}, bf16[2,4,96,384]{3,2,1,0:T(8,128)(2,1)S(1)}, u32[]{:S(2)}, u32[]{:S(2)}) collective-permute-start(bf16[2,4,96,384]{3,2,1,0:T(8,128)(2,1)} %get-tuple-element.130), channel_id=1, source_target_pairs={{0,16},{16,0},{1,17},{17,1},{2,18},{18,2},{3,19},{19,3},{4,20},{20... | collective-permute-start | bytes 1769480 | tf_op jit(solution)/shard_map/ppermute | solution.py:467
  157.6 13.3 %collective-permute-start.35 = (bf16[8,4,96,384]{3,2,1,0:T(8,128)(2,1)}, bf16[8,4,96,384]{3,2,1,0:T(8,128)(2,1)S(1)}, u32[]{:S(2)}, u32[]{:S(2)}) collective-permute-start(bf16[8,4,96,384]{3,2,1,0:T(8,128)(2,1)} %get-tuple-element.140), channel_id=1, source_target_pairs={{0,4},{4,0},{8,12},{12,8},{1,5},{5,1},{9,13},{13,9},{2,6},{6,2},{1... | collective-permute-start | bytes 7077896 | tf_op jit(solution)/shard_map/ppermute | solution.py:467
  157.6 13.2 %collective-permute-start.33 = (bf16[1,4,96,384]{3,2,1,0:T(8,128)(2,1)}, bf16[1,4,96,384]{3,2,1,0:T(8,128)(2,1)S(1)}, u32[]{:S(2)}, u32[]{:S(2)}) collective-permute-start(bf16[1,4,96,384]{3,2,1,0:T(8,128)(2,1)} %get-tuple-element.133.rest_9_), channel_id=1, source_target_pairs={{0,16},{16,0},{1,17},{17,1},{2,18},{18,2},{3,19},{19,3},{4,20},{20... | collective-permute-start | bytes 884744 | tf_op jit(solution)/shard_map/ppermute | solution.py:467
  159.1 11.7 %collective-permute-start.34 = (bf16[1,4,96,384]{3,2,1,0:T(8,128)(2,1)}, bf16[1,4,96,384]{3,2,1,0:T(8,128)(2,1)S(1)}, u32[]{:S(2)}, u32[]{:S(2)}) collective-permute-start(bf16[1,4,96,384]{3,2,1,0:T(8,128)(2,1)} %get-tuple-element.138), channel_id=1, source_target_pairs={{0,8},{4,12},{8,0},{12,4},{1,9},{5,13},{9,1},{13,5},{2,10},{6,14},... | collective-permute-start | bytes 884744 | tf_op jit(solution)/shard_map/ppermute | solution.py:467
  176.2 18.4 %collective-permute-start.38 = (bf16[8,4,96,384]{3,2,1,0:T(8,128)(2,1)}, bf16[8,4,96,384]{3,2,1,0:T(8,128)(2,1)S(1)}, u32[]{:S(2)}, u32[]{:S(2)}) collective-permute-start(bf16[8,4,96,384]{3,2,1,0:T(8,128)(2,1)} %get-tuple-element.150), channel_id=1, source_target_pairs={{0,4},{4,0},{8,12},{12,8},{1,5},{5,1},{9,13},{13,9},{2,6},{6,2},{1... | collective-permute-start | bytes 7077896 | tf_op jit(solution)/shard_map/ppermute | solution.py:467
  177.4 15.9 %collective-permute-start.36 = (bf16[2,4,96,384]{3,2,1,0:T(8,128)(2,1)}, bf16[2,4,96,384]{3,2,1,0:T(8,128)(2,1)S(1)}, u32[]{:S(2)}, u32[]{:S(2)}) collective-permute-start(bf16[2,4,96,384]{3,2,1,0:T(8,128)(2,1)} %get-tuple-element.147), channel_id=1, source_target_pairs={{0,8},{4,12},{8,0},{12,4},{1,9},{5,13},{9,1},{13,5},{2,10},{6,14},... | collective-permute-start | bytes 1769480 | tf_op jit(solution)/shard_map/ppermute | solution.py:467
  178.9 15.8 %collective-permute-start.37 = (bf16[2,4,96,384]{3,2,1,0:T(8,128)(2,1)}, bf16[2,4,96,384]{3,2,1,0:T(8,128)(2,1)}, u32[]{:S(2)}, u32[]{:S(2)}) collective-permute-start(bf16[2,4,96,384]{3,2,1,0:T(8,128)(2,1)} %get-tuple-element.148), channel_id=1, source_target_pairs={{0,16},{16,0},{1,17},{17,1},{2,18},{18,2},{3,19},{19,3},{4,20},{20... | collective-permute-start | bytes 1769480 | tf_op jit(solution)/shard_map/ppermute | solution.py:467
  181.1 11.8 %collective-permute-start.39 = (bf16[96,768]{1,0:T(8,128)(2,1)S(1)}, bf16[96,768]{1,0:T(8,128)(2,1)S(1)}, u32[]{:S(2)}, u32[]{:S(2)}) collective-permute-start(bf16[96,768]{1,0:T(8,128)(2,1)S(1)} %get-tuple-element.216), channel_id=1, source_target_pairs={{0,2},{1,3},{2,0},{3,1},{4,6},{5,7},{6,4},{7,5},{8,10},{9,11},{10,... | collective-permute-start | bytes 442376 | tf_op jit(solution)/shard_map/ppermute | solution.py:472
  181.1 11.8 %collective-permute-start.40 = (bf16[96,768]{1,0:T(8,128)(2,1)S(1)}, bf16[96,768]{1,0:T(8,128)(2,1)S(1)}, u32[]{:S(2)}, u32[]{:S(2)}) collective-permute-start(bf16[96,768]{1,0:T(8,128)(2,1)S(1)} %get-tuple-element.215), channel_id=1, source_target_pairs={{0,1},{1,2},{2,3},{3,0},{4,5},{5,6},{6,7},{7,4},{8,9},{9,10},{10,1... | collective-permute-start | bytes 442376 | tf_op jit(solution)/shard_map/ppermute | solution.py:472
  192.9 21.0 %collective-permute-start.45 = (bf16[96,768]{1,0:T(8,128)(2,1)}, bf16[96,768]{1,0:T(8,128)(2,1)S(1)}, u32[]{:S(2)}, u32[]{:S(2)}) collective-permute-start(bf16[96,768]{1,0:T(8,128)(2,1)} %get-tuple-element.214), channel_id=1, source_target_pairs={{0,3},{1,0},{2,1},{3,2},{4,7},{5,4},{6,5},{7,6},{8,11},{9,8},{10,9... | collective-permute-start | bytes 442376 | tf_op jit(solution)/shard_map/ppermute | solution.py:472
  199.6 14.4 %collective-permute-start.41 = (bf16[1,4,96,384]{3,2,1,0:T(8,128)(2,1)}, bf16[1,4,96,384]{3,2,1,0:T(8,128)(2,1)S(1)}, u32[]{:S(2)}, u32[]{:S(2)}) collective-permute-start(bf16[1,4,96,384]{3,2,1,0:T(8,128)(2,1)} %get-tuple-element.151.rest_23_), channel_id=1, source_target_pairs={{0,16},{16,0},{1,17},{17,1},{2,18},{18,2},{3,19},{19,3},{4,20},{20... | collective-permute-start | bytes 884744 | tf_op jit(solution)/shard_map/ppermute | solution.py:467
  200.1 13.9 %collective-permute-start.42 = (bf16[1,4,96,384]{3,2,1,0:T(8,128)(2,1)}, bf16[1,4,96,384]{3,2,1,0:T(8,128)(2,1)S(1)}, u32[]{:S(2)}, u32[]{:S(2)}) collective-permute-start(bf16[1,4,96,384]{3,2,1,0:T(8,128)(2,1)} %get-tuple-element.154), channel_id=1, source_target_pairs={{0,8},{4,12},{8,0},{12,4},{1,9},{5,13},{9,1},{13,5},{2,10},{6,14},... | collective-permute-start | bytes 884744 | tf_op jit(solution)/shard_map/ppermute | solution.py:467
  200.6 20.6 %collective-permute-start.43 = (bf16[2,4,96,384]{3,2,1,0:T(8,128)(2,1)}, bf16[2,4,96,384]{3,2,1,0:T(8,128)(2,1)S(1)}, u32[]{:S(2)}, u32[]{:S(2)}) collective-permute-start(bf16[2,4,96,384]{3,2,1,0:T(8,128)(2,1)} %get-tuple-element.155), channel_id=1, source_target_pairs={{0,8},{4,12},{8,0},{12,4},{1,9},{5,13},{9,1},{13,5},{2,10},{6,14},... | collective-permute-start | bytes 1769480 | tf_op jit(solution)/shard_map/ppermute | solution.py:467
  202.1 19.1 %collective-permute-start.44 = (bf16[2,4,96,384]{3,2,1,0:T(8,128)(2,1)}, bf16[2,4,96,384]{3,2,1,0:T(8,128)(2,1)S(1)}, u32[]{:S(2)}, u32[]{:S(2)}) collective-permute-start(bf16[2,4,96,384]{3,2,1,0:T(8,128)(2,1)} %get-tuple-element.156), channel_id=1, source_target_pairs={{0,16},{16,0},{1,17},{17,1},{2,18},{18,2},{3,19},{19,3},{4,20},{20... | collective-permute-start | bytes 1769480 | tf_op jit(solution)/shard_map/ppermute | solution.py:467
  225.7 13.1 %collective-permute-start.49 = (bf16[1,4,96,384]{3,2,1,0:T(8,128)(2,1)}, bf16[1,4,96,384]{3,2,1,0:T(8,128)(2,1)S(1)}, u32[]{:S(2)}, u32[]{:S(2)}) collective-permute-start(bf16[1,4,96,384]{3,2,1,0:T(8,128)(2,1)} %get-tuple-element.159), channel_id=1, source_target_pairs={{0,16},{16,0},{1,17},{17,1},{2,18},{18,2},{3,19},{19,3},{4,20},{20... | collective-permute-start | bytes 884744 | tf_op jit(solution)/shard_map/ppermute | solution.py:467
  227.1 13.0 %collective-permute-start.50 = (bf16[1,4,96,384]{3,2,1,0:T(8,128)(2,1)}, bf16[1,4,96,384]{3,2,1,0:T(8,128)(2,1)S(1)}, u32[]{:S(2)}, u32[]{:S(2)}) collective-permute-start(bf16[1,4,96,384]{3,2,1,0:T(8,128)(2,1)} %get-tuple-element.160), channel_id=1, source_target_pairs={{0,8},{4,12},{8,0},{12,4},{1,9},{5,13},{9,1},{13,5},{2,10},{6,14},... | collective-permute-start | bytes 884744 | tf_op jit(solution)/shard_map/ppermute | solution.py:467
  229.2 22.9 %collective-permute-start.52 = (bf16[96,1536]{1,0:T(8,128)(2,1)S(1)}, bf16[96,1536]{1,0:T(8,128)(2,1)S(1)}, u32[]{:S(2)}, u32[]{:S(2)}) collective-permute-start(bf16[96,1536]{1,0:T(8,128)(2,1)S(1)} %pad_maximum_fusion.12), channel_id=1, source_target_pairs={{0,2},{1,3},{2,0},{3,1},{4,6},{5,7},{6,4},{7,5},{8,10},{9,11},{10,... | collective-permute-start | bytes 884744 | tf_op jit(solution)/shard_map/ppermute | solution.py:472
  229.6 22.5 %collective-permute-start.53 = (bf16[96,1536]{1,0:T(8,128)(2,1)S(1)}, bf16[96,1536]{1,0:T(8,128)(2,1)}, u32[]{:S(2)}, u32[]{:S(2)}) collective-permute-start(bf16[96,1536]{1,0:T(8,128)(2,1)S(1)} %pad_maximum_fusion.13), channel_id=1, source_target_pairs={{0,1},{1,2},{2,3},{3,0},{4,5},{5,6},{6,7},{7,4},{8,9},{9,10},{10,1... | collective-permute-start | bytes 884744 | tf_op jit(solution)/shard_map/ppermute | solution.py:472
  244.7 13.2 %collective-permute-start.51 = (bf16[96,1536]{1,0:T(8,128)(2,1)S(1)}, bf16[96,1536]{1,0:T(8,128)(2,1)}, u32[]{:S(2)}, u32[]{:S(2)}) collective-permute-start(bf16[96,1536]{1,0:T(8,128)(2,1)S(1)} %pad_maximum_fusion.11), channel_id=1, source_target_pairs={{0,3},{1,0},{2,1},{3,2},{4,7},{5,4},{6,5},{7,6},{8,11},{9,8},{10,9... | collective-permute-start | bytes 884744 | tf_op jit(solution)/shard_map/ppermute | solution.py:472
  (66 other events, 334.0 us)

commit v3 on v2

--- a/solution.py
+++ b/solution.py
@@ -525,8 +525,7 @@
     specs, arrays, layout, shapes, plans = [], [], [], [], []
 
     def block(array, count, index):
-        shape = (count,) + array.shape[1:]
-        return pl.BlockSpec(shape, lambda s: (index,) + (0,) * (len(shape) - 1), pipeline_mode=pl.Buffered(1))
+        return pl.BlockSpec((count, 1) + array.shape[2:], lambda s: (index, s, 0, 0))
 
     for r in reductions:
         half = r.half()
@@ -550,9 +549,10 @@
         plans.append((r, half))
     out = list(pl.pallas_call(
         functools.partial(merge_kernel, layout, len(arrays), len(arrays) + len(values) + len(after)),
-        grid=(1,),
+        grid=(shapes[0][1],),
         in_specs=specs + [ANY] * (len(values) + len(after)),
-        out_specs=[full(*shape) for shape in shapes] + [ANY] * len(values),
+        out_specs=[pl.BlockSpec((shape[0], 1) + shape[2:], lambda s: (0, s, 0, 0)) for shape in shapes]
+        + [ANY] * len(values),
         out_shape=[shaped(shape, BF16) for shape in shapes] + [shaped(v.shape, v.dtype) for v in values],
         input_output_aliases={len(arrays) + n: len(shapes) + n for n in range(len(values))},
         compiler_params=pltpu.CompilerParams(vmem_limit_bytes=60 * 2**20),
@@ -655,7 +655,7 @@
     mlp_blocks = gather_col(fence([mlp_own], [attn.held[0]])[0])
     for _ in range(far):
         attn.advance()
-        phase([attn], [], [na, mlp_blocks[1], mlp_blocks[-1]] if attn.done == 1 else mlp_blocks[2:-1])
+        phase([attn], [], [na, mlp_blocks[2]] if attn.done == 1 else [mlp_blocks[1]] + mlp_blocks[3:])
     mlp_blocks = fence(mlp_blocks, attn.moving)
     attn.cross_held()
     attn.cross_moving()
@@ -717,7 +717,7 @@
         totals.update(zip((id(r) for r in ending), finished))
         return token, passed
 
-    phase(mlp[1:], [], [branch] + mlp[0].over)
+    mlp[1].held = phase(mlp[1:], mlp[1].held, [branch] + mlp[0].over)[:2]
     token, _ = go_on([attn_sum], [branch, mlp[1].moving[0]])
     mlp[1].cross_held()
     mlp[1].cross_moving()
@@ -784,13 +784,12 @@
             if len(mlp_moves) < col_size:
                 token, _ = go_on(mlp_sums, token)
     head_row, up_row = 5 + col_size, 5
-    smalls = sum_over(smalls, ("row", "dp"))
+    smalls = sum_over(smalls, ("row", "dp", "col"))
     smalls, *came = fence([smalls] + [mlp_moves[k] for k in range(1, col_size)])
     mlp_mine, mlp_other = settle([mlp_moves[0]] + came)
     g_heads = whole_block(attn_mine, attn_other).reshape(rows, local_heads, HEAD)
     g_mlp = whole_block(mlp_mine, mlp_other)
     g_up, g_down = g_mlp[:, :up_cols], g_mlp[:, up_cols:]
-    smalls = sum_over(smalls, ("col",))
     return (
         block_out,
         in_grad,

time: 275 us -> 278 us (1.011)
  waiting for transfers between devices: 65.9 us -> 59.3 us
  Pallas kernels: 104 us -> 110 us
    pallas_call x6, Pallas kernels: 18.5 us -> 24 us  [merge(): pl.pallas_call(functools.partial(merge_kernel, layout, len(arrays), len(a...]
    ppermute x12, waiting for transfers between devices: 30.6 us -> 26 us  [shifted(): lax.ppermute(value, 'col', [(i, (i + by) % size) for i in range(size)])]
    ppermute x12, starting transfers between devices: 17.4 us -> 21.3 us  [shifted(): lax.ppermute(value, 'col', [(i, (i + by) % size) for i in range(size)])]
    unnamed x118 -> x116, local copies, waits for them, and re-layouts: 14.3 us -> 15.3 us
  transfers between devices with their start and end apart: 58 -> 58, of which waited for: 16 -> 15; matrix products, arithmetic and copies ran while one was open for 11% -> 11% of each run, Pallas kernels for 34% -> 35%
where the time goes in v3:
time: 278 us; the launch traced here: 277 us
  Pallas kernels  110 us (40%)
  waiting for transfers between devices  59.3 us (21%)
  starting transfers between devices  55.6 us (20%)
  local copies, waits for them, and re-layouts  33 us (12%)
  other arithmetic  17.7 us (6%)
    pallas_call x4, Pallas kernels, block_part(): pl.pallas_call(functools.partial(kernel, orders, core_bit, len(after)), g...  51.7 us
    ppermute x46, starting transfers between devices, flipped(): lax.ppermute(value, axis, [(i, i ^ flip) for i in range(lax.axis_size(axi...  34.3 us
    ppermute x46, waiting for transfers between devices, flipped(): lax.ppermute(value, axis, [(i, i ^ flip) for i in range(lax.axis_size(axi...  33.3 us
    ppermute x12, waiting for transfers between devices, shifted(): lax.ppermute(value, 'col', [(i, (i + by) % size) for i in range(size)])  26 us
    pallas_call x6, Pallas kernels, merge(): pl.pallas_call(functools.partial(merge_kernel, layout, len(arrays), len(a...  24 us
    ppermute x12, starting transfers between devices, shifted(): lax.ppermute(value, 'col', [(i, (i + by) % size) for i in range(size)])  21.3 us
    pallas_call x2, Pallas kernels, mlp_tail_part(): pl.pallas_call(functools.partial(mlp_tail_kernel, orders, core_bit, len(s...  17.7 us
    unnamed x116, local copies, waits for them, and re-layouts  15.3 us
  transfers between devices with their start and end apart: 58, of which 15 were waited for; matrix products, arithmetic and copies ran while one was open for 11% of the time, Pallas kernels for 35%

profile of v3, /device:TPU:0, one launch (start us, length us, event | category | flops | bytes accessed | tf_op | source)
XLA Modules:
  0.0 276.8 jit_solution(10367366421692843833)
XLA Ops:
  3.1 5.1 %collective-permute-start.2 = (bf16[96,768]{1,0:T(8,128)(2,1)S(1)}, bf16[96,768]{1,0:T(8,128)(2,1)S(1)}, u32[]{:S(2)}, u32[]{:S(2)}) collective-permute-start(bf16[96,768]{1,0:T(8,128)(2,1)S(1)} %copy.76), channel_id=1, source_target_pairs={{0,3},{1,0},{2,1},{3,2},{4,7},{5,4},{6,5},{7,6},{8,11},{9,8},{10,9... | collective-permute-start | bytes 442376 | tf_op jit(solution)/shard_map/ppermute | solution.py:472
  14.5 1.3 constant_dynamic-slice_fusion.segr_ref
  15.8 4.9 %collective-permute-done.1 = bf16[96,768]{1,0:T(8,128)(2,1)S(1)} collective-permute-done((bf16[96,768]{1,0:T(8,128)(2,1)S(1)}, bf16[96,768]{1,0:T(8,128)(2,1)S(1)}, u32[]{:S(2)}, u32[]{:S(2)}) %collective-permute-start.1) | collective-permute-done | bytes 147488 | tf_op jit(solution)/shard_map/ppermute | solution.py:472
  20.9 1.6 collective-permute-start.6
  22.4 2.8 %collective-permute-start.4 = (bf16[96,1536]{1,0:T(8,128)(2,1)}, bf16[96,1536]{1,0:T(8,128)(2,1)S(1)}, u32[]{:S(2)}, u32[]{:S(2)}) collective-permute-start(bf16[96,1536]{1,0:T(8,128)(2,1)} %shard_map.254.__0_), channel_id=1, source_target_pairs={{0,2},{1,3},{2,0},{3,1},{4,6},{5,7},{6,4},{7,5},{8,10},{9,11},{10,... | collective-permute-start | bytes 884744 | tf_op jit(solution)/shard_map/ppermute | solution.py:472
  25.2 1.5 collective-permute-start.7
  26.8 6.0 %shard_map.255 = (bf16[512,768]{1,0:T(8,128)(2,1)}, bf16[768,512]{1,0:T(8,128)(2,1)}, bf16[512,768]{1,0:T(8,128)(2,1)}, bf16[768,512]{1,0:T(8,128)(2,1)}, bf16[7...) custom-call(bf16[512,768]{1,0:T(8,128)(2,1)} %rest_13_.1, ...), custom_call_target="tpu_custom_call" | custom-call | flops 6899999744 | bytes 1048576 | tf_op jit(solution)/shard_map/pallas_call | solution.py:123
  32.8 5.1 %collective-permute-done.4.__3_.__2_ = bf16[96,1536]{1,0:T(8,128)(2,1)S(1)} collective-permute-done((bf16[96,1536]{1,0:T(8,128)(2,1)}, bf16[96,1536]{1,0:T(8,128)(2,1)S(1)}, u32[]{:S(2)}, u32[]{:S(2)}) %collective-permute-start.4) | collective-permute-done | bytes 294944 | tf_op jit(solution)/shard_map/ppermute | solution.py:472
  40.8 1.6 collective-permute-start.8
  44.6 3.8 %collective-permute-start.5 = (bf16[96,1536]{1,0:T(8,128)(2,1)S(1)}, bf16[96,1536]{1,0:T(8,128)(2,1)S(1)}, u32[]{:S(2)}, u32[]{:S(2)}) collective-permute-start(bf16[96,1536]{1,0:T(8,128)(2,1)S(1)} %copy-done.11), channel_id=1, source_target_pairs={{0,3},{1,0},{2,1},{3,2},{4,7},{5,4},{6,5},{7,6},{8,11},{9,8},{10,9... | collective-permute-start | bytes 884744 | tf_op jit(solution)/shard_map/ppermute | solution.py:472
  48.5 7.8 %collective-permute-done.3.__2_.__1_ = bf16[96,1536]{1,0:T(8,128)(2,1)S(1)} collective-permute-done((bf16[96,1536]{1,0:T(8,128)(2,1)S(1)}, bf16[96,1536]{1,0:T(8,128)(2,1)S(1)}, u32[]{:S(2)}, u32[]{:S(2)}) %collective-permute-start.3) | collective-permute-done | bytes 294944 | tf_op jit(solution)/shard_map/ppermute | solution.py:472
  56.3 2.8 %collective-permute-done.5.__3_ = bf16[96,1536]{1,0:T(8,128)(2,1)S(1)} collective-permute-done((bf16[96,1536]{1,0:T(8,128)(2,1)S(1)}, bf16[96,1536]{1,0:T(8,128)(2,1)S(1)}, u32[]{:S(2)}, u32[]{:S(2)}) %collective-permute-start.5) | collective-permute-done | bytes 294944 | tf_op jit(solution)/shard_map/ppermute | solution.py:472
  67.9 1.5 collective-permute-start.13
  69.4 15.0 %shard_map.259 = (bf16[2,512,768]{2,1,0:T(8,128)(2,1)}, bf16[2,512,384]{2,1,0:T(8,128)(2,1)}, f32[2,1,768]{2,1,0:T(1,128)}, bf16[8,4,96,384]{3,2,1,0:T(8,128)(2,1)}, bf16[8,4,96,384]{3,2,1,0:T(8,128)(2,1)}) custom-call(s32[2]{0:T(128)} %pad_add_fusion.me_ref, bf16[512,768]{1,0:T(8,128)(2,1)} %get-tuple-element.94.__2_.na_ref, ...), custom_call_target="tpu_custom_call" | custom-call | flops 23000000512 | bytes 1048576 | tf_op jit(solution)/shard_map/pallas_call | solution.py:269
  89.5 14.9 %shard_map.261 = (bf16[2,512,768]{2,1,0:T(8,128)(2,1)}, bf16[2,512,384]{2,1,0:T(8,128)(2,1)}, f32[2,1,768]{2,1,0:T(1,128)}, bf16[8,4,96,384]{3,2,1,0:T(8,128)(2,1)}, bf16[8,4,96,384]{3,2,1,0:T(8,128)(2,1)}) custom-call(s32[2]{0:T(128)} %pad_add_fusion.me_ref, ...), custom_call_target="tpu_custom_call", output_to_operand_aliasing={{3}: (19, {}), {4}: (20, {})} | custom-call | flops 23000000512 | bytes 1048576 | tf_op jit(solution)/shard_map/pallas_call | solution.py:269
  106.7 1.6 collective-permute-start.18
  108.3 1.8 pad_maximum_fusion.4.__1_
  111.5 10.2 %shard_map.263 = (f32[512,768]{1,0:T(8,128)}, f32[512,768]{1,0:T(8,128)}) custom-call(s32[2]{0:T(128)} %pad_add_fusion.me_ref, bf16[2,4,96,384]{3,2,1,0:T(8,128)(2,1)} %copy-done.19, bf16[2,4,96,384]{3,2,1,0:T(8,128)(2,1)} %get-tuple-element.97.__4_.rest_1_, bf16[2,4,96,384]{3,2,1,0:T(8,128)(2,1)} %copy-done.52, ...), custom_call_target="tpu_custom_call" | custom-call | flops 12650000384 | bytes 1048576 | tf_op jit(solution)/shard_map/pallas_call | solution.py:403
  122.3 3.3 %collective-permute-done.19.__3_ = bf16[2,2,96,768]{3,2,1,0:T(8,128)(2,1)} collective-permute-done((bf16[2,2,96,768]{3,2,1,0:T(8,128)(2,1)}, bf16[2,2,96,768]{3,2,1,0:T(8,128)(2,1)}, u32[]{:S(2)}, u32[]{:S(2)}) %collective-permute-start.19) | collective-permute-done | bytes 589856 | tf_op jit(solution)/shard_map/ppermute | solution.py:467
  126.7 1.4 copy-done.3
  128.1 3.8 %shard_map.265 = (bf16[2,4,96,384]{3,2,1,0:T(8,128)(2,1)}, bf16[2,4,96,384]{3,2,1,0:T(8,128)(2,1)}) custom-call(bf16[8,4,96,384]{3,2,1,0:T(8,128)(2,1)} %get-tuple-element.131.refs_0_.refs_2_.refs_3_.refs_4_, bf16[8,4,96,384]{3,2,1,0:T(8,128)(2,1)} %copy-done.3, bf16[8,4,96,384]{3,2,1,0:T(8,128)(2,1)} %get-tuple-element.131.refs_0_.refs_2_.refs_3_.refs_4_, ...), custom_call_target="tpu_custom_call" | custom-call | flops 3449999872 | bytes 1048576 | tf_op jit(solution)/shard_map/pallas_call | solution.py:550
  133.3 11.0 %shard_map.266 = (bf16[2,512,768]{2,1,0:T(8,128)(2,1)}, bf16[2,512,768]{2,1,0:T(8,128)(2,1)}, f32[2,1,768]{2,1,0:T(1,128)}, bf16[8,4,96,384]{3,2,1,0:T(8,128)(2,1)}, bf16[8,4,96,384]{3,2,1,0:T(8,128)(2,1)}) custom-call(s32[2]{0:T(128)} %pad_add_fusion.me_ref, bf16[512,768]{1,0:T(8,128)(2,1)} %get-tuple-element.129.nm_ref, ...), custom_call_target="tpu_custom_call" | custom-call | flops 13799999488 | bytes 1048576 | tf_op jit(solution)/shard_map/pallas_call | solution.py:269
  144.4 3.1 %collective-permute-done.31.refs_2_ = bf16[2,4,96,384]{3,2,1,0:T(8,128)(2,1)S(1)} collective-permute-done((bf16[2,4,96,384]{3,2,1,0:T(8,128)(2,1)}, bf16[2,4,96,384]{3,2,1,0:T(8,128)(2,1)S(1)}, u32[]{:S(2)}, u32[]{:S(2)}) %collective-permute-start.31) | collective-permute-done | bytes 589856 | tf_op jit(solution)/shard_map/ppermute | solution.py:467
  148.9 3.5 %shard_map.267 = (bf16[1,4,96,384]{3,2,1,0:T(8,128)(2,1)}, bf16[1,4,96,384]{3,2,1,0:T(8,128)(2,1)}, bf16[8,4,96,384]{3,2,1,0:T(8,128)(2,1)}) custom-call(bf16[8,4,96,384]{3,2,1,0:T(8,128)(2,1)} %get-tuple-element.131.refs_0_.refs_2_.refs_3_.refs_4_, bf16[8,4,96,384]{3,2,1,0:T(8,128)(2,1)} %copy-done.3, ...), custom_call_target="tpu_custom_call", output_to_operand_aliasing={{2}: (6, {})} | custom-call | flops 3449999872 | bytes 1048576 | tf_op jit(solution)/shard_map/pallas_call | solution.py:550
  154.1 10.9 %shard_map.268 = (bf16[2,512,768]{2,1,0:T(8,128)(2,1)}, bf16[2,512,768]{2,1,0:T(8,128)(2,1)}, f32[2,1,768]{2,1,0:T(1,128)}, bf16[8,4,96,384]{3,2,1,0:T(8,128)(2,1)}, bf16[8,4,96,384]{3,2,1,0:T(8,128)(2,1)}) custom-call(s32[2]{0:T(128)} %pad_add_fusion.me_ref, bf16[512,768]{1,0:T(8,128)(2,1)} %get-tuple-element.129.nm_ref, ...), custom_call_target="tpu_custom_call" | custom-call | flops 13799999488 | bytes 1048576 | tf_op jit(solution)/shard_map/pallas_call | solution.py:269
  166.6 4.4 %shard_map.269 = (bf16[1,4,96,768]{3,2,1,0:T(8,128)(2,1)}, bf16[2,4,96,384]{3,2,1,0:T(8,128)(2,1)}, bf16[2,4,96,384]{3,2,1,0:T(8,128)(2,1)}, bf16[8,4,96,384]{3,2,1,0:T(8,128)(2,1)}) custom-call(bf16[8,4,96,384]{3,2,1,0:T(8,128)(2,1)} %get-tuple-element.131.refs_0_.refs_2_.refs_3_.refs_4_, ...), custom_call_target="tpu_custom_call", output_to_operand_aliasing={{3}: (12, {})} | custom-call | flops 3449999872 | bytes 1048576 | tf_op jit(solution)/shard_map/pallas_call | solution.py:550
  173.2 1.5 collective-permute-start.37
  175.8 2.4 collective-permute-start.39
  178.4 7.4 %shard_map.270 = (f32[512,768]{1,0:T(8,128)}, f32[512,768]{1,0:T(8,128)}) custom-call(s32[2]{0:T(128)} %pad_add_fusion.me_ref, bf16[2,2,96,768]{3,2,1,0:T(8,128)(2,1)} %copy-done.17, bf16[2,2,96,768]{3,2,1,0:T(8,128)(2,1)} %get-tuple-element.124.rest_1_, bf16[2,2,96,768]{3,2,1,0:T(8,128)(2,1)} %copy-done.5, ...), custom_call_target="tpu_custom_call" | custom-call | flops 10350000128 | bytes 1048576 | tf_op jit(solution)/shard_map/pallas_call | solution.py:432
  185.8 2.3 collective-permute-done.39.refs_10_
  188.1 1.4 collective-permute-start.45
  191.2 4.5 %shard_map.271 = (bf16[1,4,96,384]{3,2,1,0:T(8,128)(2,1)}, bf16[1,4,96,384]{3,2,1,0:T(8,128)(2,1)}, bf16[2,4,96,384]{3,2,1,0:T(8,128)(2,1)}, bf16[2,4,96,384]{3,...) custom-call(bf16[8,4,96,384]{3,2,1,0:T(8,128)(2,1)} %get-tuple-eleme, ...), custom_call_target="tpu_custom_call", output_to_operand_aliasing={{4}: (10, {}), {5}: (11, {})} | custom-call | flops 3449999872 | bytes 1048576 | tf_op jit(solution)/shard_map/pallas_call | solution.py:550
  198.5 1.3 collective-permute-start.44
  199.8 10.3 %shard_map.272 = (bf16[512,768]{1,0:T(8,128)(2,1)}, bf16[512,768]{1,0:T(8,128)(2,1)}, f32[16,768]{1,0:T(8,128)}) custom-call(s32[2]{0:T(128)} %pad_add_fusion.me_ref, bf16[2,2,96,768]{3,2,1,0:T(8,128)(2,1)} %get-tuple-element.125.rest_0_, bf16[2,2,96,768]{3,2,1,0:T(8,128)(2,1)} %get-tuple-element.126.refs_5_.rest_1_, bf16[2,2,96,768]{3,2,1,0:T(8,128)(2,1)} %copy-done.14, ...), custom_call_target="tpu_custom_call" | custom-call | flops 10350000128 | bytes 1048576 | tf_op jit(solution)/shard_map/pallas_call | solution.py:432
  210.2 7.2 %collective-permute-done.43.refs_10_.refs_2_ = bf16[2,4,96,384]{3,2,1,0:T(8,128)(2,1)S(1)} collective-permute-done((bf16[2,4,96,384]{3,2,1,0:T(8,128)(2,1)}, bf16[2,4,96,384]{3,2,1,0:T(8,128)(2,1)S(1)}, u32[]{:S(2)}, u32[]{:S(2)}) %collective-permute-start.43) | collective-permute-done | bytes 589856 | tf_op jit(solution)/shard_map/ppermute | solution.py:467
  218.3 4.1 %shard_map.273 = (bf16[1,4,96,768]{3,2,1,0:T(8,128)(2,1)}, bf16[1,4,96,384]{3,2,1,0:T(8,128)(2,1)}, bf16[1,4,96,384]{3,2,1,0:T(8,128)(2,1)}, f32[16,768]{1,0:T(8,128)}, bf16[96,768]{1,0:T(8,128)(2,1)}) custom-call(bf16[8,4,96,384]{3,2,1,0:T(8,128)(2,1)} %get-tuple-element.143.refs_8_.refs_10_.refs_0_.refs_3_.refs_4_, ...), custom_call_target="tpu_custom_call", output_to_operand_aliasing={{3}: (14, {}), {4}: (15, {})} | custom-call | flops 3449999872 | bytes 1048576 | tf_op jit(solution)/shard_map/pallas_call | solution.py:550
  226.0 1.9 collective-permute-start.54
  228.9 1.6 collective-permute-start.56
  231.6 3.1 %collective-permute-done.47 = f32[16,768]{1,0:T(8,128)S(1)} collective-permute-done((f32[16,768]{1,0:T(8,128)S(1)}, f32[16,768]{1,0:T(8,128)S(1)}, u32[]{:S(2)}, u32[]{:S(2)}) %collective-permute-start.47) | collective-permute-done | bytes 49184 | tf_op jit(solution)/shard_map/ppermute | solution.py:467
  235.3 3.6 %collective-permute-done.48 = f32[16,768]{1,0:T(8,128)S(1)} collective-permute-done((f32[16,768]{1,0:T(8,128)S(1)}, f32[16,768]{1,0:T(8,128)S(1)}, u32[]{:S(2)}, u32[]{:S(2)}) %collective-permute-start.48) | collective-permute-done | bytes 49184 | tf_op jit(solution)/shard_map/ppermute | solution.py:467
  240.8 8.7 %collective-permute-done.49 = f32[16,768]{1,0:T(8,128)S(1)} collective-permute-done((f32[16,768]{1,0:T(8,128)S(1)}, f32[16,768]{1,0:T(8,128)S(1)}, u32[]{:S(2)}, u32[]{:S(2)}) %collective-permute-start.49) | collective-permute-done | bytes 49184 | tf_op jit(solution)/shard_map/ppermute | solution.py:467
  251.5 3.7 %shard_map.274 = bf16[1,4,96,768]{3,2,1,0:T(8,128)(2,1)} custom-call(bf16[8,4,96,384]{3,2,1,0:T(8,128)(2,1)} %get-tuple-element.153.refs_6_.refs_8_.refs_11_.refs_0_.refs_4_, bf16[8,4,96,384]{3,2,1,0:T(8,128)(2,1)} %copy-done.4, bf16[2,4,96,384]{3,2,1,0:T(8,128)(2,1)} %copy-done.15, bf16[1,4,96,384]{3,2,1,0:T(8,128)(2,1)} %copy-done.53, ...), custom_call_target="tpu_custom_call" | custom-call | flops 3449999872 | bytes 1048576 | tf_op jit(solution)/shard_map/pallas_call | solution.py:550
  256.5 2.0 collective-permute-start.53
  261.1 1.4 add.99.__0_
  262.6 3.0 %collective-permute-done.53.__1_ = bf16[96,1536]{1,0:T(8,128)(2,1)} collective-permute-done((bf16[96,1536]{1,0:T(8,128)(2,1)S(1)}, bf16[96,1536]{1,0:T(8,128)(2,1)}, u32[]{:S(2)}, u32[]{:S(2)}) %collective-permute-start.53) | collective-permute-done | bytes 294944 | tf_op jit(solution)/shard_map/ppermute | solution.py:472
  266.9 1.3 collective-permute-start.57
  270.3 1.6 slice_reduce_fusion
  271.9 3.1 %collective-permute-done.57 = bf16[96,1536]{1,0:T(8,128)(2,1)S(1)} collective-permute-done((bf16[96,1536]{1,0:T(8,128)(2,1)S(1)}, bf16[96,1536]{1,0:T(8,128)(2,1)S(1)}, u32[]{:S(2)}, u32[]{:S(2)}) %collective-permute-start.57) | collective-permute-done | bytes 294944 | tf_op jit(solution)/shard_map/ppermute | solution.py:467
  (272 shorter events, 67.2 us)
Async XLA Ops:
  3.1 12.7 %collective-permute-start.2 = (bf16[96,768]{1,0:T(8,128)(2,1)S(1)}, bf16[96,768]{1,0:T(8,128)(2,1)S(1)}, u32[]{:S(2)}, u32[]{:S(2)}) collective-permute-start(bf16[96,768]{1,0:T(8,128)(2,1)S(1)} %copy.76), channel_id=1, source_target_pairs={{0,3},{1,0},{2,1},{3,2},{4,7},{5,4},{6,5},{7,6},{8,11},{9,8},{10,9... | collective-permute-start | bytes 442376 | tf_op jit(solution)/shard_map/ppermute | solution.py:472
  8.2 12.5 %collective-permute-start.1 = (bf16[96,768]{1,0:T(8,128)(2,1)S(1)}, bf16[96,768]{1,0:T(8,128)(2,1)S(1)}, u32[]{:S(2)}, u32[]{:S(2)}) collective-permute-start(bf16[96,768]{1,0:T(8,128)(2,1)S(1)} %copy.76), channel_id=1, source_target_pairs={{0,2},{1,3},{2,0},{3,1},{4,6},{5,7},{6,4},{7,5},{8,10},{9,11},{10,... | collective-permute-start | bytes 442376 | tf_op jit(solution)/shard_map/ppermute | solution.py:472
  8.2 12.5 %collective-permute-start = (bf16[96,768]{1,0:T(8,128)(2,1)S(1)}, bf16[96,768]{1,0:T(8,128)(2,1)S(1)}, u32[]{:S(2)}, u32[]{:S(2)}) collective-permute-start(bf16[96,768]{1,0:T(8,128)(2,1)S(1)} %copy.76), channel_id=1, source_target_pairs={{0,1},{1,2},{2,3},{3,0},{4,5},{5,6},{6,7},{7,4},{8,9},{9,10},{10,1... | collective-permute-start | bytes 442376 | tf_op jit(solution)/shard_map/ppermute | solution.py:472
  20.9 17.0 %collective-permute-start.6 = (bf16[1,4,96,384]{3,2,1,0:T(8,128)(2,1)S(1)}, bf16[1,4,96,384]{3,2,1,0:T(8,128)(2,1)S(1)}, u32[]{:S(2)}, u32[]{:S(2)}) collective-permute-start(bf16[1,4,96,384]{3,2,1,0:T(8,128)(2,1)S(1)} %get-tuple-element.226.__1_), channel_id=1, source_target_pairs={{0,8},{4,12},{8,0},{12,4},{1,9},{5,13},{9,1},{13,5},{2,10},{6,14},... | collective-permute-start | bytes 884744 | tf_op jit(solution)/shard_map/ppermute | solution.py:467
  22.4 15.5 %collective-permute-start.4 = (bf16[96,1536]{1,0:T(8,128)(2,1)}, bf16[96,1536]{1,0:T(8,128)(2,1)S(1)}, u32[]{:S(2)}, u32[]{:S(2)}) collective-permute-start(bf16[96,1536]{1,0:T(8,128)(2,1)} %shard_map.254.__0_), channel_id=1, source_target_pairs={{0,2},{1,3},{2,0},{3,1},{4,6},{5,7},{6,4},{7,5},{8,10},{9,11},{10,... | collective-permute-start | bytes 884744 | tf_op jit(solution)/shard_map/ppermute | solution.py:472
  25.2 12.7 %collective-permute-start.7 = (bf16[1,4,96,384]{3,2,1,0:T(8,128)(2,1)S(1)}, bf16[1,4,96,384]{3,2,1,0:T(8,128)(2,1)S(1)}, u32[]{:S(2)}, u32[]{:S(2)}) collective-permute-start(bf16[1,4,96,384]{3,2,1,0:T(8,128)(2,1)S(1)} %get-tuple-element.225), channel_id=1, source_target_pairs={{0,16},{16,0},{1,17},{17,1},{2,18},{18,2},{3,19},{19,3},{4,20},{20... | collective-permute-start | bytes 884744 | tf_op jit(solution)/shard_map/ppermute | solution.py:467
  40.8 18.4 %collective-permute-start.8 = (bf16[2,4,96,384]{3,2,1,0:T(8,128)(2,1)S(1)}, bf16[2,4,96,384]{3,2,1,0:T(8,128)(2,1)}, u32[]{:S(2)}, u32[]{:S(2)}) collective-permute-start(bf16[2,4,96,384]{3,2,1,0:T(8,128)(2,1)S(1)} %pad_maximum_fusion.1.rest_0_), channel_id=1, source_target_pairs={{0,16},{16,0},{1,17},{17,1},{2,18},{18,2},{3,19},{19,3},{4,20},{20... | collective-permute-start | bytes 1769480 | tf_op jit(solution)/shard_map/ppermute | solution.py:467
  43.4 15.8 %collective-permute-start.9 = (bf16[2,4,96,384]{3,2,1,0:T(8,128)(2,1)S(1)}, bf16[2,4,96,384]{3,2,1,0:T(8,128)(2,1)}, u32[]{:S(2)}, u32[]{:S(2)}) collective-permute-start(bf16[2,4,96,384]{3,2,1,0:T(8,128)(2,1)S(1)} %pad_maximum_fusion.2.rest_4_), channel_id=1, source_target_pairs={{0,8},{4,12},{8,0},{12,4},{1,9},{5,13},{9,1},{13,5},{2,10},{6,14},... | collective-permute-start | bytes 1769480 | tf_op jit(solution)/shard_map/ppermute | solution.py:467
  44.5 11.8 %collective-permute-start.3 = (bf16[96,1536]{1,0:T(8,128)(2,1)S(1)}, bf16[96,1536]{1,0:T(8,128)(2,1)S(1)}, u32[]{:S(2)}, u32[]{:S(2)}) collective-permute-start(bf16[96,1536]{1,0:T(8,128)(2,1)S(1)} %copy-done.11), channel_id=1, source_target_pairs={{0,1},{1,2},{2,3},{3,0},{4,5},{5,6},{6,7},{7,4},{8,9},{9,10},{10,1... | collective-permute-start | bytes 884744 | tf_op jit(solution)/shard_map/ppermute | solution.py:472
  44.6 14.6 %collective-permute-start.5 = (bf16[96,1536]{1,0:T(8,128)(2,1)S(1)}, bf16[96,1536]{1,0:T(8,128)(2,1)S(1)}, u32[]{:S(2)}, u32[]{:S(2)}) collective-permute-start(bf16[96,1536]{1,0:T(8,128)(2,1)S(1)} %copy-done.11), channel_id=1, source_target_pairs={{0,3},{1,0},{2,1},{3,2},{4,7},{5,4},{6,5},{7,6},{8,11},{9,8},{10,9... | collective-permute-start | bytes 884744 | tf_op jit(solution)/shard_map/ppermute | solution.py:472
  48.4 17.9 %collective-permute-start.14 = (bf16[2,4,96,384]{3,2,1,0:T(8,128)(2,1)S(1)}, bf16[2,4,96,384]{3,2,1,0:T(8,128)(2,1)S(1)}, u32[]{:S(2)}, u32[]{:S(2)}) collective-permute-start(bf16[2,4,96,384]{3,2,1,0:T(8,128)(2,1)S(1)} %pad_maximum_fusion.1.rest_0_), channel_id=1, source_target_pairs={{0,4},{4,0},{8,12},{12,8},{1,5},{5,1},{9,13},{13,9},{2,6},{6,2},{1... | collective-permute-start | bytes 1769480 | tf_op jit(solution)/shard_map/ppermute | solution.py:467
  56.3 10.6 %collective-permute-start.16 = (bf16[2,4,96,384]{3,2,1,0:T(8,128)(2,1)S(1)}, bf16[2,4,96,384]{3,2,1,0:T(8,128)(2,1)}, u32[]{:S(2)}, u32[]{:S(2)}) collective-permute-start(bf16[2,4,96,384]{3,2,1,0:T(8,128)(2,1)S(1)} %pad_maximum_fusion.2.rest_4_), channel_id=1, source_target_pairs={{0,4},{4,0},{8,12},{12,8},{1,5},{5,1},{9,13},{13,9},{2,6},{6,2},{1... | collective-permute-start | bytes 1769480 | tf_op jit(solution)/shard_map/ppermute | solution.py:467
  64.0 20.4 %collective-permute-start.10 = (bf16[1,2,96,768]{3,2,1,0:T(8,128)(2,1)S(1)}, bf16[1,2,96,768]{3,2,1,0:T(8,128)(2,1)S(1)}, u32[]{:S(2)}, u32[]{:S(2)}) collective-permute-start(bf16[1,2,96,768]{3,2,1,0:T(8,128)(2,1)S(1)} %get-tuple-element.224), channel_id=1, source_target_pairs={{0,8},{4,12},{8,0},{12,4},{1,9},{5,13},{9,1},{13,5},{2,10},{6,14},... | collective-permute-start | bytes 884744 | tf_op jit(solution)/shard_map/ppermute | solution.py:467
  66.4 18.1 %collective-permute-start.11 = (bf16[1,2,96,768]{3,2,1,0:T(8,128)(2,1)S(1)}, bf16[1,2,96,768]{3,2,1,0:T(8,128)(2,1)S(1)}, u32[]{:S(2)}, u32[]{:S(2)}) collective-permute-start(bf16[1,2,96,768]{3,2,1,0:T(8,128)(2,1)S(1)} %get-tuple-element.223), channel_id=1, source_target_pairs={{0,16},{16,0},{1,17},{17,1},{2,18},{18,2},{3,19},{19,3},{4,20},{20... | collective-permute-start | bytes 884744 | tf_op jit(solution)/shard_map/ppermute | solution.py:467
  66.9 17.5 %collective-permute-start.12 = (bf16[1,2,96,768]{3,2,1,0:T(8,128)(2,1)S(1)}, bf16[1,2,96,768]{3,2,1,0:T(8,128)(2,1)S(1)}, u32[]{:S(2)}, u32[]{:S(2)}) collective-permute-start(bf16[1,2,96,768]{3,2,1,0:T(8,128)(2,1)S(1)} %get-tuple-element.222), channel_id=1, source_target_pairs={{0,8},{4,12},{8,0},{12,4},{1,9},{5,13},{9,1},{13,5},{2,10},{6,14},... | collective-permute-start | bytes 884744 | tf_op jit(solution)/shard_map/ppermute | solution.py:467
  67.9 16.6 %collective-permute-start.13 = (bf16[1,2,96,768]{3,2,1,0:T(8,128)(2,1)S(1)}, bf16[1,2,96,768]{3,2,1,0:T(8,128)(2,1)S(1)}, u32[]{:S(2)}, u32[]{:S(2)}) collective-permute-start(bf16[1,2,96,768]{3,2,1,0:T(8,128)(2,1)S(1)} %get-tuple-element.221), channel_id=1, source_target_pairs={{0,16},{16,0},{1,17},{17,1},{2,18},{18,2},{3,19},{19,3},{4,20},{20... | collective-permute-start | bytes 884744 | tf_op jit(solution)/shard_map/ppermute | solution.py:467
  86.5 17.9 %collective-permute-start.20 = (bf16[2,2,96,768]{3,2,1,0:T(8,128)(2,1)S(1)}, bf16[2,2,96,768]{3,2,1,0:T(8,128)(2,1)}, u32[]{:S(2)}, u32[]{:S(2)}) collective-permute-start(bf16[2,2,96,768]{3,2,1,0:T(8,128)(2,1)S(1)} %pad_maximum_fusion.5.rest_13_.rest_0_), channel_id=1, source_target_pairs={{0,16},{16,0},{1,17},{17,1},{2,18},{18,2},{3,19},{19,3},{4,20},{20... | collective-permute-start | bytes 1769480 | tf_op jit(solution)/shard_map/ppermute | solution.py:467
  87.0 17.3 %collective-permute-start.22 = (bf16[2,2,96,768]{3,2,1,0:T(8,128)(2,1)S(1)}, bf16[2,2,96,768]{3,2,1,0:T(8,128)(2,1)S(1)}, u32[]{:S(2)}, u32[]{:S(2)}) collective-permute-start(bf16[2,2,96,768]{3,2,1,0:T(8,128)(2,1)S(1)} %pad_maximum_fusion.5.rest_13_.rest_0_), channel_id=1, source_target_pairs={{0,4},{4,0},{8,12},{12,8},{1,5},{5,1},{9,13},{13,9},{2,6},{6,2},{1... | collective-permute-start | bytes 1769480 | tf_op jit(solution)/shard_map/ppermute | solution.py:467
  88.1 16.3 %collective-permute-start.21 = (bf16[2,2,96,768]{3,2,1,0:T(8,128)(2,1)S(1)}, bf16[2,2,96,768]{3,2,1,0:T(8,128)(2,1)}, u32[]{:S(2)}, u32[]{:S(2)}) collective-permute-start(bf16[2,2,96,768]{3,2,1,0:T(8,128)(2,1)S(1)} %pad_maximum_fusion.6.rest_4_), channel_id=1, source_target_pairs={{0,8},{4,12},{8,0},{12,4},{1,9},{5,13},{9,1},{13,5},{2,10},{6,14},... | collective-permute-start | bytes 1769480 | tf_op jit(solution)/shard_map/ppermute | solution.py:467
  89.2 15.1 %collective-permute-start.23 = (bf16[2,2,96,768]{3,2,1,0:T(8,128)(2,1)S(1)}, bf16[2,2,96,768]{3,2,1,0:T(8,128)(2,1)S(1)}, u32[]{:S(2)}, u32[]{:S(2)}) collective-permute-start(bf16[2,2,96,768]{3,2,1,0:T(8,128)(2,1)S(1)} %pad_maximum_fusion.6.rest_4_), channel_id=1, source_target_pairs={{0,4},{4,0},{8,12},{12,8},{1,5},{5,1},{9,13},{13,9},{2,6},{6,2},{1... | collective-permute-start | bytes 1769480 | tf_op jit(solution)/shard_map/ppermute | solution.py:467
  105.4 21.3 %collective-permute-start.30 = (bf16[8,4,96,384]{3,2,1,0:T(8,128)(2,1)}, bf16[8,4,96,384]{3,2,1,0:T(8,128)(2,1)S(1)}, u32[]{:S(2)}, u32[]{:S(2)}) collective-permute-start(bf16[8,4,96,384]{3,2,1,0:T(8,128)(2,1)} %get-tuple-element.132), channel_id=1, source_target_pairs={{0,4},{4,0},{8,12},{12,8},{1,5},{5,1},{9,13},{13,9},{2,6},{6,2},{1... | collective-permute-start | bytes 7077896 | tf_op jit(solution)/shard_map/ppermute | solution.py:467
  106.7 15.6 %collective-permute-start.18 = (bf16[2,2,96,768]{3,2,1,0:T(8,128)(2,1)S(1)}, bf16[2,2,96,768]{3,2,1,0:T(8,128)(2,1)}, u32[]{:S(2)}, u32[]{:S(2)}) collective-permute-start(bf16[2,2,96,768]{3,2,1,0:T(8,128)(2,1)S(1)} %pad_maximum_fusion.3.__0_), channel_id=1, source_target_pairs={{0,16},{16,0},{1,17},{17,1},{2,18},{18,2},{3,19},{19,3},{4,20},{20... | collective-permute-start | bytes 1769480 | tf_op jit(solution)/shard_map/ppermute | solution.py:467
  110.1 15.5 %collective-permute-start.19 = (bf16[2,2,96,768]{3,2,1,0:T(8,128)(2,1)}, bf16[2,2,96,768]{3,2,1,0:T(8,128)(2,1)}, u32[]{:S(2)}, u32[]{:S(2)}) collective-permute-start(bf16[2,2,96,768]{3,2,1,0:T(8,128)(2,1)} %pad_maximum_fusion.4.__1_), channel_id=1, source_target_pairs={{0,8},{4,12},{8,0},{12,4},{1,9},{5,13},{9,1},{13,5},{2,10},{6,14},... | collective-permute-start | bytes 1769480 | tf_op jit(solution)/shard_map/ppermute | solution.py:467
  111.0 14.6 %collective-permute-start.24 = (bf16[2,2,96,768]{3,2,1,0:T(8,128)(2,1)}, bf16[2,2,96,768]{3,2,1,0:T(8,128)(2,1)}, u32[]{:S(2)}, u32[]{:S(2)}) collective-permute-start(bf16[2,2,96,768]{3,2,1,0:T(8,128)(2,1)} %get-tuple-element.124.rest_1_), channel_id=1, source_target_pairs={{0,4},{4,0},{8,12},{12,8},{1,5},{5,1},{9,13},{13,9},{2,6},{6,2},{1... | collective-permute-start | bytes 1769480 | tf_op jit(solution)/shard_map/ppermute | solution.py:467
  111.0 14.6 %collective-permute-start.25 = (bf16[2,2,96,768]{3,2,1,0:T(8,128)(2,1)}, bf16[2,2,96,768]{3,2,1,0:T(8,128)(2,1)}, u32[]{:S(2)}, u32[]{:S(2)}) collective-permute-start(bf16[2,2,96,768]{3,2,1,0:T(8,128)(2,1)} %get-tuple-element.122.rest_12_.rest_5_), channel_id=1, source_target_pairs={{0,4},{4,0},{8,12},{12,8},{1,5},{5,1},{9,13},{13,9},{2,6},{6,2},{1... | collective-permute-start | bytes 1769480 | tf_op jit(solution)/shard_map/ppermute | solution.py:467
  125.7 18.6 %collective-permute-start.27 = (bf16[2,2,96,768]{3,2,1,0:T(8,128)(2,1)}, bf16[2,2,96,768]{3,2,1,0:T(8,128)(2,1)}, u32[]{:S(2)}, u32[]{:S(2)}) collective-permute-start(bf16[2,2,96,768]{3,2,1,0:T(8,128)(2,1)} %get-tuple-element.126.refs_5_.rest_1_), channel_id=1, source_target_pairs={{0,4},{4,0},{8,12},{12,8},{1,5},{5,1},{9,13},{13,9},{2,6},{6,2},{1... | collective-permute-start | bytes 1769480 | tf_op jit(solution)/shard_map/ppermute | solution.py:467
  126.2 18.1 %collective-permute-start.28 = (bf16[2,2,96,768]{3,2,1,0:T(8,128)(2,1)}, bf16[2,2,96,768]{3,2,1,0:T(8,128)(2,1)}, u32[]{:S(2)}, u32[]{:S(2)}) collective-permute-start(bf16[2,2,96,768]{3,2,1,0:T(8,128)(2,1)} %get-tuple-element.127.rest_4_), channel_id=1, source_target_pairs={{0,4},{4,0},{8,12},{12,8},{1,5},{5,1},{9,13},{13,9},{2,6},{6,2},{1... | collective-permute-start | bytes 1769480 | tf_op jit(solution)/shard_map/ppermute | solution.py:467
  126.3 18.1 %collective-permute-start.29 = (bf16[2,2,96,768]{3,2,1,0:T(8,128)(2,1)}, bf16[2,2,96,768]{3,2,1,0:T(8,128)(2,1)}, u32[]{:S(2)}, u32[]{:S(2)}) collective-permute-start(bf16[2,2,96,768]{3,2,1,0:T(8,128)(2,1)} %get-tuple-element.128.rest_5_), channel_id=1, source_target_pairs={{0,4},{4,0},{8,12},{12,8},{1,5},{5,1},{9,13},{13,9},{2,6},{6,2},{1... | collective-permute-start | bytes 1769480 | tf_op jit(solution)/shard_map/ppermute | solution.py:467
  131.9 15.5 %collective-permute-start.31 = (bf16[2,4,96,384]{3,2,1,0:T(8,128)(2,1)}, bf16[2,4,96,384]{3,2,1,0:T(8,128)(2,1)S(1)}, u32[]{:S(2)}, u32[]{:S(2)}) collective-permute-start(bf16[2,4,96,384]{3,2,1,0:T(8,128)(2,1)} %get-tuple-element.133.rest_9_), channel_id=1, source_target_pairs={{0,8},{4,12},{8,0},{12,4},{1,9},{5,13},{9,1},{13,5},{2,10},{6,14},... | collective-permute-start | bytes 1769480 | tf_op jit(solution)/shard_map/ppermute | solution.py:467
  132.8 15.2 %collective-permute-start.32 = (bf16[2,4,96,384]{3,2,1,0:T(8,128)(2,1)}, bf16[2,4,96,384]{3,2,1,0:T(8,128)(2,1)S(1)}, u32[]{:S(2)}, u32[]{:S(2)}) collective-permute-start(bf16[2,4,96,384]{3,2,1,0:T(8,128)(2,1)} %get-tuple-element.134), channel_id=1, source_target_pairs={{0,16},{16,0},{1,17},{17,1},{2,18},{18,2},{3,19},{19,3},{4,20},{20... | collective-permute-start | bytes 1769480 | tf_op jit(solution)/shard_map/ppermute | solution.py:467
  152.4 12.6 %collective-permute-start.35 = (bf16[8,4,96,384]{3,2,1,0:T(8,128)(2,1)}, bf16[8,4,96,384]{3,2,1,0:T(8,128)(2,1)S(1)}, u32[]{:S(2)}, u32[]{:S(2)}) collective-permute-start(bf16[8,4,96,384]{3,2,1,0:T(8,128)(2,1)} %get-tuple-element.144), channel_id=1, source_target_pairs={{0,4},{4,0},{8,12},{12,8},{1,5},{5,1},{9,13},{13,9},{2,6},{6,2},{1... | collective-permute-start | bytes 7077896 | tf_op jit(solution)/shard_map/ppermute | solution.py:467
  152.4 12.6 %collective-permute-start.33 = (bf16[1,4,96,384]{3,2,1,0:T(8,128)(2,1)}, bf16[1,4,96,384]{3,2,1,0:T(8,128)(2,1)S(1)}, u32[]{:S(2)}, u32[]{:S(2)}) collective-permute-start(bf16[1,4,96,384]{3,2,1,0:T(8,128)(2,1)} %get-tuple-element.137.rest_9_), channel_id=1, source_target_pairs={{0,16},{16,0},{1,17},{17,1},{2,18},{18,2},{3,19},{19,3},{4,20},{20... | collective-permute-start | bytes 884744 | tf_op jit(solution)/shard_map/ppermute | solution.py:467
  153.0 12.0 %collective-permute-start.34 = (bf16[1,4,96,384]{3,2,1,0:T(8,128)(2,1)}, bf16[1,4,96,384]{3,2,1,0:T(8,128)(2,1)S(1)}, u32[]{:S(2)}, u32[]{:S(2)}) collective-permute-start(bf16[1,4,96,384]{3,2,1,0:T(8,128)(2,1)} %get-tuple-element.142), channel_id=1, source_target_pairs={{0,8},{4,12},{8,0},{12,4},{1,9},{5,13},{9,1},{13,5},{2,10},{6,14},... | collective-permute-start | bytes 884744 | tf_op jit(solution)/shard_map/ppermute | solution.py:467
  171.0 18.5 %collective-permute-start.38 = (bf16[8,4,96,384]{3,2,1,0:T(8,128)(2,1)}, bf16[8,4,96,384]{3,2,1,0:T(8,128)(2,1)S(1)}, u32[]{:S(2)}, u32[]{:S(2)}) collective-permute-start(bf16[8,4,96,384]{3,2,1,0:T(8,128)(2,1)} %get-tuple-element.154), channel_id=1, source_target_pairs={{0,4},{4,0},{8,12},{12,8},{1,5},{5,1},{9,13},{13,9},{2,6},{6,2},{1... | collective-permute-start | bytes 7077896 | tf_op jit(solution)/shard_map/ppermute | solution.py:467
  172.2 17.2 %collective-permute-start.36 = (bf16[2,4,96,384]{3,2,1,0:T(8,128)(2,1)}, bf16[2,4,96,384]{3,2,1,0:T(8,128)(2,1)S(1)}, u32[]{:S(2)}, u32[]{:S(2)}) collective-permute-start(bf16[2,4,96,384]{3,2,1,0:T(8,128)(2,1)} %get-tuple-element.151), channel_id=1, source_target_pairs={{0,8},{4,12},{8,0},{12,4},{1,9},{5,13},{9,1},{13,5},{2,10},{6,14},... | collective-permute-start | bytes 1769480 | tf_op jit(solution)/shard_map/ppermute | solution.py:467
  173.2 16.3 %collective-permute-start.37 = (bf16[2,4,96,384]{3,2,1,0:T(8,128)(2,1)}, bf16[2,4,96,384]{3,2,1,0:T(8,128)(2,1)}, u32[]{:S(2)}, u32[]{:S(2)}) collective-permute-start(bf16[2,4,96,384]{3,2,1,0:T(8,128)(2,1)} %get-tuple-element.152), channel_id=1, source_target_pairs={{0,16},{16,0},{1,17},{17,1},{2,18},{18,2},{3,19},{19,3},{4,20},{20... | collective-permute-start | bytes 1769480 | tf_op jit(solution)/shard_map/ppermute | solution.py:467
  175.8 12.3 %collective-permute-start.39 = (bf16[96,768]{1,0:T(8,128)(2,1)S(1)}, bf16[96,768]{1,0:T(8,128)(2,1)S(1)}, u32[]{:S(2)}, u32[]{:S(2)}) collective-permute-start(bf16[96,768]{1,0:T(8,128)(2,1)S(1)} %get-tuple-element.220), channel_id=1, source_target_pairs={{0,2},{1,3},{2,0},{3,1},{4,6},{5,7},{6,4},{7,5},{8,10},{9,11},{10,... | collective-permute-start | bytes 442376 | tf_op jit(solution)/shard_map/ppermute | solution.py:472
  178.2 11.3 %collective-permute-start.40 = (bf16[96,768]{1,0:T(8,128)(2,1)S(1)}, bf16[96,768]{1,0:T(8,128)(2,1)S(1)}, u32[]{:S(2)}, u32[]{:S(2)}) collective-permute-start(bf16[96,768]{1,0:T(8,128)(2,1)S(1)} %get-tuple-element.219), channel_id=1, source_target_pairs={{0,1},{1,2},{2,3},{3,0},{4,5},{5,6},{6,7},{7,4},{8,9},{9,10},{10,1... | collective-permute-start | bytes 442376 | tf_op jit(solution)/shard_map/ppermute | solution.py:472
  188.1 22.0 %collective-permute-start.45 = (bf16[96,768]{1,0:T(8,128)(2,1)S(1)}, bf16[96,768]{1,0:T(8,128)(2,1)S(1)}, u32[]{:S(2)}, u32[]{:S(2)}) collective-permute-start(bf16[96,768]{1,0:T(8,128)(2,1)S(1)} %get-tuple-element.218), channel_id=1, source_target_pairs={{0,3},{1,0},{2,1},{3,2},{4,7},{5,4},{6,5},{7,6},{8,11},{9,8},{10,9... | collective-permute-start | bytes 442376 | tf_op jit(solution)/shard_map/ppermute | solution.py:472
  195.7 14.4 %collective-permute-start.41 = (bf16[1,4,96,384]{3,2,1,0:T(8,128)(2,1)}, bf16[1,4,96,384]{3,2,1,0:T(8,128)(2,1)S(1)}, u32[]{:S(2)}, u32[]{:S(2)}) collective-permute-start(bf16[1,4,96,384]{3,2,1,0:T(8,128)(2,1)} %get-tuple-element.155.rest_23_), channel_id=1, source_target_pairs={{0,16},{16,0},{1,17},{17,1},{2,18},{18,2},{3,19},{19,3},{4,20},{20... | collective-permute-start | bytes 884744 | tf_op jit(solution)/shard_map/ppermute | solution.py:467
  196.5 13.7 %collective-permute-start.42 = (bf16[1,4,96,384]{3,2,1,0:T(8,128)(2,1)}, bf16[1,4,96,384]{3,2,1,0:T(8,128)(2,1)S(1)}, u32[]{:S(2)}, u32[]{:S(2)}) collective-permute-start(bf16[1,4,96,384]{3,2,1,0:T(8,128)(2,1)} %get-tuple-element.158), channel_id=1, source_target_pairs={{0,8},{4,12},{8,0},{12,4},{1,9},{5,13},{9,1},{13,5},{2,10},{6,14},... | collective-permute-start | bytes 884744 | tf_op jit(solution)/shard_map/ppermute | solution.py:467
  197.6 19.8 %collective-permute-start.43 = (bf16[2,4,96,384]{3,2,1,0:T(8,128)(2,1)}, bf16[2,4,96,384]{3,2,1,0:T(8,128)(2,1)S(1)}, u32[]{:S(2)}, u32[]{:S(2)}) collective-permute-start(bf16[2,4,96,384]{3,2,1,0:T(8,128)(2,1)} %get-tuple-element.159), channel_id=1, source_target_pairs={{0,8},{4,12},{8,0},{12,4},{1,9},{5,13},{9,1},{13,5},{2,10},{6,14},... | collective-permute-start | bytes 1769480 | tf_op jit(solution)/shard_map/ppermute | solution.py:467
  198.5 18.8 %collective-permute-start.44 = (bf16[2,4,96,384]{3,2,1,0:T(8,128)(2,1)}, bf16[2,4,96,384]{3,2,1,0:T(8,128)(2,1)S(1)}, u32[]{:S(2)}, u32[]{:S(2)}) collective-permute-start(bf16[2,4,96,384]{3,2,1,0:T(8,128)(2,1)} %get-tuple-element.160), channel_id=1, source_target_pairs={{0,16},{16,0},{1,17},{17,1},{2,18},{18,2},{3,19},{19,3},{4,20},{20... | collective-permute-start | bytes 1769480 | tf_op jit(solution)/shard_map/ppermute | solution.py:467
  222.6 27.5 %collective-permute-start.51 = (bf16[1,4,96,384]{3,2,1,0:T(8,128)(2,1)}, bf16[1,4,96,384]{3,2,1,0:T(8,128)(2,1)S(1)}, u32[]{:S(2)}, u32[]{:S(2)}) collective-permute-start(bf16[1,4,96,384]{3,2,1,0:T(8,128)(2,1)} %get-tuple-element.163), channel_id=1, source_target_pairs={{0,16},{16,0},{1,17},{17,1},{2,18},{18,2},{3,19},{19,3},{4,20},{20... | collective-permute-start | bytes 884744 | tf_op jit(solution)/shard_map/ppermute | solution.py:467
  223.7 26.4 %collective-permute-start.52 = (bf16[1,4,96,384]{3,2,1,0:T(8,128)(2,1)}, bf16[1,4,96,384]{3,2,1,0:T(8,128)(2,1)S(1)}, u32[]{:S(2)}, u32[]{:S(2)}) collective-permute-start(bf16[1,4,96,384]{3,2,1,0:T(8,128)(2,1)} %get-tuple-element.164), channel_id=1, source_target_pairs={{0,8},{4,12},{8,0},{12,4},{1,9},{5,13},{9,1},{13,5},{2,10},{6,14},... | collective-permute-start | bytes 884744 | tf_op jit(solution)/shard_map/ppermute | solution.py:467
  226.0 36.5 %collective-permute-start.54 = (bf16[96,1536]{1,0:T(8,128)(2,1)S(1)}, bf16[96,1536]{1,0:T(8,128)(2,1)S(1)}, u32[]{:S(2)}, u32[]{:S(2)}) collective-permute-start(bf16[96,1536]{1,0:T(8,128)(2,1)S(1)} %pad_maximum_fusion.12), channel_id=1, source_target_pairs={{0,2},{1,3},{2,0},{3,1},{4,6},{5,7},{6,4},{7,5},{8,10},{9,11},{10,... | collective-permute-start | bytes 884744 | tf_op jit(solution)/shard_map/ppermute | solution.py:472
  238.9 23.7 %collective-permute-start.55 = (bf16[96,1536]{1,0:T(8,128)(2,1)S(1)}, bf16[96,1536]{1,0:T(8,128)(2,1)}, u32[]{:S(2)}, u32[]{:S(2)}) collective-permute-start(bf16[96,1536]{1,0:T(8,128)(2,1)S(1)} %pad_maximum_fusion.13), channel_id=1, source_target_pairs={{0,1},{1,2},{2,3},{3,0},{4,5},{5,6},{6,7},{7,4},{8,9},{9,10},{10,1... | collective-permute-start | bytes 884744 | tf_op jit(solution)/shard_map/ppermute | solution.py:472
  250.1 11.0 %collective-permute-start.50 = (f32[16,768]{1,0:T(8,128)}, f32[16,768]{1,0:T(8,128)}, u32[]{:S(2)}, u32[]{:S(2)}) collective-permute-start(f32[16,768]{1,0:T(8,128)} %add.98), channel_id=1, source_target_pairs={{0,2},{1,3},{2,0},{3,1},{4,6},{5,7},{6,4},{7,5},{8,10},{9,11},{10,... | collective-permute-start | bytes 147464 | tf_op jit(solution)/shard_map/ppermute | solution.py:467
  (65 other events, 342.5 us)

commit v4 on v2

--- a/solution.py
+++ b/solution.py
@@ -1,3 +1,4 @@
+import copy
 import functools
 import math
 
@@ -485,6 +486,12 @@
         self.moving = [swap(one, order[self.done]) for one, order in zip(self.held, self.orders)]
         self.done += 1
 
+    def part(self, blocks):
+        one = copy.copy(self)
+        one.held = [array[:, blocks] for array in self.held]
+        one.moving = [array[:, blocks] for array in self.moving]
+        return one
+
     def cross_held(self):
         self.over = [swap(one, self.core_bit) for one in self.held]
 
@@ -655,15 +662,14 @@
     mlp_blocks = gather_col(fence([mlp_own], [attn.held[0]])[0])
     for _ in range(far):
         attn.advance()
-        phase([attn], [], [na, mlp_blocks[1], mlp_blocks[-1]] if attn.done == 1 else mlp_blocks[2:-1])
+        phase([attn], [], [na, mlp_blocks[1]] if attn.done == 1 else mlp_blocks[2:])
     mlp_blocks = fence(mlp_blocks, attn.moving)
     attn.cross_held()
     attn.cross_moving()
     per_call = 2
     starts = list(range(0, col_size, per_call))[::-1]
-    mlp = [Gather(jnp.stack(mlp_blocks[k0 : k0 + per_call]), orders, core_bit) for k0 in starts]
-    for one in mlp:
-        one.advance()
+    mlp_all = Gather(jnp.stack(mlp_blocks), orders, core_bit)
+    mlp_all.advance()
 
     def attention_call(weights, w0, k0, count, slots, slot0, into, after):
         return block_part(
@@ -687,11 +693,12 @@
     attn_calls, into, token = [], [], []
     for n, k0 in enumerate(starts):
         if n == 1:
-            while mlp[0].done < far:
-                phase([one for one in mlp if one.done < far], [], token)
-                mlp[0].advance()
-                if mlp[1].done < far - 1:
-                    mlp[1].advance()
+            phase([mlp_all], [], token)
+            while mlp_all.done < far - 1:
+                mlp_all.advance()
+                phase([mlp_all])
+            mlp = [mlp_all.part(slice(at, at + per_call)) for at in starts]
+            mlp[0].advance()
             mlp[0].cross_held()
             token = mlp[0].held[:1]
         outs = attention_call(attn, k0, k0, per_call, (1, col_size), k0, into, token)
@@ -717,7 +724,7 @@
         totals.update(zip((id(r) for r in ending), finished))
         return token, passed
 
-    phase(mlp[1:], [], [branch] + mlp[0].over)
+    mlp[1].held = phase(mlp[1:], mlp[1].held, [branch] + mlp[0].over)[:2]
     token, _ = go_on([attn_sum], [branch, mlp[1].moving[0]])
     mlp[1].cross_held()
     mlp[1].cross_moving()
@@ -780,17 +787,19 @@
                     for i in range(per_call):
                         slots = [totals[id(r)][i * per_mlp + j] for j in range(per_mlp)]
                         part = jnp.concatenate([s[:, :cut] for s in slots] + [s[:, cut:] for s in slots], axis=1)
+                        if k1 == starts[-1] and k1 + i > 0:
+                            smalls = fence([smalls], [part])[0]
                         mlp_moves[k1 + i] = part if k1 + i == 0 else shifted(part, -(k1 + i))
             if len(mlp_moves) < col_size:
-                token, _ = go_on(mlp_sums, token)
+                token, passed = go_on(mlp_sums, token, [smalls])
+                smalls = passed[0]
     head_row, up_row = 5 + col_size, 5
-    smalls = sum_over(smalls, ("row", "dp"))
+    smalls = sum_over(smalls, ("row", "dp", "col"))
     smalls, *came = fence([smalls] + [mlp_moves[k] for k in range(1, col_size)])
     mlp_mine, mlp_other = settle([mlp_moves[0]] + came)
     g_heads = whole_block(attn_mine, attn_other).reshape(rows, local_heads, HEAD)
     g_mlp = whole_block(mlp_mine, mlp_other)
     g_up, g_down = g_mlp[:, :up_cols], g_mlp[:, up_cols:]
-    smalls = sum_over(smalls, ("col",))
     return (
         block_out,
         in_grad,

time: 275 us -> 267 us (0.971)
  waiting for transfers between devices: 65.9 us -> 43.7 us
  starting transfers between devices: 53.5 us -> 61.3 us
  local copies, waits for them, and re-layouts: 31.7 us -> 36.7 us
    ppermute x12, waiting for transfers between devices: 30.6 us -> 16.1 us  [shifted(): lax.ppermute(value, 'col', [(i, (i + by) % size) for i in range(size)])]
    ppermute x12, starting transfers between devices: 17.4 us -> 27.8 us  [shifted(): lax.ppermute(value, 'col', [(i, (i + by) % size) for i in range(size)])]
    ppermute x46 -> x44, waiting for transfers between devices: 35.3 us -> 27.6 us  [flipped(): lax.ppermute(value, axis, [(i, i ^ flip) for i in range(lax.axis_size(axi...]
    ppermute x46 -> x44, starting transfers between devices: 36.1 us -> 33.5 us  [flipped(): lax.ppermute(value, axis, [(i, i ^ flip) for i in range(lax.axis_size(axi...]
    unnamed x118 -> x112, local copies, waits for them, and re-layouts: 14.3 us -> 16 us
  transfers between devices with their start and end apart: 58 -> 56, of which waited for: 16 -> 15; matrix products, arithmetic and copies ran while one was open for 11% -> 12% of each run, Pallas kernels for 34% -> 36%
where the time goes in v4:
time: 267 us; the launch traced here: 265 us
  Pallas kernels  104 us (39%)
  starting transfers between devices  61.3 us (23%)
  waiting for transfers between devices  43.7 us (16%)
  local copies, waits for them, and re-layouts  36.7 us (14%)
  other arithmetic  17.2 us (6%)
    pallas_call x4, Pallas kernels, block_part(): pl.pallas_call(functools.partial(kernel, orders, core_bit, len(after)), g...  51.8 us
    ppermute x44, starting transfers between devices, flipped(): lax.ppermute(value, axis, [(i, i ^ flip) for i in range(lax.axis_size(axi...  33.5 us
    ppermute x12, starting transfers between devices, shifted(): lax.ppermute(value, 'col', [(i, (i + by) % size) for i in range(size)])  27.8 us
    ppermute x44, waiting for transfers between devices, flipped(): lax.ppermute(value, axis, [(i, i ^ flip) for i in range(lax.axis_size(axi...  27.6 us
    pallas_call x6, Pallas kernels, merge(): pl.pallas_call(functools.partial(merge_kernel, layout, len(arrays), len(a...  18.6 us
    pallas_call x2, Pallas kernels, mlp_tail_part(): pl.pallas_call(functools.partial(mlp_tail_kernel, orders, core_bit, len(s...  17.7 us
    ppermute x12, waiting for transfers between devices, shifted(): lax.ppermute(value, 'col', [(i, (i + by) % size) for i in range(size)])  16.1 us
    unnamed x112, local copies, waits for them, and re-layouts  16 us
  transfers between devices with their start and end apart: 56, of which 15 were waited for; matrix products, arithmetic and copies ran while one was open for 12% of the time, Pallas kernels for 36%

profile of v4, /device:TPU:0, one launch (start us, length us, event | category | flops | bytes accessed | tf_op | source)
XLA Modules:
  0.0 264.7 jit_solution(14217125375698960423)
XLA Ops:
  3.1 5.1 %collective-permute-start.2 = (bf16[96,768]{1,0:T(8,128)(2,1)S(1)}, bf16[96,768]{1,0:T(8,128)(2,1)S(1)}, u32[]{:S(2)}, u32[]{:S(2)}) collective-permute-start(bf16[96,768]{1,0:T(8,128)(2,1)S(1)} %copy.76), channel_id=1, source_target_pairs={{0,3},{1,0},{2,1},{3,2},{4,7},{5,4},{6,5},{7,6},{8,11},{9,8},{10,9... | collective-permute-start | bytes 442376 | tf_op jit(solution)/shard_map/ppermute | solution.py:473
  14.5 1.3 constant_dynamic-slice_fusion.segr_ref
  15.8 4.9 %collective-permute-done.1 = bf16[96,768]{1,0:T(8,128)(2,1)S(1)} collective-permute-done((bf16[96,768]{1,0:T(8,128)(2,1)S(1)}, bf16[96,768]{1,0:T(8,128)(2,1)S(1)}, u32[]{:S(2)}, u32[]{:S(2)}) %collective-permute-start.1) | collective-permute-done | bytes 147488 | tf_op jit(solution)/shard_map/ppermute | solution.py:473
  20.9 1.6 collective-permute-start.6
  23.3 1.5 collective-permute-start.7
  24.8 6.0 %shard_map.255 = (bf16[512,768]{1,0:T(8,128)(2,1)}, bf16[768,512]{1,0:T(8,128)(2,1)}, bf16[512,768]{1,0:T(8,128)(2,1)}, bf16[768,512]{1,0:T(8,128)(2,1)}, bf16[7...) custom-call(bf16[512,768]{1,0:T(8,128)(2,1)} %rest_13_.1, ...), custom_call_target="tpu_custom_call" | custom-call | flops 6899999744 | bytes 1048576 | tf_op jit(solution)/shard_map/pallas_call | solution.py:124
  30.9 1.5 collective-permute-done.3.__3_.__1_
  35.4 1.6 collective-permute-start.8
  41.1 2.2 collective-permute-start.5
  44.6 9.6 %collective-permute-done.4.__2_ = bf16[96,1536]{1,0:T(8,128)(2,1)S(1)} collective-permute-done((bf16[96,1536]{1,0:T(8,128)(2,1)S(1)}, bf16[96,1536]{1,0:T(8,128)(2,1)S(1)}, u32[]{:S(2)}, u32[]{:S(2)}) %collective-permute-start.4) | collective-permute-done | bytes 294944 | tf_op jit(solution)/shard_map/ppermute | solution.py:473
  55.8 1.4 pad_maximum_fusion
  57.2 1.2 collective-permute-start.10
  59.7 15.0 %shard_map.259 = (bf16[2,512,768]{2,1,0:T(8,128)(2,1)}, bf16[2,512,384]{2,1,0:T(8,128)(2,1)}, f32[2,1,768]{2,1,0:T(1,128)}, bf16[8,4,96,384]{3,2,1,0:T(8,128)(2,1)}, bf16[8,4,96,384]{3,2,1,0:T(8,128)(2,1)}) custom-call(s32[2]{0:T(128)} %pad_add_fusion.me_ref, bf16[512,768]{1,0:T(8,128)(2,1)} %get-tuple-element.94.__2_.na_ref, ...), custom_call_target="tpu_custom_call" | custom-call | flops 23000000512 | bytes 1048576 | tf_op jit(solution)/shard_map/pallas_call | solution.py:270
  75.5 2.1 fusion.10
  80.8 14.9 %shard_map.261 = (bf16[2,512,768]{2,1,0:T(8,128)(2,1)}, bf16[2,512,384]{2,1,0:T(8,128)(2,1)}, f32[2,1,768]{2,1,0:T(1,128)}, bf16[8,4,96,384]{3,2,1,0:T(8,128)(2,1)}, bf16[8,4,96,384]{3,2,1,0:T(8,128)(2,1)}) custom-call(s32[2]{0:T(128)} %pad_add_fusion.me_ref, ...), custom_call_target="tpu_custom_call", output_to_operand_aliasing={{3}: (19, {}), {4}: (20, {})} | custom-call | flops 23000000512 | bytes 1048576 | tf_op jit(solution)/shard_map/pallas_call | solution.py:270
  99.2 1.8 pad_maximum_fusion.5.__1_
  102.6 10.2 %shard_map.263 = (f32[512,768]{1,0:T(8,128)}, f32[512,768]{1,0:T(8,128)}) custom-call(s32[2]{0:T(128)} %pad_add_fusion.me_ref, bf16[2,4,96,384]{3,2,1,0:T(8,128)(2,1)} %copy-done.18, bf16[2,4,96,384]{3,2,1,0:T(8,128)(2,1)} %get-tuple-element.97.__4_.rest_1_, bf16[2,4,96,384]{3,2,1,0:T(8,128)(2,1)} %collective-permute-done.12.rest_2_, ...), custom_call_target="tpu_custom_call" | custom-call | flops 12650000384 | bytes 1048576 | tf_op jit(solution)/shard_map/pallas_call | solution.py:404
  113.7 2.8 %collective-permute-done.17.__3_ = bf16[2,2,96,768]{3,2,1,0:T(8,128)(2,1)} collective-permute-done((bf16[2,2,96,768]{3,2,1,0:T(8,128)(2,1)}, bf16[2,2,96,768]{3,2,1,0:T(8,128)(2,1)}, u32[]{:S(2)}, u32[]{:S(2)}) %collective-permute-start.17) | collective-permute-done | bytes 589856 | tf_op jit(solution)/shard_map/ppermute | solution.py:468
  117.6 1.4 copy-done.3
  119.0 2.8 %shard_map.265 = (bf16[2,4,96,384]{3,2,1,0:T(8,128)(2,1)}, bf16[2,4,96,384]{3,2,1,0:T(8,128)(2,1)}) custom-call(bf16[8,4,96,384]{3,2,1,0:T(8,128)(2,1)} %get-tuple-element.129.refs_0_.refs_2_.refs_3_.refs_4_, bf16[8,4,96,384]{3,2,1,0:T(8,128)(2,1)} %copy-done.3, bf16[8,4,96,384]{3,2,1,0:T(8,128)(2,1)} %get-tuple-element.129.refs_0_.refs_2_.refs_3_.refs_4_, ...), custom_call_target="tpu_custom_call" | custom-call | flops 3449999872 | bytes 1048576 | tf_op jit(solution)/shard_map/pallas_call | solution.py:558
  123.9 11.0 %shard_map.266 = (bf16[2,512,768]{2,1,0:T(8,128)(2,1)}, bf16[2,512,768]{2,1,0:T(8,128)(2,1)}, f32[2,1,768]{2,1,0:T(1,128)}, bf16[8,4,96,384]{3,2,1,0:T(8,128)(2,1)}, bf16[8,4,96,384]{3,2,1,0:T(8,128)(2,1)}) custom-call(s32[2]{0:T(128)} %pad_add_fusion.me_ref, bf16[512,768]{1,0:T(8,128)(2,1)} %get-tuple-element.127.nm_ref, ...), custom_call_target="tpu_custom_call" | custom-call | flops 13799999488 | bytes 1048576 | tf_op jit(solution)/shard_map/pallas_call | solution.py:270
  135.0 2.4 collective-permute-done.29.refs_2_
  139.0 2.3 shard_map.267
  143.3 11.0 %shard_map.268 = (bf16[2,512,768]{2,1,0:T(8,128)(2,1)}, bf16[2,512,768]{2,1,0:T(8,128)(2,1)}, f32[2,1,768]{2,1,0:T(1,128)}, bf16[8,4,96,384]{3,2,1,0:T(8,128)(2,1)}, bf16[8,4,96,384]{3,2,1,0:T(8,128)(2,1)}) custom-call(s32[2]{0:T(128)} %pad_add_fusion.me_ref, bf16[512,768]{1,0:T(8,128)(2,1)} %get-tuple-element.127.nm_ref, ...), custom_call_target="tpu_custom_call" | custom-call | flops 13799999488 | bytes 1048576 | tf_op jit(solution)/shard_map/pallas_call | solution.py:270
  155.9 3.8 %shard_map.269 = (bf16[1,4,96,768]{3,2,1,0:T(8,128)(2,1)}, bf16[2,4,96,384]{3,2,1,0:T(8,128)(2,1)}, bf16[2,4,96,384]{3,2,1,0:T(8,128)(2,1)}, bf16[8,4,96,384]{3,2,1,0:T(8,128)(2,1)}) custom-call(bf16[8,4,96,384]{3,2,1,0:T(8,128)(2,1)} %get-tuple-element.129.refs_0_.refs_2_.refs_3_.refs_4_, ...), custom_call_target="tpu_custom_call", output_to_operand_aliasing={{3}: (12, {})} | custom-call | flops 3449999872 | bytes 1048576 | tf_op jit(solution)/shard_map/pallas_call | solution.py:558
  163.0 1.7 slice_bitcast_fusion.13
  164.7 5.1 %collective-permute-start.37 = (bf16[96,768]{1,0:T(8,128)(2,1)S(1)}, bf16[96,768]{1,0:T(8,128)(2,1)S(1)}, u32[]{:S(2)}, u32[]{:S(2)}) collective-permute-start(bf16[96,768]{1,0:T(8,128)(2,1)S(1)} %get-tuple-element.222), channel_id=1, source_target_pairs={{0,2},{1,3},{2,0},{3,1},{4,6},{5,7},{6,4},{7,5},{8,10},{9,11},{10,... | collective-permute-start | bytes 442376 | tf_op jit(solution)/shard_map/ppermute | solution.py:473
  169.8 2.8 %collective-permute-start.38 = (bf16[96,768]{1,0:T(8,128)(2,1)S(1)}, bf16[96,768]{1,0:T(8,128)(2,1)S(1)}, u32[]{:S(2)}, u32[]{:S(2)}) collective-permute-start(bf16[96,768]{1,0:T(8,128)(2,1)S(1)} %get-tuple-element.221), channel_id=1, source_target_pairs={{0,1},{1,2},{2,3},{3,0},{4,5},{5,6},{6,7},{7,4},{8,9},{9,10},{10,1... | collective-permute-start | bytes 442376 | tf_op jit(solution)/shard_map/ppermute | solution.py:473
  172.6 7.4 %shard_map.270 = (f32[512,768]{1,0:T(8,128)}, f32[512,768]{1,0:T(8,128)}) custom-call(s32[2]{0:T(128)} %pad_add_fusion.me_ref, bf16[2,2,96,768]{3,2,1,0:T(8,128)(2,1)} %copy-done.17, bf16[2,2,96,768]{3,2,1,0:T(8,128)(2,1)} %get-tuple-element.122.rest_1_, bf16[2,2,96,768]{3,2,1,0:T(8,128)(2,1)} %copy-done.5, ...), custom_call_target="tpu_custom_call" | custom-call | flops 10350000128 | bytes 1048576 | tf_op jit(solution)/shard_map/pallas_call | solution.py:433
  180.0 1.4 collective-permute-start.43
  183.0 3.5 %shard_map.271 = (bf16[1,4,96,384]{3,2,1,0:T(8,128)(2,1)}, bf16[1,4,96,384]{3,2,1,0:T(8,128)(2,1)}, bf16[2,4,96,384]{3,2,1,0:T(8,128)(2,1)}, bf16[2,4,96,384]{3,...) custom-call(bf16[8,4,96,384]{3,2,1,0:T(8,128)(2,1)} %get-tuple-eleme, ...), custom_call_target="tpu_custom_call", output_to_operand_aliasing={{4}: (10, {}), {5}: (11, {})} | custom-call | flops 3449999872 | bytes 1048576 | tf_op jit(solution)/shard_map/pallas_call | solution.py:558
  187.6 1.2 collective-permute-start.40
  190.6 10.3 %shard_map.272 = (bf16[512,768]{1,0:T(8,128)(2,1)}, bf16[512,768]{1,0:T(8,128)(2,1)}, f32[16,768]{1,0:T(8,128)}) custom-call(s32[2]{0:T(128)} %pad_add_fusion.me_ref, bf16[2,2,96,768]{3,2,1,0:T(8,128)(2,1)} %get-tuple-element.123.rest_0_, bf16[2,2,96,768]{3,2,1,0:T(8,128)(2,1)} %get-tuple-element.124.refs_5_.rest_1_, bf16[2,2,96,768]{3,2,1,0:T(8,128)(2,1)} %copy-done.14, ...), custom_call_target="tpu_custom_call" | custom-call | flops 10350000128 | bytes 1048576 | tf_op jit(solution)/shard_map/pallas_call | solution.py:433
  200.9 6.5 %collective-permute-done.41.refs_7_ = bf16[1,4,96,384]{3,2,1,0:T(8,128)(2,1)S(1)} collective-permute-done((bf16[1,4,96,384]{3,2,1,0:T(8,128)(2,1)}, bf16[1,4,96,384]{3,2,1,0:T(8,128)(2,1)S(1)}, u32[]{:S(2)}, u32[]{:S(2)}) %collective-permute-start.41) | collective-permute-done | bytes 294944 | tf_op jit(solution)/shard_map/ppermute | solution.py:468
  209.0 3.4 %shard_map.273 = (bf16[1,4,96,768]{3,2,1,0:T(8,128)(2,1)}, bf16[1,4,96,384]{3,2,1,0:T(8,128)(2,1)}, bf16[1,4,96,384]{3,2,1,0:T(8,128)(2,1)}, f32[16,768]{1,0:T(8,128)}, bf16[96,768]{1,0:T(8,128)(2,1)}) custom-call(bf16[8,4,96,384]{3,2,1,0:T(8,128)(2,1)} %get-tuple-element.141.refs_8_.refs_10_.refs_0_.refs_3_.refs_4_, ...), custom_call_target="tpu_custom_call", output_to_operand_aliasing={{3}: (14, {}), {4}: (15, {})} | custom-call | flops 3449999872 | bytes 1048576 | tf_op jit(solution)/shard_map/pallas_call | solution.py:558
  212.5 1.3 collective-permute-start.44
  216.0 2.4 collective-permute-start.52
  221.4 2.8 %shard_map.274 = (bf16[1,4,96,768]{3,2,1,0:T(8,128)(2,1)}, f32[16,768]{1,0:T(8,128)}) custom-call(bf16[8,4,96,384]{3,2,1,0:T(8,128)(2,1)} %get-tuple-element.151.refs_6_.refs_8_.refs_11_.refs_0_.refs_4_, bf16[8,4,96,384]{3,2,1,0:T(8,128)(2,1)} %copy-done.4, bf16[2,4,96,384]{3,2,1,0:T(8,128)(2,1)} %copy-done.15, ...), custom_call_target="tpu_custom_call", output_to_operand_aliasing={{1}: (8, {})} | custom-call | flops 3449999872 | bytes 1048576 | tf_op jit(solution)/shard_map/pallas_call | solution.py:558
  226.2 3.5 %collective-permute-start.53 = (bf16[96,1536]{1,0:T(8,128)(2,1)S(1)}, bf16[96,1536]{1,0:T(8,128)(2,1)S(1)}, u32[]{:S(2)}, u32[]{:S(2)}) collective-permute-start(bf16[96,1536]{1,0:T(8,128)(2,1)S(1)} %pad_maximum_fusion.12), channel_id=1, source_target_pairs={{0,1},{1,2},{2,3},{3,0},{4,5},{5,6},{6,7},{7,4},{8,9},{9,10},{10,1... | collective-permute-start | bytes 884744 | tf_op jit(solution)/shard_map/ppermute | solution.py:473
  231.6 3.0 %collective-permute-done.47 = f32[16,768]{1,0:T(8,128)S(1)} collective-permute-done((f32[16,768]{1,0:T(8,128)S(1)}, f32[16,768]{1,0:T(8,128)S(1)}, u32[]{:S(2)}, u32[]{:S(2)}) %collective-permute-start.47) | collective-permute-done | bytes 49184 | tf_op jit(solution)/shard_map/ppermute | solution.py:468
  238.5 2.6 collective-permute-start.51
  241.9 5.6 %collective-permute-done.49 = f32[16,768]{1,0:T(8,128)S(1)} collective-permute-done((f32[16,768]{1,0:T(8,128)S(1)}, f32[16,768]{1,0:T(8,128)S(1)}, u32[]{:S(2)}, u32[]{:S(2)}) %collective-permute-start.49) | collective-permute-done | bytes 49184 | tf_op jit(solution)/shard_map/ppermute | solution.py:468
  247.6 2.3 collective-permute-start.50
  249.9 2.7 %collective-permute-done.50 = f32[16,768]{1,0:T(8,128)S(1)} collective-permute-done((f32[16,768]{1,0:T(8,128)S(1)}, f32[16,768]{1,0:T(8,128)S(1)}, u32[]{:S(2)}, u32[]{:S(2)}) %collective-permute-start.50) | collective-permute-done | bytes 49184 | tf_op jit(solution)/shard_map/ppermute | solution.py:468
  254.7 1.3 add_convert_fusion
  256.0 1.4 collective-permute-start.55
  259.6 1.6 slice_reduce_fusion
  261.2 1.6 collective-permute-done.55
  (271 shorter events, 68.3 us)
Async XLA Ops:
  3.1 12.7 %collective-permute-start.2 = (bf16[96,768]{1,0:T(8,128)(2,1)S(1)}, bf16[96,768]{1,0:T(8,128)(2,1)S(1)}, u32[]{:S(2)}, u32[]{:S(2)}) collective-permute-start(bf16[96,768]{1,0:T(8,128)(2,1)S(1)} %copy.76), channel_id=1, source_target_pairs={{0,3},{1,0},{2,1},{3,2},{4,7},{5,4},{6,5},{7,6},{8,11},{9,8},{10,9... | collective-permute-start | bytes 442376 | tf_op jit(solution)/shard_map/ppermute | solution.py:473
  8.2 12.5 %collective-permute-start.1 = (bf16[96,768]{1,0:T(8,128)(2,1)S(1)}, bf16[96,768]{1,0:T(8,128)(2,1)S(1)}, u32[]{:S(2)}, u32[]{:S(2)}) collective-permute-start(bf16[96,768]{1,0:T(8,128)(2,1)S(1)} %copy.76), channel_id=1, source_target_pairs={{0,2},{1,3},{2,0},{3,1},{4,6},{5,7},{6,4},{7,5},{8,10},{9,11},{10,... | collective-permute-start | bytes 442376 | tf_op jit(solution)/shard_map/ppermute | solution.py:473
  8.2 12.5 %collective-permute-start = (bf16[96,768]{1,0:T(8,128)(2,1)S(1)}, bf16[96,768]{1,0:T(8,128)(2,1)S(1)}, u32[]{:S(2)}, u32[]{:S(2)}) collective-permute-start(bf16[96,768]{1,0:T(8,128)(2,1)S(1)} %copy.76), channel_id=1, source_target_pairs={{0,1},{1,2},{2,3},{3,0},{4,5},{5,6},{6,7},{7,4},{8,9},{9,10},{10,1... | collective-permute-start | bytes 442376 | tf_op jit(solution)/shard_map/ppermute | solution.py:473
  20.9 11.6 %collective-permute-start.6 = (bf16[1,4,96,384]{3,2,1,0:T(8,128)(2,1)S(1)}, bf16[1,4,96,384]{3,2,1,0:T(8,128)(2,1)S(1)}, u32[]{:S(2)}, u32[]{:S(2)}) collective-permute-start(bf16[1,4,96,384]{3,2,1,0:T(8,128)(2,1)S(1)} %get-tuple-element.232.__1_), channel_id=1, source_target_pairs={{0,8},{4,12},{8,0},{12,4},{1,9},{5,13},{9,1},{13,5},{2,10},{6,14},... | collective-permute-start | bytes 884744 | tf_op jit(solution)/shard_map/ppermute | solution.py:468
  22.4 10.0 %collective-permute-start.3 = (bf16[96,1536]{1,0:T(8,128)(2,1)}, bf16[96,1536]{1,0:T(8,128)(2,1)S(1)}, u32[]{:S(2)}, u32[]{:S(2)}) collective-permute-start(bf16[96,1536]{1,0:T(8,128)(2,1)} %shard_map.254.__0_), channel_id=1, source_target_pairs={{0,1},{1,2},{2,3},{3,0},{4,5},{5,6},{6,7},{7,4},{8,9},{9,10},{10,1... | collective-permute-start | bytes 884744 | tf_op jit(solution)/shard_map/ppermute | solution.py:473
  23.3 9.2 %collective-permute-start.7 = (bf16[1,4,96,384]{3,2,1,0:T(8,128)(2,1)S(1)}, bf16[1,4,96,384]{3,2,1,0:T(8,128)(2,1)S(1)}, u32[]{:S(2)}, u32[]{:S(2)}) collective-permute-start(bf16[1,4,96,384]{3,2,1,0:T(8,128)(2,1)S(1)} %get-tuple-element.231), channel_id=1, source_target_pairs={{0,16},{16,0},{1,17},{17,1},{2,18},{18,2},{3,19},{19,3},{4,20},{20... | collective-permute-start | bytes 884744 | tf_op jit(solution)/shard_map/ppermute | solution.py:468
  35.4 18.9 %collective-permute-start.8 = (bf16[2,4,96,384]{3,2,1,0:T(8,128)(2,1)S(1)}, bf16[2,4,96,384]{3,2,1,0:T(8,128)(2,1)S(1)}, u32[]{:S(2)}, u32[]{:S(2)}) collective-permute-start(bf16[2,4,96,384]{3,2,1,0:T(8,128)(2,1)S(1)} %pad_maximum_fusion.2.rest_0_), channel_id=1, source_target_pairs={{0,16},{16,0},{1,17},{17,1},{2,18},{18,2},{3,19},{19,3},{4,20},{20... | collective-permute-start | bytes 1769480 | tf_op jit(solution)/shard_map/ppermute | solution.py:468
  38.0 16.3 %collective-permute-start.9 = (bf16[2,4,96,384]{3,2,1,0:T(8,128)(2,1)S(1)}, bf16[2,4,96,384]{3,2,1,0:T(8,128)(2,1)}, u32[]{:S(2)}, u32[]{:S(2)}) collective-permute-start(bf16[2,4,96,384]{3,2,1,0:T(8,128)(2,1)S(1)} %pad_maximum_fusion.3.rest_4_), channel_id=1, source_target_pairs={{0,8},{4,12},{8,0},{12,4},{1,9},{5,13},{9,1},{13,5},{2,10},{6,14},... | collective-permute-start | bytes 1769480 | tf_op jit(solution)/shard_map/ppermute | solution.py:468
  40.2 14.0 %collective-permute-start.4 = (bf16[96,1536]{1,0:T(8,128)(2,1)S(1)}, bf16[96,1536]{1,0:T(8,128)(2,1)S(1)}, u32[]{:S(2)}, u32[]{:S(2)}) collective-permute-start(bf16[96,1536]{1,0:T(8,128)(2,1)S(1)} %copy-done.11), channel_id=1, source_target_pairs={{0,2},{1,3},{2,0},{3,1},{4,6},{5,7},{6,4},{7,5},{8,10},{9,11},{10,... | collective-permute-start | bytes 884744 | tf_op jit(solution)/shard_map/ppermute | solution.py:473
  41.1 13.1 %collective-permute-start.5 = (bf16[96,1536]{1,0:T(8,128)(2,1)S(1)}, bf16[96,1536]{1,0:T(8,128)(2,1)S(1)}, u32[]{:S(2)}, u32[]{:S(2)}) collective-permute-start(bf16[96,1536]{1,0:T(8,128)(2,1)S(1)} %copy-done.11), channel_id=1, source_target_pairs={{0,3},{1,0},{2,1},{3,2},{4,7},{5,4},{6,5},{7,6},{8,11},{9,8},{10,9... | collective-permute-start | bytes 884744 | tf_op jit(solution)/shard_map/ppermute | solution.py:473
  44.6 13.9 %collective-permute-start.12 = (bf16[2,4,96,384]{3,2,1,0:T(8,128)(2,1)S(1)}, bf16[2,4,96,384]{3,2,1,0:T(8,128)(2,1)}, u32[]{:S(2)}, u32[]{:S(2)}) collective-permute-start(bf16[2,4,96,384]{3,2,1,0:T(8,128)(2,1)S(1)} %pad_maximum_fusion.2.rest_0_), channel_id=1, source_target_pairs={{0,4},{4,0},{8,12},{12,8},{1,5},{5,1},{9,13},{13,9},{2,6},{6,2},{1... | collective-permute-start | bytes 1769480 | tf_op jit(solution)/shard_map/ppermute | solution.py:468
  57.2 17.5 %collective-permute-start.10 = (bf16[1,4,96,768]{3,2,1,0:T(8,128)(2,1)S(1)}, bf16[1,4,96,768]{3,2,1,0:T(8,128)(2,1)}, u32[]{:S(2)}, u32[]{:S(2)}) collective-permute-start(bf16[1,4,96,768]{3,2,1,0:T(8,128)(2,1)S(1)} %get-tuple-element.209), channel_id=1, source_target_pairs={{0,8},{4,12},{8,0},{12,4},{1,9},{5,13},{9,1},{13,5},{2,10},{6,14},... | collective-permute-start | bytes 1769480 | tf_op jit(solution)/shard_map/ppermute | solution.py:468
  58.6 16.1 %collective-permute-start.11 = (bf16[1,4,96,768]{3,2,1,0:T(8,128)(2,1)S(1)}, bf16[1,4,96,768]{3,2,1,0:T(8,128)(2,1)S(1)}, u32[]{:S(2)}, u32[]{:S(2)}) collective-permute-start(bf16[1,4,96,768]{3,2,1,0:T(8,128)(2,1)S(1)} %get-tuple-element.208), channel_id=1, source_target_pairs={{0,16},{16,0},{1,17},{17,1},{2,18},{18,2},{3,19},{19,3},{4,20},{20... | collective-permute-start | bytes 1769480 | tf_op jit(solution)/shard_map/ppermute | solution.py:468
  77.7 17.9 %collective-permute-start.18 = (bf16[2,2,96,768]{3,2,1,0:T(8,128)(2,1)S(1)}, bf16[2,2,96,768]{3,2,1,0:T(8,128)(2,1)}, u32[]{:S(2)}, u32[]{:S(2)}) collective-permute-start(bf16[2,2,96,768]{3,2,1,0:T(8,128)(2,1)S(1)} %pad_maximum_fusion.6.rest_13_.rest_0_), channel_id=1, source_target_pairs={{0,16},{16,0},{1,17},{17,1},{2,18},{18,2},{3,19},{19,3},{4,20},{20... | collective-permute-start | bytes 1769480 | tf_op jit(solution)/shard_map/ppermute | solution.py:468
  78.8 17.0 %collective-permute-start.20 = (bf16[2,2,96,768]{3,2,1,0:T(8,128)(2,1)S(1)}, bf16[2,2,96,768]{3,2,1,0:T(8,128)(2,1)S(1)}, u32[]{:S(2)}, u32[]{:S(2)}) collective-permute-start(bf16[2,2,96,768]{3,2,1,0:T(8,128)(2,1)S(1)} %pad_maximum_fusion.6.rest_13_.rest_0_), channel_id=1, source_target_pairs={{0,4},{4,0},{8,12},{12,8},{1,5},{5,1},{9,13},{13,9},{2,6},{6,2},{1... | collective-permute-start | bytes 1769480 | tf_op jit(solution)/shard_map/ppermute | solution.py:468
  79.7 16.1 %collective-permute-start.19 = (bf16[2,2,96,768]{3,2,1,0:T(8,128)(2,1)}, bf16[2,2,96,768]{3,2,1,0:T(8,128)(2,1)}, u32[]{:S(2)}, u32[]{:S(2)}) collective-permute-start(bf16[2,2,96,768]{3,2,1,0:T(8,128)(2,1)} %pad_maximum_fusion.7.rest_4_), channel_id=1, source_target_pairs={{0,8},{4,12},{8,0},{12,4},{1,9},{5,13},{9,1},{13,5},{2,10},{6,14},... | collective-permute-start | bytes 1769480 | tf_op jit(solution)/shard_map/ppermute | solution.py:468
  80.6 15.2 %collective-permute-start.21 = (bf16[2,2,96,768]{3,2,1,0:T(8,128)(2,1)}, bf16[2,2,96,768]{3,2,1,0:T(8,128)(2,1)S(1)}, u32[]{:S(2)}, u32[]{:S(2)}) collective-permute-start(bf16[2,2,96,768]{3,2,1,0:T(8,128)(2,1)} %pad_maximum_fusion.7.rest_4_), channel_id=1, source_target_pairs={{0,4},{4,0},{8,12},{12,8},{1,5},{5,1},{9,13},{13,9},{2,6},{6,2},{1... | collective-permute-start | bytes 1769480 | tf_op jit(solution)/shard_map/ppermute | solution.py:468
  96.8 20.8 %collective-permute-start.28 = (bf16[8,4,96,384]{3,2,1,0:T(8,128)(2,1)}, bf16[8,4,96,384]{3,2,1,0:T(8,128)(2,1)S(1)}, u32[]{:S(2)}, u32[]{:S(2)}) collective-permute-start(bf16[8,4,96,384]{3,2,1,0:T(8,128)(2,1)} %get-tuple-element.130), channel_id=1, source_target_pairs={{0,4},{4,0},{8,12},{12,8},{1,5},{5,1},{9,13},{13,9},{2,6},{6,2},{1... | collective-permute-start | bytes 7077896 | tf_op jit(solution)/shard_map/ppermute | solution.py:468
  98.0 15.7 %collective-permute-start.16 = (bf16[2,2,96,768]{3,2,1,0:T(8,128)(2,1)S(1)}, bf16[2,2,96,768]{3,2,1,0:T(8,128)(2,1)}, u32[]{:S(2)}, u32[]{:S(2)}) collective-permute-start(bf16[2,2,96,768]{3,2,1,0:T(8,128)(2,1)S(1)} %pad_maximum_fusion.4.__0_), channel_id=1, source_target_pairs={{0,16},{16,0},{1,17},{17,1},{2,18},{18,2},{3,19},{19,3},{4,20},{20... | collective-permute-start | bytes 1769480 | tf_op jit(solution)/shard_map/ppermute | solution.py:468
  101.0 15.5 %collective-permute-start.17 = (bf16[2,2,96,768]{3,2,1,0:T(8,128)(2,1)}, bf16[2,2,96,768]{3,2,1,0:T(8,128)(2,1)}, u32[]{:S(2)}, u32[]{:S(2)}) collective-permute-start(bf16[2,2,96,768]{3,2,1,0:T(8,128)(2,1)} %pad_maximum_fusion.5.__1_), channel_id=1, source_target_pairs={{0,8},{4,12},{8,0},{12,4},{1,9},{5,13},{9,1},{13,5},{2,10},{6,14},... | collective-permute-start | bytes 1769480 | tf_op jit(solution)/shard_map/ppermute | solution.py:468
  102.1 14.4 %collective-permute-start.22 = (bf16[2,2,96,768]{3,2,1,0:T(8,128)(2,1)}, bf16[2,2,96,768]{3,2,1,0:T(8,128)(2,1)}, u32[]{:S(2)}, u32[]{:S(2)}) collective-permute-start(bf16[2,2,96,768]{3,2,1,0:T(8,128)(2,1)} %get-tuple-element.122.rest_1_), channel_id=1, source_target_pairs={{0,4},{4,0},{8,12},{12,8},{1,5},{5,1},{9,13},{13,9},{2,6},{6,2},{1... | collective-permute-start | bytes 1769480 | tf_op jit(solution)/shard_map/ppermute | solution.py:468
  102.1 14.4 %collective-permute-start.23 = (bf16[2,2,96,768]{3,2,1,0:T(8,128)(2,1)}, bf16[2,2,96,768]{3,2,1,0:T(8,128)(2,1)}, u32[]{:S(2)}, u32[]{:S(2)}) collective-permute-start(bf16[2,2,96,768]{3,2,1,0:T(8,128)(2,1)} %get-tuple-element.120.rest_12_.rest_5_), channel_id=1, source_target_pairs={{0,4},{4,0},{8,12},{12,8},{1,5},{5,1},{9,13},{13,9},{2,6},{6,2},{1... | collective-permute-start | bytes 1769480 | tf_op jit(solution)/shard_map/ppermute | solution.py:468
  116.5 6.4 %collective-permute-start.24 = (bf16[2,2,96,768]{3,2,1,0:T(8,128)(2,1)}, bf16[2,2,96,768]{3,2,1,0:T(8,128)(2,1)S(1)}, u32[]{:S(2)}, u32[]{:S(2)}) collective-permute-start(bf16[2,2,96,768]{3,2,1,0:T(8,128)(2,1)} %get-tuple-element.123.rest_0_), channel_id=1, source_target_pairs={{0,4},{4,0},{8,12},{12,8},{1,5},{5,1},{9,13},{13,9},{2,6},{6,2},{1... | collective-permute-start | bytes 1769480 | tf_op jit(solution)/shard_map/ppermute | solution.py:468
  116.6 18.3 %collective-permute-start.25 = (bf16[2,2,96,768]{3,2,1,0:T(8,128)(2,1)}, bf16[2,2,96,768]{3,2,1,0:T(8,128)(2,1)}, u32[]{:S(2)}, u32[]{:S(2)}) collective-permute-start(bf16[2,2,96,768]{3,2,1,0:T(8,128)(2,1)} %get-tuple-element.124.refs_5_.rest_1_), channel_id=1, source_target_pairs={{0,4},{4,0},{8,12},{12,8},{1,5},{5,1},{9,13},{13,9},{2,6},{6,2},{1... | collective-permute-start | bytes 1769480 | tf_op jit(solution)/shard_map/ppermute | solution.py:468
  117.1 17.8 %collective-permute-start.26 = (bf16[2,2,96,768]{3,2,1,0:T(8,128)(2,1)}, bf16[2,2,96,768]{3,2,1,0:T(8,128)(2,1)}, u32[]{:S(2)}, u32[]{:S(2)}) collective-permute-start(bf16[2,2,96,768]{3,2,1,0:T(8,128)(2,1)} %get-tuple-element.125.rest_4_), channel_id=1, source_target_pairs={{0,4},{4,0},{8,12},{12,8},{1,5},{5,1},{9,13},{13,9},{2,6},{6,2},{1... | collective-permute-start | bytes 1769480 | tf_op jit(solution)/shard_map/ppermute | solution.py:468
  117.2 17.8 %collective-permute-start.27 = (bf16[2,2,96,768]{3,2,1,0:T(8,128)(2,1)}, bf16[2,2,96,768]{3,2,1,0:T(8,128)(2,1)}, u32[]{:S(2)}, u32[]{:S(2)}) collective-permute-start(bf16[2,2,96,768]{3,2,1,0:T(8,128)(2,1)} %get-tuple-element.126.rest_5_), channel_id=1, source_target_pairs={{0,4},{4,0},{8,12},{12,8},{1,5},{5,1},{9,13},{13,9},{2,6},{6,2},{1... | collective-permute-start | bytes 1769480 | tf_op jit(solution)/shard_map/ppermute | solution.py:468
  121.8 15.5 %collective-permute-start.29 = (bf16[2,4,96,384]{3,2,1,0:T(8,128)(2,1)}, bf16[2,4,96,384]{3,2,1,0:T(8,128)(2,1)S(1)}, u32[]{:S(2)}, u32[]{:S(2)}) collective-permute-start(bf16[2,4,96,384]{3,2,1,0:T(8,128)(2,1)} %get-tuple-element.131.rest_9_), channel_id=1, source_target_pairs={{0,8},{4,12},{8,0},{12,4},{1,9},{5,13},{9,1},{13,5},{2,10},{6,14},... | collective-permute-start | bytes 1769480 | tf_op jit(solution)/shard_map/ppermute | solution.py:468
  122.9 15.2 %collective-permute-start.30 = (bf16[2,4,96,384]{3,2,1,0:T(8,128)(2,1)}, bf16[2,4,96,384]{3,2,1,0:T(8,128)(2,1)S(1)}, u32[]{:S(2)}, u32[]{:S(2)}) collective-permute-start(bf16[2,4,96,384]{3,2,1,0:T(8,128)(2,1)} %get-tuple-element.132), channel_id=1, source_target_pairs={{0,16},{16,0},{1,17},{17,1},{2,18},{18,2},{3,19},{19,3},{4,20},{20... | collective-permute-start | bytes 1769480 | tf_op jit(solution)/shard_map/ppermute | solution.py:468
  141.3 13.0 %collective-permute-start.33 = (bf16[8,4,96,384]{3,2,1,0:T(8,128)(2,1)}, bf16[8,4,96,384]{3,2,1,0:T(8,128)(2,1)S(1)}, u32[]{:S(2)}, u32[]{:S(2)}) collective-permute-start(bf16[8,4,96,384]{3,2,1,0:T(8,128)(2,1)} %get-tuple-element.142), channel_id=1, source_target_pairs={{0,4},{4,0},{8,12},{12,8},{1,5},{5,1},{9,13},{13,9},{2,6},{6,2},{1... | collective-permute-start | bytes 7077896 | tf_op jit(solution)/shard_map/ppermute | solution.py:468
  141.3 12.9 %collective-permute-start.31 = (bf16[1,4,96,384]{3,2,1,0:T(8,128)(2,1)}, bf16[1,4,96,384]{3,2,1,0:T(8,128)(2,1)S(1)}, u32[]{:S(2)}, u32[]{:S(2)}) collective-permute-start(bf16[1,4,96,384]{3,2,1,0:T(8,128)(2,1)} %get-tuple-element.135.rest_9_), channel_id=1, source_target_pairs={{0,16},{16,0},{1,17},{17,1},{2,18},{18,2},{3,19},{19,3},{4,20},{20... | collective-permute-start | bytes 884744 | tf_op jit(solution)/shard_map/ppermute | solution.py:468
  142.4 12.0 %collective-permute-start.32 = (bf16[1,4,96,384]{3,2,1,0:T(8,128)(2,1)}, bf16[1,4,96,384]{3,2,1,0:T(8,128)(2,1)S(1)}, u32[]{:S(2)}, u32[]{:S(2)}) collective-permute-start(bf16[1,4,96,384]{3,2,1,0:T(8,128)(2,1)} %get-tuple-element.140), channel_id=1, source_target_pairs={{0,8},{4,12},{8,0},{12,4},{1,9},{5,13},{9,1},{13,5},{2,10},{6,14},... | collective-permute-start | bytes 884744 | tf_op jit(solution)/shard_map/ppermute | solution.py:468
  159.7 21.7 %collective-permute-start.36 = (bf16[8,4,96,384]{3,2,1,0:T(8,128)(2,1)}, bf16[8,4,96,384]{3,2,1,0:T(8,128)(2,1)S(1)}, u32[]{:S(2)}, u32[]{:S(2)}) collective-permute-start(bf16[8,4,96,384]{3,2,1,0:T(8,128)(2,1)} %get-tuple-element.152), channel_id=1, source_target_pairs={{0,4},{4,0},{8,12},{12,8},{1,5},{5,1},{9,13},{13,9},{2,6},{6,2},{1... | collective-permute-start | bytes 7077896 | tf_op jit(solution)/shard_map/ppermute | solution.py:468
  160.9 20.5 %collective-permute-start.34 = (bf16[2,4,96,384]{3,2,1,0:T(8,128)(2,1)}, bf16[2,4,96,384]{3,2,1,0:T(8,128)(2,1)S(1)}, u32[]{:S(2)}, u32[]{:S(2)}) collective-permute-start(bf16[2,4,96,384]{3,2,1,0:T(8,128)(2,1)} %get-tuple-element.149), channel_id=1, source_target_pairs={{0,8},{4,12},{8,0},{12,4},{1,9},{5,13},{9,1},{13,5},{2,10},{6,14},... | collective-permute-start | bytes 1769480 | tf_op jit(solution)/shard_map/ppermute | solution.py:468
  162.0 19.5 %collective-permute-start.35 = (bf16[2,4,96,384]{3,2,1,0:T(8,128)(2,1)}, bf16[2,4,96,384]{3,2,1,0:T(8,128)(2,1)}, u32[]{:S(2)}, u32[]{:S(2)}) collective-permute-start(bf16[2,4,96,384]{3,2,1,0:T(8,128)(2,1)} %get-tuple-element.150), channel_id=1, source_target_pairs={{0,16},{16,0},{1,17},{17,1},{2,18},{18,2},{3,19},{19,3},{4,20},{20... | collective-permute-start | bytes 1769480 | tf_op jit(solution)/shard_map/ppermute | solution.py:468
  164.7 15.3 %collective-permute-start.37 = (bf16[96,768]{1,0:T(8,128)(2,1)S(1)}, bf16[96,768]{1,0:T(8,128)(2,1)S(1)}, u32[]{:S(2)}, u32[]{:S(2)}) collective-permute-start(bf16[96,768]{1,0:T(8,128)(2,1)S(1)} %get-tuple-element.222), channel_id=1, source_target_pairs={{0,2},{1,3},{2,0},{3,1},{4,6},{5,7},{6,4},{7,5},{8,10},{9,11},{10,... | collective-permute-start | bytes 442376 | tf_op jit(solution)/shard_map/ppermute | solution.py:473
  169.8 11.6 %collective-permute-start.38 = (bf16[96,768]{1,0:T(8,128)(2,1)S(1)}, bf16[96,768]{1,0:T(8,128)(2,1)S(1)}, u32[]{:S(2)}, u32[]{:S(2)}) collective-permute-start(bf16[96,768]{1,0:T(8,128)(2,1)S(1)} %get-tuple-element.221), channel_id=1, source_target_pairs={{0,1},{1,2},{2,3},{3,0},{4,5},{5,6},{6,7},{7,4},{8,9},{9,10},{10,1... | collective-permute-start | bytes 442376 | tf_op jit(solution)/shard_map/ppermute | solution.py:473
  180.0 20.9 %collective-permute-start.43 = (bf16[96,768]{1,0:T(8,128)(2,1)}, bf16[96,768]{1,0:T(8,128)(2,1)S(1)}, u32[]{:S(2)}, u32[]{:S(2)}) collective-permute-start(bf16[96,768]{1,0:T(8,128)(2,1)} %get-tuple-element.220), channel_id=1, source_target_pairs={{0,3},{1,0},{2,1},{3,2},{4,7},{5,4},{6,5},{7,6},{8,11},{9,8},{10,9... | collective-permute-start | bytes 442376 | tf_op jit(solution)/shard_map/ppermute | solution.py:473
  186.5 20.9 %collective-permute-start.39 = (bf16[2,4,96,384]{3,2,1,0:T(8,128)(2,1)}, bf16[2,4,96,384]{3,2,1,0:T(8,128)(2,1)S(1)}, u32[]{:S(2)}, u32[]{:S(2)}) collective-permute-start(bf16[2,4,96,384]{3,2,1,0:T(8,128)(2,1)} %get-tuple-element.156), channel_id=1, source_target_pairs={{0,8},{4,12},{8,0},{12,4},{1,9},{5,13},{9,1},{13,5},{2,10},{6,14},... | collective-permute-start | bytes 1769480 | tf_op jit(solution)/shard_map/ppermute | solution.py:468
  187.6 13.3 %collective-permute-start.40 = (bf16[1,4,96,384]{3,2,1,0:T(8,128)(2,1)}, bf16[1,4,96,384]{3,2,1,0:T(8,128)(2,1)S(1)}, u32[]{:S(2)}, u32[]{:S(2)}) collective-permute-start(bf16[1,4,96,384]{3,2,1,0:T(8,128)(2,1)} %get-tuple-element.153.rest_23_), channel_id=1, source_target_pairs={{0,16},{16,0},{1,17},{17,1},{2,18},{18,2},{3,19},{19,3},{4,20},{20... | collective-permute-start | bytes 884744 | tf_op jit(solution)/shard_map/ppermute | solution.py:468
  188.9 18.6 %collective-permute-start.41 = (bf16[1,4,96,384]{3,2,1,0:T(8,128)(2,1)}, bf16[1,4,96,384]{3,2,1,0:T(8,128)(2,1)S(1)}, u32[]{:S(2)}, u32[]{:S(2)}) collective-permute-start(bf16[1,4,96,384]{3,2,1,0:T(8,128)(2,1)} %get-tuple-element.157), channel_id=1, source_target_pairs={{0,8},{4,12},{8,0},{12,4},{1,9},{5,13},{9,1},{13,5},{2,10},{6,14},... | collective-permute-start | bytes 884744 | tf_op jit(solution)/shard_map/ppermute | solution.py:468
  189.8 18.4 %collective-permute-start.42 = (bf16[2,4,96,384]{3,2,1,0:T(8,128)(2,1)}, bf16[2,4,96,384]{3,2,1,0:T(8,128)(2,1)S(1)}, u32[]{:S(2)}, u32[]{:S(2)}) collective-permute-start(bf16[2,4,96,384]{3,2,1,0:T(8,128)(2,1)} %get-tuple-element.158), channel_id=1, source_target_pairs={{0,16},{16,0},{1,17},{17,1},{2,18},{18,2},{3,19},{19,3},{4,20},{20... | collective-permute-start | bytes 1769480 | tf_op jit(solution)/shard_map/ppermute | solution.py:468
  212.5 7.9 %collective-permute-start.44 = (bf16[1,4,96,384]{3,2,1,0:T(8,128)(2,1)}, bf16[1,4,96,384]{3,2,1,0:T(8,128)(2,1)S(1)}, u32[]{:S(2)}, u32[]{:S(2)}) collective-permute-start(bf16[1,4,96,384]{3,2,1,0:T(8,128)(2,1)} %get-tuple-element.160), channel_id=1, source_target_pairs={{0,16},{16,0},{1,17},{17,1},{2,18},{18,2},{3,19},{19,3},{4,20},{20... | collective-permute-start | bytes 884744 | tf_op jit(solution)/shard_map/ppermute | solution.py:468
  213.8 6.9 %collective-permute-start.45 = (bf16[1,4,96,384]{3,2,1,0:T(8,128)(2,1)}, bf16[1,4,96,384]{3,2,1,0:T(8,128)(2,1)S(1)}, u32[]{:S(2)}, u32[]{:S(2)}) collective-permute-start(bf16[1,4,96,384]{3,2,1,0:T(8,128)(2,1)} %get-tuple-element.161), channel_id=1, source_target_pairs={{0,8},{4,12},{8,0},{12,4},{1,9},{5,13},{9,1},{13,5},{2,10},{6,14},... | collective-permute-start | bytes 884744 | tf_op jit(solution)/shard_map/ppermute | solution.py:468
  216.0 37.3 %collective-permute-start.52 = (bf16[96,1536]{1,0:T(8,128)(2,1)S(1)}, bf16[96,1536]{1,0:T(8,128)(2,1)S(1)}, u32[]{:S(2)}, u32[]{:S(2)}) collective-permute-start(bf16[96,1536]{1,0:T(8,128)(2,1)S(1)} %pad_maximum_fusion.11), channel_id=1, source_target_pairs={{0,2},{1,3},{2,0},{3,1},{4,6},{5,7},{6,4},{7,5},{8,10},{9,11},{10,... | collective-permute-start | bytes 884744 | tf_op jit(solution)/shard_map/ppermute | solution.py:473
  219.4 12.0 %collective-permute-start.54 = (bf16[96,768]{1,0:T(8,128)(2,1)S(1)}, bf16[96,768]{1,0:T(8,128)(2,1)S(1)}, u32[]{:S(2)}, u32[]{:S(2)}) collective-permute-start(bf16[96,768]{1,0:T(8,128)(2,1)S(1)} %fusion.2), channel_id=1, source_target_pairs={{0,16},{16,0},{1,17},{17,1},{2,18},{18,2},{3,19},{19,3},{4,20},{20... | collective-permute-start | bytes 442376 | tf_op jit(solution)/shard_map/ppermute | solution.py:468
  226.2 27.1 %collective-permute-start.53 = (bf16[96,1536]{1,0:T(8,128)(2,1)S(1)}, bf16[96,1536]{1,0:T(8,128)(2,1)S(1)}, u32[]{:S(2)}, u32[]{:S(2)}) collective-permute-start(bf16[96,1536]{1,0:T(8,128)(2,1)S(1)} %pad_maximum_fusion.12), channel_id=1, source_target_pairs={{0,1},{1,2},{2,3},{3,0},{4,5},{5,6},{6,7},{7,4},{8,9},{9,10},{10,1... | collective-permute-start | bytes 884744 | tf_op jit(solution)/shard_map/ppermute | solution.py:473
  238.5 14.8 %collective-permute-start.51 = (bf16[96,1536]{1,0:T(8,128)(2,1)S(1)}, bf16[96,1536]{1,0:T(8,128)(2,1)S(1)}, u32[]{:S(2)}, u32[]{:S(2)}) collective-permute-start(bf16[96,1536]{1,0:T(8,128)(2,1)S(1)} %copy-done.30), channel_id=1, source_target_pairs={{0,3},{1,0},{2,1},{3,2},{4,7},{5,4},{6,5},{7,6},{8,11},{9,8},{10,9... | collective-permute-start | bytes 884744 | tf_op jit(solution)/shard_map/ppermute | solution.py:473
  256.0 6.8 %collective-permute-start.55 = (bf16[96,1536]{1,0:T(8,128)(2,1)S(1)}, bf16[96,1536]{1,0:T(8,128)(2,1)S(1)}, u32[]{:S(2)}, u32[]{:S(2)}) collective-permute-start(bf16[96,1536]{1,0:T(8,128)(2,1)S(1)} %add_convert_fusion), channel_id=1, source_target_pairs={{0,16},{16,0},{1,17},{17,1},{2,18},{18,2},{3,19},{19,3},{4,20},{20... | collective-permute-start | bytes 884744 | tf_op jit(solution)/shard_map/ppermute | solution.py:468
  (61 other events, 262.4 us)

commit v5 on v4

--- a/solution.py
+++ b/solution.py
@@ -787,16 +787,22 @@
                     for i in range(per_call):
                         slots = [totals[id(r)][i * per_mlp + j] for j in range(per_mlp)]
                         part = jnp.concatenate([s[:, :cut] for s in slots] + [s[:, cut:] for s in slots], axis=1)
-                        if k1 == starts[-1] and k1 + i > 0:
-                            smalls = fence([smalls], [part])[0]
                         mlp_moves[k1 + i] = part if k1 + i == 0 else shifted(part, -(k1 + i))
             if len(mlp_moves) < col_size:
-                token, passed = go_on(mlp_sums, token, [smalls])
+                smalls = sum_over(smalls, ("row", "dp"))
+                late = [mlp_moves[col_size - 1]] if col_size - 1 in mlp_moves else []
+                token, passed = go_on(mlp_sums, token, [smalls] + late)
                 smalls = passed[0]
+                if late:
+                    mlp_moves[col_size - 1] = passed[1]
     head_row, up_row = 5 + col_size, 5
-    smalls = sum_over(smalls, ("row", "dp", "col"))
+    col_flips = [1 << n for n in range(col_size.bit_length() - 1)]
+    for flip in col_flips[:-1]:
+        smalls = smalls + flipped(smalls, "col", flip)
     smalls, *came = fence([smalls] + [mlp_moves[k] for k in range(1, col_size)])
     mlp_mine, mlp_other = settle([mlp_moves[0]] + came)
+    smalls = fence([smalls], [mlp_mine])[0]
+    smalls = smalls + flipped(smalls, "col", col_flips[-1])
     g_heads = whole_block(attn_mine, attn_other).reshape(rows, local_heads, HEAD)
     g_mlp = whole_block(mlp_mine, mlp_other)
     g_up, g_down = g_mlp[:, :up_cols], g_mlp[:, up_cols:]

time: 267 us -> 264 us (0.989)
  waiting for transfers between devices: 43.7 us -> 48.6 us
    ppermute x12, waiting for transfers between devices: 16.1 us -> 21.7 us  [shifted(): lax.ppermute(value, 'col', [(i, (i + by) % size) for i in range(size)])]
    unnamed x112 -> x118, local copies, waits for them, and re-layouts: 16 us -> 16.1 us
  transfers between devices with their start and end apart: 56 -> 56, of which waited for: 15 -> 16; matrix products, arithmetic and copies ran while one was open for 12% -> 10% of each run, Pallas kernels for 36% -> 36%
where the time goes in v5:
time: 264 us; the launch traced here: 263 us
  Pallas kernels  104 us (39%)
  starting transfers between devices  59.1 us (22%)
  waiting for transfers between devices  48.6 us (18%)
  local copies, waits for them, and re-layouts  34.3 us (13%)
  other arithmetic  15.6 us (6%)
    pallas_call x4, Pallas kernels, block_part(): pl.pallas_call(functools.partial(kernel, orders, core_bit, len(after)), g...  51.9 us
    ppermute x44, starting transfers between devices, flipped(): lax.ppermute(value, axis, [(i, i ^ flip) for i in range(lax.axis_size(axi...  32.3 us
    ppermute x44, waiting for transfers between devices, flipped(): lax.ppermute(value, axis, [(i, i ^ flip) for i in range(lax.axis_size(axi...  26.9 us
    ppermute x12, starting transfers between devices, shifted(): lax.ppermute(value, 'col', [(i, (i + by) % size) for i in range(size)])  26.9 us
    ppermute x12, waiting for transfers between devices, shifted(): lax.ppermute(value, 'col', [(i, (i + by) % size) for i in range(size)])  21.7 us
    pallas_call x6, Pallas kernels, merge(): pl.pallas_call(functools.partial(merge_kernel, layout, len(arrays), len(a...  18.5 us
    pallas_call x2, Pallas kernels, mlp_tail_part(): pl.pallas_call(functools.partial(mlp_tail_kernel, orders, core_bit, len(s...  17.7 us
    unnamed x118, local copies, waits for them, and re-layouts  16.1 us
  transfers between devices with their start and end apart: 56, of which 16 were waited for; matrix products, arithmetic and copies ran while one was open for 10% of the time, Pallas kernels for 36%

profile of v5, /device:TPU:0, one launch (start us, length us, event | category | flops | bytes accessed | tf_op | source)
XLA Modules:
  0.0 263.4 jit_solution(8717132731162812257)
XLA Ops:
  3.1 5.1 %collective-permute-start.2 = (bf16[96,768]{1,0:T(8,128)(2,1)S(1)}, bf16[96,768]{1,0:T(8,128)(2,1)S(1)}, u32[]{:S(2)}, u32[]{:S(2)}) collective-permute-start(bf16[96,768]{1,0:T(8,128)(2,1)S(1)} %copy.77), channel_id=1, source_target_pairs={{0,3},{1,0},{2,1},{3,2},{4,7},{5,4},{6,5},{7,6},{8,11},{9,8},{10,9... | collective-permute-start | bytes 442376 | tf_op jit(solution)/shard_map/ppermute | solution.py:473
  14.5 1.3 constant_dynamic-slice_fusion.segr_ref
  15.8 4.9 %collective-permute-done.1 = bf16[96,768]{1,0:T(8,128)(2,1)S(1)} collective-permute-done((bf16[96,768]{1,0:T(8,128)(2,1)S(1)}, bf16[96,768]{1,0:T(8,128)(2,1)S(1)}, u32[]{:S(2)}, u32[]{:S(2)}) %collective-permute-start.1) | collective-permute-done | bytes 147488 | tf_op jit(solution)/shard_map/ppermute | solution.py:473
  20.9 1.6 collective-permute-start.6
  23.3 1.5 collective-permute-start.7
  24.8 6.0 %shard_map.255 = (bf16[512,768]{1,0:T(8,128)(2,1)}, bf16[768,512]{1,0:T(8,128)(2,1)}, bf16[512,768]{1,0:T(8,128)(2,1)}, bf16[768,512]{1,0:T(8,128)(2,1)}, bf16[7...) custom-call(bf16[512,768]{1,0:T(8,128)(2,1)} %rest_13_.1, ...), custom_call_target="tpu_custom_call" | custom-call | flops 6899999744 | bytes 1048576 | tf_op jit(solution)/shard_map/pallas_call | solution.py:124
  30.9 1.6 collective-permute-done.3.__3_.__1_
  35.4 1.6 collective-permute-start.8
  41.1 2.2 collective-permute-start.5
  44.6 9.6 %collective-permute-done.4.__2_ = bf16[96,1536]{1,0:T(8,128)(2,1)S(1)} collective-permute-done((bf16[96,1536]{1,0:T(8,128)(2,1)S(1)}, bf16[96,1536]{1,0:T(8,128)(2,1)S(1)}, u32[]{:S(2)}, u32[]{:S(2)}) %collective-permute-start.4) | collective-permute-done | bytes 294944 | tf_op jit(solution)/shard_map/ppermute | solution.py:473
  55.8 1.4 pad_maximum_fusion
  57.2 1.2 collective-permute-start.10
  59.6 15.1 %shard_map.259 = (bf16[2,512,768]{2,1,0:T(8,128)(2,1)}, bf16[2,512,384]{2,1,0:T(8,128)(2,1)}, f32[2,1,768]{2,1,0:T(1,128)}, bf16[8,4,96,384]{3,2,1,0:T(8,128)(2,1)}, bf16[8,4,96,384]{3,2,1,0:T(8,128)(2,1)}) custom-call(s32[2]{0:T(128)} %pad_add_fusion.me_ref, bf16[512,768]{1,0:T(8,128)(2,1)} %get-tuple-element.95.__2_.na_ref, ...), custom_call_target="tpu_custom_call" | custom-call | flops 23000000512 | bytes 1048576 | tf_op jit(solution)/shard_map/pallas_call | solution.py:270
  75.6 2.1 fusion.10
  80.8 14.9 %shard_map.261 = (bf16[2,512,768]{2,1,0:T(8,128)(2,1)}, bf16[2,512,384]{2,1,0:T(8,128)(2,1)}, f32[2,1,768]{2,1,0:T(1,128)}, bf16[8,4,96,384]{3,2,1,0:T(8,128)(2,1)}, bf16[8,4,96,384]{3,2,1,0:T(8,128)(2,1)}) custom-call(s32[2]{0:T(128)} %pad_add_fusion.me_ref, ...), custom_call_target="tpu_custom_call", output_to_operand_aliasing={{3}: (19, {}), {4}: (20, {})} | custom-call | flops 23000000512 | bytes 1048576 | tf_op jit(solution)/shard_map/pallas_call | solution.py:270
  99.2 1.8 pad_maximum_fusion.5.__1_
  102.7 10.2 %shard_map.263 = (f32[512,768]{1,0:T(8,128)}, f32[512,768]{1,0:T(8,128)}) custom-call(s32[2]{0:T(128)} %pad_add_fusion.me_ref, bf16[2,4,96,384]{3,2,1,0:T(8,128)(2,1)} %copy-done.19, bf16[2,4,96,384]{3,2,1,0:T(8,128)(2,1)} %get-tuple-element.98.__4_.rest_1_, bf16[2,4,96,384]{3,2,1,0:T(8,128)(2,1)} %collective-permute-done.12.rest_2_, ...), custom_call_target="tpu_custom_call" | custom-call | flops 12650000384 | bytes 1048576 | tf_op jit(solution)/shard_map/pallas_call | solution.py:404
  113.8 2.8 %collective-permute-done.17.__3_ = bf16[2,2,96,768]{3,2,1,0:T(8,128)(2,1)} collective-permute-done((bf16[2,2,96,768]{3,2,1,0:T(8,128)(2,1)}, bf16[2,2,96,768]{3,2,1,0:T(8,128)(2,1)}, u32[]{:S(2)}, u32[]{:S(2)}) %collective-permute-start.17) | collective-permute-done | bytes 589856 | tf_op jit(solution)/shard_map/ppermute | solution.py:468
  117.6 1.4 copy-done.3
  119.0 2.8 %shard_map.265 = (bf16[2,4,96,384]{3,2,1,0:T(8,128)(2,1)}, bf16[2,4,96,384]{3,2,1,0:T(8,128)(2,1)}) custom-call(bf16[8,4,96,384]{3,2,1,0:T(8,128)(2,1)} %get-tuple-element.130.refs_0_.refs_2_.refs_3_.refs_4_, bf16[8,4,96,384]{3,2,1,0:T(8,128)(2,1)} %copy-done.3, bf16[8,4,96,384]{3,2,1,0:T(8,128)(2,1)} %get-tuple-element.130.refs_0_.refs_2_.refs_3_.refs_4_, ...), custom_call_target="tpu_custom_call" | custom-call | flops 3449999872 | bytes 1048576 | tf_op jit(solution)/shard_map/pallas_call | solution.py:558
  123.9 11.0 %shard_map.266 = (bf16[2,512,768]{2,1,0:T(8,128)(2,1)}, bf16[2,512,768]{2,1,0:T(8,128)(2,1)}, f32[2,1,768]{2,1,0:T(1,128)}, bf16[8,4,96,384]{3,2,1,0:T(8,128)(2,1)}, bf16[8,4,96,384]{3,2,1,0:T(8,128)(2,1)}) custom-call(s32[2]{0:T(128)} %pad_add_fusion.me_ref, bf16[512,768]{1,0:T(8,128)(2,1)} %get-tuple-element.128.nm_ref, ...), custom_call_target="tpu_custom_call" | custom-call | flops 13799999488 | bytes 1048576 | tf_op jit(solution)/shard_map/pallas_call | solution.py:270
  135.0 2.4 collective-permute-done.29.refs_2_
  139.0 2.3 shard_map.267
  143.3 10.9 %shard_map.268 = (bf16[2,512,768]{2,1,0:T(8,128)(2,1)}, bf16[2,512,768]{2,1,0:T(8,128)(2,1)}, f32[2,1,768]{2,1,0:T(1,128)}, bf16[8,4,96,384]{3,2,1,0:T(8,128)(2,1)}, bf16[8,4,96,384]{3,2,1,0:T(8,128)(2,1)}) custom-call(s32[2]{0:T(128)} %pad_add_fusion.me_ref, bf16[512,768]{1,0:T(8,128)(2,1)} %get-tuple-element.128.nm_ref, ...), custom_call_target="tpu_custom_call" | custom-call | flops 13799999488 | bytes 1048576 | tf_op jit(solution)/shard_map/pallas_call | solution.py:270
  155.9 3.8 %shard_map.269 = (bf16[1,4,96,768]{3,2,1,0:T(8,128)(2,1)}, bf16[2,4,96,384]{3,2,1,0:T(8,128)(2,1)}, bf16[2,4,96,384]{3,2,1,0:T(8,128)(2,1)}, bf16[8,4,96,384]{3,2,1,0:T(8,128)(2,1)}) custom-call(bf16[8,4,96,384]{3,2,1,0:T(8,128)(2,1)} %get-tuple-element.130.refs_0_.refs_2_.refs_3_.refs_4_, ...), custom_call_target="tpu_custom_call", output_to_operand_aliasing={{3}: (12, {})} | custom-call | flops 3449999872 | bytes 1048576 | tf_op jit(solution)/shard_map/pallas_call | solution.py:558
  164.0 5.2 %collective-permute-start.37 = (bf16[96,768]{1,0:T(8,128)(2,1)S(1)}, bf16[96,768]{1,0:T(8,128)(2,1)S(1)}, u32[]{:S(2)}, u32[]{:S(2)}) collective-permute-start(bf16[96,768]{1,0:T(8,128)(2,1)S(1)} %get-tuple-element.224), channel_id=1, source_target_pairs={{0,2},{1,3},{2,0},{3,1},{4,6},{5,7},{6,4},{7,5},{8,10},{9,11},{10,... | collective-permute-start | bytes 442376 | tf_op jit(solution)/shard_map/ppermute | solution.py:473
  169.2 2.8 %collective-permute-start.38 = (bf16[96,768]{1,0:T(8,128)(2,1)S(1)}, bf16[96,768]{1,0:T(8,128)(2,1)S(1)}, u32[]{:S(2)}, u32[]{:S(2)}) collective-permute-start(bf16[96,768]{1,0:T(8,128)(2,1)S(1)} %get-tuple-element.223), channel_id=1, source_target_pairs={{0,1},{1,2},{2,3},{3,0},{4,5},{5,6},{6,7},{7,4},{8,9},{9,10},{10,1... | collective-permute-start | bytes 442376 | tf_op jit(solution)/shard_map/ppermute | solution.py:473
  172.0 7.4 %shard_map.270 = (f32[512,768]{1,0:T(8,128)}, f32[512,768]{1,0:T(8,128)}) custom-call(s32[2]{0:T(128)} %pad_add_fusion.me_ref, bf16[2,2,96,768]{3,2,1,0:T(8,128)(2,1)} %copy-done.18, bf16[2,2,96,768]{3,2,1,0:T(8,128)(2,1)} %get-tuple-element.123.rest_1_, bf16[2,2,96,768]{3,2,1,0:T(8,128)(2,1)} %copy-done.5, ...), custom_call_target="tpu_custom_call" | custom-call | flops 10350000128 | bytes 1048576 | tf_op jit(solution)/shard_map/pallas_call | solution.py:433
  179.4 1.3 collective-permute-start.43
  182.4 3.5 %shard_map.271 = (bf16[1,4,96,384]{3,2,1,0:T(8,128)(2,1)}, bf16[1,4,96,384]{3,2,1,0:T(8,128)(2,1)}, bf16[2,4,96,384]{3,2,1,0:T(8,128)(2,1)}, bf16[2,4,96,384]{3,...) custom-call(bf16[8,4,96,384]{3,2,1,0:T(8,128)(2,1)} %get-tuple-eleme, ...), custom_call_target="tpu_custom_call", output_to_operand_aliasing={{4}: (10, {}), {5}: (11, {})} | custom-call | flops 3449999872 | bytes 1048576 | tf_op jit(solution)/shard_map/pallas_call | solution.py:558
  187.0 1.2 collective-permute-start.40
  190.0 10.3 %shard_map.272 = (bf16[512,768]{1,0:T(8,128)(2,1)}, bf16[512,768]{1,0:T(8,128)(2,1)}, f32[16,768]{1,0:T(8,128)}) custom-call(s32[2]{0:T(128)} %pad_add_fusion.me_ref, bf16[2,2,96,768]{3,2,1,0:T(8,128)(2,1)} %get-tuple-element.124.rest_0_, bf16[2,2,96,768]{3,2,1,0:T(8,128)(2,1)} %get-tuple-element.125.refs_5_.rest_1_, bf16[2,2,96,768]{3,2,1,0:T(8,128)(2,1)} %copy-done.15, ...), custom_call_target="tpu_custom_call" | custom-call | flops 10350000128 | bytes 1048576 | tf_op jit(solution)/shard_map/pallas_call | solution.py:433
  200.3 6.5 %collective-permute-done.41.refs_7_ = bf16[1,4,96,384]{3,2,1,0:T(8,128)(2,1)S(1)} collective-permute-done((bf16[1,4,96,384]{3,2,1,0:T(8,128)(2,1)}, bf16[1,4,96,384]{3,2,1,0:T(8,128)(2,1)S(1)}, u32[]{:S(2)}, u32[]{:S(2)}) %collective-permute-start.41) | collective-permute-done | bytes 294944 | tf_op jit(solution)/shard_map/ppermute | solution.py:468
  208.4 3.4 %shard_map.273 = (bf16[1,4,96,768]{3,2,1,0:T(8,128)(2,1)}, bf16[1,4,96,384]{3,2,1,0:T(8,128)(2,1)}, bf16[1,4,96,384]{3,2,1,0:T(8,128)(2,1)}, f32[16,768]{1,0:T(8,128)}, bf16[96,768]{1,0:T(8,128)(2,1)}) custom-call(bf16[8,4,96,384]{3,2,1,0:T(8,128)(2,1)} %get-tuple-element.142.refs_8_.refs_10_.refs_0_.refs_3_.refs_4_, ...), custom_call_target="tpu_custom_call", output_to_operand_aliasing={{3}: (14, {}), {4}: (15, {})} | custom-call | flops 3449999872 | bytes 1048576 | tf_op jit(solution)/shard_map/pallas_call | solution.py:558
  211.9 1.3 collective-permute-start.44
  215.3 3.0 %collective-permute-start.49 = (bf16[96,1536]{1,0:T(8,128)(2,1)S(1)}, bf16[96,1536]{1,0:T(8,128)(2,1)S(1)}, u32[]{:S(2)}, u32[]{:S(2)}) collective-permute-start(bf16[96,1536]{1,0:T(8,128)(2,1)S(1)} %pad_maximum_fusion.10), channel_id=1, source_target_pairs={{0,1},{1,2},{2,3},{3,0},{4,5},{5,6},{6,7},{7,4},{8,9},{9,10},{10,1... | collective-permute-start | bytes 884744 | tf_op jit(solution)/shard_map/ppermute | solution.py:473
  219.4 1.3 collective-permute-start.54
  221.9 3.0 %collective-permute-done.47 = f32[16,768]{1,0:T(8,128)S(1)} collective-permute-done((f32[16,768]{1,0:T(8,128)S(1)}, f32[16,768]{1,0:T(8,128)S(1)}, u32[]{:S(2)}, u32[]{:S(2)}) %collective-permute-start.47) | collective-permute-done | bytes 49184 | tf_op jit(solution)/shard_map/ppermute | solution.py:468
  224.9 1.5 collective-permute-start.52
  226.3 1.2 collective-permute-start.48
  227.7 2.8 %collective-permute-done.48 = f32[16,768]{1,0:T(8,128)S(1)} collective-permute-done((f32[16,768]{1,0:T(8,128)S(1)}, f32[16,768]{1,0:T(8,128)S(1)}, u32[]{:S(2)}, u32[]{:S(2)}) %collective-permute-start.48) | collective-permute-done | bytes 49184 | tf_op jit(solution)/shard_map/ppermute | solution.py:468
  232.7 2.7 %shard_map.274 = (bf16[1,4,96,768]{3,2,1,0:T(8,128)(2,1)}, f32[16,768]{1,0:T(8,128)}, bf16[96,1536]{1,0:T(8,128)(2,1)}) custom-call(bf16[8,4,96,384]{3,2,1,0:T(8,128)(2,1)} %get-tuple-element.152.refs_6_.refs_8_.refs_11_.refs_0_.refs_4_, bf16[8,4,96,384]{3,2,1,0:T(8,128)(2,1)} %copy-done.4, ...), custom_call_target="tpu_custom_call", output_to_operand_aliasing={{1}: (8, {}), {2}: (9, {})} | custom-call | flops 3449999872 | bytes 1048576 | tf_op jit(solution)/shard_map/pallas_call | solution.py:558
  236.6 3.0 %collective-permute-start.51 = (bf16[96,1536]{1,0:T(8,128)(2,1)S(1)}, bf16[96,1536]{1,0:T(8,128)(2,1)S(1)}, u32[]{:S(2)}, u32[]{:S(2)}) collective-permute-start(bf16[96,1536]{1,0:T(8,128)(2,1)S(1)} %pad_maximum_fusion.11), channel_id=1, source_target_pairs={{0,3},{1,0},{2,1},{3,2},{4,7},{5,4},{6,5},{7,6},{8,11},{9,8},{10,9... | collective-permute-start | bytes 884744 | tf_op jit(solution)/shard_map/ppermute | solution.py:473
  239.6 1.4 collective-permute-done.50
  241.6 5.6 %collective-permute-done.51.__1_ = bf16[96,1536]{1,0:T(8,128)(2,1)S(1)} collective-permute-done((bf16[96,1536]{1,0:T(8,128)(2,1)S(1)}, bf16[96,1536]{1,0:T(8,128)(2,1)S(1)}, u32[]{:S(2)}, u32[]{:S(2)}) %collective-permute-start.51) | collective-permute-done | bytes 294944 | tf_op jit(solution)/shard_map/ppermute | solution.py:473
  247.9 2.0 add_convert_fusion.__1_
  254.1 1.2 collective-permute-done.53
  257.3 4.3 %collective-permute-done.55 = bf16[96,1536]{1,0:T(8,128)(2,1)S(1)} collective-permute-done((bf16[96,1536]{1,0:T(8,128)(2,1)S(1)}, bf16[96,1536]{1,0:T(8,128)(2,1)S(1)}, u32[]{:S(2)}, u32[]{:S(2)}) %collective-permute-start.55) | collective-permute-done | bytes 294944 | tf_op jit(solution)/shard_map/ppermute | solution.py:468
  (277 shorter events, 66.8 us)
Async XLA Ops:
  3.1 12.7 %collective-permute-start.2 = (bf16[96,768]{1,0:T(8,128)(2,1)S(1)}, bf16[96,768]{1,0:T(8,128)(2,1)S(1)}, u32[]{:S(2)}, u32[]{:S(2)}) collective-permute-start(bf16[96,768]{1,0:T(8,128)(2,1)S(1)} %copy.77), channel_id=1, source_target_pairs={{0,3},{1,0},{2,1},{3,2},{4,7},{5,4},{6,5},{7,6},{8,11},{9,8},{10,9... | collective-permute-start | bytes 442376 | tf_op jit(solution)/shard_map/ppermute | solution.py:473
  8.2 12.5 %collective-permute-start.1 = (bf16[96,768]{1,0:T(8,128)(2,1)S(1)}, bf16[96,768]{1,0:T(8,128)(2,1)S(1)}, u32[]{:S(2)}, u32[]{:S(2)}) collective-permute-start(bf16[96,768]{1,0:T(8,128)(2,1)S(1)} %copy.77), channel_id=1, source_target_pairs={{0,2},{1,3},{2,0},{3,1},{4,6},{5,7},{6,4},{7,5},{8,10},{9,11},{10,... | collective-permute-start | bytes 442376 | tf_op jit(solution)/shard_map/ppermute | solution.py:473
  8.2 12.5 %collective-permute-start = (bf16[96,768]{1,0:T(8,128)(2,1)S(1)}, bf16[96,768]{1,0:T(8,128)(2,1)S(1)}, u32[]{:S(2)}, u32[]{:S(2)}) collective-permute-start(bf16[96,768]{1,0:T(8,128)(2,1)S(1)} %copy.77), channel_id=1, source_target_pairs={{0,1},{1,2},{2,3},{3,0},{4,5},{5,6},{6,7},{7,4},{8,9},{9,10},{10,1... | collective-permute-start | bytes 442376 | tf_op jit(solution)/shard_map/ppermute | solution.py:473
  20.9 11.6 %collective-permute-start.6 = (bf16[1,4,96,384]{3,2,1,0:T(8,128)(2,1)S(1)}, bf16[1,4,96,384]{3,2,1,0:T(8,128)(2,1)S(1)}, u32[]{:S(2)}, u32[]{:S(2)}) collective-permute-start(bf16[1,4,96,384]{3,2,1,0:T(8,128)(2,1)S(1)} %get-tuple-element.234.__1_), channel_id=1, source_target_pairs={{0,8},{4,12},{8,0},{12,4},{1,9},{5,13},{9,1},{13,5},{2,10},{6,14},... | collective-permute-start | bytes 884744 | tf_op jit(solution)/shard_map/ppermute | solution.py:468
  22.4 10.0 %collective-permute-start.3 = (bf16[96,1536]{1,0:T(8,128)(2,1)}, bf16[96,1536]{1,0:T(8,128)(2,1)S(1)}, u32[]{:S(2)}, u32[]{:S(2)}) collective-permute-start(bf16[96,1536]{1,0:T(8,128)(2,1)} %shard_map.254.__0_), channel_id=1, source_target_pairs={{0,1},{1,2},{2,3},{3,0},{4,5},{5,6},{6,7},{7,4},{8,9},{9,10},{10,1... | collective-permute-start | bytes 884744 | tf_op jit(solution)/shard_map/ppermute | solution.py:473
  23.3 9.2 %collective-permute-start.7 = (bf16[1,4,96,384]{3,2,1,0:T(8,128)(2,1)S(1)}, bf16[1,4,96,384]{3,2,1,0:T(8,128)(2,1)S(1)}, u32[]{:S(2)}, u32[]{:S(2)}) collective-permute-start(bf16[1,4,96,384]{3,2,1,0:T(8,128)(2,1)S(1)} %get-tuple-element.233), channel_id=1, source_target_pairs={{0,16},{16,0},{1,17},{17,1},{2,18},{18,2},{3,19},{19,3},{4,20},{20... | collective-permute-start | bytes 884744 | tf_op jit(solution)/shard_map/ppermute | solution.py:468
  35.4 18.9 %collective-permute-start.8 = (bf16[2,4,96,384]{3,2,1,0:T(8,128)(2,1)S(1)}, bf16[2,4,96,384]{3,2,1,0:T(8,128)(2,1)S(1)}, u32[]{:S(2)}, u32[]{:S(2)}) collective-permute-start(bf16[2,4,96,384]{3,2,1,0:T(8,128)(2,1)S(1)} %pad_maximum_fusion.2.rest_0_), channel_id=1, source_target_pairs={{0,16},{16,0},{1,17},{17,1},{2,18},{18,2},{3,19},{19,3},{4,20},{20... | collective-permute-start | bytes 1769480 | tf_op jit(solution)/shard_map/ppermute | solution.py:468
  38.0 16.3 %collective-permute-start.9 = (bf16[2,4,96,384]{3,2,1,0:T(8,128)(2,1)S(1)}, bf16[2,4,96,384]{3,2,1,0:T(8,128)(2,1)}, u32[]{:S(2)}, u32[]{:S(2)}) collective-permute-start(bf16[2,4,96,384]{3,2,1,0:T(8,128)(2,1)S(1)} %pad_maximum_fusion.3.rest_4_), channel_id=1, source_target_pairs={{0,8},{4,12},{8,0},{12,4},{1,9},{5,13},{9,1},{13,5},{2,10},{6,14},... | collective-permute-start | bytes 1769480 | tf_op jit(solution)/shard_map/ppermute | solution.py:468
  40.2 14.0 %collective-permute-start.4 = (bf16[96,1536]{1,0:T(8,128)(2,1)S(1)}, bf16[96,1536]{1,0:T(8,128)(2,1)S(1)}, u32[]{:S(2)}, u32[]{:S(2)}) collective-permute-start(bf16[96,1536]{1,0:T(8,128)(2,1)S(1)} %copy-done.11), channel_id=1, source_target_pairs={{0,2},{1,3},{2,0},{3,1},{4,6},{5,7},{6,4},{7,5},{8,10},{9,11},{10,... | collective-permute-start | bytes 884744 | tf_op jit(solution)/shard_map/ppermute | solution.py:473
  41.1 13.1 %collective-permute-start.5 = (bf16[96,1536]{1,0:T(8,128)(2,1)S(1)}, bf16[96,1536]{1,0:T(8,128)(2,1)S(1)}, u32[]{:S(2)}, u32[]{:S(2)}) collective-permute-start(bf16[96,1536]{1,0:T(8,128)(2,1)S(1)} %copy-done.11), channel_id=1, source_target_pairs={{0,3},{1,0},{2,1},{3,2},{4,7},{5,4},{6,5},{7,6},{8,11},{9,8},{10,9... | collective-permute-start | bytes 884744 | tf_op jit(solution)/shard_map/ppermute | solution.py:473
  44.6 13.9 %collective-permute-start.12 = (bf16[2,4,96,384]{3,2,1,0:T(8,128)(2,1)S(1)}, bf16[2,4,96,384]{3,2,1,0:T(8,128)(2,1)}, u32[]{:S(2)}, u32[]{:S(2)}) collective-permute-start(bf16[2,4,96,384]{3,2,1,0:T(8,128)(2,1)S(1)} %pad_maximum_fusion.2.rest_0_), channel_id=1, source_target_pairs={{0,4},{4,0},{8,12},{12,8},{1,5},{5,1},{9,13},{13,9},{2,6},{6,2},{1... | collective-permute-start | bytes 1769480 | tf_op jit(solution)/shard_map/ppermute | solution.py:468
  57.2 17.5 %collective-permute-start.10 = (bf16[1,4,96,768]{3,2,1,0:T(8,128)(2,1)S(1)}, bf16[1,4,96,768]{3,2,1,0:T(8,128)(2,1)}, u32[]{:S(2)}, u32[]{:S(2)}) collective-permute-start(bf16[1,4,96,768]{3,2,1,0:T(8,128)(2,1)S(1)} %get-tuple-element.211), channel_id=1, source_target_pairs={{0,8},{4,12},{8,0},{12,4},{1,9},{5,13},{9,1},{13,5},{2,10},{6,14},... | collective-permute-start | bytes 1769480 | tf_op jit(solution)/shard_map/ppermute | solution.py:468
  58.6 16.2 %collective-permute-start.11 = (bf16[1,4,96,768]{3,2,1,0:T(8,128)(2,1)S(1)}, bf16[1,4,96,768]{3,2,1,0:T(8,128)(2,1)S(1)}, u32[]{:S(2)}, u32[]{:S(2)}) collective-permute-start(bf16[1,4,96,768]{3,2,1,0:T(8,128)(2,1)S(1)} %get-tuple-element.210), channel_id=1, source_target_pairs={{0,16},{16,0},{1,17},{17,1},{2,18},{18,2},{3,19},{19,3},{4,20},{20... | collective-permute-start | bytes 1769480 | tf_op jit(solution)/shard_map/ppermute | solution.py:468
  77.8 17.9 %collective-permute-start.18 = (bf16[2,2,96,768]{3,2,1,0:T(8,128)(2,1)S(1)}, bf16[2,2,96,768]{3,2,1,0:T(8,128)(2,1)}, u32[]{:S(2)}, u32[]{:S(2)}) collective-permute-start(bf16[2,2,96,768]{3,2,1,0:T(8,128)(2,1)S(1)} %pad_maximum_fusion.6.rest_13_.rest_0_), channel_id=1, source_target_pairs={{0,16},{16,0},{1,17},{17,1},{2,18},{18,2},{3,19},{19,3},{4,20},{20... | collective-permute-start | bytes 1769480 | tf_op jit(solution)/shard_map/ppermute | solution.py:468
  78.9 16.9 %collective-permute-start.20 = (bf16[2,2,96,768]{3,2,1,0:T(8,128)(2,1)S(1)}, bf16[2,2,96,768]{3,2,1,0:T(8,128)(2,1)S(1)}, u32[]{:S(2)}, u32[]{:S(2)}) collective-permute-start(bf16[2,2,96,768]{3,2,1,0:T(8,128)(2,1)S(1)} %pad_maximum_fusion.6.rest_13_.rest_0_), channel_id=1, source_target_pairs={{0,4},{4,0},{8,12},{12,8},{1,5},{5,1},{9,13},{13,9},{2,6},{6,2},{1... | collective-permute-start | bytes 1769480 | tf_op jit(solution)/shard_map/ppermute | solution.py:468
  79.8 16.1 %collective-permute-start.19 = (bf16[2,2,96,768]{3,2,1,0:T(8,128)(2,1)}, bf16[2,2,96,768]{3,2,1,0:T(8,128)(2,1)}, u32[]{:S(2)}, u32[]{:S(2)}) collective-permute-start(bf16[2,2,96,768]{3,2,1,0:T(8,128)(2,1)} %pad_maximum_fusion.7.rest_4_), channel_id=1, source_target_pairs={{0,8},{4,12},{8,0},{12,4},{1,9},{5,13},{9,1},{13,5},{2,10},{6,14},... | collective-permute-start | bytes 1769480 | tf_op jit(solution)/shard_map/ppermute | solution.py:468
  80.6 15.2 %collective-permute-start.21 = (bf16[2,2,96,768]{3,2,1,0:T(8,128)(2,1)}, bf16[2,2,96,768]{3,2,1,0:T(8,128)(2,1)S(1)}, u32[]{:S(2)}, u32[]{:S(2)}) collective-permute-start(bf16[2,2,96,768]{3,2,1,0:T(8,128)(2,1)} %pad_maximum_fusion.7.rest_4_), channel_id=1, source_target_pairs={{0,4},{4,0},{8,12},{12,8},{1,5},{5,1},{9,13},{13,9},{2,6},{6,2},{1... | collective-permute-start | bytes 1769480 | tf_op jit(solution)/shard_map/ppermute | solution.py:468
  96.8 20.8 %collective-permute-start.28 = (bf16[8,4,96,384]{3,2,1,0:T(8,128)(2,1)}, bf16[8,4,96,384]{3,2,1,0:T(8,128)(2,1)S(1)}, u32[]{:S(2)}, u32[]{:S(2)}) collective-permute-start(bf16[8,4,96,384]{3,2,1,0:T(8,128)(2,1)} %get-tuple-element.131), channel_id=1, source_target_pairs={{0,4},{4,0},{8,12},{12,8},{1,5},{5,1},{9,13},{13,9},{2,6},{6,2},{1... | collective-permute-start | bytes 7077896 | tf_op jit(solution)/shard_map/ppermute | solution.py:468
  98.1 15.7 %collective-permute-start.16 = (bf16[2,2,96,768]{3,2,1,0:T(8,128)(2,1)S(1)}, bf16[2,2,96,768]{3,2,1,0:T(8,128)(2,1)}, u32[]{:S(2)}, u32[]{:S(2)}) collective-permute-start(bf16[2,2,96,768]{3,2,1,0:T(8,128)(2,1)S(1)} %pad_maximum_fusion.4.__0_), channel_id=1, source_target_pairs={{0,16},{16,0},{1,17},{17,1},{2,18},{18,2},{3,19},{19,3},{4,20},{20... | collective-permute-start | bytes 1769480 | tf_op jit(solution)/shard_map/ppermute | solution.py:468
  101.0 15.5 %collective-permute-start.17 = (bf16[2,2,96,768]{3,2,1,0:T(8,128)(2,1)}, bf16[2,2,96,768]{3,2,1,0:T(8,128)(2,1)}, u32[]{:S(2)}, u32[]{:S(2)}) collective-permute-start(bf16[2,2,96,768]{3,2,1,0:T(8,128)(2,1)} %pad_maximum_fusion.5.__1_), channel_id=1, source_target_pairs={{0,8},{4,12},{8,0},{12,4},{1,9},{5,13},{9,1},{13,5},{2,10},{6,14},... | collective-permute-start | bytes 1769480 | tf_op jit(solution)/shard_map/ppermute | solution.py:468
  102.2 14.4 %collective-permute-start.22 = (bf16[2,2,96,768]{3,2,1,0:T(8,128)(2,1)}, bf16[2,2,96,768]{3,2,1,0:T(8,128)(2,1)}, u32[]{:S(2)}, u32[]{:S(2)}) collective-permute-start(bf16[2,2,96,768]{3,2,1,0:T(8,128)(2,1)} %get-tuple-element.123.rest_1_), channel_id=1, source_target_pairs={{0,4},{4,0},{8,12},{12,8},{1,5},{5,1},{9,13},{13,9},{2,6},{6,2},{1... | collective-permute-start | bytes 1769480 | tf_op jit(solution)/shard_map/ppermute | solution.py:468
  102.2 14.4 %collective-permute-start.23 = (bf16[2,2,96,768]{3,2,1,0:T(8,128)(2,1)}, bf16[2,2,96,768]{3,2,1,0:T(8,128)(2,1)}, u32[]{:S(2)}, u32[]{:S(2)}) collective-permute-start(bf16[2,2,96,768]{3,2,1,0:T(8,128)(2,1)} %get-tuple-element.121.rest_12_.rest_5_), channel_id=1, source_target_pairs={{0,4},{4,0},{8,12},{12,8},{1,5},{5,1},{9,13},{13,9},{2,6},{6,2},{1... | collective-permute-start | bytes 1769480 | tf_op jit(solution)/shard_map/ppermute | solution.py:468
  116.6 18.3 %collective-permute-start.25 = (bf16[2,2,96,768]{3,2,1,0:T(8,128)(2,1)}, bf16[2,2,96,768]{3,2,1,0:T(8,128)(2,1)}, u32[]{:S(2)}, u32[]{:S(2)}) collective-permute-start(bf16[2,2,96,768]{3,2,1,0:T(8,128)(2,1)} %get-tuple-element.125.refs_5_.rest_1_), channel_id=1, source_target_pairs={{0,4},{4,0},{8,12},{12,8},{1,5},{5,1},{9,13},{13,9},{2,6},{6,2},{1... | collective-permute-start | bytes 1769480 | tf_op jit(solution)/shard_map/ppermute | solution.py:468
  117.1 17.8 %collective-permute-start.26 = (bf16[2,2,96,768]{3,2,1,0:T(8,128)(2,1)}, bf16[2,2,96,768]{3,2,1,0:T(8,128)(2,1)}, u32[]{:S(2)}, u32[]{:S(2)}) collective-permute-start(bf16[2,2,96,768]{3,2,1,0:T(8,128)(2,1)} %get-tuple-element.126.rest_4_), channel_id=1, source_target_pairs={{0,4},{4,0},{8,12},{12,8},{1,5},{5,1},{9,13},{13,9},{2,6},{6,2},{1... | collective-permute-start | bytes 1769480 | tf_op jit(solution)/shard_map/ppermute | solution.py:468
  117.2 17.7 %collective-permute-start.27 = (bf16[2,2,96,768]{3,2,1,0:T(8,128)(2,1)}, bf16[2,2,96,768]{3,2,1,0:T(8,128)(2,1)}, u32[]{:S(2)}, u32[]{:S(2)}) collective-permute-start(bf16[2,2,96,768]{3,2,1,0:T(8,128)(2,1)} %get-tuple-element.127.rest_5_), channel_id=1, source_target_pairs={{0,4},{4,0},{8,12},{12,8},{1,5},{5,1},{9,13},{13,9},{2,6},{6,2},{1... | collective-permute-start | bytes 1769480 | tf_op jit(solution)/shard_map/ppermute | solution.py:468
  121.8 15.5 %collective-permute-start.29 = (bf16[2,4,96,384]{3,2,1,0:T(8,128)(2,1)}, bf16[2,4,96,384]{3,2,1,0:T(8,128)(2,1)S(1)}, u32[]{:S(2)}, u32[]{:S(2)}) collective-permute-start(bf16[2,4,96,384]{3,2,1,0:T(8,128)(2,1)} %get-tuple-element.132.rest_9_), channel_id=1, source_target_pairs={{0,8},{4,12},{8,0},{12,4},{1,9},{5,13},{9,1},{13,5},{2,10},{6,14},... | collective-permute-start | bytes 1769480 | tf_op jit(solution)/shard_map/ppermute | solution.py:468
  122.9 15.2 %collective-permute-start.30 = (bf16[2,4,96,384]{3,2,1,0:T(8,128)(2,1)}, bf16[2,4,96,384]{3,2,1,0:T(8,128)(2,1)S(1)}, u32[]{:S(2)}, u32[]{:S(2)}) collective-permute-start(bf16[2,4,96,384]{3,2,1,0:T(8,128)(2,1)} %get-tuple-element.133), channel_id=1, source_target_pairs={{0,16},{16,0},{1,17},{17,1},{2,18},{18,2},{3,19},{19,3},{4,20},{20... | collective-permute-start | bytes 1769480 | tf_op jit(solution)/shard_map/ppermute | solution.py:468
  141.3 12.9 %collective-permute-start.33 = (bf16[8,4,96,384]{3,2,1,0:T(8,128)(2,1)}, bf16[8,4,96,384]{3,2,1,0:T(8,128)(2,1)S(1)}, u32[]{:S(2)}, u32[]{:S(2)}) collective-permute-start(bf16[8,4,96,384]{3,2,1,0:T(8,128)(2,1)} %get-tuple-element.143), channel_id=1, source_target_pairs={{0,4},{4,0},{8,12},{12,8},{1,5},{5,1},{9,13},{13,9},{2,6},{6,2},{1... | collective-permute-start | bytes 7077896 | tf_op jit(solution)/shard_map/ppermute | solution.py:468
  141.3 12.9 %collective-permute-start.31 = (bf16[1,4,96,384]{3,2,1,0:T(8,128)(2,1)}, bf16[1,4,96,384]{3,2,1,0:T(8,128)(2,1)S(1)}, u32[]{:S(2)}, u32[]{:S(2)}) collective-permute-start(bf16[1,4,96,384]{3,2,1,0:T(8,128)(2,1)} %get-tuple-element.136.rest_9_), channel_id=1, source_target_pairs={{0,16},{16,0},{1,17},{17,1},{2,18},{18,2},{3,19},{19,3},{4,20},{20... | collective-permute-start | bytes 884744 | tf_op jit(solution)/shard_map/ppermute | solution.py:468
  142.3 11.9 %collective-permute-start.32 = (bf16[1,4,96,384]{3,2,1,0:T(8,128)(2,1)}, bf16[1,4,96,384]{3,2,1,0:T(8,128)(2,1)S(1)}, u32[]{:S(2)}, u32[]{:S(2)}) collective-permute-start(bf16[1,4,96,384]{3,2,1,0:T(8,128)(2,1)} %get-tuple-element.141), channel_id=1, source_target_pairs={{0,8},{4,12},{8,0},{12,4},{1,9},{5,13},{9,1},{13,5},{2,10},{6,14},... | collective-permute-start | bytes 884744 | tf_op jit(solution)/shard_map/ppermute | solution.py:468
  159.6 21.1 %collective-permute-start.36 = (bf16[8,4,96,384]{3,2,1,0:T(8,128)(2,1)}, bf16[8,4,96,384]{3,2,1,0:T(8,128)(2,1)S(1)}, u32[]{:S(2)}, u32[]{:S(2)}) collective-permute-start(bf16[8,4,96,384]{3,2,1,0:T(8,128)(2,1)} %get-tuple-element.153), channel_id=1, source_target_pairs={{0,4},{4,0},{8,12},{12,8},{1,5},{5,1},{9,13},{13,9},{2,6},{6,2},{1... | collective-permute-start | bytes 7077896 | tf_op jit(solution)/shard_map/ppermute | solution.py:468
  160.8 19.9 %collective-permute-start.34 = (bf16[2,4,96,384]{3,2,1,0:T(8,128)(2,1)}, bf16[2,4,96,384]{3,2,1,0:T(8,128)(2,1)S(1)}, u32[]{:S(2)}, u32[]{:S(2)}) collective-permute-start(bf16[2,4,96,384]{3,2,1,0:T(8,128)(2,1)} %get-tuple-element.150), channel_id=1, source_target_pairs={{0,8},{4,12},{8,0},{12,4},{1,9},{5,13},{9,1},{13,5},{2,10},{6,14},... | collective-permute-start | bytes 1769480 | tf_op jit(solution)/shard_map/ppermute | solution.py:468
  161.9 18.8 %collective-permute-start.35 = (bf16[2,4,96,384]{3,2,1,0:T(8,128)(2,1)}, bf16[2,4,96,384]{3,2,1,0:T(8,128)(2,1)}, u32[]{:S(2)}, u32[]{:S(2)}) collective-permute-start(bf16[2,4,96,384]{3,2,1,0:T(8,128)(2,1)} %get-tuple-element.151), channel_id=1, source_target_pairs={{0,16},{16,0},{1,17},{17,1},{2,18},{18,2},{3,19},{19,3},{4,20},{20... | collective-permute-start | bytes 1769480 | tf_op jit(solution)/shard_map/ppermute | solution.py:468
  164.0 15.4 %collective-permute-start.37 = (bf16[96,768]{1,0:T(8,128)(2,1)S(1)}, bf16[96,768]{1,0:T(8,128)(2,1)S(1)}, u32[]{:S(2)}, u32[]{:S(2)}) collective-permute-start(bf16[96,768]{1,0:T(8,128)(2,1)S(1)} %get-tuple-element.224), channel_id=1, source_target_pairs={{0,2},{1,3},{2,0},{3,1},{4,6},{5,7},{6,4},{7,5},{8,10},{9,11},{10,... | collective-permute-start | bytes 442376 | tf_op jit(solution)/shard_map/ppermute | solution.py:473
  169.2 11.5 %collective-permute-start.38 = (bf16[96,768]{1,0:T(8,128)(2,1)S(1)}, bf16[96,768]{1,0:T(8,128)(2,1)S(1)}, u32[]{:S(2)}, u32[]{:S(2)}) collective-permute-start(bf16[96,768]{1,0:T(8,128)(2,1)S(1)} %get-tuple-element.223), channel_id=1, source_target_pairs={{0,1},{1,2},{2,3},{3,0},{4,5},{5,6},{6,7},{7,4},{8,9},{9,10},{10,1... | collective-permute-start | bytes 442376 | tf_op jit(solution)/shard_map/ppermute | solution.py:473
  179.4 20.9 %collective-permute-start.43 = (bf16[96,768]{1,0:T(8,128)(2,1)S(1)}, bf16[96,768]{1,0:T(8,128)(2,1)S(1)}, u32[]{:S(2)}, u32[]{:S(2)}) collective-permute-start(bf16[96,768]{1,0:T(8,128)(2,1)S(1)} %get-tuple-element.222), channel_id=1, source_target_pairs={{0,3},{1,0},{2,1},{3,2},{4,7},{5,4},{6,5},{7,6},{8,11},{9,8},{10,9... | collective-permute-start | bytes 442376 | tf_op jit(solution)/shard_map/ppermute | solution.py:473
  185.9 20.9 %collective-permute-start.39 = (bf16[2,4,96,384]{3,2,1,0:T(8,128)(2,1)}, bf16[2,4,96,384]{3,2,1,0:T(8,128)(2,1)S(1)}, u32[]{:S(2)}, u32[]{:S(2)}) collective-permute-start(bf16[2,4,96,384]{3,2,1,0:T(8,128)(2,1)} %get-tuple-element.157), channel_id=1, source_target_pairs={{0,8},{4,12},{8,0},{12,4},{1,9},{5,13},{9,1},{13,5},{2,10},{6,14},... | collective-permute-start | bytes 1769480 | tf_op jit(solution)/shard_map/ppermute | solution.py:468
  187.0 13.2 %collective-permute-start.40 = (bf16[1,4,96,384]{3,2,1,0:T(8,128)(2,1)}, bf16[1,4,96,384]{3,2,1,0:T(8,128)(2,1)S(1)}, u32[]{:S(2)}, u32[]{:S(2)}) collective-permute-start(bf16[1,4,96,384]{3,2,1,0:T(8,128)(2,1)} %get-tuple-element.154.rest_23_), channel_id=1, source_target_pairs={{0,16},{16,0},{1,17},{17,1},{2,18},{18,2},{3,19},{19,3},{4,20},{20... | collective-permute-start | bytes 884744 | tf_op jit(solution)/shard_map/ppermute | solution.py:468
  188.3 18.5 %collective-permute-start.41 = (bf16[1,4,96,384]{3,2,1,0:T(8,128)(2,1)}, bf16[1,4,96,384]{3,2,1,0:T(8,128)(2,1)S(1)}, u32[]{:S(2)}, u32[]{:S(2)}) collective-permute-start(bf16[1,4,96,384]{3,2,1,0:T(8,128)(2,1)} %get-tuple-element.158), channel_id=1, source_target_pairs={{0,8},{4,12},{8,0},{12,4},{1,9},{5,13},{9,1},{13,5},{2,10},{6,14},... | collective-permute-start | bytes 884744 | tf_op jit(solution)/shard_map/ppermute | solution.py:468
  189.2 18.4 %collective-permute-start.42 = (bf16[2,4,96,384]{3,2,1,0:T(8,128)(2,1)}, bf16[2,4,96,384]{3,2,1,0:T(8,128)(2,1)S(1)}, u32[]{:S(2)}, u32[]{:S(2)}) collective-permute-start(bf16[2,4,96,384]{3,2,1,0:T(8,128)(2,1)} %get-tuple-element.159), channel_id=1, source_target_pairs={{0,16},{16,0},{1,17},{17,1},{2,18},{18,2},{3,19},{19,3},{4,20},{20... | collective-permute-start | bytes 1769480 | tf_op jit(solution)/shard_map/ppermute | solution.py:468
  211.9 19.2 %collective-permute-start.44 = (bf16[1,4,96,384]{3,2,1,0:T(8,128)(2,1)}, bf16[1,4,96,384]{3,2,1,0:T(8,128)(2,1)S(1)}, u32[]{:S(2)}, u32[]{:S(2)}) collective-permute-start(bf16[1,4,96,384]{3,2,1,0:T(8,128)(2,1)} %get-tuple-element.161), channel_id=1, source_target_pairs={{0,16},{16,0},{1,17},{17,1},{2,18},{18,2},{3,19},{19,3},{4,20},{20... | collective-permute-start | bytes 884744 | tf_op jit(solution)/shard_map/ppermute | solution.py:468
  213.2 17.9 %collective-permute-start.45 = (bf16[1,4,96,384]{3,2,1,0:T(8,128)(2,1)}, bf16[1,4,96,384]{3,2,1,0:T(8,128)(2,1)S(1)}, u32[]{:S(2)}, u32[]{:S(2)}) collective-permute-start(bf16[1,4,96,384]{3,2,1,0:T(8,128)(2,1)} %get-tuple-element.162), channel_id=1, source_target_pairs={{0,8},{4,12},{8,0},{12,4},{1,9},{5,13},{9,1},{13,5},{2,10},{6,14},... | collective-permute-start | bytes 884744 | tf_op jit(solution)/shard_map/ppermute | solution.py:468
  214.1 6.6 %collective-permute-start.46 = (f32[16,768]{1,0:T(8,128)}, f32[16,768]{1,0:T(8,128)S(1)}, u32[]{:S(2)}, u32[]{:S(2)}) collective-permute-start(f32[16,768]{1,0:T(8,128)} %get-tuple-element.163), channel_id=1, source_target_pairs={{0,4},{4,0},{8,12},{12,8},{1,5},{5,1},{9,13},{13,9},{2,6},{6,2},{1... | collective-permute-start | bytes 147464 | tf_op jit(solution)/shard_map/ppermute | solution.py:468
  215.3 15.8 %collective-permute-start.49 = (bf16[96,1536]{1,0:T(8,128)(2,1)S(1)}, bf16[96,1536]{1,0:T(8,128)(2,1)S(1)}, u32[]{:S(2)}, u32[]{:S(2)}) collective-permute-start(bf16[96,1536]{1,0:T(8,128)(2,1)S(1)} %pad_maximum_fusion.10), channel_id=1, source_target_pairs={{0,1},{1,2},{2,3},{3,0},{4,5},{5,6},{6,7},{7,4},{8,9},{9,10},{10,1... | collective-permute-start | bytes 884744 | tf_op jit(solution)/shard_map/ppermute | solution.py:473
  219.4 6.9 %collective-permute-start.54 = (bf16[96,768]{1,0:T(8,128)(2,1)S(1)}, bf16[96,768]{1,0:T(8,128)(2,1)S(1)}, u32[]{:S(2)}, u32[]{:S(2)}) collective-permute-start(bf16[96,768]{1,0:T(8,128)(2,1)S(1)} %fusion.2), channel_id=1, source_target_pairs={{0,16},{16,0},{1,17},{17,1},{2,18},{18,2},{3,19},{19,3},{4,20},{20... | collective-permute-start | bytes 442376 | tf_op jit(solution)/shard_map/ppermute | solution.py:468
  224.9 16.8 %collective-permute-start.52 = (bf16[96,1536]{1,0:T(8,128)(2,1)S(1)}, bf16[96,1536]{1,0:T(8,128)(2,1)S(1)}, u32[]{:S(2)}, u32[]{:S(2)}) collective-permute-start(bf16[96,1536]{1,0:T(8,128)(2,1)S(1)} %pad_maximum_fusion.12), channel_id=1, source_target_pairs={{0,2},{1,3},{2,0},{3,1},{4,6},{5,7},{6,4},{7,5},{8,10},{9,11},{10,... | collective-permute-start | bytes 884744 | tf_op jit(solution)/shard_map/ppermute | solution.py:473
  236.6 10.6 %collective-permute-start.51 = (bf16[96,1536]{1,0:T(8,128)(2,1)S(1)}, bf16[96,1536]{1,0:T(8,128)(2,1)S(1)}, u32[]{:S(2)}, u32[]{:S(2)}) collective-permute-start(bf16[96,1536]{1,0:T(8,128)(2,1)S(1)} %pad_maximum_fusion.11), channel_id=1, source_target_pairs={{0,3},{1,0},{2,1},{3,2},{4,7},{5,4},{6,5},{7,6},{8,11},{9,8},{10,9... | collective-permute-start | bytes 884744 | tf_op jit(solution)/shard_map/ppermute | solution.py:473
  253.0 8.5 %collective-permute-start.55 = (bf16[96,1536]{1,0:T(8,128)(2,1)S(1)}, bf16[96,1536]{1,0:T(8,128)(2,1)S(1)}, u32[]{:S(2)}, u32[]{:S(2)}) collective-permute-start(bf16[96,1536]{1,0:T(8,128)(2,1)S(1)} %copy-done.12), channel_id=1, source_target_pairs={{0,16},{16,0},{1,17},{17,1},{2,18},{18,2},{3,19},{19,3},{4,20},{20... | collective-permute-start | bytes 884744 | tf_op jit(solution)/shard_map/ppermute | solution.py:468
  (64 other events, 290.0 us)

commit v6 on v5

--- a/solution.py
+++ b/solution.py
@@ -789,7 +789,7 @@
                         part = jnp.concatenate([s[:, :cut] for s in slots] + [s[:, cut:] for s in slots], axis=1)
                         mlp_moves[k1 + i] = part if k1 + i == 0 else shifted(part, -(k1 + i))
             if len(mlp_moves) < col_size:
-                smalls = sum_over(smalls, ("row", "dp"))
+                smalls = sum_over(smalls, ("row",))
                 late = [mlp_moves[col_size - 1]] if col_size - 1 in mlp_moves else []
                 token, passed = go_on(mlp_sums, token, [smalls] + late)
                 smalls = passed[0]
@@ -797,6 +797,7 @@
                     mlp_moves[col_size - 1] = passed[1]
     head_row, up_row = 5 + col_size, 5
     col_flips = [1 << n for n in range(col_size.bit_length() - 1)]
+    smalls = sum_over(smalls, ("dp",))
     for flip in col_flips[:-1]:
         smalls = smalls + flipped(smalls, "col", flip)
     smalls, *came = fence([smalls] + [mlp_moves[k] for k in range(1, col_size)])

time: 264 us -> 265 us (level)
    ppermute x44, waiting for transfers between devices: 26.9 us -> 34.6 us  [flipped(): lax.ppermute(value, axis, [(i, i ^ flip) for i in range(lax.axis_size(axi...]
    ppermute x12, waiting for transfers between devices: 21.7 us -> 16.1 us  [shifted(): lax.ppermute(value, 'col', [(i, (i + by) % size) for i in range(size)])]
  transfers between devices with their start and end apart: 56 -> 56, of which waited for: 16 -> 15; matrix products, arithmetic and copies ran while one was open for 10% -> 10% of each run, Pallas kernels for 36% -> 36%
where the time goes in v6:
time: 265 us; the launch traced here: 264 us
  Pallas kernels  104 us (39%)
  starting transfers between devices  57.7 us (22%)
  waiting for transfers between devices  50.7 us (19%)
  local copies, waits for them, and re-layouts  34.3 us (13%)
  other arithmetic  15.6 us (6%)
    pallas_call x4, Pallas kernels, block_part(): pl.pallas_call(functools.partial(kernel, orders, core_bit, len(after)), g...  51.9 us
    ppermute x44, waiting for transfers between devices, flipped(): lax.ppermute(value, axis, [(i, i ^ flip) for i in range(lax.axis_size(axi...  34.6 us
    ppermute x44, starting transfers between devices, flipped(): lax.ppermute(value, axis, [(i, i ^ flip) for i in range(lax.axis_size(axi...  31.7 us
    ppermute x12, starting transfers between devices, shifted(): lax.ppermute(value, 'col', [(i, (i + by) % size) for i in range(size)])  25.9 us
    pallas_call x6, Pallas kernels, merge(): pl.pallas_call(functools.partial(merge_kernel, layout, len(arrays), len(a...  18.5 us
    pallas_call x2, Pallas kernels, mlp_tail_part(): pl.pallas_call(functools.partial(mlp_tail_kernel, orders, core_bit, len(s...  17.7 us
    ppermute x12, waiting for transfers between devices, shifted(): lax.ppermute(value, 'col', [(i, (i + by) % size) for i in range(size)])  16.1 us
    unnamed x118, local copies, waits for them, and re-layouts  16.1 us
  transfers between devices with their start and end apart: 56, of which 15 were waited for; matrix products, arithmetic and copies ran while one was open for 10% of the time, Pallas kernels for 36%

profile of v6, /device:TPU:0, one launch (start us, length us, event | category | flops | bytes accessed | tf_op | source)
XLA Modules:
  0.0 264.2 jit_solution(2281388576120137887)
XLA Ops:
  3.1 5.1 %collective-permute-start.2 = (bf16[96,768]{1,0:T(8,128)(2,1)S(1)}, bf16[96,768]{1,0:T(8,128)(2,1)S(1)}, u32[]{:S(2)}, u32[]{:S(2)}) collective-permute-start(bf16[96,768]{1,0:T(8,128)(2,1)S(1)} %copy.77), channel_id=1, source_target_pairs={{0,3},{1,0},{2,1},{3,2},{4,7},{5,4},{6,5},{7,6},{8,11},{9,8},{10,9... | collective-permute-start | bytes 442376 | tf_op jit(solution)/shard_map/ppermute | solution.py:473
  14.5 1.3 constant_dynamic-slice_fusion.segr_ref
  15.8 4.9 %collective-permute-done.1 = bf16[96,768]{1,0:T(8,128)(2,1)S(1)} collective-permute-done((bf16[96,768]{1,0:T(8,128)(2,1)S(1)}, bf16[96,768]{1,0:T(8,128)(2,1)S(1)}, u32[]{:S(2)}, u32[]{:S(2)}) %collective-permute-start.1) | collective-permute-done | bytes 147488 | tf_op jit(solution)/shard_map/ppermute | solution.py:473
  20.9 1.6 collective-permute-start.6
  23.3 1.5 collective-permute-start.7
  24.8 6.0 %shard_map.255 = (bf16[512,768]{1,0:T(8,128)(2,1)}, bf16[768,512]{1,0:T(8,128)(2,1)}, bf16[512,768]{1,0:T(8,128)(2,1)}, bf16[768,512]{1,0:T(8,128)(2,1)}, bf16[7...) custom-call(bf16[512,768]{1,0:T(8,128)(2,1)} %rest_13_.1, ...), custom_call_target="tpu_custom_call" | custom-call | flops 6899999744 | bytes 1048576 | tf_op jit(solution)/shard_map/pallas_call | solution.py:124
  30.9 1.6 collective-permute-done.3.__3_.__1_
  35.4 1.6 collective-permute-start.8
  41.1 2.2 collective-permute-start.5
  44.6 9.6 %collective-permute-done.4.__2_ = bf16[96,1536]{1,0:T(8,128)(2,1)S(1)} collective-permute-done((bf16[96,1536]{1,0:T(8,128)(2,1)S(1)}, bf16[96,1536]{1,0:T(8,128)(2,1)S(1)}, u32[]{:S(2)}, u32[]{:S(2)}) %collective-permute-start.4) | collective-permute-done | bytes 294944 | tf_op jit(solution)/shard_map/ppermute | solution.py:473
  55.8 1.4 pad_maximum_fusion
  57.2 1.2 collective-permute-start.10
  59.6 15.1 %shard_map.259 = (bf16[2,512,768]{2,1,0:T(8,128)(2,1)}, bf16[2,512,384]{2,1,0:T(8,128)(2,1)}, f32[2,1,768]{2,1,0:T(1,128)}, bf16[8,4,96,384]{3,2,1,0:T(8,128)(2,1)}, bf16[8,4,96,384]{3,2,1,0:T(8,128)(2,1)}) custom-call(s32[2]{0:T(128)} %pad_add_fusion.me_ref, bf16[512,768]{1,0:T(8,128)(2,1)} %get-tuple-element.95.__2_.na_ref, ...), custom_call_target="tpu_custom_call" | custom-call | flops 23000000512 | bytes 1048576 | tf_op jit(solution)/shard_map/pallas_call | solution.py:270
  75.6 2.1 fusion.10
  80.8 14.9 %shard_map.261 = (bf16[2,512,768]{2,1,0:T(8,128)(2,1)}, bf16[2,512,384]{2,1,0:T(8,128)(2,1)}, f32[2,1,768]{2,1,0:T(1,128)}, bf16[8,4,96,384]{3,2,1,0:T(8,128)(2,1)}, bf16[8,4,96,384]{3,2,1,0:T(8,128)(2,1)}) custom-call(s32[2]{0:T(128)} %pad_add_fusion.me_ref, ...), custom_call_target="tpu_custom_call", output_to_operand_aliasing={{3}: (19, {}), {4}: (20, {})} | custom-call | flops 23000000512 | bytes 1048576 | tf_op jit(solution)/shard_map/pallas_call | solution.py:270
  99.2 1.8 pad_maximum_fusion.5.__1_
  102.7 10.2 %shard_map.263 = (f32[512,768]{1,0:T(8,128)}, f32[512,768]{1,0:T(8,128)}) custom-call(s32[2]{0:T(128)} %pad_add_fusion.me_ref, bf16[2,4,96,384]{3,2,1,0:T(8,128)(2,1)} %copy-done.19, bf16[2,4,96,384]{3,2,1,0:T(8,128)(2,1)} %get-tuple-element.98.__4_.rest_1_, bf16[2,4,96,384]{3,2,1,0:T(8,128)(2,1)} %collective-permute-done.12.rest_2_, ...), custom_call_target="tpu_custom_call" | custom-call | flops 12650000384 | bytes 1048576 | tf_op jit(solution)/shard_map/pallas_call | solution.py:404
  113.8 2.8 %collective-permute-done.17.__3_ = bf16[2,2,96,768]{3,2,1,0:T(8,128)(2,1)} collective-permute-done((bf16[2,2,96,768]{3,2,1,0:T(8,128)(2,1)}, bf16[2,2,96,768]{3,2,1,0:T(8,128)(2,1)}, u32[]{:S(2)}, u32[]{:S(2)}) %collective-permute-start.17) | collective-permute-done | bytes 589856 | tf_op jit(solution)/shard_map/ppermute | solution.py:468
  117.6 1.4 copy-done.3
  119.0 2.8 %shard_map.265 = (bf16[2,4,96,384]{3,2,1,0:T(8,128)(2,1)}, bf16[2,4,96,384]{3,2,1,0:T(8,128)(2,1)}) custom-call(bf16[8,4,96,384]{3,2,1,0:T(8,128)(2,1)} %get-tuple-element.130.refs_0_.refs_2_.refs_3_.refs_4_, bf16[8,4,96,384]{3,2,1,0:T(8,128)(2,1)} %copy-done.3, bf16[8,4,96,384]{3,2,1,0:T(8,128)(2,1)} %get-tuple-element.130.refs_0_.refs_2_.refs_3_.refs_4_, ...), custom_call_target="tpu_custom_call" | custom-call | flops 3449999872 | bytes 1048576 | tf_op jit(solution)/shard_map/pallas_call | solution.py:558
  123.9 11.0 %shard_map.266 = (bf16[2,512,768]{2,1,0:T(8,128)(2,1)}, bf16[2,512,768]{2,1,0:T(8,128)(2,1)}, f32[2,1,768]{2,1,0:T(1,128)}, bf16[8,4,96,384]{3,2,1,0:T(8,128)(2,1)}, bf16[8,4,96,384]{3,2,1,0:T(8,128)(2,1)}) custom-call(s32[2]{0:T(128)} %pad_add_fusion.me_ref, bf16[512,768]{1,0:T(8,128)(2,1)} %get-tuple-element.128.nm_ref, ...), custom_call_target="tpu_custom_call" | custom-call | flops 13799999488 | bytes 1048576 | tf_op jit(solution)/shard_map/pallas_call | solution.py:270
  135.0 2.4 collective-permute-done.29.refs_2_
  139.0 2.3 shard_map.267
  143.3 10.9 %shard_map.268 = (bf16[2,512,768]{2,1,0:T(8,128)(2,1)}, bf16[2,512,768]{2,1,0:T(8,128)(2,1)}, f32[2,1,768]{2,1,0:T(1,128)}, bf16[8,4,96,384]{3,2,1,0:T(8,128)(2,1)}, bf16[8,4,96,384]{3,2,1,0:T(8,128)(2,1)}) custom-call(s32[2]{0:T(128)} %pad_add_fusion.me_ref, bf16[512,768]{1,0:T(8,128)(2,1)} %get-tuple-element.128.nm_ref, ...), custom_call_target="tpu_custom_call" | custom-call | flops 13799999488 | bytes 1048576 | tf_op jit(solution)/shard_map/pallas_call | solution.py:270
  155.9 3.8 %shard_map.269 = (bf16[1,4,96,768]{3,2,1,0:T(8,128)(2,1)}, bf16[2,4,96,384]{3,2,1,0:T(8,128)(2,1)}, bf16[2,4,96,384]{3,2,1,0:T(8,128)(2,1)}, bf16[8,4,96,384]{3,2,1,0:T(8,128)(2,1)}) custom-call(bf16[8,4,96,384]{3,2,1,0:T(8,128)(2,1)} %get-tuple-element.130.refs_0_.refs_2_.refs_3_.refs_4_, ...), custom_call_target="tpu_custom_call", output_to_operand_aliasing={{3}: (12, {})} | custom-call | flops 3449999872 | bytes 1048576 | tf_op jit(solution)/shard_map/pallas_call | solution.py:558
  164.0 5.2 %collective-permute-start.37 = (bf16[96,768]{1,0:T(8,128)(2,1)S(1)}, bf16[96,768]{1,0:T(8,128)(2,1)S(1)}, u32[]{:S(2)}, u32[]{:S(2)}) collective-permute-start(bf16[96,768]{1,0:T(8,128)(2,1)S(1)} %get-tuple-element.224), channel_id=1, source_target_pairs={{0,2},{1,3},{2,0},{3,1},{4,6},{5,7},{6,4},{7,5},{8,10},{9,11},{10,... | collective-permute-start | bytes 442376 | tf_op jit(solution)/shard_map/ppermute | solution.py:473
  169.2 2.8 %collective-permute-start.38 = (bf16[96,768]{1,0:T(8,128)(2,1)S(1)}, bf16[96,768]{1,0:T(8,128)(2,1)S(1)}, u32[]{:S(2)}, u32[]{:S(2)}) collective-permute-start(bf16[96,768]{1,0:T(8,128)(2,1)S(1)} %get-tuple-element.223), channel_id=1, source_target_pairs={{0,1},{1,2},{2,3},{3,0},{4,5},{5,6},{6,7},{7,4},{8,9},{9,10},{10,1... | collective-permute-start | bytes 442376 | tf_op jit(solution)/shard_map/ppermute | solution.py:473
  172.0 7.4 %shard_map.270 = (f32[512,768]{1,0:T(8,128)}, f32[512,768]{1,0:T(8,128)}) custom-call(s32[2]{0:T(128)} %pad_add_fusion.me_ref, bf16[2,2,96,768]{3,2,1,0:T(8,128)(2,1)} %copy-done.18, bf16[2,2,96,768]{3,2,1,0:T(8,128)(2,1)} %get-tuple-element.123.rest_1_, bf16[2,2,96,768]{3,2,1,0:T(8,128)(2,1)} %copy-done.5, ...), custom_call_target="tpu_custom_call" | custom-call | flops 10350000128 | bytes 1048576 | tf_op jit(solution)/shard_map/pallas_call | solution.py:433
  179.4 1.3 collective-permute-start.43
  182.4 3.5 %shard_map.271 = (bf16[1,4,96,384]{3,2,1,0:T(8,128)(2,1)}, bf16[1,4,96,384]{3,2,1,0:T(8,128)(2,1)}, bf16[2,4,96,384]{3,2,1,0:T(8,128)(2,1)}, bf16[2,4,96,384]{3,...) custom-call(bf16[8,4,96,384]{3,2,1,0:T(8,128)(2,1)} %get-tuple-eleme, ...), custom_call_target="tpu_custom_call", output_to_operand_aliasing={{4}: (10, {}), {5}: (11, {})} | custom-call | flops 3449999872 | bytes 1048576 | tf_op jit(solution)/shard_map/pallas_call | solution.py:558
  187.0 1.2 collective-permute-start.40
  190.0 10.3 %shard_map.272 = (bf16[512,768]{1,0:T(8,128)(2,1)}, bf16[512,768]{1,0:T(8,128)(2,1)}, f32[16,768]{1,0:T(8,128)}) custom-call(s32[2]{0:T(128)} %pad_add_fusion.me_ref, bf16[2,2,96,768]{3,2,1,0:T(8,128)(2,1)} %get-tuple-element.124.rest_0_, bf16[2,2,96,768]{3,2,1,0:T(8,128)(2,1)} %get-tuple-element.125.refs_5_.rest_1_, bf16[2,2,96,768]{3,2,1,0:T(8,128)(2,1)} %copy-done.15, ...), custom_call_target="tpu_custom_call" | custom-call | flops 10350000128 | bytes 1048576 | tf_op jit(solution)/shard_map/pallas_call | solution.py:433
  200.3 6.5 %collective-permute-done.41.refs_7_ = bf16[1,4,96,384]{3,2,1,0:T(8,128)(2,1)S(1)} collective-permute-done((bf16[1,4,96,384]{3,2,1,0:T(8,128)(2,1)}, bf16[1,4,96,384]{3,2,1,0:T(8,128)(2,1)S(1)}, u32[]{:S(2)}, u32[]{:S(2)}) %collective-permute-start.41) | collective-permute-done | bytes 294944 | tf_op jit(solution)/shard_map/ppermute | solution.py:468
  208.4 3.4 %shard_map.273 = (bf16[1,4,96,768]{3,2,1,0:T(8,128)(2,1)}, bf16[1,4,96,384]{3,2,1,0:T(8,128)(2,1)}, bf16[1,4,96,384]{3,2,1,0:T(8,128)(2,1)}, f32[16,768]{1,0:T(8,128)}, bf16[96,768]{1,0:T(8,128)(2,1)}) custom-call(bf16[8,4,96,384]{3,2,1,0:T(8,128)(2,1)} %get-tuple-element.142.refs_8_.refs_10_.refs_0_.refs_3_.refs_4_, ...), custom_call_target="tpu_custom_call", output_to_operand_aliasing={{3}: (14, {}), {4}: (15, {})} | custom-call | flops 3449999872 | bytes 1048576 | tf_op jit(solution)/shard_map/pallas_call | solution.py:558
  211.9 1.3 collective-permute-start.44
  214.1 1.2 slice_bitcast_fusion.8
  215.3 3.0 %collective-permute-start.48 = (bf16[96,1536]{1,0:T(8,128)(2,1)S(1)}, bf16[96,1536]{1,0:T(8,128)(2,1)S(1)}, u32[]{:S(2)}, u32[]{:S(2)}) collective-permute-start(bf16[96,1536]{1,0:T(8,128)(2,1)S(1)} %pad_maximum_fusion.10), channel_id=1, source_target_pairs={{0,1},{1,2},{2,3},{3,0},{4,5},{5,6},{6,7},{7,4},{8,9},{9,10},{10,1... | collective-permute-start | bytes 884744 | tf_op jit(solution)/shard_map/ppermute | solution.py:473
  219.4 1.3 collective-permute-start.54
  220.7 1.2 collective-permute-start.47
  221.9 3.0 %collective-permute-done.47 = f32[16,768]{1,0:T(8,128)S(1)} collective-permute-done((f32[16,768]{1,0:T(8,128)S(1)}, f32[16,768]{1,0:T(8,128)S(1)}, u32[]{:S(2)}, u32[]{:S(2)}) %collective-permute-start.47) | collective-permute-done | bytes 49184 | tf_op jit(solution)/shard_map/ppermute | solution.py:468
  224.9 1.5 collective-permute-start.52
  228.7 2.7 %shard_map.274 = (bf16[1,4,96,768]{3,2,1,0:T(8,128)(2,1)}, f32[16,768]{1,0:T(8,128)}, bf16[96,1536]{1,0:T(8,128)(2,1)}) custom-call(bf16[8,4,96,384]{3,2,1,0:T(8,128)(2,1)} %get-tuple-element.152.refs_6_.refs_8_.refs_11_.refs_0_.refs_4_, bf16[8,4,96,384]{3,2,1,0:T(8,128)(2,1)} %copy-done.4, ...), custom_call_target="tpu_custom_call", output_to_operand_aliasing={{1}: (8, {}), {2}: (9, {})} | custom-call | flops 3449999872 | bytes 1048576 | tf_op jit(solution)/shard_map/pallas_call | solution.py:558
  232.5 1.2 slice_bitcast_fusion.6
  233.8 2.1 collective-permute-start.51
  236.0 11.3 %collective-permute-done.50 = f32[16,768]{1,0:T(8,128)S(1)} collective-permute-done((f32[16,768]{1,0:T(8,128)S(1)}, f32[16,768]{1,0:T(8,128)S(1)}, u32[]{:S(2)}, u32[]{:S(2)}) %collective-permute-start.50) | collective-permute-done | bytes 49184 | tf_op jit(solution)/shard_map/ppermute | solution.py:468
  248.7 2.0 add_convert_fusion.__1_
  254.2 1.7 collective-permute-done.53
  257.9 4.4 %collective-permute-done.55 = bf16[96,1536]{1,0:T(8,128)(2,1)S(1)} collective-permute-done((bf16[96,1536]{1,0:T(8,128)(2,1)S(1)}, bf16[96,1536]{1,0:T(8,128)(2,1)S(1)}, u32[]{:S(2)}, u32[]{:S(2)}) %collective-permute-start.55) | collective-permute-done | bytes 294944 | tf_op jit(solution)/shard_map/ppermute | solution.py:468
  (277 shorter events, 64.0 us)
Async XLA Ops:
  3.1 12.7 %collective-permute-start.2 = (bf16[96,768]{1,0:T(8,128)(2,1)S(1)}, bf16[96,768]{1,0:T(8,128)(2,1)S(1)}, u32[]{:S(2)}, u32[]{:S(2)}) collective-permute-start(bf16[96,768]{1,0:T(8,128)(2,1)S(1)} %copy.77), channel_id=1, source_target_pairs={{0,3},{1,0},{2,1},{3,2},{4,7},{5,4},{6,5},{7,6},{8,11},{9,8},{10,9... | collective-permute-start | bytes 442376 | tf_op jit(solution)/shard_map/ppermute | solution.py:473
  8.2 12.5 %collective-permute-start.1 = (bf16[96,768]{1,0:T(8,128)(2,1)S(1)}, bf16[96,768]{1,0:T(8,128)(2,1)S(1)}, u32[]{:S(2)}, u32[]{:S(2)}) collective-permute-start(bf16[96,768]{1,0:T(8,128)(2,1)S(1)} %copy.77), channel_id=1, source_target_pairs={{0,2},{1,3},{2,0},{3,1},{4,6},{5,7},{6,4},{7,5},{8,10},{9,11},{10,... | collective-permute-start | bytes 442376 | tf_op jit(solution)/shard_map/ppermute | solution.py:473
  8.2 12.5 %collective-permute-start = (bf16[96,768]{1,0:T(8,128)(2,1)S(1)}, bf16[96,768]{1,0:T(8,128)(2,1)S(1)}, u32[]{:S(2)}, u32[]{:S(2)}) collective-permute-start(bf16[96,768]{1,0:T(8,128)(2,1)S(1)} %copy.77), channel_id=1, source_target_pairs={{0,1},{1,2},{2,3},{3,0},{4,5},{5,6},{6,7},{7,4},{8,9},{9,10},{10,1... | collective-permute-start | bytes 442376 | tf_op jit(solution)/shard_map/ppermute | solution.py:473
  20.9 11.6 %collective-permute-start.6 = (bf16[1,4,96,384]{3,2,1,0:T(8,128)(2,1)S(1)}, bf16[1,4,96,384]{3,2,1,0:T(8,128)(2,1)S(1)}, u32[]{:S(2)}, u32[]{:S(2)}) collective-permute-start(bf16[1,4,96,384]{3,2,1,0:T(8,128)(2,1)S(1)} %get-tuple-element.234.__1_), channel_id=1, source_target_pairs={{0,8},{4,12},{8,0},{12,4},{1,9},{5,13},{9,1},{13,5},{2,10},{6,14},... | collective-permute-start | bytes 884744 | tf_op jit(solution)/shard_map/ppermute | solution.py:468
  22.4 10.0 %collective-permute-start.3 = (bf16[96,1536]{1,0:T(8,128)(2,1)}, bf16[96,1536]{1,0:T(8,128)(2,1)S(1)}, u32[]{:S(2)}, u32[]{:S(2)}) collective-permute-start(bf16[96,1536]{1,0:T(8,128)(2,1)} %shard_map.254.__0_), channel_id=1, source_target_pairs={{0,1},{1,2},{2,3},{3,0},{4,5},{5,6},{6,7},{7,4},{8,9},{9,10},{10,1... | collective-permute-start | bytes 884744 | tf_op jit(solution)/shard_map/ppermute | solution.py:473
  23.3 9.2 %collective-permute-start.7 = (bf16[1,4,96,384]{3,2,1,0:T(8,128)(2,1)S(1)}, bf16[1,4,96,384]{3,2,1,0:T(8,128)(2,1)S(1)}, u32[]{:S(2)}, u32[]{:S(2)}) collective-permute-start(bf16[1,4,96,384]{3,2,1,0:T(8,128)(2,1)S(1)} %get-tuple-element.233), channel_id=1, source_target_pairs={{0,16},{16,0},{1,17},{17,1},{2,18},{18,2},{3,19},{19,3},{4,20},{20... | collective-permute-start | bytes 884744 | tf_op jit(solution)/shard_map/ppermute | solution.py:468
  35.4 18.9 %collective-permute-start.8 = (bf16[2,4,96,384]{3,2,1,0:T(8,128)(2,1)S(1)}, bf16[2,4,96,384]{3,2,1,0:T(8,128)(2,1)S(1)}, u32[]{:S(2)}, u32[]{:S(2)}) collective-permute-start(bf16[2,4,96,384]{3,2,1,0:T(8,128)(2,1)S(1)} %pad_maximum_fusion.2.rest_0_), channel_id=1, source_target_pairs={{0,16},{16,0},{1,17},{17,1},{2,18},{18,2},{3,19},{19,3},{4,20},{20... | collective-permute-start | bytes 1769480 | tf_op jit(solution)/shard_map/ppermute | solution.py:468
  38.0 16.3 %collective-permute-start.9 = (bf16[2,4,96,384]{3,2,1,0:T(8,128)(2,1)S(1)}, bf16[2,4,96,384]{3,2,1,0:T(8,128)(2,1)}, u32[]{:S(2)}, u32[]{:S(2)}) collective-permute-start(bf16[2,4,96,384]{3,2,1,0:T(8,128)(2,1)S(1)} %pad_maximum_fusion.3.rest_4_), channel_id=1, source_target_pairs={{0,8},{4,12},{8,0},{12,4},{1,9},{5,13},{9,1},{13,5},{2,10},{6,14},... | collective-permute-start | bytes 1769480 | tf_op jit(solution)/shard_map/ppermute | solution.py:468
  40.2 14.0 %collective-permute-start.4 = (bf16[96,1536]{1,0:T(8,128)(2,1)S(1)}, bf16[96,1536]{1,0:T(8,128)(2,1)S(1)}, u32[]{:S(2)}, u32[]{:S(2)}) collective-permute-start(bf16[96,1536]{1,0:T(8,128)(2,1)S(1)} %copy-done.11), channel_id=1, source_target_pairs={{0,2},{1,3},{2,0},{3,1},{4,6},{5,7},{6,4},{7,5},{8,10},{9,11},{10,... | collective-permute-start | bytes 884744 | tf_op jit(solution)/shard_map/ppermute | solution.py:473
  41.1 13.1 %collective-permute-start.5 = (bf16[96,1536]{1,0:T(8,128)(2,1)S(1)}, bf16[96,1536]{1,0:T(8,128)(2,1)S(1)}, u32[]{:S(2)}, u32[]{:S(2)}) collective-permute-start(bf16[96,1536]{1,0:T(8,128)(2,1)S(1)} %copy-done.11), channel_id=1, source_target_pairs={{0,3},{1,0},{2,1},{3,2},{4,7},{5,4},{6,5},{7,6},{8,11},{9,8},{10,9... | collective-permute-start | bytes 884744 | tf_op jit(solution)/shard_map/ppermute | solution.py:473
  44.6 13.9 %collective-permute-start.12 = (bf16[2,4,96,384]{3,2,1,0:T(8,128)(2,1)S(1)}, bf16[2,4,96,384]{3,2,1,0:T(8,128)(2,1)}, u32[]{:S(2)}, u32[]{:S(2)}) collective-permute-start(bf16[2,4,96,384]{3,2,1,0:T(8,128)(2,1)S(1)} %pad_maximum_fusion.2.rest_0_), channel_id=1, source_target_pairs={{0,4},{4,0},{8,12},{12,8},{1,5},{5,1},{9,13},{13,9},{2,6},{6,2},{1... | collective-permute-start | bytes 1769480 | tf_op jit(solution)/shard_map/ppermute | solution.py:468
  57.2 17.5 %collective-permute-start.10 = (bf16[1,4,96,768]{3,2,1,0:T(8,128)(2,1)S(1)}, bf16[1,4,96,768]{3,2,1,0:T(8,128)(2,1)}, u32[]{:S(2)}, u32[]{:S(2)}) collective-permute-start(bf16[1,4,96,768]{3,2,1,0:T(8,128)(2,1)S(1)} %get-tuple-element.211), channel_id=1, source_target_pairs={{0,8},{4,12},{8,0},{12,4},{1,9},{5,13},{9,1},{13,5},{2,10},{6,14},... | collective-permute-start | bytes 1769480 | tf_op jit(solution)/shard_map/ppermute | solution.py:468
  58.6 16.2 %collective-permute-start.11 = (bf16[1,4,96,768]{3,2,1,0:T(8,128)(2,1)S(1)}, bf16[1,4,96,768]{3,2,1,0:T(8,128)(2,1)S(1)}, u32[]{:S(2)}, u32[]{:S(2)}) collective-permute-start(bf16[1,4,96,768]{3,2,1,0:T(8,128)(2,1)S(1)} %get-tuple-element.210), channel_id=1, source_target_pairs={{0,16},{16,0},{1,17},{17,1},{2,18},{18,2},{3,19},{19,3},{4,20},{20... | collective-permute-start | bytes 1769480 | tf_op jit(solution)/shard_map/ppermute | solution.py:468
  77.8 17.9 %collective-permute-start.18 = (bf16[2,2,96,768]{3,2,1,0:T(8,128)(2,1)S(1)}, bf16[2,2,96,768]{3,2,1,0:T(8,128)(2,1)}, u32[]{:S(2)}, u32[]{:S(2)}) collective-permute-start(bf16[2,2,96,768]{3,2,1,0:T(8,128)(2,1)S(1)} %pad_maximum_fusion.6.rest_13_.rest_0_), channel_id=1, source_target_pairs={{0,16},{16,0},{1,17},{17,1},{2,18},{18,2},{3,19},{19,3},{4,20},{20... | collective-permute-start | bytes 1769480 | tf_op jit(solution)/shard_map/ppermute | solution.py:468
  78.9 16.9 %collective-permute-start.20 = (bf16[2,2,96,768]{3,2,1,0:T(8,128)(2,1)S(1)}, bf16[2,2,96,768]{3,2,1,0:T(8,128)(2,1)S(1)}, u32[]{:S(2)}, u32[]{:S(2)}) collective-permute-start(bf16[2,2,96,768]{3,2,1,0:T(8,128)(2,1)S(1)} %pad_maximum_fusion.6.rest_13_.rest_0_), channel_id=1, source_target_pairs={{0,4},{4,0},{8,12},{12,8},{1,5},{5,1},{9,13},{13,9},{2,6},{6,2},{1... | collective-permute-start | bytes 1769480 | tf_op jit(solution)/shard_map/ppermute | solution.py:468
  79.8 16.1 %collective-permute-start.19 = (bf16[2,2,96,768]{3,2,1,0:T(8,128)(2,1)}, bf16[2,2,96,768]{3,2,1,0:T(8,128)(2,1)}, u32[]{:S(2)}, u32[]{:S(2)}) collective-permute-start(bf16[2,2,96,768]{3,2,1,0:T(8,128)(2,1)} %pad_maximum_fusion.7.rest_4_), channel_id=1, source_target_pairs={{0,8},{4,12},{8,0},{12,4},{1,9},{5,13},{9,1},{13,5},{2,10},{6,14},... | collective-permute-start | bytes 1769480 | tf_op jit(solution)/shard_map/ppermute | solution.py:468
  80.6 15.2 %collective-permute-start.21 = (bf16[2,2,96,768]{3,2,1,0:T(8,128)(2,1)}, bf16[2,2,96,768]{3,2,1,0:T(8,128)(2,1)S(1)}, u32[]{:S(2)}, u32[]{:S(2)}) collective-permute-start(bf16[2,2,96,768]{3,2,1,0:T(8,128)(2,1)} %pad_maximum_fusion.7.rest_4_), channel_id=1, source_target_pairs={{0,4},{4,0},{8,12},{12,8},{1,5},{5,1},{9,13},{13,9},{2,6},{6,2},{1... | collective-permute-start | bytes 1769480 | tf_op jit(solution)/shard_map/ppermute | solution.py:468
  96.8 20.8 %collective-permute-start.28 = (bf16[8,4,96,384]{3,2,1,0:T(8,128)(2,1)}, bf16[8,4,96,384]{3,2,1,0:T(8,128)(2,1)S(1)}, u32[]{:S(2)}, u32[]{:S(2)}) collective-permute-start(bf16[8,4,96,384]{3,2,1,0:T(8,128)(2,1)} %get-tuple-element.131), channel_id=1, source_target_pairs={{0,4},{4,0},{8,12},{12,8},{1,5},{5,1},{9,13},{13,9},{2,6},{6,2},{1... | collective-permute-start | bytes 7077896 | tf_op jit(solution)/shard_map/ppermute | solution.py:468
  98.1 15.7 %collective-permute-start.16 = (bf16[2,2,96,768]{3,2,1,0:T(8,128)(2,1)S(1)}, bf16[2,2,96,768]{3,2,1,0:T(8,128)(2,1)}, u32[]{:S(2)}, u32[]{:S(2)}) collective-permute-start(bf16[2,2,96,768]{3,2,1,0:T(8,128)(2,1)S(1)} %pad_maximum_fusion.4.__0_), channel_id=1, source_target_pairs={{0,16},{16,0},{1,17},{17,1},{2,18},{18,2},{3,19},{19,3},{4,20},{20... | collective-permute-start | bytes 1769480 | tf_op jit(solution)/shard_map/ppermute | solution.py:468
  101.0 15.5 %collective-permute-start.17 = (bf16[2,2,96,768]{3,2,1,0:T(8,128)(2,1)}, bf16[2,2,96,768]{3,2,1,0:T(8,128)(2,1)}, u32[]{:S(2)}, u32[]{:S(2)}) collective-permute-start(bf16[2,2,96,768]{3,2,1,0:T(8,128)(2,1)} %pad_maximum_fusion.5.__1_), channel_id=1, source_target_pairs={{0,8},{4,12},{8,0},{12,4},{1,9},{5,13},{9,1},{13,5},{2,10},{6,14},... | collective-permute-start | bytes 1769480 | tf_op jit(solution)/shard_map/ppermute | solution.py:468
  102.2 14.4 %collective-permute-start.22 = (bf16[2,2,96,768]{3,2,1,0:T(8,128)(2,1)}, bf16[2,2,96,768]{3,2,1,0:T(8,128)(2,1)}, u32[]{:S(2)}, u32[]{:S(2)}) collective-permute-start(bf16[2,2,96,768]{3,2,1,0:T(8,128)(2,1)} %get-tuple-element.123.rest_1_), channel_id=1, source_target_pairs={{0,4},{4,0},{8,12},{12,8},{1,5},{5,1},{9,13},{13,9},{2,6},{6,2},{1... | collective-permute-start | bytes 1769480 | tf_op jit(solution)/shard_map/ppermute | solution.py:468
  102.2 14.4 %collective-permute-start.23 = (bf16[2,2,96,768]{3,2,1,0:T(8,128)(2,1)}, bf16[2,2,96,768]{3,2,1,0:T(8,128)(2,1)}, u32[]{:S(2)}, u32[]{:S(2)}) collective-permute-start(bf16[2,2,96,768]{3,2,1,0:T(8,128)(2,1)} %get-tuple-element.121.rest_12_.rest_5_), channel_id=1, source_target_pairs={{0,4},{4,0},{8,12},{12,8},{1,5},{5,1},{9,13},{13,9},{2,6},{6,2},{1... | collective-permute-start | bytes 1769480 | tf_op jit(solution)/shard_map/ppermute | solution.py:468
  116.6 18.3 %collective-permute-start.25 = (bf16[2,2,96,768]{3,2,1,0:T(8,128)(2,1)}, bf16[2,2,96,768]{3,2,1,0:T(8,128)(2,1)}, u32[]{:S(2)}, u32[]{:S(2)}) collective-permute-start(bf16[2,2,96,768]{3,2,1,0:T(8,128)(2,1)} %get-tuple-element.125.refs_5_.rest_1_), channel_id=1, source_target_pairs={{0,4},{4,0},{8,12},{12,8},{1,5},{5,1},{9,13},{13,9},{2,6},{6,2},{1... | collective-permute-start | bytes 1769480 | tf_op jit(solution)/shard_map/ppermute | solution.py:468
  117.1 17.8 %collective-permute-start.26 = (bf16[2,2,96,768]{3,2,1,0:T(8,128)(2,1)}, bf16[2,2,96,768]{3,2,1,0:T(8,128)(2,1)}, u32[]{:S(2)}, u32[]{:S(2)}) collective-permute-start(bf16[2,2,96,768]{3,2,1,0:T(8,128)(2,1)} %get-tuple-element.126.rest_4_), channel_id=1, source_target_pairs={{0,4},{4,0},{8,12},{12,8},{1,5},{5,1},{9,13},{13,9},{2,6},{6,2},{1... | collective-permute-start | bytes 1769480 | tf_op jit(solution)/shard_map/ppermute | solution.py:468
  117.2 17.7 %collective-permute-start.27 = (bf16[2,2,96,768]{3,2,1,0:T(8,128)(2,1)}, bf16[2,2,96,768]{3,2,1,0:T(8,128)(2,1)}, u32[]{:S(2)}, u32[]{:S(2)}) collective-permute-start(bf16[2,2,96,768]{3,2,1,0:T(8,128)(2,1)} %get-tuple-element.127.rest_5_), channel_id=1, source_target_pairs={{0,4},{4,0},{8,12},{12,8},{1,5},{5,1},{9,13},{13,9},{2,6},{6,2},{1... | collective-permute-start | bytes 1769480 | tf_op jit(solution)/shard_map/ppermute | solution.py:468
  121.8 15.5 %collective-permute-start.29 = (bf16[2,4,96,384]{3,2,1,0:T(8,128)(2,1)}, bf16[2,4,96,384]{3,2,1,0:T(8,128)(2,1)S(1)}, u32[]{:S(2)}, u32[]{:S(2)}) collective-permute-start(bf16[2,4,96,384]{3,2,1,0:T(8,128)(2,1)} %get-tuple-element.132.rest_9_), channel_id=1, source_target_pairs={{0,8},{4,12},{8,0},{12,4},{1,9},{5,13},{9,1},{13,5},{2,10},{6,14},... | collective-permute-start | bytes 1769480 | tf_op jit(solution)/shard_map/ppermute | solution.py:468
  122.9 15.2 %collective-permute-start.30 = (bf16[2,4,96,384]{3,2,1,0:T(8,128)(2,1)}, bf16[2,4,96,384]{3,2,1,0:T(8,128)(2,1)S(1)}, u32[]{:S(2)}, u32[]{:S(2)}) collective-permute-start(bf16[2,4,96,384]{3,2,1,0:T(8,128)(2,1)} %get-tuple-element.133), channel_id=1, source_target_pairs={{0,16},{16,0},{1,17},{17,1},{2,18},{18,2},{3,19},{19,3},{4,20},{20... | collective-permute-start | bytes 1769480 | tf_op jit(solution)/shard_map/ppermute | solution.py:468
  141.3 12.9 %collective-permute-start.33 = (bf16[8,4,96,384]{3,2,1,0:T(8,128)(2,1)}, bf16[8,4,96,384]{3,2,1,0:T(8,128)(2,1)S(1)}, u32[]{:S(2)}, u32[]{:S(2)}) collective-permute-start(bf16[8,4,96,384]{3,2,1,0:T(8,128)(2,1)} %get-tuple-element.143), channel_id=1, source_target_pairs={{0,4},{4,0},{8,12},{12,8},{1,5},{5,1},{9,13},{13,9},{2,6},{6,2},{1... | collective-permute-start | bytes 7077896 | tf_op jit(solution)/shard_map/ppermute | solution.py:468
  141.3 12.9 %collective-permute-start.31 = (bf16[1,4,96,384]{3,2,1,0:T(8,128)(2,1)}, bf16[1,4,96,384]{3,2,1,0:T(8,128)(2,1)S(1)}, u32[]{:S(2)}, u32[]{:S(2)}) collective-permute-start(bf16[1,4,96,384]{3,2,1,0:T(8,128)(2,1)} %get-tuple-element.136.rest_9_), channel_id=1, source_target_pairs={{0,16},{16,0},{1,17},{17,1},{2,18},{18,2},{3,19},{19,3},{4,20},{20... | collective-permute-start | bytes 884744 | tf_op jit(solution)/shard_map/ppermute | solution.py:468
  142.3 11.9 %collective-permute-start.32 = (bf16[1,4,96,384]{3,2,1,0:T(8,128)(2,1)}, bf16[1,4,96,384]{3,2,1,0:T(8,128)(2,1)S(1)}, u32[]{:S(2)}, u32[]{:S(2)}) collective-permute-start(bf16[1,4,96,384]{3,2,1,0:T(8,128)(2,1)} %get-tuple-element.141), channel_id=1, source_target_pairs={{0,8},{4,12},{8,0},{12,4},{1,9},{5,13},{9,1},{13,5},{2,10},{6,14},... | collective-permute-start | bytes 884744 | tf_op jit(solution)/shard_map/ppermute | solution.py:468
  159.6 21.1 %collective-permute-start.36 = (bf16[8,4,96,384]{3,2,1,0:T(8,128)(2,1)}, bf16[8,4,96,384]{3,2,1,0:T(8,128)(2,1)S(1)}, u32[]{:S(2)}, u32[]{:S(2)}) collective-permute-start(bf16[8,4,96,384]{3,2,1,0:T(8,128)(2,1)} %get-tuple-element.153), channel_id=1, source_target_pairs={{0,4},{4,0},{8,12},{12,8},{1,5},{5,1},{9,13},{13,9},{2,6},{6,2},{1... | collective-permute-start | bytes 7077896 | tf_op jit(solution)/shard_map/ppermute | solution.py:468
  160.8 19.9 %collective-permute-start.34 = (bf16[2,4,96,384]{3,2,1,0:T(8,128)(2,1)}, bf16[2,4,96,384]{3,2,1,0:T(8,128)(2,1)S(1)}, u32[]{:S(2)}, u32[]{:S(2)}) collective-permute-start(bf16[2,4,96,384]{3,2,1,0:T(8,128)(2,1)} %get-tuple-element.150), channel_id=1, source_target_pairs={{0,8},{4,12},{8,0},{12,4},{1,9},{5,13},{9,1},{13,5},{2,10},{6,14},... | collective-permute-start | bytes 1769480 | tf_op jit(solution)/shard_map/ppermute | solution.py:468
  161.9 18.8 %collective-permute-start.35 = (bf16[2,4,96,384]{3,2,1,0:T(8,128)(2,1)}, bf16[2,4,96,384]{3,2,1,0:T(8,128)(2,1)}, u32[]{:S(2)}, u32[]{:S(2)}) collective-permute-start(bf16[2,4,96,384]{3,2,1,0:T(8,128)(2,1)} %get-tuple-element.151), channel_id=1, source_target_pairs={{0,16},{16,0},{1,17},{17,1},{2,18},{18,2},{3,19},{19,3},{4,20},{20... | collective-permute-start | bytes 1769480 | tf_op jit(solution)/shard_map/ppermute | solution.py:468
  164.0 15.4 %collective-permute-start.37 = (bf16[96,768]{1,0:T(8,128)(2,1)S(1)}, bf16[96,768]{1,0:T(8,128)(2,1)S(1)}, u32[]{:S(2)}, u32[]{:S(2)}) collective-permute-start(bf16[96,768]{1,0:T(8,128)(2,1)S(1)} %get-tuple-element.224), channel_id=1, source_target_pairs={{0,2},{1,3},{2,0},{3,1},{4,6},{5,7},{6,4},{7,5},{8,10},{9,11},{10,... | collective-permute-start | bytes 442376 | tf_op jit(solution)/shard_map/ppermute | solution.py:473
  169.2 11.5 %collective-permute-start.38 = (bf16[96,768]{1,0:T(8,128)(2,1)S(1)}, bf16[96,768]{1,0:T(8,128)(2,1)S(1)}, u32[]{:S(2)}, u32[]{:S(2)}) collective-permute-start(bf16[96,768]{1,0:T(8,128)(2,1)S(1)} %get-tuple-element.223), channel_id=1, source_target_pairs={{0,1},{1,2},{2,3},{3,0},{4,5},{5,6},{6,7},{7,4},{8,9},{9,10},{10,1... | collective-permute-start | bytes 442376 | tf_op jit(solution)/shard_map/ppermute | solution.py:473
  179.4 20.9 %collective-permute-start.43 = (bf16[96,768]{1,0:T(8,128)(2,1)S(1)}, bf16[96,768]{1,0:T(8,128)(2,1)S(1)}, u32[]{:S(2)}, u32[]{:S(2)}) collective-permute-start(bf16[96,768]{1,0:T(8,128)(2,1)S(1)} %get-tuple-element.222), channel_id=1, source_target_pairs={{0,3},{1,0},{2,1},{3,2},{4,7},{5,4},{6,5},{7,6},{8,11},{9,8},{10,9... | collective-permute-start | bytes 442376 | tf_op jit(solution)/shard_map/ppermute | solution.py:473
  185.9 20.9 %collective-permute-start.39 = (bf16[2,4,96,384]{3,2,1,0:T(8,128)(2,1)}, bf16[2,4,96,384]{3,2,1,0:T(8,128)(2,1)S(1)}, u32[]{:S(2)}, u32[]{:S(2)}) collective-permute-start(bf16[2,4,96,384]{3,2,1,0:T(8,128)(2,1)} %get-tuple-element.157), channel_id=1, source_target_pairs={{0,8},{4,12},{8,0},{12,4},{1,9},{5,13},{9,1},{13,5},{2,10},{6,14},... | collective-permute-start | bytes 1769480 | tf_op jit(solution)/shard_map/ppermute | solution.py:468
  187.0 13.2 %collective-permute-start.40 = (bf16[1,4,96,384]{3,2,1,0:T(8,128)(2,1)}, bf16[1,4,96,384]{3,2,1,0:T(8,128)(2,1)S(1)}, u32[]{:S(2)}, u32[]{:S(2)}) collective-permute-start(bf16[1,4,96,384]{3,2,1,0:T(8,128)(2,1)} %get-tuple-element.154.rest_23_), channel_id=1, source_target_pairs={{0,16},{16,0},{1,17},{17,1},{2,18},{18,2},{3,19},{19,3},{4,20},{20... | collective-permute-start | bytes 884744 | tf_op jit(solution)/shard_map/ppermute | solution.py:468
  188.3 18.5 %collective-permute-start.41 = (bf16[1,4,96,384]{3,2,1,0:T(8,128)(2,1)}, bf16[1,4,96,384]{3,2,1,0:T(8,128)(2,1)S(1)}, u32[]{:S(2)}, u32[]{:S(2)}) collective-permute-start(bf16[1,4,96,384]{3,2,1,0:T(8,128)(2,1)} %get-tuple-element.158), channel_id=1, source_target_pairs={{0,8},{4,12},{8,0},{12,4},{1,9},{5,13},{9,1},{13,5},{2,10},{6,14},... | collective-permute-start | bytes 884744 | tf_op jit(solution)/shard_map/ppermute | solution.py:468
  189.2 18.4 %collective-permute-start.42 = (bf16[2,4,96,384]{3,2,1,0:T(8,128)(2,1)}, bf16[2,4,96,384]{3,2,1,0:T(8,128)(2,1)S(1)}, u32[]{:S(2)}, u32[]{:S(2)}) collective-permute-start(bf16[2,4,96,384]{3,2,1,0:T(8,128)(2,1)} %get-tuple-element.159), channel_id=1, source_target_pairs={{0,16},{16,0},{1,17},{17,1},{2,18},{18,2},{3,19},{19,3},{4,20},{20... | collective-permute-start | bytes 1769480 | tf_op jit(solution)/shard_map/ppermute | solution.py:468
  211.9 15.2 %collective-permute-start.44 = (bf16[1,4,96,384]{3,2,1,0:T(8,128)(2,1)}, bf16[1,4,96,384]{3,2,1,0:T(8,128)(2,1)S(1)}, u32[]{:S(2)}, u32[]{:S(2)}) collective-permute-start(bf16[1,4,96,384]{3,2,1,0:T(8,128)(2,1)} %get-tuple-element.161), channel_id=1, source_target_pairs={{0,16},{16,0},{1,17},{17,1},{2,18},{18,2},{3,19},{19,3},{4,20},{20... | collective-permute-start | bytes 884744 | tf_op jit(solution)/shard_map/ppermute | solution.py:468
  213.2 14.0 %collective-permute-start.45 = (bf16[1,4,96,384]{3,2,1,0:T(8,128)(2,1)}, bf16[1,4,96,384]{3,2,1,0:T(8,128)(2,1)S(1)}, u32[]{:S(2)}, u32[]{:S(2)}) collective-permute-start(bf16[1,4,96,384]{3,2,1,0:T(8,128)(2,1)} %get-tuple-element.162), channel_id=1, source_target_pairs={{0,8},{4,12},{8,0},{12,4},{1,9},{5,13},{9,1},{13,5},{2,10},{6,14},... | collective-permute-start | bytes 884744 | tf_op jit(solution)/shard_map/ppermute | solution.py:468
  215.3 11.9 %collective-permute-start.48 = (bf16[96,1536]{1,0:T(8,128)(2,1)S(1)}, bf16[96,1536]{1,0:T(8,128)(2,1)S(1)}, u32[]{:S(2)}, u32[]{:S(2)}) collective-permute-start(bf16[96,1536]{1,0:T(8,128)(2,1)S(1)} %pad_maximum_fusion.10), channel_id=1, source_target_pairs={{0,1},{1,2},{2,3},{3,0},{4,5},{5,6},{6,7},{7,4},{8,9},{9,10},{10,1... | collective-permute-start | bytes 884744 | tf_op jit(solution)/shard_map/ppermute | solution.py:473
  219.4 7.5 %collective-permute-start.54 = (bf16[96,768]{1,0:T(8,128)(2,1)S(1)}, bf16[96,768]{1,0:T(8,128)(2,1)S(1)}, u32[]{:S(2)}, u32[]{:S(2)}) collective-permute-start(bf16[96,768]{1,0:T(8,128)(2,1)S(1)} %fusion.2), channel_id=1, source_target_pairs={{0,16},{16,0},{1,17},{17,1},{2,18},{18,2},{3,19},{19,3},{4,20},{20... | collective-permute-start | bytes 442376 | tf_op jit(solution)/shard_map/ppermute | solution.py:468
  224.9 23.0 %collective-permute-start.52 = (bf16[96,1536]{1,0:T(8,128)(2,1)S(1)}, bf16[96,1536]{1,0:T(8,128)(2,1)S(1)}, u32[]{:S(2)}, u32[]{:S(2)}) collective-permute-start(bf16[96,1536]{1,0:T(8,128)(2,1)S(1)} %pad_maximum_fusion.12), channel_id=1, source_target_pairs={{0,2},{1,3},{2,0},{3,1},{4,6},{5,7},{6,4},{7,5},{8,10},{9,11},{10,... | collective-permute-start | bytes 884744 | tf_op jit(solution)/shard_map/ppermute | solution.py:473
  233.8 14.1 %collective-permute-start.51 = (bf16[96,1536]{1,0:T(8,128)(2,1)S(1)}, bf16[96,1536]{1,0:T(8,128)(2,1)S(1)}, u32[]{:S(2)}, u32[]{:S(2)}) collective-permute-start(bf16[96,1536]{1,0:T(8,128)(2,1)S(1)} %pad_maximum_fusion.11), channel_id=1, source_target_pairs={{0,3},{1,0},{2,1},{3,2},{4,7},{5,4},{6,5},{7,6},{8,11},{9,8},{10,9... | collective-permute-start | bytes 884744 | tf_op jit(solution)/shard_map/ppermute | solution.py:473
  235.9 11.4 %collective-permute-start.50 = (f32[16,768]{1,0:T(8,128)S(1)}, f32[16,768]{1,0:T(8,128)S(1)}, u32[]{:S(2)}, u32[]{:S(2)}) collective-permute-start(f32[16,768]{1,0:T(8,128)S(1)} %add.97), channel_id=1, source_target_pairs={{0,1},{1,0},{2,3},{3,2},{4,5},{5,4},{6,7},{7,6},{8,9},{9,8},{10,11... | collective-permute-start | bytes 147464 | tf_op jit(solution)/shard_map/ppermute | solution.py:468
  253.3 8.9 %collective-permute-start.55 = (bf16[96,1536]{1,0:T(8,128)(2,1)S(1)}, bf16[96,1536]{1,0:T(8,128)(2,1)S(1)}, u32[]{:S(2)}, u32[]{:S(2)}) collective-permute-start(bf16[96,1536]{1,0:T(8,128)(2,1)S(1)} %copy-done.12), channel_id=1, source_target_pairs={{0,16},{16,0},{1,17},{17,1},{2,18},{18,2},{3,19},{19,3},{4,20},{20... | collective-permute-start | bytes 884744 | tf_op jit(solution)/shard_map/ppermute | solution.py:468
  (64 other events, 285.5 us)
